TPU v7x, 32 devices: a whole 2x2x4 slice. The times are simulated.
32 devices in a mesh: gx: 8 (over y, x, core), gy: 4 (over z).
Axes of the slice: x: 2, y: 2, z: 4, core: 2. Of those that a mesh axis runs over, the one named last changes fastest.
Arguments:
- right_side: float32 [3, 32, 16, 128], P(None, 'gx', 'gy'), may hold values from -10 to 10
- node_mass: float32 [32, 16, 128], P('gx', 'gy'), may hold values from 0.5 to 4
- gradients: float32 [8, 4, 8, 3, 27, 128], P('gx', 'gy'), may hold values from -3 to 3
- stiffness: float32 [8, 4, 8, 128], P('gx', 'gy'), may hold values from 0.2 to 2
- valid: int32 [8, 4, 8, 128], P('gx', 'gy'), may hold values 0 or 1
- node_base: int32 [8, 4, 8, 128], P('gx', 'gy'), may hold values from 0 to 2857, as said below
Outputs:
- solution: float32 [3, 32, 16, 128], P(None, 'gx', 'gy')
- residual: float32 [3, 32, 16, 128], P(None, 'gx', 'gy')
Inputs may be any that keep to these rules, and one draw needn't show every extreme that they name: node_base = (i * 6 + j) * 130 + k with 0 <= i < 4, 0 <= j < 4, 0 <= k < 128.
All inputs are finite; a program needn't handle non-finite values. No bound on the sum of `valid` on one device may be relied on, other than what follows from the above.
Results may differ from a plain program's by a relative error of at most 0.00011.
Values sent between devices are 32-bit elements; how exact they have to be, the bound alone decides.
No kernel may reach another device: no remote copies, remote signals or barrier semaphores. Data moves between devices by JAX's collectives and lax.ppermute only.
A program may use at most 64 MiB of HBM per device.

v0:
```python
import jax
import jax.numpy as jnp
from jax import lax
from jax.sharding import PartitionSpec as P

ITERS = 2
SWEEPS = 4


POISSON = 0.3
DAMPING = 0.7
LAPLACE_WEIGHT = 1.0


def padded_2(array, sides, width):
    for axis, dim in sides:
        count, length = (lax.axis_size(axis), array.shape[dim])
        up = [(i, (i + 1) % count) for i in range(count - 1)]
        down = [(j, i) for i, j in up]
        last = lax.slice_in_dim(array, length - width, length, axis=dim)
        leading = lax.slice_in_dim(array, 0, width, axis=dim)
        before = lax.ppermute(last, axis, up)
        after = lax.ppermute(leading, axis, down)
        array = jnp.concatenate([before, array, after], axis=dim)
    return array


def particle_forces(values, gradients, stiffness):
    grad_disp = jnp.einsum(
        "...inp,...jnp->...ijp", values, gradients, precision=lax.Precision.HIGHEST
    )
    strain_trace = grad_disp[..., 0, 0, :] + grad_disp[..., 1, 1, :] + grad_disp[..., 2, 2, :]
    first_lame = stiffness * (POISSON / ((1.0 + POISSON) * (1.0 - 2.0 * POISSON)))
    shear_mod = stiffness * (0.5 / (1.0 + POISSON))
    identity = jnp.eye(3, dtype=values.dtype).reshape(3, 3, 1)
    stress = shear_mod[..., None, None, :] * (grad_disp + jnp.swapaxes(grad_disp, -3, -2))
    stress = stress + identity * (first_lame * strain_trace)[..., None, None, :]
    return jnp.einsum("...ijp,...jnp->...inp", stress, gradients, precision=lax.Precision.HIGHEST)


def grid_from_padded(padded, mass_diag, coupling):
    center = padded[:, 1:-1, 1:-1, 1:-1]
    beside = padded[:, 2:, 1:-1, 1:-1] + padded[:, :-2, 1:-1, 1:-1]
    beside = beside + padded[:, 1:-1, 2:, 1:-1] + padded[:, 1:-1, :-2, 1:-1]
    beside = beside + padded[:, 1:-1, 1:-1, 2:] + padded[:, 1:-1, 1:-1, :-2]
    return mass_diag * center + coupling * (6.0 * center - beside)


def grid_local(nodal, mass_diag, coupling):
    rimmed = padded_2(nodal, (("gx", 1), ("gy", 2)), 1)
    return grid_from_padded(jnp.pad(rimmed, ((0, 0), (0, 0), (0, 0), (1, 1))), mass_diag, coupling)


def grid_coarse(nodal, mass_diag, coupling):
    rimmed = padded_2(nodal, (("gx", 1), ("gy", 2)), 1)
    return grid_from_padded(jnp.pad(rimmed, ((0, 0), (0, 0), (0, 0), (1, 1))), mass_diag, coupling)


def aggregate(nodal):
    dims_in = nodal.shape
    leading = dims_in[:-3]
    blocked = nodal.reshape(
        leading + (dims_in[-3] // 2, 2, dims_in[-2] // 2, 2, dims_in[-1] // 2, 2)
    )
    return blocked.sum(axis=(-5, -3, -1))


def expand(nodal):
    return jnp.repeat(jnp.repeat(jnp.repeat(nodal, 2, axis=-3), 2, axis=-2), 2, axis=-1)


def coarse_sweeps(source, mass_diag, coupling, apply_fn):
    diagonal = mass_diag + 6.0 * coupling
    estimate = DAMPING * source / diagonal
    for sweep_index in range(SWEEPS - 1):
        estimate = (
            estimate + DAMPING * (source - apply_fn(estimate, mass_diag, coupling)) / diagonal
        )
    return estimate


def vcycle(source, masses, depth_index, whole_mass):
    mass_diag = masses[depth_index]
    coupling = LAPLACE_WEIGHT * 2.0**depth_index
    if depth_index == 2:
        return coarse_sweeps(source, mass_diag, coupling, grid_coarse)
    diagonal = mass_diag + 6.0 * coupling
    estimate = DAMPING * source / diagonal
    remainder = source - grid_local(estimate, mass_diag, coupling)
    estimate = estimate + expand(vcycle(aggregate(remainder), masses, depth_index + 1, whole_mass))
    return estimate + DAMPING * (source - grid_local(estimate, mass_diag, coupling)) / diagonal


def compact_bases(node_base, rows_y, rows_z):
    local_z = node_base % (rows_z + 2)
    quotient = node_base // (rows_z + 2)
    local_y = quotient % (rows_y + 2)
    local_x = quotient // (rows_y + 2)
    return (local_x * rows_y + local_y) * rows_z + local_z


def stiffness_local(nodal, gradients, effective, compact):
    rows_x = nodal.shape[1]
    rows_y = nodal.shape[2]
    rows_z = nodal.shape[3]
    node_count = rows_x * rows_y * rows_z
    rimmed = padded_2(nodal, (("gx", 1), ("gy", 2)), 1)
    padded = jnp.pad(rimmed, ((0, 0), (0, 0), (0, 0), (1, 1)))
    shifted = []
    for tile_pos in range(27):
        off_a = tile_pos // 9
        off_b = tile_pos // 3 % 3
        off_c = tile_pos % 3
        window = padded[:, off_a : off_a + rows_x, off_b : off_b + rows_y, off_c : off_c + rows_z]
        shifted.append(window.reshape(3, node_count))
    stacked = jnp.stack(shifted, axis=0).reshape(81, node_count)
    node_iota = jnp.arange(node_count, dtype=jnp.int32)

    def per_block(accumulated, block):
        grad_blk, stiff_blk, base_blk = block
        one_hot = (base_blk[:, None] == node_iota[None, :]).astype(jnp.float32)
        picked = lax.dot_general(
            stacked,
            one_hot,
            (((1,), (1,)), ((), ())),
            precision=lax.Precision.HIGHEST,
            preferred_element_type=jnp.float32,
        )
        values = jnp.swapaxes(picked.reshape(27, 3, -1), 0, 1)
        forces = particle_forces(values, grad_blk, stiff_blk)
        force_rows = jnp.swapaxes(forces, 0, 1).reshape(81, -1)
        accumulated = accumulated + jnp.dot(
            force_rows, one_hot, precision=lax.Precision.HIGHEST, preferred_element_type=jnp.float32
        )
        return (accumulated, None)

    initial = jnp.zeros((81, node_count), jnp.float32)
    summed, unused = lax.scan(per_block, initial, (gradients, effective, compact))
    summed = summed.reshape(27, 3, rows_x, rows_y, rows_z)
    spread = jnp.zeros((3, rows_x + 2, rows_y + 2, rows_z + 2), jnp.float32)
    for tile_pos in range(27):
        off_a = tile_pos // 9
        off_b = tile_pos // 3 % 3
        off_c = tile_pos % 3
        spread = spread.at[
            :, off_a : off_a + rows_x, off_b : off_b + rows_y, off_c : off_c + rows_z
        ].add(summed[tile_pos])
    spread = spread[..., 1:-1]
    rim_pair = jnp.concatenate((spread[:, :1], spread[:, rows_x + 1 :]), axis=1)
    received = padded_2(rim_pair, (("gx", 1),), 1)
    inner_part = spread[:, 1 : rows_x + 1]
    inner_part = inner_part.at[:, 0].add(received[:, 0]).at[:, rows_x - 1].add(received[:, 3])
    rim_pair = jnp.concatenate((inner_part[:, :, :1], inner_part[:, :, rows_y + 1 :]), axis=2)
    received = padded_2(rim_pair, (("gy", 2),), 1)
    inner_part = inner_part[:, :, 1 : rows_y + 1]
    return inner_part.at[:, :, 0].add(received[:, :, 0]).at[:, :, rows_y - 1].add(received[:, :, 3])


def both_inner(residual, precond, applied):
    return lax.psum((jnp.sum(residual * precond), jnp.sum(applied * precond)), ("gx", "gy"))


def per_device(right_side, node_mass, gradients, stiffness, valid, node_base):
    grads_local = gradients[0, 0]
    effective = stiffness[0, 0] * valid[0, 0].astype(jnp.float32)
    compact = compact_bases(node_base[0, 0], right_side.shape[2], right_side.shape[3])
    masses = [node_mass, aggregate(node_mass), aggregate(aggregate(node_mass))]
    whole_mass = None

    def operator(nodal):
        return node_mass * nodal + stiffness_local(nodal, grads_local, effective, compact)

    def precondition(nodal):
        return vcycle(nodal, masses, 0, whole_mass)

    solution = jnp.zeros_like(right_side)
    residual = right_side
    precond = precondition(residual)
    applied = operator(precond)
    inner_now, curvature_sum = both_inner(residual, precond, applied)
    step_size = inner_now / curvature_sum
    direction = precond
    applied_dir = applied
    for iteration in range(ITERS):
        solution = solution + step_size * direction
        residual = residual - step_size * applied_dir
        if iteration + 1 < ITERS:
            precond = precondition(residual)
            applied = operator(precond)
            inner_next, curvature_sum = both_inner(residual, precond, applied)
            ratio_next = inner_next / inner_now
            step_size = inner_next / (curvature_sum - ratio_next * inner_next / step_size)
            direction = precond + ratio_next * direction
            applied_dir = applied + ratio_next * applied_dir
            inner_now = inner_next
    return (solution, residual)


def solution(mesh):
    return jax.shard_map(
        per_device,
        mesh=mesh,
        in_specs=(
            P(None, "gx", "gy", None),
            P("gx", "gy", None),
            P("gx", "gy", None, None, None, None),
            P("gx", "gy", None, None),
            P("gx", "gy", None, None),
            P("gx", "gy", None, None),
        ),
        out_specs=(P(None, "gx", "gy", None), P(None, "gx", "gy", None)),
        check_vma=False,
    )
```

profile of v0, /device:TPU:0, one launch (start us, length us, event | category | flops | bytes accessed | tf_op | source)
XLA Modules:
  0.0 698.7 jit_solution(3392668106007379912)
XLA Ops:
  9.1 5.6 collective-permute-start.3
  25.5 4.8 collective-permute-start.7
  47.2 5.0 collective-permute-start.13
  61.6 5.0 collective-permute-start.17
  76.3 5.0 collective-permute-start.21
  91.6 5.0 collective-permute-start.25
  98.8 4.5 collective-permute-start.27
  105.0 4.9 collective-permute-start.28
  128.2 73.4 %while.84 = (s32[]{:T(128)}, f32[81,2048]{1,0:T(8,128)S(1)}, f32[8,3,27,128]{2,1,3,0:T(4,128)}, f32[8,128]{1,0:T(8,128)S(1)}, s32[8,128]{1,0:T(8,128)S(1)}, /*index=5*/f32[81,2048]{1,0:T(8,128)S(1)}, s32[]{:T(128)}, s32[]{:T(128)}) while((s32[]{:T(128)}, f32[81,2048]{1,0:T(8,128)S(1)}, f32[8,3,27,128]{2,1,3,0:T(4,128)}, ...), condition=%wide.region_10.11_spmd.clone, body=%wide.region_9.10_spmd.clone.sunk | while | flops 511215744 | bytes 3045039 | solution.py:138
  216.5 5.7 scatter-add.215
  288.1 6.0 collective-permute-done.33
  304.3 44.5 %all-reduce.19 = (f32[]{:T(128)}, f32[]{:T(128)}) all-reduce(f32[]{:T(128)} %get-tuple-element.881, f32[]{:T(128)} %get-tuple-element.880), channel_id=1, replica_groups=mesh['gx'=8,'gy'=4] {'gx','gy'}, use_global_device_ids=true, to_apply=%region_8.9 | all-reduce | flops 2 | bytes 16 | tf_op jit(solution)/shard_map/psum | solution.py:160
  371.3 4.6 collective-permute-start.43
  379.0 5.2 collective-permute-start.45
  393.7 5.0 collective-permute-start.49
  408.1 5.0 collective-permute-start.53
  422.8 5.0 collective-permute-start.57
  438.1 5.0 collective-permute-start.61
  451.4 4.6 collective-permute-start.64
  457.4 5.2 collective-permute-done.65
  474.5 73.3 %while.85 = (s32[]{:T(128)}, f32[81,2048]{1,0:T(8,128)S(1)}, f32[8,3,27,128]{2,1,3,0:T(4,128)}, f32[8,128]{1,0:T(8,128)S(1)}, s32[8,128]{1,0:T(8,128)S(1)}, /*index=5*/f32[81,2048]{1,0:T(8,128)S(1)}, s32[]{:T(128)}, s32[]{:T(128)}) while((s32[]{:T(128)}, f32[81,2048]{1,0:T(8,128)S(1)}, f32[8,3,27,128]{2,1,3,0:T(4,128)}, ...), condition=%wide.region_19.20_spmd.clone, body=%wide.region_18.19_spmd.clone.sunk | while | flops 511215744 | bytes 3045039 | solution.py:138
  562.6 5.7 scatter-add.266
  633.9 6.0 collective-permute-done.69
  650.1 43.1 %all-reduce.18 = (f32[]{:T(128)}, f32[]{:T(128)}) all-reduce(f32[]{:T(128)} %get-tuple-element.879, f32[]{:T(128)} %get-tuple-element.878), channel_id=1, replica_groups=mesh['gx'=8,'gy'=4] {'gx','gy'}, use_global_device_ids=true, to_apply=%region_17.18 | all-reduce | flops 2 | bytes 16 | tf_op jit(solution)/shard_map/psum | solution.py:160
  (789 shorter events, 496.9 us)
Async XLA Ops:
  7.8 6.9 collective-permute-start.2
  9.1 6.9 collective-permute-start.3
  24.2 6.1 collective-permute-start.6
  25.5 6.2 collective-permute-start.7
  45.9 6.3 collective-permute-start.12
  60.3 6.3 collective-permute-start.16
  75.0 6.3 collective-permute-start.20
  90.3 6.3 collective-permute-start.24
  98.8 5.9 collective-permute-start.27
  105.0 8.8 %collective-permute-start.28 = (f32[3,1,4,128]{3,2,1,0:T(4,128)S(1)}, f32[3,1,4,128]{3,2,1,0:T(4,128)S(1)}, u32[]{:S(2)}, u32[]{:S(2)}) collective-permute-start(f32[3,1,4,128]{3,2,1,0:T(4,128)S(1)} %get-tuple-element.1054), channel_id=1, source_target_pairs={{0,4},{4,8},{8,12},{12,16},{16,20},{20,24},{24,28},{1,5},{5,9},{9,... | collective-permute-start | bytes 18440 | tf_op jit(solution)/shard_map/ppermute | solution.py:22
  109.8 6.6 collective-permute-start.29
  286.7 7.4 %collective-permute-start.33 = (f32[3,1,6,128]{3,2,1,0:T(8,128)S(1)}, f32[3,1,6,128]{3,2,1,0:T(8,128)S(1)}, u32[]{:S(2)}, u32[]{:S(2)}) collective-permute-start(f32[3,1,6,128]{3,2,1,0:T(8,128)S(1)} %get-tuple-element.990), channel_id=1, source_target_pairs={{4,0},{8,4},{12,8},{16,12},{20,16},{24,20},{28,24},{5,1},{9,5},{13... | collective-permute-start | bytes 27656 | tf_op jit(solution)/shard_map/ppermute | solution.py:23
  370.0 5.9 collective-permute-start.42
  371.3 5.9 collective-permute-start.43
  377.7 6.5 collective-permute-start.44
  379.0 6.0 collective-permute-start.45
  392.4 6.3 collective-permute-start.48
  406.8 6.3 collective-permute-start.52
  421.5 6.3 collective-permute-start.56
  436.8 6.3 collective-permute-start.60
  445.2 5.9 collective-permute-start.63
  451.4 6.0 collective-permute-start.64
  456.1 6.6 collective-permute-start.65
  632.5 7.4 %collective-permute-start.69 = (f32[3,1,6,128]{3,2,1,0:T(8,128)S(1)}, f32[3,1,6,128]{3,2,1,0:T(8,128)S(1)}, u32[]{:S(2)}, u32[]{:S(2)}) collective-permute-start(f32[3,1,6,128]{3,2,1,0:T(8,128)S(1)} %get-tuple-element.970), channel_id=1, source_target_pairs={{4,0},{8,4},{12,8},{16,12},{20,16},{24,20},{28,24},{5,1},{9,5},{13... | collective-permute-start | bytes 27656 | tf_op jit(solution)/shard_map/ppermute | solution.py:23
  (54 other events, 756.7 us)
where the time goes:
time: 708 us; the launch traced here: 699 us
  starting transfers between devices  208 us (29%)
  local copies, waits for them, and re-layouts  188 us (27%)
  matrix products  90.9 us (13%)
  blocking collectives  87.6 us (12%)
  waiting for transfers between devices  64.9 us (9%)
  other arithmetic  48 us (7%)
  between operations  9.48 us (1%)
    ppermute x36, starting transfers between devices, padded_2(): before = lax.ppermute(last, axis, up)  162 us
    scatter-add x50, local copies, waits for them, and re-layouts, stiffness_local(): spread = spread.at[:, off_a:off_a + rows_x, off_b:off_b + rows_y, off_c:o...  151 us
    psum x2, blocking collectives, both_inner(): lax.psum((jnp.sum(residual * precond), jnp.sum(applied * precond)), ('gx'...  87.6 us
    ppermute x36, starting transfers between devices, padded_2(): after = lax.ppermute(leading, axis, down)  46.5 us
    ppermute x36, waiting for transfers between devices, padded_2(): after = lax.ppermute(leading, axis, down)  36.5 us
    dot_general x16, matrix products, particle_forces(): jnp.einsum('...ijp,...jnp->...inp', stress, gradients, precision=lax.Prec...  33.5 us
    mul x16, other arithmetic, particle_forces(): stress = stress + identity * (first_lame * strain_trace)[..., None, None, :]  32.2 us
    dot_general x16, matrix products, particle_forces(): jnp.einsum('...inp,...jnp->...ijp', values, gradients, precision=lax.Prec...  30.9 us
  transfers between devices with their start and end apart: 72, of which 35 were waited for; matrix products, arithmetic and copies ran while one was open for 1% of the time, Pallas kernels for 0%

commit v1 on v0

v1 whole, which is shorter than its diff:
```python
import functools

import jax
import jax.numpy as jnp
from jax import lax
from jax.experimental import pallas as pl
from jax.experimental.pallas import tpu as pltpu
from jax.sharding import PartitionSpec as P

POISSON = 0.3
DAMPING = 0.7
SWEEPS = 4
LANES = 128
BRICK = 4
AXES = ("gx", "gy")
VMEM_BYTES = 40 * 1024 * 1024
F32 = jnp.float32


def pairing_even(count):
    return [(i, i ^ 1) for i in range(count)]


def pairing_odd(count):
    return [(i, (i + 1) % count if i % 2 else (i - 1) % count) for i in range(count)]


def exchange(first, second, axis, count):
    return (
        lax.ppermute(first, axis, pairing_even(count)),
        lax.ppermute(second, axis, pairing_odd(count)),
    )


def lane_index():
    return lax.broadcasted_iota(jnp.int32, (1, LANES), 1)


def as_f32(cond):
    return jnp.where(cond, 1.0, 0.0).astype(F32)


def turn(x, shift):
    return pltpu.roll(x, shift % LANES, x.ndim - 1)


class Place:
    def __init__(self, count_x, count_y):
        self.gx = lax.axis_index("gx")
        self.gy = lax.axis_index("gy")
        self.count_x, self.count_y = count_x, count_y
        flag = lambda cond: jnp.where(cond, 1.0, 0.0).astype(F32)
        self.even_x = flag(self.gx % 2 == 0)
        self.even_y = flag(self.gy % 2 == 0)
        self.in_x = {-1: flag(self.gx > 0), 0: None, 1: flag(self.gx < count_x - 1)}
        self.in_y = {-1: flag(self.gy > 0), 0: None, 1: flag(self.gy < count_y - 1)}

    def keep(self, value, x, y, size):
        side_x = -1 if x < 0 else 1 if x >= size else 0
        side_y = -1 if y < 0 else 1 if y >= size else 0
        if side_x:
            value = value * self.in_x[side_x]
        if side_y:
            value = value * self.in_y[side_y]
        return value


class Shifts:
    def __init__(self):
        lane = lane_index()
        self.low = {d: as_f32(lane >= d) for d in (1, 2, 4)}
        self.high = {d: as_f32(lane < LANES - d) for d in (1, 2, 4)}
        self.even = as_f32(lane % 2 == 0)
        self.odd = 1.0 - self.even
        self.half = as_f32(lane % 4 < 2)

    def beside(self, x, d):
        return turn(x, d) * self.low[d] + turn(x, -d) * self.high[d]

    def pair_sum(self, x):
        t = (x + turn(x, -1)) * self.even
        return t + turn(t, 1)

    def quad_sum(self, x):
        t = (x + turn(x, -2)) * self.half
        return t + turn(t, 2)


def memo(fn):
    kept = {}

    def wrapped(x, y):
        if (x, y) not in kept:
            kept[(x, y)] = fn(x, y)
        return kept[(x, y)]

    return wrapped


def grid_apply(e, mass, coupling, shifts, step):
    def at(x, y):
        c = e(x, y)
        beside = e(x + 1, y) + e(x - 1, y) + e(x, y + 1) + e(x, y - 1) + shifts.beside(c, step)
        return mass(x, y) * c + coupling * (6.0 * c - beside)

    return at


def restriction(r, mass0, weight0, mass1, weight1, place, shifts):
    e0 = memo(lambda x, y: weight0(x, y) * r(x, y))
    g0 = grid_apply(e0, mass0, 1.0, shifts, 1)
    rem0 = memo(lambda x, y: r(x, y) - g0(x, y))

    def r1_at(x, y):
        total = rem0(2 * x, 2 * y) + rem0(2 * x + 1, 2 * y) + rem0(2 * x, 2 * y + 1) + rem0(2 * x + 1, 2 * y + 1)
        return place.keep(shifts.pair_sum(total), x, y, 2)

    r1 = memo(r1_at)
    e1 = memo(lambda x, y: weight1(x, y) * r1(x, y))
    g1 = grid_apply(e1, mass1, 2.0, shifts, 2)
    total = 0.0
    for x in range(2):
        for y in range(2):
            total = total + (r1(x, y) - g1(x, y))
    return r1, shifts.quad_sum(total)


def pack_slot(r1, r2_row, dots_row, shifts):
    top = r1(0, 0) * shifts.even + r1(0, 1) * shifts.odd
    low = r1(1, 0) * shifts.even + r1(1, 1) * shifts.odd
    return jnp.concatenate([top[0:3], r2_row, low[0:3], dots_row], axis=0)


def pack_quads(column):
    lane = lax.broadcasted_iota(jnp.int32, (4, LANES), 1)
    row = lax.broadcasted_iota(jnp.int32, (4, LANES), 0)
    return jnp.sum(column * as_f32(lane % 4 == row), axis=0, keepdims=True)


def unpack_quads(row):
    lane = lax.broadcasted_iota(jnp.int32, (4, LANES), 1)
    index = lax.broadcasted_iota(jnp.int32, (4, LANES), 0)
    x = jnp.broadcast_to(row, (4, LANES)) * as_f32(lane % 4 == index)
    return spread_quads(x, lane)


def spread_quads(x, lane):
    even = as_f32(lane % 2 == 0)
    odd = 1.0 - even
    x = x + turn(x, -1) * even + turn(x, 1) * odd
    half = as_f32(lane % 4 < 2)
    return x + turn(x, -2) * half + turn(x, 2) * (1.0 - half)


def coarse_solve(r2, m2, count_x, count_y):
    rows = count_x * count_y
    lane = lax.broadcasted_iota(jnp.int32, (rows, LANES), 1)
    row = lax.broadcasted_iota(jnp.int32, (rows, LANES), 0)
    column = row % count_y
    z_low, z_high = as_f32(lane >= 4), as_f32(lane < LANES - 4)
    x_low, x_high = as_f32(row >= count_y), as_f32(row < rows - count_y)
    y_low, y_high = as_f32(column > 0), as_f32(column < count_y - 1)
    up = lambda v, k: pltpu.roll(v, k % rows, 0)
    weight = DAMPING / (m2 + 24.0)
    e = weight * r2
    for _ in range(SWEEPS - 1):
        beside = turn(e, 4) * z_low + turn(e, -4) * z_high
        beside = beside + up(e, count_y) * x_low + up(e, -count_y) * x_high
        beside = beside + up(e, 1) * y_low + up(e, -1) * y_high
        e = e + weight * (r2 - (m2 * e + 4.0 * (6.0 * e - beside)))
    return e


def prolongation(r, r1, e2, mass0, weight0, mass1, weight1, place, shifts):
    e1 = memo(lambda x, y: weight1(x, y) * r1(x, y) + e2(x // 2, y // 2))
    g1 = grid_apply(e1, mass1, 2.0, shifts, 2)
    f1 = memo(lambda x, y: place.keep(e1(x, y) + weight1(x, y) * (r1(x, y) - g1(x, y)), x, y, 2))
    e0 = memo(lambda x, y: weight0(x, y) * r(x, y) + f1(x // 2, y // 2))
    g0 = grid_apply(e0, mass0, 1.0, shifts, 1)
    return memo(lambda x, y: place.keep(e0(x, y) + weight0(x, y) * (r(x, y) - g0(x, y)), x, y, BRICK))


def stiffness_apply(z, base_ref, stiff_ref, valid_ref, grad_ref, hot, stack, picked, spread_sums, shifts):
    blocks = grad_ref.shape[0]
    particles = blocks * LANES
    nodes = BRICK * BRICK * LANES

    base = base_ref[...]
    plane = base // (LANES + 2)
    depth = base - plane * (LANES + 2)
    node_xy = (plane // (BRICK + 2)) * BRICK + plane % (BRICK + 2)
    sub = lax.broadcasted_iota(jnp.int32, (LANES, LANES), 0)
    for s in range(blocks):
        depth_s, xy_s = depth[s : s + 1], node_xy[s : s + 1]
        for q in range(BRICK * BRICK):
            wanted = jnp.where(xy_s == q, depth_s, -1)
            hot[q * LANES : (q + 1) * LANES, s * LANES : (s + 1) * LANES] = as_f32(sub == wanted).astype(jnp.bfloat16)

    def halves(x):
        high = x.astype(jnp.bfloat16).astype(F32)
        return jnp.concatenate([high, x - high], axis=0)

    split = {}
    for x in range(BRICK + 2):
        for y in range(BRICK + 2):
            whole = halves(z(x - 1, y - 1))
            split[x, y, 1] = whole
            split[x, y, 0] = turn(whole, 1) * shifts.low[1]
            split[x, y, 2] = turn(whole, -1) * shifts.high[1]
    tiles = [(a, b, c) for a in range(3) for b in range(3) for c in range(3)]
    zero = jnp.zeros((8, LANES), F32)
    for i in range(BRICK):
        for j in range(BRICK):
            q = i * BRICK + j
            parts = [split[i + a, j + b, c] for a, b, c in tiles] + [zero]
            for t in range(0, 28, 2):
                pair = jnp.concatenate([parts[t], parts[t + 1]], axis=0).astype(jnp.bfloat16)
                stack[t * 8 : t * 8 + 16, q * LANES : (q + 1) * LANES] = pair
    picked[...] = jnp.dot(stack[...], hot[...], preferred_element_type=F32)

    first = POISSON / ((1.0 + POISSON) * (1.0 - 2.0 * POISSON))
    shear_of = 0.5 / (1.0 + POISSON)
    row4 = lax.broadcasted_iota(jnp.int32, (8, LANES), 0) % 4
    row_is = [as_f32(row4 == m) for m in range(3)]
    is_high = as_f32(lax.broadcasted_iota(jnp.int32, (8, LANES), 0) < 4)
    wide = lambda row: jnp.broadcast_to(row, (8, LANES))
    for s in range(blocks):
        lanes = slice(s * LANES, (s + 1) * LANES)
        grad = lambda l, t: wide(grad_ref[s, l, t : t + 1, :])
        h = [None] * 3
        for t in range(27):
            value = picked[t * 8 : t * 8 + 8, lanes]
            for l in range(3):
                term = value * grad(l, t)
                h[l] = term if h[l] is None else h[l] + term
        h = [x[0:4] + x[4:8] for x in h]
        h = [[h[l][m : m + 1] for l in range(3)] for m in range(3)]
        effective = stiff_ref[s : s + 1] * valid_ref[s : s + 1].astype(F32)
        shear = effective * shear_of
        bulk = effective * first * (h[0][0] + h[1][1] + h[2][2])
        stress = []
        for l in range(3):
            column = 0.0
            for m in range(3):
                entry = shear * (h[m][l] + h[l][m])
                if l == m:
                    entry = entry + bulk
                column = column + wide(entry) * row_is[m]
            stress.append(column)
        parts = []
        for t in range(28):
            if t < 27:
                f = stress[0] * grad(0, t) + stress[1] * grad(1, t) + stress[2] * grad(2, t)
                high = f.astype(jnp.bfloat16).astype(F32)
                parts.append(is_high * high + (1.0 - is_high) * (f - high))
            else:
                parts.append(zero)
            if t % 2:
                pair = jnp.concatenate(parts, axis=0).astype(jnp.bfloat16)
                stack[t * 8 - 8 : t * 8 + 8, lanes] = pair
                parts = []
    spread_sums[...] = lax.dot_general(
        stack[:, :particles], hot[...], (((1,), (1,)), ((), ())), preferred_element_type=F32
    )
    out = {}
    for x in range(BRICK + 2):
        for y in range(BRICK + 2):
            sums = [0.0, 0.0, 0.0]
            for t, (a, b, c) in enumerate(tiles):
                i, j = x - a, y - b
                if 0 <= i < BRICK and 0 <= j < BRICK:
                    q = i * BRICK + j
                    sums[c] = sums[c] + spread_sums[t * 8 : t * 8 + 8, q * LANES : (q + 1) * LANES]
            total = sums[1] + turn(sums[0], -1) * shifts.high[1] + turn(sums[2], 1) * shifts.low[1]
            out[x - 1, y - 1] = total[0:4] + total[4:8]
    return out


def start_kernel(counts, wide_ref, up_ref, down_ref, r_ref, mass0_ref, weight0_ref, mass1_ref, weight1_ref, slot_ref):
    place, shifts = Place(*counts), Shifts()
    below = (place.in_y[-1] * place.even_y, place.in_y[-1] * (1.0 - place.even_y))
    above = (place.in_y[1] * (1.0 - place.even_y), place.in_y[1] * place.even_y)

    def load(x, y):
        if 0 <= y < BRICK:
            return wide_ref[x + 4, y]
        odd, even = below if y < 0 else above
        return down_ref[x + 4, y % BRICK] * odd + up_ref[x + 4, y % BRICK] * even

    load = memo(load)
    live = as_f32(lax.broadcasted_iota(jnp.int32, (4, LANES), 0) < 3)
    r = memo(lambda x, y: load(x, y) * live)
    mass0 = memo(lambda x, y: jnp.broadcast_to(load(x, y)[3:4], (4, LANES)))
    weight0 = memo(lambda x, y: DAMPING / (mass0(x, y) + 6.0))

    def mass1_at(x, y):
        total = mass0(2 * x, 2 * y) + mass0(2 * x + 1, 2 * y) + mass0(2 * x, 2 * y + 1) + mass0(2 * x + 1, 2 * y + 1)
        return shifts.pair_sum(total)

    mass1 = memo(mass1_at)
    weight1 = memo(lambda x, y: DAMPING / (mass1(x, y) + 12.0))
    r1, r2 = restriction(r, mass0, weight0, mass1, weight1, place, shifts)
    m2 = shifts.quad_sum(mass1(0, 0) + mass1(0, 1) + mass1(1, 0) + mass1(1, 1))
    r2_row = pack_quads(jnp.concatenate([r2[0:3], m2[3:4]], axis=0))
    slot_ref[...] = pack_slot(r1, r2_row, jnp.zeros((1, LANES), F32), shifts)
    for x in range(-3, 7):
        for y in range(-3, 7):
            mass0_ref[x + 3, y + 3] = mass0(x, y)
            weight0_ref[x + 3, y + 3] = weight0(x, y)
            if -2 <= x < 6 and -2 <= y < 6:
                r_ref[x + 2, y + 2] = r(x, y)
    for x in range(-2, 4):
        for y in range(-2, 4):
            mass1_ref[x + 2, y + 2] = mass1(x, y)
            weight1_ref[x + 2, y + 2] = weight1(x, y)


def reader(ref, offset):
    return memo(lambda x, y: ref[x + offset, y + offset])


def cycle_and_apply(place, shifts, r, gathered, mass_rows, fields, particles, scratch):
    count_x, count_y = place.count_x, place.count_y
    mass0, weight0, mass1, weight1 = fields
    coarse, hot, stack, picked, spread_sums = scratch
    bricks = count_x * count_y
    r2 = gathered(3, bricks, 8)
    lane = lax.broadcasted_iota(jnp.int32, (bricks, LANES), 1)
    m2 = spread_quads(mass_rows * as_f32(lane % 4 == 3), lane)
    margin = coarse.shape[0] - bricks
    coarse[...] = jnp.zeros_like(coarse)
    coarse[margin // 2 : margin // 2 + bricks, :] = coarse_solve(r2, m2, count_x, count_y)

    def e2_at(x, y):
        row = (place.gx + x) * count_y + place.gy + y + margin // 2
        return place.keep(unpack_quads(coarse[pl.ds(row, 1), :]), x, y, 1)

    e2 = memo(e2_at)

    def neighbour(x, y):
        other_x = jnp.clip(place.gx + x, 0, count_x - 1)
        other_y = jnp.clip(place.gy + y, 0, count_y - 1)
        row = pl.multiple_of((other_x * count_y + other_y) * 8, 8)
        slot = gathered(row, 8, 1)
        first, second = slot * shifts.even, slot * shifts.odd
        return first + turn(first, 1), second + turn(second, -1)

    neighbour = memo(neighbour)

    def r1_at(x, y):
        both = neighbour(x // 2, y // 2)[y % 2]
        return place.keep(both[4 * (x % 2) : 4 * (x % 2) + 4], x, y, 2)

    r1 = memo(r1_at)
    live = as_f32(lax.broadcasted_iota(jnp.int32, (4, LANES), 0) < 3)
    full = prolongation(r, r1, e2, mass0, weight0, mass1, weight1, place, shifts)
    z = memo(lambda x, y: full(x, y) * live)
    image = stiffness_apply(z, *particles, hot, stack, picked, spread_sums, shifts)
    for x in range(BRICK):
        for y in range(BRICK):
            image[x, y] = image[x, y] + mass0(x, y) * z(x, y)
    return z, image


def total_of(pairs):
    acc = 0.0
    for a, b in pairs:
        acc = acc + a * b
    return jnp.sum(jnp.sum(acc, axis=0, keepdims=True), axis=1, keepdims=True)


def dots_row(*values):
    lane = lane_index()
    row = 0.0
    for k, v in enumerate(values):
        row = row + as_f32(lane == k) * v
    return row


INNER = [(x, y) for x in range(BRICK) for y in range(BRICK)]
RIMMED = [(x, y) for x in range(-1, BRICK + 1) for y in range(-1, BRICK + 1)]


def first_kernel(counts, level_ref, r_ref, mass0_ref, weight0_ref, mass1_ref, weight1_ref,
                 base_ref, stiff_ref, valid_ref, grad_ref, z_ref, image_ref, even_ref, odd_ref, dots_ref, *scratch):
    place, shifts = Place(*counts), Shifts()
    r = reader(r_ref, 2)
    gathered = lambda start, size, stride: level_ref[pl.ds(start, size, stride=stride) if stride > 1 else pl.ds(start, size), :]
    fields = (reader(mass0_ref, 3), reader(weight0_ref, 3), reader(mass1_ref, 2), reader(weight1_ref, 2))
    mass_rows = gathered(3, counts[0] * counts[1], 8)
    particles = (base_ref, stiff_ref, valid_ref, grad_ref)
    z, image = cycle_and_apply(place, shifts, r, gathered, mass_rows, fields, particles, scratch)
    for x, y in INNER:
        z_ref[x, y] = z(x, y)
    for x, y in RIMMED:
        image_ref[x + 1, y + 1] = image[x, y]
    even = place.even_x
    for k in range(4):
        for y in range(-1, BRICK + 1):
            right, left = image[k + 1, y], image[k - 1, y]
            even_ref[k, y + 1] = right * even + left * (1.0 - even)
            odd_ref[k, y + 1] = left * even + right * (1.0 - even)
    rz = total_of((r(x, y), z(x, y)) for x, y in INNER)
    zaz = total_of((image[x, y], z(x, y)) for x, y in RIMMED)
    dots_ref[...] = dots_row(rz, zaz)


def along_x_kernel(counts, image_ref, even_ref, odd_ref, wide_ref, up_ref, down_ref):
    place = Place(*counts)
    left_of = (place.in_x[-1] * place.even_x, place.in_x[-1] * (1.0 - place.even_x))
    right_of = (place.in_x[1] * (1.0 - place.even_x), place.in_x[1] * place.even_x)

    def value(x, y):
        total = None
        if -1 <= x <= 4:
            total = place.keep(image_ref[x + 1, y + 1], x, 0, BRICK)
        if x <= 0:
            part = odd_ref[x + 3, y + 1] * left_of[0] + even_ref[x + 3, y + 1] * left_of[1]
            total = part if total is None else total + part
        if x >= 3:
            part = odd_ref[x - 3, y + 1] * right_of[0] + even_ref[x - 3, y + 1] * right_of[1]
            total = part if total is None else total + part
        return total

    value = memo(value)
    even = place.even_y
    for x in range(-3, 7):
        for y in range(-1, BRICK + 1):
            wide_ref[x + 3, y + 1] = value(x, y)
        for k in range(4):
            above, below = value(x, k + 1), value(x, k - 1)
            up_ref[x + 3, k] = above * even + below * (1.0 - even)
            down_ref[x + 3, k] = below * even + above * (1.0 - even)


def middle_kernel(counts, wide_ref, up_ref, down_ref, mass0_ref, weight0_ref, mass1_ref, weight1_ref, dots_ref,
                  w_ref, slot_ref):
    place, shifts = Place(*counts), Shifts()
    below = (place.in_y[-1] * place.even_y, place.in_y[-1] * (1.0 - place.even_y))
    above = (place.in_y[1] * (1.0 - place.even_y), place.in_y[1] * place.even_y)

    def value(x, y):
        total = None
        if -1 <= y <= 4:
            total = place.keep(wide_ref[x + 3, y + 1], 0, y, BRICK)
        if y <= 0:
            part = down_ref[x + 3, y + 3] * below[0] + up_ref[x + 3, y + 3] * below[1]
            total = part if total is None else total + part
        if y >= 3:
            part = down_ref[x + 3, y - 3] * above[0] + up_ref[x + 3, y - 3] * above[1]
            total = part if total is None else total + part
        return total

    w = memo(value)
    r1, r2 = restriction(w, reader(mass0_ref, 3), reader(weight0_ref, 3), reader(mass1_ref, 2), reader(weight1_ref, 2),
                         place, shifts)
    slot_ref[...] = pack_slot(r1, pack_quads(r2), dots_ref[...], shifts)
    for x in range(-2, 6):
        for y in range(-2, 6):
            w_ref[x + 2, y + 2] = w(x, y)


def sums_of(ref, count, first, stride):
    return jnp.sum(ref[pl.ds(first, count, stride=stride), :], axis=0, keepdims=True)


def second_kernel(counts, level_ref, change_ref, r_ref, w_ref, mass0_ref, weight0_ref, mass1_ref, weight1_ref,
                  base_ref, stiff_ref, valid_ref, grad_ref, z_ref, image_ref, slots_ref, *scratch):
    place, shifts = Place(*counts), Shifts()
    bricks = counts[0] * counts[1]
    sums = sums_of(change_ref, bricks, 7, 8)
    step = sums[:, 0:1] / sums[:, 1:2]
    r = memo(lambda x, y: r_ref[x + 2, y + 2] - step * w_ref[x + 2, y + 2])

    def gathered(start, size, stride):
        rows = pl.ds(start, size, stride=stride) if stride > 1 else pl.ds(start, size)
        return level_ref[rows, :] - step * change_ref[rows, :]

    mass_rows = level_ref[pl.ds(3, bricks, stride=8), :]
    fields = (reader(mass0_ref, 3), reader(weight0_ref, 3), reader(mass1_ref, 2), reader(weight1_ref, 2))
    particles = (base_ref, stiff_ref, valid_ref, grad_ref)
    z, image = cycle_and_apply(place, shifts, r, gathered, mass_rows, fields, particles, scratch)
    for x, y in INNER:
        z_ref[x, y] = z(x, y)
        image_ref[x, y] = image[x, y]
    rz = total_of((r(x, y), z(x, y)) for x, y in INNER)
    zaz = total_of((image[x, y], z(x, y)) for x, y in RIMMED)
    zw = total_of((w_ref[x + 2, y + 2], z(x, y)) for x, y in INNER)
    row = dots_row(rz, zaz, zw)
    filled = jnp.concatenate([jnp.zeros((3, LANES), F32), row] + [jnp.zeros((4, LANES), F32)] * 3, axis=0)

    def fill(k, carry):
        slots_ref[k] = filled
        return carry

    lax.fori_loop(0, bricks, fill, 0)
    for dx in (-1, 0, 1):
        for dy in (-1, 0, 1):
            if dx == 0 and dy == 0:
                continue
            xs = [-1] if dx < 0 else [BRICK] if dx > 0 else range(BRICK)
            ys = [-1] if dy < 0 else [BRICK] if dy > 0 else range(BRICK)
            columns = [image[x, y] for x in xs for y in ys]
            there_x = (place.gx + dx >= 0) & (place.gx + dx < counts[0])
            there_y = (place.gy + dy >= 0) & (place.gy + dy < counts[1])

            @pl.when(there_x & there_y)
            def _(columns=columns, dx=dx, dy=dy):
                other = (place.gx + dx) * counts[1] + place.gy + dy
                for k, column in enumerate(columns):
                    slots_ref[other, 4 * k : 4 * k + 3, :] = column[0:3]


def last_kernel(counts, slots_ref, change_ref, z1_ref, z2_ref, r_ref, w_ref, image_ref, solution_ref, residual_ref):
    place = Place(*counts)
    bricks = counts[0] * counts[1]
    sums1 = sums_of(change_ref, bricks, 7, 8)
    sums2 = sums_of(slots_ref, bricks, 3, 16)
    rz1, zaz1 = sums1[:, 0:1], sums1[:, 1:2]
    rz2, zaz2, zw = sums2[:, 0:1], sums2[:, 1:2], sums2[:, 2:3]
    step1 = rz1 / zaz1
    ratio = rz2 / rz1
    step2 = rz2 / (zaz2 + 2.0 * ratio * zw + ratio * ratio * zaz1)
    image = {(x, y): image_ref[x, y] for x, y in INNER}
    for dx in (-1, 0, 1):
        for dy in (-1, 0, 1):
            if dx == 0 and dy == 0:
                continue
            xs = [0] if dx < 0 else [BRICK - 1] if dx > 0 else range(BRICK)
            ys = [0] if dy < 0 else [BRICK - 1] if dy > 0 else range(BRICK)
            other_x = jnp.clip(place.gx + dx, 0, counts[0] - 1)
            other_y = jnp.clip(place.gy + dy, 0, counts[1] - 1)
            row = pl.multiple_of((other_x * counts[1] + other_y) * 16, 16)
            block = slots_ref[pl.ds(row, 16), :]
            for k, (x, y) in enumerate((x, y) for x in xs for y in ys):
                image[x, y] = image[x, y] + place.keep(block[4 * k : 4 * k + 4], dx, dy, 1)
    for x, y in INNER:
        w = w_ref[x + 2, y + 2]
        z1 = z1_ref[x, y]
        solution = step1 * z1 + step2 * (z2_ref[x, y] + ratio * z1)
        residual = r_ref[x + 2, y + 2] - step1 * w - step2 * (image[x, y] + ratio * w)
        for m in range(3):
            solution_ref[m, x, y : y + 1, :] = solution[m : m + 1]
            residual_ref[m, x, y : y + 1, :] = residual[m : m + 1]


def call(kernel, counts, shapes, *args, scratch=()):
    out = [jax.ShapeDtypeStruct(s, F32) for s in shapes]
    return pl.pallas_call(
        functools.partial(kernel, counts),
        out_shape=out,
        scratch_shapes=scratch,
        compiler_params=pltpu.CompilerParams(vmem_limit_bytes=VMEM_BYTES),
    )(*args)


def per_device(counts, right_side, node_mass, gradients, stiffness, valid, node_base):
    count_x, count_y = counts
    bricks = count_x * count_y
    blocks = gradients.shape[2]
    particles = (node_base[0, 0], stiffness[0, 0], valid[0, 0], gradients[0, 0])
    nodes = BRICK * BRICK * LANES
    scratch = (
        pltpu.VMEM((bricks + 2 * (8 + count_y), LANES), F32),
        pltpu.VMEM((nodes, blocks * LANES), jnp.bfloat16),
        pltpu.VMEM((224, nodes), jnp.bfloat16),
        pltpu.VMEM((224, blocks * LANES), F32),
        pltpu.VMEM((224, nodes), F32),
    )
    gx, gy = lax.axis_index("gx"), lax.axis_index("gy")

    own = jnp.concatenate([right_side, node_mass[None]], axis=0).transpose(1, 2, 0, 3)
    even, odd = exchange(own, own, "gx", count_x)
    is_even = gx % 2 == 0
    left = jnp.where(gx > 0, jnp.where(is_even, odd, even), 0.0)
    right = jnp.where(gx < count_x - 1, jnp.where(is_even, even, odd), 0.0)
    wide = jnp.concatenate([left, own, right], axis=0)
    up, down = exchange(wide, wide, "gy", count_y)
    r, *fields, slot = call(
        start_kernel, counts,
        [(8, 8, 4, LANES), (10, 10, 4, LANES), (10, 10, 4, LANES), (6, 6, 4, LANES), (6, 6, 4, LANES), (8, LANES)],
        wide, up, down,
    )

    def share(slot):
        sent = jnp.broadcast_to(slot[None], (bricks, 8, LANES))
        return lax.all_to_all(sent, AXES, 0, 0).reshape(bricks * 8, LANES)

    level = share(slot)
    z1, image, to_even, to_odd, dots = call(
        first_kernel, counts,
        [(4, 4, 4, LANES), (6, 6, 4, LANES), (4, 6, 4, LANES), (4, 6, 4, LANES), (1, LANES)],
        level, r, *fields, *particles, scratch=scratch,
    )
    even, odd = exchange(to_even, to_odd, "gx", count_x)
    wide, to_up, to_down = call(
        along_x_kernel, counts, [(10, 6, 4, LANES), (10, 4, 4, LANES), (10, 4, 4, LANES)], image, even, odd
    )
    up, down = exchange(to_up, to_down, "gy", count_y)
    w, slot = call(middle_kernel, counts, [(8, 8, 4, LANES), (8, LANES)], wide, up, down, *fields, dots)
    change = share(slot)
    z2, image, slots = call(
        second_kernel, counts, [(4, 4, 4, LANES), (4, 4, 4, LANES), (bricks, 16, LANES)],
        level, change, r, w, *fields, *particles, scratch=scratch,
    )
    slots = lax.all_to_all(slots, AXES, 0, 0).reshape(bricks * 16, LANES)
    return tuple(
        call(last_kernel, counts, [right_side.shape, right_side.shape], slots, change, z1, z2, r, w, image)
    )


def solution(mesh):
    counts = (mesh.shape["gx"], mesh.shape["gy"])
    return jax.shard_map(
        functools.partial(per_device, counts),
        mesh=mesh,
        in_specs=(
            P(None, "gx", "gy", None),
            P("gx", "gy", None),
            P("gx", "gy", None, None, None, None),
            P("gx", "gy", None, None),
            P("gx", "gy", None, None),
            P("gx", "gy", None, None),
        ),
        out_specs=(P(None, "gx", "gy", None), P(None, "gx", "gy", None)),
        check_vma=False,
    )
```

time: 708 us -> 76.3 us (0.11); the launches traced: 699 us -> 76 us
  starting transfers between devices: 208 us -> 14.6 us
  local copies, waits for them, and re-layouts: 188 us -> 2.23 us
  matrix products: 90.9 us -> 0 us
  blocking collectives: 87.6 us -> 22.6 us
  other arithmetic: 48 us -> 0.06 us
  waiting for transfers between devices: 64.9 us -> 23.7 us
  Pallas kernels: 0 us -> 12 us
  between operations: 9.48 us -> 0.75 us
    ppermute x72 -> x8, starting transfers between devices: 208 us -> 10.6 us  [the longest x4 9.98 us: exchange(): lax.ppermute(second, axis, pairing_odd(count))]
    scatter-add x54 -> x0, local copies, waits for them, and re-layouts: 151 us -> none  [the longest x50 151 us: stiffness_local(): spread = spread.at[:, off_a:off_a + rows_x, off_b:off_b + rows_y, off_c:o...]
    dot_general x64 -> x0, matrix products: 90.9 us -> none  [the longest x16 33.5 us: particle_forces(): jnp.einsum('...ijp,...jnp->...inp', stress, gradients, precision=lax.Prec...]
    psum x2 -> x0, blocking collectives: 87.6 us -> none  [both_inner(): lax.psum((jnp.sum(residual * precond), jnp.sum(applied * precond)), ('gx'...]
    ppermute x72 -> x8, waiting for transfers between devices: 64.9 us -> 15.4 us  [the longest x4 10.1 us: exchange(): lax.ppermute(second, axis, pairing_odd(count))]
    mul x33 -> x0, other arithmetic: 32.4 us -> none  [the longest x16 32.2 us: particle_forces(): stress = stress + identity * (first_lame * strain_trace)[..., None, None, :]]
    all_to_all x0 -> x2, blocking collectives: none -> 22.6 us  [the longest x1 11.9 us: per_device(): slots = lax.all_to_all(slots, AXES, 0, 0).reshape(bricks * 16, LANES)]
    dot_general x16 -> x0, local copies, waits for them, and re-layouts: 14.2 us -> none  [particle_forces(): jnp.einsum('...inp,...jnp->...ijp', values, gradients, precision=lax.Prec...]
  transfers between devices with their start and end apart: 72 -> 9, of which waited for: 35 -> 8; matrix products, arithmetic and copies ran while one was open for 1% -> 0% of each run, Pallas kernels for 0% -> 0%
where the time goes in v1:
time: 76.3 us; the launch traced here: 76 us
  waiting for transfers between devices  23.7 us (31%)
  blocking collectives  22.6 us (30%)
  starting transfers between devices  14.6 us (19%)
  Pallas kernels  12 us (16%)
  local copies, waits for them, and re-layouts  2.23 us (3%)
    pallas_call x6, Pallas kernels, call(): pl.pallas_call(functools.partial(kernel, counts), out_shape=out, scratch_...  12 us
    all_to_all x1, blocking collectives, per_device(): slots = lax.all_to_all(slots, AXES, 0, 0).reshape(bricks * 16, LANES)  11.9 us
    all_to_all x1, blocking collectives, share(): return lax.all_to_all(sent, AXES, 0, 0).reshape(bricks * 8, LANES)  10.7 us
    ppermute x4, waiting for transfers between devices, exchange(): lax.ppermute(second, axis, pairing_odd(count))  10.1 us
    ppermute x4, starting transfers between devices, exchange(): lax.ppermute(second, axis, pairing_odd(count))  9.98 us
    all_to_all x1, waiting for transfers between devices, share(): return lax.all_to_all(sent, AXES, 0, 0).reshape(bricks * 8, LANES)  8.32 us
    ppermute x4, waiting for transfers between devices, exchange(): lax.ppermute(first, axis, pairing_even(count))  5.25 us
    all_to_all x1, starting transfers between devices, share(): return lax.all_to_all(sent, AXES, 0, 0).reshape(bricks * 8, LANES)  4.07 us
  transfers between devices with their start and end apart: 9, of which 8 were waited for; matrix products, arithmetic and copies ran while one was open for 0% of the time, Pallas kernels for 0%

profile of v1, /device:TPU:0, one launch (start us, length us, event | category | flops | bytes accessed | tf_op | source)
XLA Modules:
  0.0 76.0 jit_solution(1632476295351946642)
XLA Ops:
  0.6 0.8 copy.8
  1.4 0.5 collective-permute-start.1
  2.0 3.6 %collective-permute-start = (f32[4,4,4,128]{3,2,1,0:T(4,128)S(1)}, f32[4,4,4,128]{3,2,1,0:T(4,128)S(1)}, u32[]{:S(2)}, u32[]{:S(2)}) collective-permute-start(f32[4,4,4,128]{3,2,1,0:T(4,128)S(1)} %maximum_bitcast_fusion), channel_id=1, source_target_pairs={{0,28},{4,8},{8,4},{12,16},{16,12},{20,24},{24,20},{28,0},{1,29},{... | collective-permute-start | bytes 98312 | tf_op jit(solution)/shard_map/ppermute | solution.py:31
  5.5 1.6 %collective-permute-done = f32[4,4,4,128]{3,2,1,0:T(4,128)S(1)} collective-permute-done((f32[4,4,4,128]{3,2,1,0:T(4,128)S(1)}, f32[4,4,4,128]{3,2,1,0:T(4,128)S(1)}, u32[]{:S(2)}, u32[]{:S(2)}) %collective-permute-start) | collective-permute-done | bytes 32800 | tf_op jit(solution)/shard_map/ppermute | solution.py:31
  7.2 3.8 %collective-permute-start.3 = (f32[12,4,4,128]{3,2,1,0:T(4,128)S(1)}, f32[12,4,4,128]{3,2,1,0:T(4,128)S(1)}, u32[]{:S(2)}, u32[]{:S(2)}) collective-permute-start(f32[12,4,4,128]{3,2,1,0:T(4,128)S(1)} %pad_maximum_fusion.wide_ref), channel_id=1, source_target_pairs={{0,3},{1,2},{2,1},{3,0},{4,7},{5,6},{6,5},{7,4},{8,11},{9,10},{10,... | collective-permute-start | bytes 294920 | tf_op jit(solution)/shard_map/ppermute | solution.py:31
  11.0 3.7 %collective-permute-done.3.down_ref = f32[12,4,4,128]{3,2,1,0:T(4,128)S(1)} collective-permute-done((f32[12,4,4,128]{3,2,1,0:T(4,128)S(1)}, f32[12,4,4,128]{3,2,1,0:T(4,128)S(1)}, u32[]{:S(2)}, u32[]{:S(2)}) %collective-permute-start.3) | collective-permute-done | bytes 98336 | tf_op jit(solution)/shard_map/ppermute | solution.py:31
  14.7 1.3 %collective-permute-done.2.up_ref = f32[12,4,4,128]{3,2,1,0:T(4,128)S(1)} collective-permute-done((f32[12,4,4,128]{3,2,1,0:T(4,128)S(1)}, f32[12,4,4,128]{3,2,1,0:T(4,128)S(1)}, u32[]{:S(2)}, u32[]{:S(2)}) %collective-permute-start.2) | collective-permute-done | bytes 98336 | tf_op jit(solution)/shard_map/ppermute | solution.py:30
  16.0 0.5 shard_map.77
  16.6 0.7 broadcast_in_dim.22
  17.2 4.1 %all-to-all-start = ((f32[32,8,128]{2,1,0:T(8,128)}), f32[32,8,128]{2,1,0:T(8,128)S(1)}, u32[]{:S(2)}, u32[]{:S(2)}) async-start(f32[32,8,128]{2,1,0:T(8,128)} %broadcast_in_dim.22), calls=%async_computation | async-start | bytes 262144 | tf_op jit(solution)/shard_map/all_to_all | solution.py:587
  21.4 8.3 %all-to-all-done = f32[32,8,128]{2,1,0:T(8,128)S(1)} async-done(((f32[32,8,128]{2,1,0:T(8,128)}), f32[32,8,128]{2,1,0:T(8,128)S(1)}, u32[]{:S(2)}, u32[]{:S(2)}) %all-to-all-start) | async-done | bytes 131104 | tf_op jit(solution)/shard_map/all_to_all | solution.py:587
  29.7 0.7 copy-done.2
  30.4 4.9 %shard_map.78 = (f32[4,4,4,128]{3,2,1,0:T(4,128)S(1)}, f32[6,6,4,128]{3,2,1,0:T(4,128)S(1)}, f32[4,6,4,128]{3,2,1,0:T(4,128)S(1)}, f32[4,6,4,128]{3,2,1,0:T(4,128)S(1)}, f32[1,128]{1,0:T(1,128)S(1)}) custom-call(f32[256,128]{1,0:T(8,128)S(1)} %bitcast.14, f32[8,8,4,128]{3,2,1,0:T(4,128)S(1)} %get-tuple-element.22.r_ref, ...), custom_call_target="tpu_custom_call" | custom-call | tf_op jit(solution)/shard_map/pallas_call | solution.py:549
  35.3 0.8 %collective-permute-start.5 = (f32[4,6,4,128]{3,2,1,0:T(4,128)S(1)}, f32[4,6,4,128]{3,2,1,0:T(4,128)S(1)}, u32[]{:S(2)}, u32[]{:S(2)}) collective-permute-start(f32[4,6,4,128]{3,2,1,0:T(4,128)S(1)} %get-tuple-element.29), channel_id=1, source_target_pairs={{0,28},{4,8},{8,4},{12,16},{16,12},{20,24},{24,20},{28,0},{1,29},{... | collective-permute-start | bytes 147464 | tf_op jit(solution)/shard_map/ppermute | solution.py:31
  36.2 0.4 collective-permute-done.4.even_ref
  36.6 3.7 %collective-permute-done.5.odd_ref = f32[4,6,4,128]{3,2,1,0:T(4,128)S(1)} collective-permute-done((f32[4,6,4,128]{3,2,1,0:T(4,128)S(1)}, f32[4,6,4,128]{3,2,1,0:T(4,128)S(1)}, u32[]{:S(2)}, u32[]{:S(2)}) %collective-permute-start.5) | collective-permute-done | bytes 49184 | tf_op jit(solution)/shard_map/ppermute | solution.py:31
  40.4 1.7 %collective-permute-start.7 = (f32[10,4,4,128]{3,2,1,0:T(4,128)S(1)}, f32[10,4,4,128]{3,2,1,0:T(4,128)S(1)}, u32[]{:S(2)}, u32[]{:S(2)}) collective-permute-start(f32[10,4,4,128]{3,2,1,0:T(4,128)S(1)} %get-tuple-element.32), channel_id=1, source_target_pairs={{0,3},{1,2},{2,1},{3,0},{4,7},{5,6},{6,5},{7,4},{8,11},{9,10},{10,... | collective-permute-start | bytes 245768 | tf_op jit(solution)/shard_map/ppermute | solution.py:31
  42.2 3.6 %collective-permute-done.6.up_ref = f32[10,4,4,128]{3,2,1,0:T(4,128)S(1)} collective-permute-done((f32[10,4,4,128]{3,2,1,0:T(4,128)S(1)}, f32[10,4,4,128]{3,2,1,0:T(4,128)S(1)}, u32[]{:S(2)}, u32[]{:S(2)}) %collective-permute-start.6) | collective-permute-done | bytes 81952 | tf_op jit(solution)/shard_map/ppermute | solution.py:30
  45.8 1.1 %collective-permute-done.7.down_ref = f32[10,4,4,128]{3,2,1,0:T(4,128)S(1)} collective-permute-done((f32[10,4,4,128]{3,2,1,0:T(4,128)S(1)}, f32[10,4,4,128]{3,2,1,0:T(4,128)S(1)}, u32[]{:S(2)}, u32[]{:S(2)}) %collective-permute-start.7) | collective-permute-done | bytes 81952 | tf_op jit(solution)/shard_map/ppermute | solution.py:31
  46.8 0.5 shard_map.80
  47.3 10.7 %all_to_all.15 = f32[32,8,128]{2,1,0:T(8,128)S(1)} all-to-all(f32[32,8,128]{2,1,0:T(8,128)S(1)} %broadcast_in_dim.23), channel_id=1, replica_groups=mesh['gx'=8,'gy'=4] {'gx','gy'}, dimensions={0} | all-to-all | bytes 262144 | tf_op jit(solution)/shard_map/all_to_all | solution.py:587
  58.1 5.1 %shard_map.81 = (f32[4,4,4,128]{3,2,1,0:T(4,128)S(1)}, f32[4,4,4,128]{3,2,1,0:T(4,128)S(1)}, f32[32,16,128]{2,1,0:T(8,128)S(1)}) custom-call(f32[256,128]{1,0:T(8,128)S(1)} %bitcast.15, f32[256,128]{1,0:T(8,128)S(1)} %bitcast.16, f32[8,8,4,128]{3,2,1,0:T(4,128)S(1)} %get-tuple-element.22.r_ref, f32[8,8,4,128]{3,2,1,0:T(4,128)S(1)} %get-tuple-element.35.w_ref, ...), custom_call_target="tpu_custom_call" | custom-call | tf_op jit(solution)/shard_map/pallas_call | solution.py:549
  63.2 11.9 %all_to_all.16 = f32[32,16,128]{2,1,0:T(8,128)S(1)} all-to-all(f32[32,16,128]{2,1,0:T(8,128)S(1)} %get-tuple-element.36), channel_id=1, replica_groups=mesh['gx'=8,'gy'=4] {'gx','gy'}, dimensions={0} | all-to-all | bytes 524288 | tf_op jit(solution)/shard_map/all_to_all | solution.py:606
  75.1 0.9 %shard_map.82 = (f32[3,4,4,128]{3,2,1,0:T(4,128)}, f32[3,4,4,128]{3,2,1,0:T(4,128)}) custom-call(f32[512,128]{1,0:T(8,128)S(1)} %bitcast.18, f32[256,128]{1,0:T(8,128)S(1)} %bitcast.17, f32[4,4,4,128]{3,2,1,0:T(4,128)S(1)} %get-tuple-element.37.z1_ref, f32[4,4,4,128]{3,2,1,0:T(4,128)S(1)} %get-tuple-element.38.z2_ref, ...), custom_call_target="tpu_custom_call" | custom-call | tf_op jit(solution)/shard_map/pallas_call | solution.py:549
  (19 shorter events, 0.3 us)
Async XLA Ops:
  0.6 0.8 %copy-start.4 = (f32[4,4,128]{2,1,0:T(4,128)S(1)}, f32[4,4,128]{2,1,0:T(4,128)}, u32[]{:S(2)}) copy-start(f32[4,4,128]{2,1,0:T(4,128)} %param.7) | copy-start | bytes 24580
  1.4 4.1 %collective-permute-start.1 = (f32[4,4,4,128]{3,2,1,0:T(4,128)S(1)}, f32[4,4,4,128]{3,2,1,0:T(4,128)S(1)}, u32[]{:S(2)}, u32[]{:S(2)}) collective-permute-start(f32[4,4,4,128]{3,2,1,0:T(4,128)S(1)} %maximum_bitcast_fusion), channel_id=1, source_target_pairs={{0,4},{4,0},{8,12},{12,8},{16,20},{20,16},{24,28},{28,24},{1,5},{5... | collective-permute-start | bytes 98312 | tf_op jit(solution)/shard_map/ppermute | solution.py:30
  2.0 5.2 %collective-permute-start = (f32[4,4,4,128]{3,2,1,0:T(4,128)S(1)}, f32[4,4,4,128]{3,2,1,0:T(4,128)S(1)}, u32[]{:S(2)}, u32[]{:S(2)}) collective-permute-start(f32[4,4,4,128]{3,2,1,0:T(4,128)S(1)} %maximum_bitcast_fusion), channel_id=1, source_target_pairs={{0,28},{4,8},{8,4},{12,16},{16,12},{20,24},{24,20},{28,0},{1,29},{... | collective-permute-start | bytes 98312 | tf_op jit(solution)/shard_map/ppermute | solution.py:31
  7.2 14.2 %copy-start.3 = (f32[1,1,8,3,27,128]{5,2,4,3,1,0:T(8,128)S(1)}, f32[1,1,8,3,27,128]{5,2,4,3,1,0:T(8,128)}, u32[]{:S(2)}) copy-start(f32[1,1,8,3,27,128]{5,2,4,3,1,0:T(8,128)} %param.8) | copy-start | bytes 995332
  7.2 7.6 %collective-permute-start.3 = (f32[12,4,4,128]{3,2,1,0:T(4,128)S(1)}, f32[12,4,4,128]{3,2,1,0:T(4,128)S(1)}, u32[]{:S(2)}, u32[]{:S(2)}) collective-permute-start(f32[12,4,4,128]{3,2,1,0:T(4,128)S(1)} %pad_maximum_fusion.wide_ref), channel_id=1, source_target_pairs={{0,3},{1,2},{2,1},{3,0},{4,7},{5,6},{6,5},{7,4},{8,11},{9,10},{10,... | collective-permute-start | bytes 294920 | tf_op jit(solution)/shard_map/ppermute | solution.py:31
  11.0 5.0 %collective-permute-start.2 = (f32[12,4,4,128]{3,2,1,0:T(4,128)S(1)}, f32[12,4,4,128]{3,2,1,0:T(4,128)S(1)}, u32[]{:S(2)}, u32[]{:S(2)}) collective-permute-start(f32[12,4,4,128]{3,2,1,0:T(4,128)S(1)} %pad_maximum_fusion.wide_ref), channel_id=1, source_target_pairs={{0,1},{1,0},{2,3},{3,2},{4,5},{5,4},{6,7},{7,6},{8,9},{9,8},{10,11... | collective-permute-start | bytes 294920 | tf_op jit(solution)/shard_map/ppermute | solution.py:30
  17.2 12.5 %all-to-all-start = ((f32[32,8,128]{2,1,0:T(8,128)}), f32[32,8,128]{2,1,0:T(8,128)S(1)}, u32[]{:S(2)}, u32[]{:S(2)}) async-start(f32[32,8,128]{2,1,0:T(8,128)} %broadcast_in_dim.22), calls=%async_computation | async-start | bytes 262144 | tf_op jit(solution)/shard_map/all_to_all | solution.py:587
  29.7 0.7 copy-start.2
  29.7 0.7 copy-start.1
  29.7 0.7 copy-start
  35.3 1.2 %collective-permute-start.4 = (f32[4,6,4,128]{3,2,1,0:T(4,128)S(1)}, f32[4,6,4,128]{3,2,1,0:T(4,128)S(1)}, u32[]{:S(2)}, u32[]{:S(2)}) collective-permute-start(f32[4,6,4,128]{3,2,1,0:T(4,128)S(1)} %get-tuple-element.28), channel_id=1, source_target_pairs={{0,4},{4,0},{8,12},{12,8},{16,20},{20,16},{24,28},{28,24},{1,5},{5... | collective-permute-start | bytes 147464 | tf_op jit(solution)/shard_map/ppermute | solution.py:30
  35.3 4.9 %collective-permute-start.5 = (f32[4,6,4,128]{3,2,1,0:T(4,128)S(1)}, f32[4,6,4,128]{3,2,1,0:T(4,128)S(1)}, u32[]{:S(2)}, u32[]{:S(2)}) collective-permute-start(f32[4,6,4,128]{3,2,1,0:T(4,128)S(1)} %get-tuple-element.29), channel_id=1, source_target_pairs={{0,28},{4,8},{8,4},{12,16},{16,12},{20,24},{24,20},{28,0},{1,29},{... | collective-permute-start | bytes 147464 | tf_op jit(solution)/shard_map/ppermute | solution.py:31
  40.4 5.4 %collective-permute-start.6 = (f32[10,4,4,128]{3,2,1,0:T(4,128)S(1)}, f32[10,4,4,128]{3,2,1,0:T(4,128)S(1)}, u32[]{:S(2)}, u32[]{:S(2)}) collective-permute-start(f32[10,4,4,128]{3,2,1,0:T(4,128)S(1)} %get-tuple-element.31), channel_id=1, source_target_pairs={{0,1},{1,0},{2,3},{3,2},{4,5},{5,4},{6,7},{7,6},{8,9},{9,8},{10,11... | collective-permute-start | bytes 245768 | tf_op jit(solution)/shard_map/ppermute | solution.py:30
  40.4 6.4 %collective-permute-start.7 = (f32[10,4,4,128]{3,2,1,0:T(4,128)S(1)}, f32[10,4,4,128]{3,2,1,0:T(4,128)S(1)}, u32[]{:S(2)}, u32[]{:S(2)}) collective-permute-start(f32[10,4,4,128]{3,2,1,0:T(4,128)S(1)} %get-tuple-element.32), channel_id=1, source_target_pairs={{0,3},{1,2},{2,1},{3,0},{4,7},{5,6},{6,5},{7,4},{8,11},{9,10},{10,... | collective-permute-start | bytes 245768 | tf_op jit(solution)/shard_map/ppermute | solution.py:31

commit v2 on v1

--- a/solution.py
+++ b/solution.py
@@ -13,23 +13,45 @@
 LANES = 128
 BRICK = 4
 AXES = ("gx", "gy")
-VMEM_BYTES = 40 * 1024 * 1024
+VMEM_BYTES = 24 * 1024 * 1024
 F32 = jnp.float32
 
 
-def pairing_even(count):
-    return [(i, i ^ 1) for i in range(count)]
-
-
-def pairing_odd(count):
-    return [(i, (i + 1) % count if i % 2 else (i - 1) % count) for i in range(count)]
-
-
-def exchange(first, second, axis, count):
-    return (
-        lax.ppermute(first, axis, pairing_even(count)),
-        lax.ppermute(second, axis, pairing_odd(count)),
-    )
+def pairings(axis, counts):
+    count_x, count_y = counts
+    even, odd = [], []
+    for x in range(count_x):
+        for y in range(count_y):
+            k, count = (x, count_x) if axis == "gx" else (y, count_y)
+            move = lambda to: (to, y) if axis == "gx" else (x, to)
+            even.append(((x, y), move(k ^ 1)))
+            if 0 < k < count - 1:
+                odd.append(((x, y), move(k + 1 if k % 2 else k - 1)))
+            else:
+                odd.append(((x, y), (x, y ^ 1) if axis == "gx" else (x ^ 1, y)))
+    flat = lambda pairs: [(a * count_y + b, c * count_y + d) for (a, b), (c, d) in pairs]
+    return flat(even), flat(odd)
+
+
+def exchange(first, second, axis, counts):
+    even, odd = pairings(axis, counts)
+    return lax.ppermute(first, AXES, even), lax.ppermute(second, AXES, odd)
+
+
+SIDE = (
+    [(x, -1) for x in range(-2, 6)] + [(x, -2) for x in range(-1, 5)] + [(x, -3) for x in range(4)]
+)
+SIDE_MASS = [(x, y) for y in (-1, -2) for x in range(-4, 8)] + [(x, y) for y in (-3, -4) for x in range(-2, 6)]
+SIDE_IMAGE = [(x, 0) for x in range(-3, 7)] + SIDE
+SIDE_X = [(x, y) for x in range(-3, 1) for y in range(-1, 5)]
+
+
+def mirror(x, y):
+    return x, BRICK - 1 - y
+
+
+def mirror_x(x, y):
+    return BRICK - 1 - x, y
 
 
 def lane_index():
@@ -180,21 +202,23 @@
     return memo(lambda x, y: place.keep(e0(x, y) + weight0(x, y) * (r(x, y) - g0(x, y)), x, y, BRICK))
 
 
-def stiffness_apply(z, base_ref, stiff_ref, valid_ref, grad_ref, hot, stack, picked, spread_sums, shifts):
-    blocks = grad_ref.shape[0]
-    particles = blocks * LANES
-    nodes = BRICK * BRICK * LANES
-
+def one_hot_kernel(counts, base_ref, grad_in_ref, hot_ref, grad_ref):
+    grad_ref[...] = grad_in_ref[...]
     base = base_ref[...]
     plane = base // (LANES + 2)
     depth = base - plane * (LANES + 2)
     node_xy = (plane // (BRICK + 2)) * BRICK + plane % (BRICK + 2)
     sub = lax.broadcasted_iota(jnp.int32, (LANES, LANES), 0)
-    for s in range(blocks):
+    for s in range(base_ref.shape[0]):
         depth_s, xy_s = depth[s : s + 1], node_xy[s : s + 1]
         for q in range(BRICK * BRICK):
             wanted = jnp.where(xy_s == q, depth_s, -1)
-            hot[q * LANES : (q + 1) * LANES, s * LANES : (s + 1) * LANES] = as_f32(sub == wanted).astype(jnp.bfloat16)
+            hot_ref[q * LANES : (q + 1) * LANES, s * LANES : (s + 1) * LANES] = as_f32(sub == wanted).astype(jnp.bfloat16)
+
+
+def stiffness_apply(z, hot, stiff_ref, valid_ref, grad_ref, stack, picked, spread_sums, shifts):
+    blocks = grad_ref.shape[0]
+    particles = blocks * LANES
 
     def halves(x):
         high = x.astype(jnp.bfloat16).astype(F32)
@@ -276,21 +300,78 @@
     return out
 
 
-def start_kernel(counts, wide_ref, up_ref, down_ref, r_ref, mass0_ref, weight0_ref, mass1_ref, weight1_ref, slot_ref):
+def side_parts(even_ref, odd_ref, is_even, inside_low, inside_high):
+    odd = 1.0 - is_even
+    below_odd, below_even = inside_low * is_even, inside_low * odd
+    above_odd, above_even = inside_high * odd, inside_high * is_even
+
+    def below(row, size):
+        return odd_ref[row : row + size, :] * below_odd + even_ref[row : row + size, :] * below_even
+
+    def above(row, size):
+        return odd_ref[row : row + size, :] * above_odd + even_ref[row : row + size, :] * above_even
+
+    return below, above
+
+
+def put_sides(to_even_ref, to_odd_ref, row, size, up, down, is_even):
+    odd = 1.0 - is_even
+    to_even_ref[row : row + size, :] = (up * is_even + down * odd)[0:size]
+    to_odd_ref[row : row + size, :] = (down * is_even + up * odd)[0:size]
+
+
+def clear_tail(*refs):
+    for ref in refs:
+        ref[ref.shape[0] - 8 :, :] = jnp.zeros((8, LANES), F32)
+
+
+def widen_kernel(counts, own_ref, even_ref, odd_ref, wide_ref, to_even_ref, to_odd_ref):
+    place = Place(*counts)
+    odd_x = 1.0 - place.even_x
+    left = (place.in_x[-1] * place.even_x, place.in_x[-1] * odd_x)
+    right = (place.in_x[1] * odd_x, place.in_x[1] * place.even_x)
+
+    def value(x, y):
+        if 0 <= x < BRICK:
+            return own_ref[x, y]
+        odd, even = left if x < 0 else right
+        return odd_ref[x % BRICK, y] * odd + even_ref[x % BRICK, y] * even
+
+    value = memo(value)
+    for x in range(-4, 8):
+        for y in range(BRICK):
+            wide_ref[x + 4, y] = value(x, y)
+    clear_tail(to_even_ref, to_odd_ref)
+    for k, (x, y) in enumerate(SIDE):
+        put_sides(to_even_ref, to_odd_ref, 3 * k, 3, value(x, y + 4), value(x, -1 - y), place.even_y)
+    first = 3 * len(SIDE)
+    for k, (x, y) in enumerate(SIDE_MASS):
+        put_sides(to_even_ref, to_odd_ref, first + k, 1, value(x, y + 4)[3:4], value(x, -1 - y)[3:4], place.even_y)
+
+
+def start_kernel(counts, wide_ref, even_ref, odd_ref, r_ref, mass0_ref, weight0_ref, mass1_ref, weight1_ref, slot_ref):
     place, shifts = Place(*counts), Shifts()
-    below = (place.in_y[-1] * place.even_y, place.in_y[-1] * (1.0 - place.even_y))
-    above = (place.in_y[1] * (1.0 - place.even_y), place.in_y[1] * place.even_y)
-
-    def load(x, y):
+    below, above = side_parts(even_ref, odd_ref, place.even_y, place.in_y[-1], place.in_y[1])
+    live = as_f32(lax.broadcasted_iota(jnp.int32, (4, LANES), 0) < 3)
+    zero = jnp.zeros((4, LANES), F32)
+
+    def r_at(x, y):
         if 0 <= y < BRICK:
-            return wide_ref[x + 4, y]
-        odd, even = below if y < 0 else above
-        return down_ref[x + 4, y % BRICK] * odd + up_ref[x + 4, y % BRICK] * even
-
-    load = memo(load)
-    live = as_f32(lax.broadcasted_iota(jnp.int32, (4, LANES), 0) < 3)
-    r = memo(lambda x, y: load(x, y) * live)
-    mass0 = memo(lambda x, y: jnp.broadcast_to(load(x, y)[3:4], (4, LANES)))
+            return wide_ref[x + 4, y] * live
+        part = below if y < 0 else above
+        key = (x, y) if y < 0 else mirror(x, y)
+        return part(3 * SIDE.index(key), 4) * live if key in SIDE else zero
+
+    def mass0_at(x, y):
+        if 0 <= y < BRICK:
+            return jnp.broadcast_to(wide_ref[x + 4, y, 3:4, :], (4, LANES))
+        part = below if y < 0 else above
+        key = (x, y) if y < 0 else mirror(x, y)
+        if key not in SIDE_MASS:
+            return zero
+        return jnp.broadcast_to(part(3 * len(SIDE) + SIDE_MASS.index(key), 1), (4, LANES))
+
+    r, mass0 = memo(r_at), memo(mass0_at)
     weight0 = memo(lambda x, y: DAMPING / (mass0(x, y) + 6.0))
 
     def mass1_at(x, y):
@@ -322,7 +403,7 @@
 def cycle_and_apply(place, shifts, r, gathered, mass_rows, fields, particles, scratch):
     count_x, count_y = place.count_x, place.count_y
     mass0, weight0, mass1, weight1 = fields
-    coarse, hot, stack, picked, spread_sums = scratch
+    coarse, stack, picked, spread_sums = scratch
     bricks = count_x * count_y
     r2 = gathered(3, bricks, 8)
     lane = lax.broadcasted_iota(jnp.int32, (bricks, LANES), 1)
@@ -355,7 +436,7 @@
     live = as_f32(lax.broadcasted_iota(jnp.int32, (4, LANES), 0) < 3)
     full = prolongation(r, r1, e2, mass0, weight0, mass1, weight1, place, shifts)
     z = memo(lambda x, y: full(x, y) * live)
-    image = stiffness_apply(z, *particles, hot, stack, picked, spread_sums, shifts)
+    image = stiffness_apply(z, *particles, stack, picked, spread_sums, shifts)
     for x in range(BRICK):
         for y in range(BRICK):
             image[x, y] = image[x, y] + mass0(x, y) * z(x, y)
@@ -382,74 +463,64 @@
 
 
 def first_kernel(counts, level_ref, r_ref, mass0_ref, weight0_ref, mass1_ref, weight1_ref,
-                 base_ref, stiff_ref, valid_ref, grad_ref, z_ref, image_ref, even_ref, odd_ref, dots_ref, *scratch):
+                 hot_ref, stiff_ref, valid_ref, grad_ref, z_ref, image_ref, even_ref, odd_ref, dots_ref, *scratch):
     place, shifts = Place(*counts), Shifts()
     r = reader(r_ref, 2)
     gathered = lambda start, size, stride: level_ref[pl.ds(start, size, stride=stride) if stride > 1 else pl.ds(start, size), :]
     fields = (reader(mass0_ref, 3), reader(weight0_ref, 3), reader(mass1_ref, 2), reader(weight1_ref, 2))
     mass_rows = gathered(3, counts[0] * counts[1], 8)
-    particles = (base_ref, stiff_ref, valid_ref, grad_ref)
+    particles = (hot_ref, stiff_ref, valid_ref, grad_ref)
     z, image = cycle_and_apply(place, shifts, r, gathered, mass_rows, fields, particles, scratch)
     for x, y in INNER:
         z_ref[x, y] = z(x, y)
     for x, y in RIMMED:
         image_ref[x + 1, y + 1] = image[x, y]
-    even = place.even_x
-    for k in range(4):
-        for y in range(-1, BRICK + 1):
-            right, left = image[k + 1, y], image[k - 1, y]
-            even_ref[k, y + 1] = right * even + left * (1.0 - even)
-            odd_ref[k, y + 1] = left * even + right * (1.0 - even)
+    clear_tail(even_ref, odd_ref)
+    for k, (x, y) in enumerate(SIDE_X):
+        put_sides(even_ref, odd_ref, 3 * k, 3, image[x + 4, y], image[-1 - x, y], place.even_x)
     rz = total_of((r(x, y), z(x, y)) for x, y in INNER)
     zaz = total_of((image[x, y], z(x, y)) for x, y in RIMMED)
     dots_ref[...] = dots_row(rz, zaz)
 
 
-def along_x_kernel(counts, image_ref, even_ref, odd_ref, wide_ref, up_ref, down_ref):
+def along_x_kernel(counts, image_ref, even_ref, odd_ref, wide_ref, to_even_ref, to_odd_ref):
     place = Place(*counts)
-    left_of = (place.in_x[-1] * place.even_x, place.in_x[-1] * (1.0 - place.even_x))
-    right_of = (place.in_x[1] * (1.0 - place.even_x), place.in_x[1] * place.even_x)
+    left, right = side_parts(even_ref, odd_ref, place.even_x, place.in_x[-1], place.in_x[1])
 
     def value(x, y):
         total = None
         if -1 <= x <= 4:
             total = place.keep(image_ref[x + 1, y + 1], x, 0, BRICK)
-        if x <= 0:
-            part = odd_ref[x + 3, y + 1] * left_of[0] + even_ref[x + 3, y + 1] * left_of[1]
-            total = part if total is None else total + part
-        if x >= 3:
-            part = odd_ref[x - 3, y + 1] * right_of[0] + even_ref[x - 3, y + 1] * right_of[1]
-            total = part if total is None else total + part
+        for part, key in ((left, (x, y)), (right, mirror_x(x, y))):
+            if key in SIDE_X:
+                more = part(3 * SIDE_X.index(key), 4)
+                total = more if total is None else total + more
         return total
 
     value = memo(value)
-    even = place.even_y
     for x in range(-3, 7):
         for y in range(-1, BRICK + 1):
             wide_ref[x + 3, y + 1] = value(x, y)
-        for k in range(4):
-            above, below = value(x, k + 1), value(x, k - 1)
-            up_ref[x + 3, k] = above * even + below * (1.0 - even)
-            down_ref[x + 3, k] = below * even + above * (1.0 - even)
-
-
-def middle_kernel(counts, wide_ref, up_ref, down_ref, mass0_ref, weight0_ref, mass1_ref, weight1_ref, dots_ref,
+    clear_tail(to_even_ref, to_odd_ref)
+    for k, (x, y) in enumerate(SIDE_IMAGE):
+        put_sides(to_even_ref, to_odd_ref, 3 * k, 3, value(x, y + 4), value(x, -1 - y), place.even_y)
+
+
+def middle_kernel(counts, wide_ref, even_ref, odd_ref, mass0_ref, weight0_ref, mass1_ref, weight1_ref, dots_ref,
                   w_ref, slot_ref):
     place, shifts = Place(*counts), Shifts()
-    below = (place.in_y[-1] * place.even_y, place.in_y[-1] * (1.0 - place.even_y))
-    above = (place.in_y[1] * (1.0 - place.even_y), place.in_y[1] * place.even_y)
+    below, above = side_parts(even_ref, odd_ref, place.even_y, place.in_y[-1], place.in_y[1])
+    live = as_f32(lax.broadcasted_iota(jnp.int32, (4, LANES), 0) < 3)
 
     def value(x, y):
         total = None
         if -1 <= y <= 4:
             total = place.keep(wide_ref[x + 3, y + 1], 0, y, BRICK)
-        if y <= 0:
-            part = down_ref[x + 3, y + 3] * below[0] + up_ref[x + 3, y + 3] * below[1]
-            total = part if total is None else total + part
-        if y >= 3:
-            part = down_ref[x + 3, y - 3] * above[0] + up_ref[x + 3, y - 3] * above[1]
-            total = part if total is None else total + part
-        return total
+        for part, key in ((below, (x, y)), (above, mirror(x, y))):
+            if key in SIDE_IMAGE:
+                more = part(3 * SIDE_IMAGE.index(key), 4)
+                total = more if total is None else total + more
+        return jnp.zeros((4, LANES), F32) if total is None else total * live
 
     w = memo(value)
     r1, r2 = restriction(w, reader(mass0_ref, 3), reader(weight0_ref, 3), reader(mass1_ref, 2), reader(weight1_ref, 2),
@@ -465,7 +536,7 @@
 
 
 def second_kernel(counts, level_ref, change_ref, r_ref, w_ref, mass0_ref, weight0_ref, mass1_ref, weight1_ref,
-                  base_ref, stiff_ref, valid_ref, grad_ref, z_ref, image_ref, slots_ref, *scratch):
+                  hot_ref, stiff_ref, valid_ref, grad_ref, z_ref, image_ref, slots_ref, *scratch):
     place, shifts = Place(*counts), Shifts()
     bricks = counts[0] * counts[1]
     sums = sums_of(change_ref, bricks, 7, 8)
@@ -478,7 +549,7 @@
 
     mass_rows = level_ref[pl.ds(3, bricks, stride=8), :]
     fields = (reader(mass0_ref, 3), reader(weight0_ref, 3), reader(mass1_ref, 2), reader(weight1_ref, 2))
-    particles = (base_ref, stiff_ref, valid_ref, grad_ref)
+    particles = (hot_ref, stiff_ref, valid_ref, grad_ref)
     z, image = cycle_and_apply(place, shifts, r, gathered, mass_rows, fields, particles, scratch)
     for x, y in INNER:
         z_ref[x, y] = z(x, y)
@@ -487,10 +558,11 @@
     zaz = total_of((image[x, y], z(x, y)) for x, y in RIMMED)
     zw = total_of((w_ref[x + 2, y + 2], z(x, y)) for x, y in INNER)
     row = dots_row(rz, zaz, zw)
-    filled = jnp.concatenate([jnp.zeros((3, LANES), F32), row] + [jnp.zeros((4, LANES), F32)] * 3, axis=0)
+    none = jnp.zeros((12, 1, LANES), F32)
 
     def fill(k, carry):
-        slots_ref[k] = filled
+        slots_ref[k, 0:12] = none
+        slots_ref[k, 12] = row
         return carry
 
     lax.fori_loop(0, bricks, fill, 0)
@@ -508,14 +580,15 @@
             def _(columns=columns, dx=dx, dy=dy):
                 other = (place.gx + dx) * counts[1] + place.gy + dy
                 for k, column in enumerate(columns):
-                    slots_ref[other, 4 * k : 4 * k + 3, :] = column[0:3]
+                    for m in range(3):
+                        slots_ref[other, 3 * k + m] = column[m : m + 1]
 
 
 def last_kernel(counts, slots_ref, change_ref, z1_ref, z2_ref, r_ref, w_ref, image_ref, solution_ref, residual_ref):
     place = Place(*counts)
     bricks = counts[0] * counts[1]
     sums1 = sums_of(change_ref, bricks, 7, 8)
-    sums2 = sums_of(slots_ref, bricks, 3, 16)
+    sums2 = jnp.sum(slots_ref[:, 12], axis=0)
     rz1, zaz1 = sums1[:, 0:1], sums1[:, 1:2]
     rz2, zaz2, zw = sums2[:, 0:1], sums2[:, 1:2], sums2[:, 2:3]
     step1 = rz1 / zaz1
@@ -530,10 +603,10 @@
             ys = [0] if dy < 0 else [BRICK - 1] if dy > 0 else range(BRICK)
             other_x = jnp.clip(place.gx + dx, 0, counts[0] - 1)
             other_y = jnp.clip(place.gy + dy, 0, counts[1] - 1)
-            row = pl.multiple_of((other_x * counts[1] + other_y) * 16, 16)
-            block = slots_ref[pl.ds(row, 16), :]
+            other = other_x * counts[1] + other_y
             for k, (x, y) in enumerate((x, y) for x in xs for y in ys):
-                image[x, y] = image[x, y] + place.keep(block[4 * k : 4 * k + 4], dx, dy, 1)
+                rows = [slots_ref[other, 3 * k + m] for m in range(3)] + [jnp.zeros((1, LANES), F32)]
+                image[x, y] = image[x, y] + place.keep(jnp.concatenate(rows, axis=0), dx, dy, 1)
     for x, y in INNER:
         w = w_ref[x + 2, y + 2]
         z1 = z1_ref[x, y]
@@ -545,7 +618,7 @@
 
 
 def call(kernel, counts, shapes, *args, scratch=()):
-    out = [jax.ShapeDtypeStruct(s, F32) for s in shapes]
+    out = [jax.ShapeDtypeStruct(*s) if isinstance(s[0], tuple) else jax.ShapeDtypeStruct(s, F32) for s in shapes]
     return pl.pallas_call(
         functools.partial(kernel, counts),
         out_shape=out,
@@ -555,31 +628,31 @@
 
 
 def per_device(counts, right_side, node_mass, gradients, stiffness, valid, node_base):
-    count_x, count_y = counts
-    bricks = count_x * count_y
+    bricks = counts[0] * counts[1]
     blocks = gradients.shape[2]
-    particles = (node_base[0, 0], stiffness[0, 0], valid[0, 0], gradients[0, 0])
     nodes = BRICK * BRICK * LANES
     scratch = (
-        pltpu.VMEM((bricks + 2 * (8 + count_y), LANES), F32),
-        pltpu.VMEM((nodes, blocks * LANES), jnp.bfloat16),
+        pltpu.VMEM((bricks + 2 * (8 + counts[1]), LANES), F32),
         pltpu.VMEM((224, nodes), jnp.bfloat16),
         pltpu.VMEM((224, blocks * LANES), F32),
         pltpu.VMEM((224, nodes), F32),
     )
-    gx, gy = lax.axis_index("gx"), lax.axis_index("gy")
+    rows = lambda columns, more=0: (-(-(3 * len(columns) + more + 1) // 8) * 8, LANES)
 
     own = jnp.concatenate([right_side, node_mass[None]], axis=0).transpose(1, 2, 0, 3)
-    even, odd = exchange(own, own, "gx", count_x)
-    is_even = gx % 2 == 0
-    left = jnp.where(gx > 0, jnp.where(is_even, odd, even), 0.0)
-    right = jnp.where(gx < count_x - 1, jnp.where(is_even, even, odd), 0.0)
-    wide = jnp.concatenate([left, own, right], axis=0)
-    up, down = exchange(wide, wide, "gy", count_y)
+    even, odd = exchange(own, own, "gx", counts)
+    side = rows(SIDE, len(SIDE_MASS))
+    wide, to_even, to_odd = call(widen_kernel, counts, [(12, 4, 4, LANES), side, side], own, even, odd)
+    even, odd = exchange(to_even, to_odd, "gy", counts)
+    hot, grads = call(
+        one_hot_kernel, counts, [((nodes, blocks * LANES), jnp.bfloat16), gradients.shape[2:]],
+        node_base[0, 0], gradients[0, 0],
+    )
+    particles = (hot, stiffness[0, 0], valid[0, 0], grads)
     r, *fields, slot = call(
         start_kernel, counts,
         [(8, 8, 4, LANES), (10, 10, 4, LANES), (10, 10, 4, LANES), (6, 6, 4, LANES), (6, 6, 4, LANES), (8, LANES)],
-        wide, up, down,
+        wide, even, odd,
     )
 
     def share(slot):
@@ -589,21 +662,21 @@
     level = share(slot)
     z1, image, to_even, to_odd, dots = call(
         first_kernel, counts,
-        [(4, 4, 4, LANES), (6, 6, 4, LANES), (4, 6, 4, LANES), (4, 6, 4, LANES), (1, LANES)],
+        [(4, 4, 4, LANES), (6, 6, 4, LANES), rows(SIDE_X), rows(SIDE_X), (1, LANES)],
         level, r, *fields, *particles, scratch=scratch,
     )
-    even, odd = exchange(to_even, to_odd, "gx", count_x)
-    wide, to_up, to_down = call(
-        along_x_kernel, counts, [(10, 6, 4, LANES), (10, 4, 4, LANES), (10, 4, 4, LANES)], image, even, odd
-    )
-    up, down = exchange(to_up, to_down, "gy", count_y)
-    w, slot = call(middle_kernel, counts, [(8, 8, 4, LANES), (8, LANES)], wide, up, down, *fields, dots)
+    even, odd = exchange(to_even, to_odd, "gx", counts)
+    wide, to_even, to_odd = call(
+        along_x_kernel, counts, [(10, 6, 4, LANES), rows(SIDE_IMAGE), rows(SIDE_IMAGE)], image, even, odd
+    )
+    even, odd = exchange(to_even, to_odd, "gy", counts)
+    w, slot = call(middle_kernel, counts, [(8, 8, 4, LANES), (8, LANES)], wide, even, odd, *fields, dots)
     change = share(slot)
     z2, image, slots = call(
-        second_kernel, counts, [(4, 4, 4, LANES), (4, 4, 4, LANES), (bricks, 16, LANES)],
+        second_kernel, counts, [(4, 4, 4, LANES), (4, 4, 4, LANES), (bricks, 13, 1, LANES)],
         level, change, r, w, *fields, *particles, scratch=scratch,
     )
-    slots = lax.all_to_all(slots, AXES, 0, 0).reshape(bricks * 16, LANES)
+    slots = lax.all_to_all(slots, AXES, 0, 0)
     return tuple(
         call(last_kernel, counts, [right_side.shape, right_side.shape], slots, change, z1, z2, r, w, image)
     )

time: 76.3 us -> 72.1 us (0.945)
  waiting for transfers between devices: 23.7 us -> 15 us
  local copies, waits for them, and re-layouts: 2.23 us -> 8.67 us
  starting transfers between devices: 14.6 us -> 12.4 us
    unnamed x12 -> x14, local copies, waits for them, and re-layouts: 1.56 us -> 7.98 us
    all_to_all x1, waiting for transfers between devices: 8.32 us -> 3.46 us  [share(): return lax.all_to_all(sent, AXES, 0, 0).reshape(bricks * 8, LANES)]
    ppermute x8, starting transfers between devices: 10.6 us -> 5.81 us  [exchange(): return (lax.ppermute(first, AXES, even), lax.ppermute(second, AXES, odd))]
    ppermute x8, waiting for transfers between devices: 15.4 us -> 11.5 us  [exchange(): return (lax.ppermute(first, AXES, even), lax.ppermute(second, AXES, odd))]
    all_to_all x1, starting transfers between devices: 4.07 us -> 6.59 us  [share(): return lax.all_to_all(sent, AXES, 0, 0).reshape(bricks * 8, LANES)]
    pallas_call x6 -> x8, Pallas kernels: 12 us -> 11.6 us  [call(): pl.pallas_call(functools.partial(kernel, counts), out_shape=out, scratch_...]
  transfers between devices with their start and end apart: 9 -> 9, of which waited for: 8 -> 6; matrix products, arithmetic and copies ran while one was open for 0% -> 1% of each run, Pallas kernels for 0% -> 2%
where the time goes in v2:
time: 72.1 us; the launch traced here: 71.6 us
  blocking collectives  22.5 us (31%)
  waiting for transfers between devices  15 us (21%)
  starting transfers between devices  12.4 us (17%)
  Pallas kernels  11.6 us (16%)
  local copies, waits for them, and re-layouts  8.67 us (12%)
    pallas_call x8, Pallas kernels, call(): pl.pallas_call(functools.partial(kernel, counts), out_shape=out, scratch_...  11.6 us
    ppermute x8, waiting for transfers between devices, exchange(): return (lax.ppermute(first, AXES, even), lax.ppermute(second, AXES, odd))  11.5 us
    all_to_all x1, blocking collectives, share(): return lax.all_to_all(sent, AXES, 0, 0).reshape(bricks * 8, LANES)  11.3 us
    all_to_all x1, blocking collectives, per_device(): slots = lax.all_to_all(slots, AXES, 0, 0)  11.3 us
    unnamed x14, local copies, waits for them, and re-layouts  7.98 us
    all_to_all x1, starting transfers between devices, share(): return lax.all_to_all(sent, AXES, 0, 0).reshape(bricks * 8, LANES)  6.59 us
    ppermute x8, starting transfers between devices, exchange(): return (lax.ppermute(first, AXES, even), lax.ppermute(second, AXES, odd))  5.81 us
    all_to_all x1, waiting for transfers between devices, share(): return lax.all_to_all(sent, AXES, 0, 0).reshape(bricks * 8, LANES)  3.46 us
  transfers between devices with their start and end apart: 9, of which 6 were waited for; matrix products, arithmetic and copies ran while one was open for 1% of the time, Pallas kernels for 2%

profile of v2, /device:TPU:0, one launch (start us, length us, event | category | flops | bytes accessed | tf_op | source)
XLA Modules:
  0.0 71.6 jit_solution(16175910464126722022)
XLA Ops:
  0.6 0.8 %copy.8 = f32[3,4,4,128]{3,0,2,1:T(4,128)S(1)} copy(f32[3,4,4,128]{3,2,1,0:T(4,128)} %param.6) | data formatting | bytes 49152 | tf_op args[0]
  1.4 0.7 %maximum_bitcast_fusion.own_ref = f32[4,4,4,128]{3,2,1,0:T(4,128)S(1)} fusion(f32[1,4,4,128]{3,0,2,1:T(1,128)} %bitcast.21, f32[3,4,4,128]{3,0,2,1:T(4,128)S(1)} %copy.8), kind=kLoop, calls=%fused_computation.1 | loop fusion | flops 8192 | bytes 65536 | tf_op jit(solution)/shard_map/transpose | solution.py:642
  2.1 3.1 %collective-permute-start.1 = (f32[4,4,4,128]{3,2,1,0:T(4,128)S(1)}, f32[4,4,4,128]{3,2,1,0:T(4,128)S(1)}, u32[]{:S(2)}, u32[]{:S(2)}) collective-permute-start(f32[4,4,4,128]{3,2,1,0:T(4,128)S(1)} %maximum_bitcast_fusion.own_ref), channel_id=1, source_target_pairs={{0,1},{1,0},{2,3},{3,2},{4,8},{5,9},{6,10},{7,11},{8,4},{9,5},{10,... | collective-permute-start | bytes 98312 | tf_op jit(solution)/shard_map/ppermute | solution.py:38
  5.2 1.9 %collective-permute-done.1.odd_ref = f32[4,4,4,128]{3,2,1,0:T(4,128)S(1)} collective-permute-done((f32[4,4,4,128]{3,2,1,0:T(4,128)S(1)}, f32[4,4,4,128]{3,2,1,0:T(4,128)S(1)}, u32[]{:S(2)}, u32[]{:S(2)}) %collective-permute-start.1) | collective-permute-done | bytes 32800 | tf_op jit(solution)/shard_map/ppermute | solution.py:38
  7.2 2.1 %collective-permute-start.2 = (f32[96,128]{1,0:T(8,128)S(1)}, f32[96,128]{1,0:T(8,128)S(1)}, u32[]{:S(2)}, u32[]{:S(2)}) collective-permute-start(f32[96,128]{1,0:T(8,128)S(1)} %get-tuple-element.27), channel_id=1, source_target_pairs={{0,1},{1,0},{2,3},{3,2},{4,5},{5,4},{6,7},{7,6},{8,9},{9,8},{10,11... | collective-permute-start | bytes 147464 | tf_op jit(solution)/shard_map/ppermute | solution.py:38
  9.2 2.1 %collective-permute-done.2.even_ref = f32[96,128]{1,0:T(8,128)S(1)} collective-permute-done((f32[96,128]{1,0:T(8,128)S(1)}, f32[96,128]{1,0:T(8,128)S(1)}, u32[]{:S(2)}, u32[]{:S(2)}) %collective-permute-start.2) | collective-permute-done | bytes 49184 | tf_op jit(solution)/shard_map/ppermute | solution.py:38
  11.9 0.7 broadcast_in_dim.7
  12.6 6.6 %all-to-all-start = ((f32[32,8,128]{2,1,0:T(8,128)}), f32[32,8,128]{2,1,0:T(8,128)S(1)}, u32[]{:S(2)}, u32[]{:S(2)}) async-start(f32[32,8,128]{2,1,0:T(8,128)} %broadcast_in_dim.7), calls=%async_computation | async-start | bytes 262144 | tf_op jit(solution)/shard_map/all_to_all | solution.py:660
  19.1 1.0 %copy.11 = f32[1,1,8,3,27,128]{5,4,3,2,1,0:T(8,128)S(1)} copy(f32[1,1,8,3,27,128]{5,2,4,3,1,0:T(8,128)} %param.8) | data formatting | bytes 663552 | tf_op args[2]
  20.2 0.7 copy-done.5
  20.9 1.2 %shard_map.79 = (bf16[2048,1024]{1,0:T(8,128)(2,1)S(1)}, f32[8,3,27,128]{3,2,1,0:T(8,128)S(1)}) custom-call(s32[8,128]{1,0:T(8,128)S(1)} %bitcast.20, f32[8,3,27,128]{3,2,1,0:T(8,128)S(1)} %bitcast.11), custom_call_target="tpu_custom_call" | custom-call | tf_op jit(solution)/shard_map/pallas_call | solution.py:622
  22.2 1.9 %copy-done = bf16[2048,1024]{1,0:T(8,128)(2,1)} copy-done((bf16[2048,1024]{1,0:T(8,128)(2,1)}, bf16[2048,1024]{1,0:T(8,128)(2,1)S(1)}, u32[]{:S(2)}) %copy-start) | copy-done | bytes 4194328
  24.1 3.5 %all-to-all-done = f32[32,8,128]{2,1,0:T(8,128)S(1)} async-done(((f32[32,8,128]{2,1,0:T(8,128)}), f32[32,8,128]{2,1,0:T(8,128)S(1)}, u32[]{:S(2)}, u32[]{:S(2)}) %all-to-all-start) | async-done | bytes 131104 | tf_op jit(solution)/shard_map/all_to_all | solution.py:660
  27.6 2.2 %copy-done.1 = bf16[2048,1024]{1,0:T(8,128)(2,1)S(1)} copy-done((bf16[2048,1024]{1,0:T(8,128)(2,1)S(1)}, bf16[2048,1024]{1,0:T(8,128)(2,1)}, u32[]{:S(2)}) %copy-start.1) | copy-done | bytes 4194328
  29.7 0.7 copy-done.3
  30.4 0.7 copy-done.4
  31.1 3.9 %shard_map.80 = (f32[4,4,4,128]{3,2,1,0:T(4,128)S(1)}, f32[6,6,4,128]{3,2,1,0:T(4,128)S(1)}, f32[80,128]{1,0:T(8,128)S(1)}, f32[80,128]{1,0:T(8,128)S(1)}, f32[1,128]{1,0:T(1,128)S(1)}) custom-call(f32[256,128]{1,0:T(8,128)S(1)} %bitcast.14, f32[8,8,4,128]{3,2,1,0:T(4,128)S(1)} %get-tuple-element.30.r_ref, ...), custom_call_target="tpu_custom_call" | custom-call | tf_op jit(solution)/shard_map/pallas_call | solution.py:622
  35.3 0.9 %collective-permute-done.4.even_ref = f32[80,128]{1,0:T(8,128)S(1)} collective-permute-done((f32[80,128]{1,0:T(8,128)S(1)}, f32[80,128]{1,0:T(8,128)S(1)}, u32[]{:S(2)}, u32[]{:S(2)}) %collective-permute-start.4) | collective-permute-done | bytes 40992 | tf_op jit(solution)/shard_map/ppermute | solution.py:38
  36.3 2.9 %collective-permute-done.5.odd_ref = f32[80,128]{1,0:T(8,128)S(1)} collective-permute-done((f32[80,128]{1,0:T(8,128)S(1)}, f32[80,128]{1,0:T(8,128)S(1)}, u32[]{:S(2)}, u32[]{:S(2)}) %collective-permute-start.5) | collective-permute-done | bytes 40992 | tf_op jit(solution)/shard_map/ppermute | solution.py:38
  39.5 3.8 %collective-permute-done.6.even_ref = f32[88,128]{1,0:T(8,128)S(1)} collective-permute-done((f32[88,128]{1,0:T(8,128)S(1)}, f32[88,128]{1,0:T(8,128)S(1)}, u32[]{:S(2)}, u32[]{:S(2)}) %collective-permute-start.6) | collective-permute-done | bytes 45088 | tf_op jit(solution)/shard_map/ppermute | solution.py:38
  43.8 11.3 %all_to_all.15 = f32[32,8,128]{2,1,0:T(8,128)S(1)} all-to-all(f32[32,8,128]{2,1,0:T(8,128)S(1)} %broadcast_in_dim.8), channel_id=1, replica_groups=mesh['gx'=8,'gy'=4] {'gx','gy'}, dimensions={0} | all-to-all | bytes 262144 | tf_op jit(solution)/shard_map/all_to_all | solution.py:660
  55.1 4.3 %shard_map.83 = (f32[4,4,4,128]{3,2,1,0:T(4,128)S(1)}, f32[4,4,4,128]{3,2,1,0:T(4,128)S(1)}, f32[32,13,1,128]{3,2,1,0:T(1,128)S(1)}) custom-call(f32[256,128]{1,0:T(8,128)S(1)} %bitcast.15, f32[256,128]{1,0:T(8,128)S(1)} %bitcast.12, f32[8,8,4,128]{3,2,1,0:T(4,128)S(1)} %get-tuple-element.30.r_ref, f32[8,8,4,128]{3,2,1,0:T(4,128)S(1)} %get-tuple-element.45.w_ref, ...), custom_call_target="tpu_custom_call" | custom-call | tf_op jit(solution)/shard_map/pallas_call | solution.py:622
  59.4 11.3 %all_to_all.16.slots_ref = f32[32,13,1,128]{3,2,1,0:T(1,128)S(1)} all-to-all(f32[32,13,1,128]{3,2,1,0:T(1,128)S(1)} %get-tuple-element.46), channel_id=1, replica_groups=mesh['gx'=8,'gy'=4] {'gx','gy'}, dimensions={0} | all-to-all | bytes 425984 | tf_op jit(solution)/shard_map/all_to_all | solution.py:679
  70.7 0.9 %shard_map.84 = (f32[3,4,4,128]{3,2,1,0:T(4,128)}, f32[3,4,4,128]{3,2,1,0:T(4,128)}) custom-call(f32[32,13,1,128]{3,2,1,0:T(1,128)S(1)} %all_to_all.16.slots_ref, f32[256,128]{1,0:T(8,128)S(1)} %bitcast.13, f32[4,4,4,128]{3,2,1,0:T(4,128)S(1)} %get-tuple-element.47.z1_ref, f32[4,4,4,128]{3,2,1,0:T(4,128)S(1)} %get-tuple-element.48.z2_ref, ...), custom_call_target="tpu_custom_call" | custom-call | tf_op jit(solution)/shard_map/pallas_call | solution.py:622
  (21 shorter events, 1.8 us)
Async XLA Ops:
  2.1 5.0 %collective-permute-start.1 = (f32[4,4,4,128]{3,2,1,0:T(4,128)S(1)}, f32[4,4,4,128]{3,2,1,0:T(4,128)S(1)}, u32[]{:S(2)}, u32[]{:S(2)}) collective-permute-start(f32[4,4,4,128]{3,2,1,0:T(4,128)S(1)} %maximum_bitcast_fusion.own_ref), channel_id=1, source_target_pairs={{0,1},{1,0},{2,3},{3,2},{4,8},{5,9},{6,10},{7,11},{8,4},{9,5},{10,... | collective-permute-start | bytes 98312 | tf_op jit(solution)/shard_map/ppermute | solution.py:38
  5.2 1.9 %collective-permute-start = (f32[4,4,4,128]{3,2,1,0:T(4,128)S(1)}, f32[4,4,4,128]{3,2,1,0:T(4,128)S(1)}, u32[]{:S(2)}, u32[]{:S(2)}) collective-permute-start(f32[4,4,4,128]{3,2,1,0:T(4,128)S(1)} %maximum_bitcast_fusion.own_ref), channel_id=1, source_target_pairs={{0,4},{1,5},{2,6},{3,7},{4,0},{5,1},{6,2},{7,3},{8,12},{9,13},{10,... | collective-permute-start | bytes 98312 | tf_op jit(solution)/shard_map/ppermute | solution.py:38
  7.2 4.2 %collective-permute-start.2 = (f32[96,128]{1,0:T(8,128)S(1)}, f32[96,128]{1,0:T(8,128)S(1)}, u32[]{:S(2)}, u32[]{:S(2)}) collective-permute-start(f32[96,128]{1,0:T(8,128)S(1)} %get-tuple-element.27), channel_id=1, source_target_pairs={{0,1},{1,0},{2,3},{3,2},{4,5},{5,4},{6,7},{7,6},{8,9},{9,8},{10,11... | collective-permute-start | bytes 147464 | tf_op jit(solution)/shard_map/ppermute | solution.py:38
  9.2 2.1 %collective-permute-start.3 = (f32[96,128]{1,0:T(8,128)S(1)}, f32[96,128]{1,0:T(8,128)S(1)}, u32[]{:S(2)}, u32[]{:S(2)}) collective-permute-start(f32[96,128]{1,0:T(8,128)S(1)} %get-tuple-element.28), channel_id=1, source_target_pairs={{0,4},{1,2},{2,1},{3,7},{4,0},{5,6},{6,5},{7,3},{8,12},{9,10},{10,... | collective-permute-start | bytes 147464 | tf_op jit(solution)/shard_map/ppermute | solution.py:38
  12.6 15.0 %all-to-all-start = ((f32[32,8,128]{2,1,0:T(8,128)}), f32[32,8,128]{2,1,0:T(8,128)S(1)}, u32[]{:S(2)}, u32[]{:S(2)}) async-start(f32[32,8,128]{2,1,0:T(8,128)} %broadcast_in_dim.7), calls=%async_computation | async-start | bytes 262144 | tf_op jit(solution)/shard_map/all_to_all | solution.py:660
  20.2 0.7 copy-start.5
  22.1 1.9 %copy-start = (bf16[2048,1024]{1,0:T(8,128)(2,1)}, bf16[2048,1024]{1,0:T(8,128)(2,1)S(1)}, u32[]{:S(2)}) copy-start(bf16[2048,1024]{1,0:T(8,128)(2,1)S(1)} %get-tuple-element.35.hot_ref) | copy-start | bytes 12582916
  27.5 2.2 %copy-start.1 = (bf16[2048,1024]{1,0:T(8,128)(2,1)S(1)}, bf16[2048,1024]{1,0:T(8,128)(2,1)}, u32[]{:S(2)}) copy-start(bf16[2048,1024]{1,0:T(8,128)(2,1)} %copy-done) | copy-start | bytes 12582916
  29.7 0.7 copy-start.3
  30.4 0.7 copy-start.4
  31.1 24.0 %copy-start.2 = (bf16[2048,1024]{1,0:T(8,128)(2,1)S(1)}, bf16[2048,1024]{1,0:T(8,128)(2,1)}, u32[]{:S(2)}) copy-start(bf16[2048,1024]{1,0:T(8,128)(2,1)} %copy-done) | copy-start | bytes 12582916
  35.0 1.2 %collective-permute-start.4 = (f32[80,128]{1,0:T(8,128)S(1)}, f32[80,128]{1,0:T(8,128)S(1)}, u32[]{:S(2)}, u32[]{:S(2)}) collective-permute-start(f32[80,128]{1,0:T(8,128)S(1)} %get-tuple-element.38), channel_id=1, source_target_pairs={{0,4},{1,5},{2,6},{3,7},{4,0},{5,1},{6,2},{7,3},{8,12},{9,13},{10,... | collective-permute-start | bytes 122888 | tf_op jit(solution)/shard_map/ppermute | solution.py:38
  35.0 4.1 %collective-permute-start.5 = (f32[80,128]{1,0:T(8,128)S(1)}, f32[80,128]{1,0:T(8,128)S(1)}, u32[]{:S(2)}, u32[]{:S(2)}) collective-permute-start(f32[80,128]{1,0:T(8,128)S(1)} %get-tuple-element.39), channel_id=1, source_target_pairs={{0,1},{1,0},{2,3},{3,2},{4,8},{5,9},{6,10},{7,11},{8,4},{9,5},{10,... | collective-permute-start | bytes 122888 | tf_op jit(solution)/shard_map/ppermute | solution.py:38
  39.2 4.1 %collective-permute-start.6 = (f32[88,128]{1,0:T(8,128)S(1)}, f32[88,128]{1,0:T(8,128)S(1)}, u32[]{:S(2)}, u32[]{:S(2)}) collective-permute-start(f32[88,128]{1,0:T(8,128)S(1)} %get-tuple-element.41), channel_id=1, source_target_pairs={{0,1},{1,0},{2,3},{3,2},{4,5},{5,4},{6,7},{7,6},{8,9},{9,8},{10,11... | collective-permute-start | bytes 135176 | tf_op jit(solution)/shard_map/ppermute | solution.py:38
  39.5 3.8 %collective-permute-start.7 = (f32[88,128]{1,0:T(8,128)S(1)}, f32[88,128]{1,0:T(8,128)S(1)}, u32[]{:S(2)}, u32[]{:S(2)}) collective-permute-start(f32[88,128]{1,0:T(8,128)S(1)} %get-tuple-element.42), channel_id=1, source_target_pairs={{0,4},{1,2},{2,1},{3,7},{4,0},{5,6},{6,5},{7,3},{8,12},{9,10},{10,... | collective-permute-start | bytes 135176 | tf_op jit(solution)/shard_map/ppermute | solution.py:38

commit v3 on v2

--- a/solution.py
+++ b/solution.py
@@ -202,61 +202,63 @@
     return memo(lambda x, y: place.keep(e0(x, y) + weight0(x, y) * (r(x, y) - g0(x, y)), x, y, BRICK))
 
 
-def one_hot_kernel(counts, base_ref, grad_in_ref, hot_ref, grad_ref):
-    grad_ref[...] = grad_in_ref[...]
-    base = base_ref[...]
-    plane = base // (LANES + 2)
-    depth = base - plane * (LANES + 2)
-    node_xy = (plane // (BRICK + 2)) * BRICK + plane % (BRICK + 2)
-    sub = lax.broadcasted_iota(jnp.int32, (LANES, LANES), 0)
-    for s in range(base_ref.shape[0]):
-        depth_s, xy_s = depth[s : s + 1], node_xy[s : s + 1]
-        for q in range(BRICK * BRICK):
-            wanted = jnp.where(xy_s == q, depth_s, -1)
-            hot_ref[q * LANES : (q + 1) * LANES, s * LANES : (s + 1) * LANES] = as_f32(sub == wanted).astype(jnp.bfloat16)
-
-
-def stiffness_apply(z, hot, stiff_ref, valid_ref, grad_ref, stack, picked, spread_sums, shifts):
+def stiffness_apply(z, fetched, base_ref, stiff_ref, valid_ref, grad_ref, hot, nodes, forces, picked, spread_sums, shifts):
     blocks = grad_ref.shape[0]
-    particles = blocks * LANES
+    turns = [(b, c) for b in range(3) for c in range(3)]
+    span = BRICK + 2
 
     def halves(x):
         high = x.astype(jnp.bfloat16).astype(F32)
         return jnp.concatenate([high, x - high], axis=0)
 
     split = {}
-    for x in range(BRICK + 2):
-        for y in range(BRICK + 2):
+    for x in range(span):
+        for y in range(span):
             whole = halves(z(x - 1, y - 1))
             split[x, y, 1] = whole
             split[x, y, 0] = turn(whole, 1) * shifts.low[1]
             split[x, y, 2] = turn(whole, -1) * shifts.high[1]
-    tiles = [(a, b, c) for a in range(3) for b in range(3) for c in range(3)]
-    zero = jnp.zeros((8, LANES), F32)
-    for i in range(BRICK):
+    for u, (b, c) in enumerate(turns):
         for j in range(BRICK):
-            q = i * BRICK + j
-            parts = [split[i + a, j + b, c] for a, b, c in tiles] + [zero]
-            for t in range(0, 28, 2):
-                pair = jnp.concatenate([parts[t], parts[t + 1]], axis=0).astype(jnp.bfloat16)
-                stack[t * 8 : t * 8 + 16, q * LANES : (q + 1) * LANES] = pair
-    picked[...] = jnp.dot(stack[...], hot[...], preferred_element_type=F32)
+            for x in range(0, span, 2):
+                pair = jnp.concatenate([split[x, j + b, c], split[x + 1, j + b, c]], axis=0).astype(jnp.bfloat16)
+                row = (u * span + x) * 8
+                nodes[row : row + 16, j * LANES : (j + 1) * LANES] = pair
+
+    fetched()
+    base = base_ref[...]
+    plane = base // (LANES + 2)
+    depth = base - plane * (LANES + 2)
+    node_x = plane // span
+    node_y = plane - node_x * span
+    sub = lax.broadcasted_iota(jnp.int32, (LANES, LANES), 0)
+    for s in range(blocks):
+        for j in range(BRICK):
+            wanted = jnp.where(node_y[s : s + 1] == j, depth[s : s + 1], -1)
+            hot[j * LANES : (j + 1) * LANES, s * LANES : (s + 1) * LANES] = as_f32(sub == wanted).astype(jnp.bfloat16)
+    picked[...] = jnp.dot(nodes[...], hot[...], preferred_element_type=F32)
 
     first = POISSON / ((1.0 + POISSON) * (1.0 - 2.0 * POISSON))
     shear_of = 0.5 / (1.0 + POISSON)
-    row4 = lax.broadcasted_iota(jnp.int32, (8, LANES), 0) % 4
-    row_is = [as_f32(row4 == m) for m in range(3)]
-    is_high = as_f32(lax.broadcasted_iota(jnp.int32, (8, LANES), 0) < 4)
+    row8 = lax.broadcasted_iota(jnp.int32, (8, LANES), 0)
+    row_is = [as_f32(row8 % 4 == m) for m in range(3)]
+    is_high = row8 < 4
+    zero = jnp.zeros((8, LANES), F32)
     wide = lambda row: jnp.broadcast_to(row, (8, LANES))
     for s in range(blocks):
         lanes = slice(s * LANES, (s + 1) * LANES)
-        grad = lambda l, t: wide(grad_ref[s, l, t : t + 1, :])
+        grad = lambda l, a, b, c: wide(grad_ref[s, l, 9 * a + 3 * b + c : 9 * a + 3 * b + c + 1, :])
+        at_x = [wide(node_x[s : s + 1]) == i for i in range(BRICK)]
         h = [None] * 3
-        for t in range(27):
-            value = picked[t * 8 : t * 8 + 8, lanes]
-            for l in range(3):
-                term = value * grad(l, t)
-                h[l] = term if h[l] is None else h[l] + term
+        for u, (b, c) in enumerate(turns):
+            tiles = [picked[(u * span + x) * 8 : (u * span + x) * 8 + 8, lanes] for x in range(span)]
+            for a in range(3):
+                value = tiles[3 + a]
+                for i in (2, 1, 0):
+                    value = jnp.where(at_x[i], tiles[i + a], value)
+                for l in range(3):
+                    term = value * grad(l, a, b, c)
+                    h[l] = term if h[l] is None else h[l] + term
         h = [x[0:4] + x[4:8] for x in h]
         h = [[h[l][m : m + 1] for l in range(3)] for m in range(3)]
         effective = stiff_ref[s : s + 1] * valid_ref[s : s + 1].astype(F32)
@@ -271,33 +273,50 @@
                     entry = entry + bulk
                 column = column + wide(entry) * row_is[m]
             stress.append(column)
-        parts = []
-        for t in range(28):
-            if t < 27:
-                f = stress[0] * grad(0, t) + stress[1] * grad(1, t) + stress[2] * grad(2, t)
+        for u, (b, c) in enumerate(turns):
+            parts = []
+            for a in range(3):
+                f = stress[0] * grad(0, a, b, c) + stress[1] * grad(1, a, b, c) + stress[2] * grad(2, a, b, c)
                 high = f.astype(jnp.bfloat16).astype(F32)
-                parts.append(is_high * high + (1.0 - is_high) * (f - high))
-            else:
-                parts.append(zero)
-            if t % 2:
-                pair = jnp.concatenate(parts, axis=0).astype(jnp.bfloat16)
-                stack[t * 8 - 8 : t * 8 + 8, lanes] = pair
-                parts = []
+                parts.append(jnp.where(is_high, high, f - high))
+            tiles = []
+            for x in range(span):
+                tile = zero
+                for a in range(3):
+                    if 0 <= x - a < BRICK:
+                        tile = jnp.where(at_x[x - a], parts[a], tile)
+                tiles.append(tile)
+            for x in range(0, span, 2):
+                row = (u * span + x) * 8
+                pair = jnp.concatenate([tiles[x], tiles[x + 1]], axis=0).astype(jnp.bfloat16)
+                forces[row : row + 16, lanes] = pair
     spread_sums[...] = lax.dot_general(
-        stack[:, :particles], hot[...], (((1,), (1,)), ((), ())), preferred_element_type=F32
+        forces[...], hot[...], (((1,), (1,)), ((), ())), preferred_element_type=F32
     )
     out = {}
-    for x in range(BRICK + 2):
-        for y in range(BRICK + 2):
+    for x in range(span):
+        for y in range(span):
             sums = [0.0, 0.0, 0.0]
-            for t, (a, b, c) in enumerate(tiles):
-                i, j = x - a, y - b
-                if 0 <= i < BRICK and 0 <= j < BRICK:
-                    q = i * BRICK + j
-                    sums[c] = sums[c] + spread_sums[t * 8 : t * 8 + 8, q * LANES : (q + 1) * LANES]
+            for u, (b, c) in enumerate(turns):
+                j = y - b
+                if 0 <= j < BRICK:
+                    row = (u * span + x) * 8
+                    sums[c] = sums[c] + spread_sums[row : row + 8, j * LANES : (j + 1) * LANES]
             total = sums[1] + turn(sums[0], -1) * shifts.high[1] + turn(sums[2], 1) * shifts.low[1]
             out[x - 1, y - 1] = total[0:4] + total[4:8]
     return out
+
+
+def fetch(sources, targets, semaphores):
+    copies = [pltpu.make_async_copy(a, b, semaphores.at[k]) for k, (a, b) in enumerate(zip(sources, targets))]
+    for copy in copies:
+        copy.start()
+
+    def wait():
+        for copy in copies:
+            copy.wait()
+
+    return wait
 
 
 def side_parts(even_ref, odd_ref, is_even, inside_low, inside_high):
@@ -323,6 +342,14 @@
 def clear_tail(*refs):
     for ref in refs:
         ref[ref.shape[0] - 8 :, :] = jnp.zeros((8, LANES), F32)
+
+
+def pack_kernel(counts, right_ref, mass_ref, own_ref):
+    for x in range(BRICK):
+        for y in range(BRICK):
+            for m in range(3):
+                own_ref[x, y, m : m + 1, :] = right_ref[m, x, y : y + 1, :]
+            own_ref[x, y, 3:4, :] = mass_ref[x, y : y + 1, :]
 
 
 def widen_kernel(counts, own_ref, even_ref, odd_ref, wide_ref, to_even_ref, to_odd_ref):
@@ -400,10 +427,10 @@
     return memo(lambda x, y: ref[x + offset, y + offset])
 
 
-def cycle_and_apply(place, shifts, r, gathered, mass_rows, fields, particles, scratch):
+def cycle_and_apply(place, shifts, r, gathered, mass_rows, fields, fetched, particles, scratch):
     count_x, count_y = place.count_x, place.count_y
     mass0, weight0, mass1, weight1 = fields
-    coarse, stack, picked, spread_sums = scratch
+    coarse, *work = scratch
     bricks = count_x * count_y
     r2 = gathered(3, bricks, 8)
     lane = lax.broadcasted_iota(jnp.int32, (bricks, LANES), 1)
@@ -436,7 +463,7 @@
     live = as_f32(lax.broadcasted_iota(jnp.int32, (4, LANES), 0) < 3)
     full = prolongation(r, r1, e2, mass0, weight0, mass1, weight1, place, shifts)
     z = memo(lambda x, y: full(x, y) * live)
-    image = stiffness_apply(z, *particles, stack, picked, spread_sums, shifts)
+    image = stiffness_apply(z, fetched, *particles, *work, shifts)
     for x in range(BRICK):
         for y in range(BRICK):
             image[x, y] = image[x, y] + mass0(x, y) * z(x, y)
@@ -463,14 +490,16 @@
 
 
 def first_kernel(counts, level_ref, r_ref, mass0_ref, weight0_ref, mass1_ref, weight1_ref,
-                 hot_ref, stiff_ref, valid_ref, grad_ref, z_ref, image_ref, even_ref, odd_ref, dots_ref, *scratch):
+                 base_in, stiff_in, valid_in, grad_in, z_ref, image_ref, even_ref, odd_ref, dots_ref,
+                 base_ref, stiff_ref, valid_ref, grad_ref, semaphores, *scratch):
+    particles = (base_ref, stiff_ref, valid_ref, grad_ref)
+    fetched = fetch((base_in, stiff_in, valid_in, grad_in), particles, semaphores)
     place, shifts = Place(*counts), Shifts()
     r = reader(r_ref, 2)
     gathered = lambda start, size, stride: level_ref[pl.ds(start, size, stride=stride) if stride > 1 else pl.ds(start, size), :]
     fields = (reader(mass0_ref, 3), reader(weight0_ref, 3), reader(mass1_ref, 2), reader(weight1_ref, 2))
     mass_rows = gathered(3, counts[0] * counts[1], 8)
-    particles = (hot_ref, stiff_ref, valid_ref, grad_ref)
-    z, image = cycle_and_apply(place, shifts, r, gathered, mass_rows, fields, particles, scratch)
+    z, image = cycle_and_apply(place, shifts, r, gathered, mass_rows, fields, fetched, particles, scratch)
     for x, y in INNER:
         z_ref[x, y] = z(x, y)
     for x, y in RIMMED:
@@ -536,7 +565,10 @@
 
 
 def second_kernel(counts, level_ref, change_ref, r_ref, w_ref, mass0_ref, weight0_ref, mass1_ref, weight1_ref,
-                  hot_ref, stiff_ref, valid_ref, grad_ref, z_ref, image_ref, slots_ref, *scratch):
+                  base_in, stiff_in, valid_in, grad_in, z_ref, image_ref, slots_ref,
+                  base_ref, stiff_ref, valid_ref, grad_ref, semaphores, *scratch):
+    particles = (base_ref, stiff_ref, valid_ref, grad_ref)
+    fetched = fetch((base_in, stiff_in, valid_in, grad_in), particles, semaphores)
     place, shifts = Place(*counts), Shifts()
     bricks = counts[0] * counts[1]
     sums = sums_of(change_ref, bricks, 7, 8)
@@ -549,8 +581,7 @@
 
     mass_rows = level_ref[pl.ds(3, bricks, stride=8), :]
     fields = (reader(mass0_ref, 3), reader(weight0_ref, 3), reader(mass1_ref, 2), reader(weight1_ref, 2))
-    particles = (hot_ref, stiff_ref, valid_ref, grad_ref)
-    z, image = cycle_and_apply(place, shifts, r, gathered, mass_rows, fields, particles, scratch)
+    z, image = cycle_and_apply(place, shifts, r, gathered, mass_rows, fields, fetched, particles, scratch)
     for x, y in INNER:
         z_ref[x, y] = z(x, y)
         image_ref[x, y] = image[x, y]
@@ -617,11 +648,12 @@
             residual_ref[m, x, y : y + 1, :] = residual[m : m + 1]
 
 
-def call(kernel, counts, shapes, *args, scratch=()):
-    out = [jax.ShapeDtypeStruct(*s) if isinstance(s[0], tuple) else jax.ShapeDtypeStruct(s, F32) for s in shapes]
+def call(kernel, counts, shapes, *args, scratch=(), far=0):
+    near = len(args) - far
     return pl.pallas_call(
         functools.partial(kernel, counts),
-        out_shape=out,
+        out_shape=[jax.ShapeDtypeStruct(s, F32) for s in shapes],
+        in_specs=[pl.BlockSpec(memory_space=pltpu.VMEM)] * near + [pl.BlockSpec(memory_space=pl.ANY)] * far,
         scratch_shapes=scratch,
         compiler_params=pltpu.CompilerParams(vmem_limit_bytes=VMEM_BYTES),
     )(*args)
@@ -630,25 +662,27 @@
 def per_device(counts, right_side, node_mass, gradients, stiffness, valid, node_base):
     bricks = counts[0] * counts[1]
     blocks = gradients.shape[2]
-    nodes = BRICK * BRICK * LANES
+    particles = (node_base[0, 0], stiffness[0, 0], valid[0, 0], gradients[0, 0])
+    tiles = 9 * (BRICK + 2) * 8
+    depth = BRICK * LANES
+    width = blocks * LANES
     scratch = (
+        *(pltpu.VMEM(p.shape, p.dtype) for p in particles),
+        pltpu.SemaphoreType.DMA((4,)),
         pltpu.VMEM((bricks + 2 * (8 + counts[1]), LANES), F32),
-        pltpu.VMEM((224, nodes), jnp.bfloat16),
-        pltpu.VMEM((224, blocks * LANES), F32),
-        pltpu.VMEM((224, nodes), F32),
+        pltpu.VMEM((depth, width), jnp.bfloat16),
+        pltpu.VMEM((tiles, depth), jnp.bfloat16),
+        pltpu.VMEM((tiles, width), jnp.bfloat16),
+        pltpu.VMEM((tiles, width), F32),
+        pltpu.VMEM((tiles, depth), F32),
     )
     rows = lambda columns, more=0: (-(-(3 * len(columns) + more + 1) // 8) * 8, LANES)
 
-    own = jnp.concatenate([right_side, node_mass[None]], axis=0).transpose(1, 2, 0, 3)
+    (own,) = call(pack_kernel, counts, [(4, 4, 4, LANES)], right_side, node_mass)
     even, odd = exchange(own, own, "gx", counts)
     side = rows(SIDE, len(SIDE_MASS))
     wide, to_even, to_odd = call(widen_kernel, counts, [(12, 4, 4, LANES), side, side], own, even, odd)
     even, odd = exchange(to_even, to_odd, "gy", counts)
-    hot, grads = call(
-        one_hot_kernel, counts, [((nodes, blocks * LANES), jnp.bfloat16), gradients.shape[2:]],
-        node_base[0, 0], gradients[0, 0],
-    )
-    particles = (hot, stiffness[0, 0], valid[0, 0], grads)
     r, *fields, slot = call(
         start_kernel, counts,
         [(8, 8, 4, LANES), (10, 10, 4, LANES), (10, 10, 4, LANES), (6, 6, 4, LANES), (6, 6, 4, LANES), (8, LANES)],
@@ -663,7 +697,7 @@
     z1, image, to_even, to_odd, dots = call(
         first_kernel, counts,
         [(4, 4, 4, LANES), (6, 6, 4, LANES), rows(SIDE_X), rows(SIDE_X), (1, LANES)],
-        level, r, *fields, *particles, scratch=scratch,
+        level, r, *fields, *particles, scratch=scratch, far=4,
     )
     even, odd = exchange(to_even, to_odd, "gx", counts)
     wide, to_even, to_odd = call(
@@ -674,7 +708,7 @@
     change = share(slot)
     z2, image, slots = call(
         second_kernel, counts, [(4, 4, 4, LANES), (4, 4, 4, LANES), (bricks, 13, 1, LANES)],
-        level, change, r, w, *fields, *particles, scratch=scratch,
+        level, change, r, w, *fields, *particles, scratch=scratch, far=4,
     )
     slots = lax.all_to_all(slots, AXES, 0, 0)
     return tuple(

time: 72.1 us -> 66.8 us (0.926)
  local copies, waits for them, and re-layouts: 8.67 us -> 2.89 us
  waiting for transfers between devices: 15 us -> 19.9 us
  Pallas kernels: 11.6 us -> 8.03 us
    unnamed x14 -> x13, local copies, waits for them, and re-layouts: 7.98 us -> 2.22 us
    all_to_all x1, waiting for transfers between devices: 3.46 us -> 8.32 us  [share(): return lax.all_to_all(sent, AXES, 0, 0).reshape(bricks * 8, LANES)]
    pallas_call x8, Pallas kernels: 11.6 us -> 8.03 us  [call(): pl.pallas_call(functools.partial(kernel, counts), out_shape=[jax.ShapeDty...]
  transfers between devices with their start and end apart: 9 -> 9, of which waited for: 6 -> 6; matrix products, arithmetic and copies ran while one was open for 1% -> 0% of each run, Pallas kernels for 2% -> 0%
where the time goes in v3:
time: 66.8 us; the launch traced here: 66.5 us
  blocking collectives  22.6 us (34%)
  waiting for transfers between devices  19.9 us (30%)
  starting transfers between devices  12.4 us (19%)
  Pallas kernels  8.03 us (12%)
  local copies, waits for them, and re-layouts  2.89 us (4%)
  between operations  0.73 us (1%)
    ppermute x8, waiting for transfers between devices, exchange(): return (lax.ppermute(first, AXES, even), lax.ppermute(second, AXES, odd))  11.5 us
    all_to_all x1, blocking collectives, share(): return lax.all_to_all(sent, AXES, 0, 0).reshape(bricks * 8, LANES)  11.3 us
    all_to_all x1, blocking collectives, per_device(): slots = lax.all_to_all(slots, AXES, 0, 0)  11.3 us
    all_to_all x1, waiting for transfers between devices, share(): return lax.all_to_all(sent, AXES, 0, 0).reshape(bricks * 8, LANES)  8.32 us
    pallas_call x8, Pallas kernels, call(): pl.pallas_call(functools.partial(kernel, counts), out_shape=[jax.ShapeDty...  8.03 us
    all_to_all x1, starting transfers between devices, share(): return lax.all_to_all(sent, AXES, 0, 0).reshape(bricks * 8, LANES)  6.59 us
    ppermute x8, starting transfers between devices, exchange(): return (lax.ppermute(first, AXES, even), lax.ppermute(second, AXES, odd))  5.85 us
    unnamed x13, local copies, waits for them, and re-layouts  2.22 us
  transfers between devices with their start and end apart: 9, of which 6 were waited for; matrix products, arithmetic and copies ran while one was open for 0% of the time, Pallas kernels for 0%

profile of v3, /device:TPU:0, one launch (start us, length us, event | category | flops | bytes accessed | tf_op | source)
XLA Modules:
  0.0 66.5 jit_solution(13334952980590502823)
XLA Ops:
  0.6 0.7 %copy-done = f32[3,4,4,128]{3,2,1,0:T(4,128)S(1)} copy-done((f32[3,4,4,128]{3,2,1,0:T(4,128)S(1)}, f32[3,4,4,128]{3,2,1,0:T(4,128)}, u32[]{:S(2)}) %copy-start) | copy-done | bytes 24600
  1.4 0.7 %copy-done.4 = f32[4,4,128]{2,1,0:T(4,128)S(1)} copy-done((f32[4,4,128]{2,1,0:T(4,128)S(1)}, f32[4,4,128]{2,1,0:T(4,128)}, u32[]{:S(2)}) %copy-start.4) | copy-done | bytes 8216
  2.1 3.1 %collective-permute-start.1 = (f32[4,4,4,128]{3,2,1,0:T(4,128)S(1)}, f32[4,4,4,128]{3,2,1,0:T(4,128)S(1)}, u32[]{:S(2)}, u32[]{:S(2)}) collective-permute-start(f32[4,4,4,128]{3,2,1,0:T(4,128)S(1)} %shard_map.77.own_ref), channel_id=1, source_target_pairs={{0,1},{1,0},{2,3},{3,2},{4,8},{5,9},{6,10},{7,11},{8,4},{9,5},{10,... | collective-permute-start | bytes 98312 | tf_op jit(solution)/shard_map/ppermute | solution.py:38
  5.2 1.9 %collective-permute-done.1.odd_ref = f32[4,4,4,128]{3,2,1,0:T(4,128)S(1)} collective-permute-done((f32[4,4,4,128]{3,2,1,0:T(4,128)S(1)}, f32[4,4,4,128]{3,2,1,0:T(4,128)S(1)}, u32[]{:S(2)}, u32[]{:S(2)}) %collective-permute-start.1) | collective-permute-done | bytes 32800 | tf_op jit(solution)/shard_map/ppermute | solution.py:38
  7.2 2.1 %collective-permute-start.2 = (f32[96,128]{1,0:T(8,128)S(1)}, f32[96,128]{1,0:T(8,128)S(1)}, u32[]{:S(2)}, u32[]{:S(2)}) collective-permute-start(f32[96,128]{1,0:T(8,128)S(1)} %get-tuple-element.25), channel_id=1, source_target_pairs={{0,1},{1,0},{2,3},{3,2},{4,5},{5,4},{6,7},{7,6},{8,9},{9,8},{10,11... | collective-permute-start | bytes 147464 | tf_op jit(solution)/shard_map/ppermute | solution.py:38
  9.2 2.1 %collective-permute-done.2.even_ref = f32[96,128]{1,0:T(8,128)S(1)} collective-permute-done((f32[96,128]{1,0:T(8,128)S(1)}, f32[96,128]{1,0:T(8,128)S(1)}, u32[]{:S(2)}, u32[]{:S(2)}) %collective-permute-start.2) | collective-permute-done | bytes 49184 | tf_op jit(solution)/shard_map/ppermute | solution.py:38
  11.3 0.5 shard_map.79
  11.9 0.7 broadcast_in_dim.4
  12.5 6.6 %all-to-all-start = ((f32[32,8,128]{2,1,0:T(8,128)}), f32[32,8,128]{2,1,0:T(8,128)S(1)}, u32[]{:S(2)}, u32[]{:S(2)}) async-start(f32[32,8,128]{2,1,0:T(8,128)} %broadcast_in_dim.4), calls=%async_computation | async-start | bytes 262144 | tf_op jit(solution)/shard_map/all_to_all | solution.py:694
  19.1 0.1 copy.10
  19.2 8.3 %all-to-all-done = f32[32,8,128]{2,1,0:T(8,128)S(1)} async-done(((f32[32,8,128]{2,1,0:T(8,128)}), f32[32,8,128]{2,1,0:T(8,128)S(1)}, u32[]{:S(2)}, u32[]{:S(2)}) %all-to-all-start) | async-done | bytes 131104 | tf_op jit(solution)/shard_map/all_to_all | solution.py:694
  27.5 0.7 %copy-done.3 = s32[1,1,8,128]{3,2,1,0:T(8,128)S(1)} copy-done((s32[1,1,8,128]{3,2,1,0:T(8,128)S(1)}, s32[1,1,8,128]{3,2,1,0:T(8,128)}, u32[]{:S(2)}) %copy-start.3) | copy-done | bytes 4120
  28.2 2.8 %shard_map.80 = (f32[4,4,4,128]{3,2,1,0:T(4,128)S(1)}, f32[6,6,4,128]{3,2,1,0:T(4,128)S(1)}, f32[80,128]{1,0:T(8,128)S(1)}, f32[80,128]{1,0:T(8,128)S(1)}, f32[1,128]{1,0:T(1,128)S(1)}) custom-call(f32[256,128]{1,0:T(8,128)S(1)} %bitcast.10, f32[8,8,4,128]{3,2,1,0:T(4,128)S(1)} %get-tuple-element.28.r_ref, ...), custom_call_target="tpu_custom_call" | custom-call | tf_op jit(solution)/shard_map/pallas_call | solution.py:653
  31.1 0.1 collective-permute-start.4
  31.2 0.3 collective-permute-start.5
  31.4 0.9 %collective-permute-done.4.even_ref = f32[80,128]{1,0:T(8,128)S(1)} collective-permute-done((f32[80,128]{1,0:T(8,128)S(1)}, f32[80,128]{1,0:T(8,128)S(1)}, u32[]{:S(2)}, u32[]{:S(2)}) %collective-permute-start.4) | collective-permute-done | bytes 40992 | tf_op jit(solution)/shard_map/ppermute | solution.py:38
  32.4 2.9 %collective-permute-done.5.odd_ref = f32[80,128]{1,0:T(8,128)S(1)} collective-permute-done((f32[80,128]{1,0:T(8,128)S(1)}, f32[80,128]{1,0:T(8,128)S(1)}, u32[]{:S(2)}, u32[]{:S(2)}) %collective-permute-start.5) | collective-permute-done | bytes 40992 | tf_op jit(solution)/shard_map/ppermute | solution.py:38
  35.3 0.3 collective-permute-start.6
  35.6 3.8 %collective-permute-done.6.even_ref = f32[88,128]{1,0:T(8,128)S(1)} collective-permute-done((f32[88,128]{1,0:T(8,128)S(1)}, f32[88,128]{1,0:T(8,128)S(1)}, u32[]{:S(2)}, u32[]{:S(2)}) %collective-permute-start.6) | collective-permute-done | bytes 45088 | tf_op jit(solution)/shard_map/ppermute | solution.py:38
  39.4 0.5 shard_map.82
  39.9 11.3 %all_to_all.15 = f32[32,8,128]{2,1,0:T(8,128)S(1)} all-to-all(f32[32,8,128]{2,1,0:T(8,128)S(1)} %broadcast_in_dim.5), channel_id=1, replica_groups=mesh['gx'=8,'gy'=4] {'gx','gy'}, dimensions={0} | all-to-all | bytes 262144 | tf_op jit(solution)/shard_map/all_to_all | solution.py:694
  51.2 3.1 %shard_map.83 = (f32[4,4,4,128]{3,2,1,0:T(4,128)S(1)}, f32[4,4,4,128]{3,2,1,0:T(4,128)S(1)}, f32[32,13,1,128]{3,2,1,0:T(1,128)S(1)}) custom-call(f32[256,128]{1,0:T(8,128)S(1)} %bitcast.11, f32[256,128]{1,0:T(8,128)S(1)} %bitcast.12, f32[8,8,4,128]{3,2,1,0:T(4,128)S(1)} %get-tuple-element.28.r_ref, f32[8,8,4,128]{3,2,1,0:T(4,128)S(1)} %get-tuple-element.41.w_ref, ...), custom_call_target="tpu_custom_call" | custom-call | tf_op jit(solution)/shard_map/pallas_call | solution.py:653
  54.3 11.3 %all_to_all.16.slots_ref = f32[32,13,1,128]{3,2,1,0:T(1,128)S(1)} all-to-all(f32[32,13,1,128]{3,2,1,0:T(1,128)S(1)} %get-tuple-element.42), channel_id=1, replica_groups=mesh['gx'=8,'gy'=4] {'gx','gy'}, dimensions={0} | all-to-all | bytes 425984 | tf_op jit(solution)/shard_map/all_to_all | solution.py:713
  65.6 0.9 %shard_map.84 = (f32[3,4,4,128]{3,2,1,0:T(4,128)}, f32[3,4,4,128]{3,2,1,0:T(4,128)}) custom-call(f32[32,13,1,128]{3,2,1,0:T(1,128)S(1)} %all_to_all.16.slots_ref, f32[256,128]{1,0:T(8,128)S(1)} %bitcast.13, f32[4,4,4,128]{3,2,1,0:T(4,128)S(1)} %get-tuple-element.43.z1_ref, f32[4,4,4,128]{3,2,1,0:T(4,128)S(1)} %get-tuple-element.44.z2_ref, ...), custom_call_target="tpu_custom_call" | custom-call | tf_op jit(solution)/shard_map/pallas_call | solution.py:653
  (19 shorter events, 0.3 us)
Async XLA Ops:
  0.6 0.7 %copy-start = (f32[3,4,4,128]{3,2,1,0:T(4,128)S(1)}, f32[3,4,4,128]{3,2,1,0:T(4,128)}, u32[]{:S(2)}) copy-start(f32[3,4,4,128]{3,2,1,0:T(4,128)} %right_ref.1) | copy-start | bytes 73732
  1.4 0.7 %copy-start.4 = (f32[4,4,128]{2,1,0:T(4,128)S(1)}, f32[4,4,128]{2,1,0:T(4,128)}, u32[]{:S(2)}) copy-start(f32[4,4,128]{2,1,0:T(4,128)} %mass_ref.1) | copy-start | bytes 24580
  2.1 17.0 %copy-start.5 = (f32[1,1,8,3,27,128]{5,2,4,3,1,0:T(8,128)S(1)}, f32[1,1,8,3,27,128]{5,2,4,3,1,0:T(8,128)}, u32[]{:S(2)}) copy-start(f32[1,1,8,3,27,128]{5,2,4,3,1,0:T(8,128)} %param.8) | copy-start | bytes 995332
  2.1 5.0 %collective-permute-start.1 = (f32[4,4,4,128]{3,2,1,0:T(4,128)S(1)}, f32[4,4,4,128]{3,2,1,0:T(4,128)S(1)}, u32[]{:S(2)}, u32[]{:S(2)}) collective-permute-start(f32[4,4,4,128]{3,2,1,0:T(4,128)S(1)} %shard_map.77.own_ref), channel_id=1, source_target_pairs={{0,1},{1,0},{2,3},{3,2},{4,8},{5,9},{6,10},{7,11},{8,4},{9,5},{10,... | collective-permute-start | bytes 98312 | tf_op jit(solution)/shard_map/ppermute | solution.py:38
  5.2 1.9 %collective-permute-start = (f32[4,4,4,128]{3,2,1,0:T(4,128)S(1)}, f32[4,4,4,128]{3,2,1,0:T(4,128)S(1)}, u32[]{:S(2)}, u32[]{:S(2)}) collective-permute-start(f32[4,4,4,128]{3,2,1,0:T(4,128)S(1)} %shard_map.77.own_ref), channel_id=1, source_target_pairs={{0,4},{1,5},{2,6},{3,7},{4,0},{5,1},{6,2},{7,3},{8,12},{9,13},{10,... | collective-permute-start | bytes 98312 | tf_op jit(solution)/shard_map/ppermute | solution.py:38
  7.2 4.2 %collective-permute-start.2 = (f32[96,128]{1,0:T(8,128)S(1)}, f32[96,128]{1,0:T(8,128)S(1)}, u32[]{:S(2)}, u32[]{:S(2)}) collective-permute-start(f32[96,128]{1,0:T(8,128)S(1)} %get-tuple-element.25), channel_id=1, source_target_pairs={{0,1},{1,0},{2,3},{3,2},{4,5},{5,4},{6,7},{7,6},{8,9},{9,8},{10,11... | collective-permute-start | bytes 147464 | tf_op jit(solution)/shard_map/ppermute | solution.py:38
  9.2 2.1 %collective-permute-start.3 = (f32[96,128]{1,0:T(8,128)S(1)}, f32[96,128]{1,0:T(8,128)S(1)}, u32[]{:S(2)}, u32[]{:S(2)}) collective-permute-start(f32[96,128]{1,0:T(8,128)S(1)} %get-tuple-element.26), channel_id=1, source_target_pairs={{0,4},{1,2},{2,1},{3,7},{4,0},{5,6},{6,5},{7,3},{8,12},{9,10},{10,... | collective-permute-start | bytes 147464 | tf_op jit(solution)/shard_map/ppermute | solution.py:38
  12.5 15.0 %all-to-all-start = ((f32[32,8,128]{2,1,0:T(8,128)}), f32[32,8,128]{2,1,0:T(8,128)S(1)}, u32[]{:S(2)}, u32[]{:S(2)}) async-start(f32[32,8,128]{2,1,0:T(8,128)} %broadcast_in_dim.4), calls=%async_computation | async-start | bytes 262144 | tf_op jit(solution)/shard_map/all_to_all | solution.py:694
  27.5 0.7 %copy-start.3 = (s32[1,1,8,128]{3,2,1,0:T(8,128)S(1)}, s32[1,1,8,128]{3,2,1,0:T(8,128)}, u32[]{:S(2)}) copy-start(s32[1,1,8,128]{3,2,1,0:T(8,128)} %param.10) | copy-start | bytes 12292
  27.5 0.7 %copy-start.2 = (f32[1,1,8,128]{3,2,1,0:T(8,128)S(1)}, f32[1,1,8,128]{3,2,1,0:T(8,128)}, u32[]{:S(2)}) copy-start(f32[1,1,8,128]{3,2,1,0:T(8,128)} %param.9) | copy-start | bytes 12292
  27.5 0.7 %copy-start.1 = (s32[1,1,8,128]{3,2,1,0:T(8,128)S(1)}, s32[1,1,8,128]{3,2,1,0:T(8,128)}, u32[]{:S(2)}) copy-start(s32[1,1,8,128]{3,2,1,0:T(8,128)} %param.11) | copy-start | bytes 12292
  31.1 1.3 %collective-permute-start.4 = (f32[80,128]{1,0:T(8,128)S(1)}, f32[80,128]{1,0:T(8,128)S(1)}, u32[]{:S(2)}, u32[]{:S(2)}) collective-permute-start(f32[80,128]{1,0:T(8,128)S(1)} %get-tuple-element.34), channel_id=1, source_target_pairs={{0,4},{1,5},{2,6},{3,7},{4,0},{5,1},{6,2},{7,3},{8,12},{9,13},{10,... | collective-permute-start | bytes 122888 | tf_op jit(solution)/shard_map/ppermute | solution.py:38
  31.2 4.1 %collective-permute-start.5 = (f32[80,128]{1,0:T(8,128)S(1)}, f32[80,128]{1,0:T(8,128)S(1)}, u32[]{:S(2)}, u32[]{:S(2)}) collective-permute-start(f32[80,128]{1,0:T(8,128)S(1)} %get-tuple-element.35), channel_id=1, source_target_pairs={{0,1},{1,0},{2,3},{3,2},{4,8},{5,9},{6,10},{7,11},{8,4},{9,5},{10,... | collective-permute-start | bytes 122888 | tf_op jit(solution)/shard_map/ppermute | solution.py:38
  35.3 4.1 %collective-permute-start.6 = (f32[88,128]{1,0:T(8,128)S(1)}, f32[88,128]{1,0:T(8,128)S(1)}, u32[]{:S(2)}, u32[]{:S(2)}) collective-permute-start(f32[88,128]{1,0:T(8,128)S(1)} %get-tuple-element.37), channel_id=1, source_target_pairs={{0,1},{1,0},{2,3},{3,2},{4,5},{5,4},{6,7},{7,6},{8,9},{9,8},{10,11... | collective-permute-start | bytes 135176 | tf_op jit(solution)/shard_map/ppermute | solution.py:38
  35.6 3.8 %collective-permute-start.7 = (f32[88,128]{1,0:T(8,128)S(1)}, f32[88,128]{1,0:T(8,128)S(1)}, u32[]{:S(2)}, u32[]{:S(2)}) collective-permute-start(f32[88,128]{1,0:T(8,128)S(1)} %get-tuple-element.38), channel_id=1, source_target_pairs={{0,4},{1,2},{2,1},{3,7},{4,0},{5,6},{6,5},{7,3},{8,12},{9,10},{10,... | collective-permute-start | bytes 135176 | tf_op jit(solution)/shard_map/ppermute | solution.py:38

commit v4 on v3

--- a/solution.py
+++ b/solution.py
@@ -203,7 +203,7 @@
 
 
 def stiffness_apply(z, fetched, base_ref, stiff_ref, valid_ref, grad_ref, hot, nodes, forces, picked, spread_sums, shifts):
-    blocks = grad_ref.shape[0]
+    blocks = grad_ref.shape[2]
     turns = [(b, c) for b in range(3) for c in range(3)]
     span = BRICK + 2
 
@@ -247,7 +247,7 @@
     wide = lambda row: jnp.broadcast_to(row, (8, LANES))
     for s in range(blocks):
         lanes = slice(s * LANES, (s + 1) * LANES)
-        grad = lambda l, a, b, c: wide(grad_ref[s, l, 9 * a + 3 * b + c : 9 * a + 3 * b + c + 1, :])
+        grad = lambda l, a, b, c: wide(grad_ref[l, 9 * a + 3 * b + c, s : s + 1, :])
         at_x = [wide(node_x[s : s + 1]) == i for i in range(BRICK)]
         h = [None] * 3
         for u, (b, c) in enumerate(turns):
@@ -344,7 +344,8 @@
         ref[ref.shape[0] - 8 :, :] = jnp.zeros((8, LANES), F32)
 
 
-def pack_kernel(counts, right_ref, mass_ref, own_ref):
+def pack_kernel(counts, right_in, mass_in, own_ref, right_ref, mass_ref, semaphores):
+    fetch((right_in, mass_in), (right_ref, mass_ref), semaphores)()
     for x in range(BRICK):
         for y in range(BRICK):
             for m in range(3):
@@ -653,7 +654,7 @@
     return pl.pallas_call(
         functools.partial(kernel, counts),
         out_shape=[jax.ShapeDtypeStruct(s, F32) for s in shapes],
-        in_specs=[pl.BlockSpec(memory_space=pltpu.VMEM)] * near + [pl.BlockSpec(memory_space=pl.ANY)] * far,
+        in_specs=[pl.BlockSpec(memory_space=pltpu.VMEM)] * near + [pl.BlockSpec(memory_space=pltpu.HBM)] * far,
         scratch_shapes=scratch,
         compiler_params=pltpu.CompilerParams(vmem_limit_bytes=VMEM_BYTES),
     )(*args)
@@ -662,7 +663,7 @@
 def per_device(counts, right_side, node_mass, gradients, stiffness, valid, node_base):
     bricks = counts[0] * counts[1]
     blocks = gradients.shape[2]
-    particles = (node_base[0, 0], stiffness[0, 0], valid[0, 0], gradients[0, 0])
+    particles = (node_base[0, 0], stiffness[0, 0], valid[0, 0], gradients[0, 0].transpose(1, 2, 0, 3))
     tiles = 9 * (BRICK + 2) * 8
     depth = BRICK * LANES
     width = blocks * LANES
@@ -678,7 +679,11 @@
     )
     rows = lambda columns, more=0: (-(-(3 * len(columns) + more + 1) // 8) * 8, LANES)
 
-    (own,) = call(pack_kernel, counts, [(4, 4, 4, LANES)], right_side, node_mass)
+    fields = (right_side, node_mass)
+    (own,) = call(
+        pack_kernel, counts, [(4, 4, 4, LANES)], *fields, far=2,
+        scratch=(*(pltpu.VMEM(p.shape, p.dtype) for p in fields), pltpu.SemaphoreType.DMA((2,))),
+    )
     even, odd = exchange(own, own, "gx", counts)
     side = rows(SIDE, len(SIDE_MASS))
     wide, to_even, to_odd = call(widen_kernel, counts, [(12, 4, 4, LANES), side, side], own, even, odd)

time: 66.8 us -> 66.2 us (level)
  blocking collectives: 22.6 us -> 37.3 us
  waiting for transfers between devices: 19.9 us -> 11.5 us
  starting transfers between devices: 12.4 us -> 5.84 us
  local copies, waits for them, and re-layouts: 2.89 us -> 2.17 us
    all_to_all x1 -> x2, blocking collectives: 11.3 us -> 26.1 us  [share(): return lax.all_to_all(sent, AXES, 0, 0).reshape(bricks * 8, LANES)]
    all_to_all x1 -> x0, waiting for transfers between devices: 8.32 us -> none  [share(): return lax.all_to_all(sent, AXES, 0, 0).reshape(bricks * 8, LANES)]
    all_to_all x1 -> x0, starting transfers between devices: 6.59 us -> none  [share(): return lax.all_to_all(sent, AXES, 0, 0).reshape(bricks * 8, LANES)]
    unnamed x13 -> x12, local copies, waits for them, and re-layouts: 2.22 us -> 2.14 us
  transfers between devices with their start and end apart: 9 -> 8, of which waited for: 6 -> 5; matrix products, arithmetic and copies ran while one was open for 0% -> 0% of each run, Pallas kernels for 0% -> 0%
where the time goes in v4:
time: 66.2 us; the launch traced here: 65.8 us
  blocking collectives  37.3 us (56%)
  waiting for transfers between devices  11.5 us (17%)
  Pallas kernels  8.21 us (12%)
  starting transfers between devices  5.84 us (9%)
  local copies, waits for them, and re-layouts  2.17 us (3%)
  between operations  0.73 us (1%)
    all_to_all x2, blocking collectives, share(): return lax.all_to_all(sent, AXES, 0, 0).reshape(bricks * 8, LANES)  26.1 us
    ppermute x8, waiting for transfers between devices, exchange(): return (lax.ppermute(first, AXES, even), lax.ppermute(second, AXES, odd))  11.5 us
    all_to_all x1, blocking collectives, per_device(): slots = lax.all_to_all(slots, AXES, 0, 0)  11.3 us
    pallas_call x8, Pallas kernels, call(): pl.pallas_call(functools.partial(kernel, counts), out_shape=[jax.ShapeDty...  8.21 us
    ppermute x8, starting transfers between devices, exchange(): return (lax.ppermute(first, AXES, even), lax.ppermute(second, AXES, odd))  5.84 us
    unnamed x12, local copies, waits for them, and re-layouts  2.14 us
  transfers between devices with their start and end apart: 8, of which 5 were waited for; matrix products, arithmetic and copies ran while one was open for 0% of the time, Pallas kernels for 0%

profile of v4, /device:TPU:0, one launch (start us, length us, event | category | flops | bytes accessed | tf_op | source)
XLA Modules:
  0.0 65.8 jit_solution(16287148094075584598)
XLA Ops:
  0.6 0.7 %copy-done.1 = f32[3,4,4,128]{3,2,1,0:T(4,128)S(1)} copy-done((f32[3,4,4,128]{3,2,1,0:T(4,128)S(1)}, f32[3,4,4,128]{3,2,1,0:T(4,128)}, u32[]{:S(2)}) %copy-start.1) | copy-done | bytes 24600
  1.4 0.7 %copy-done.5 = f32[4,4,128]{2,1,0:T(4,128)S(1)} copy-done((f32[4,4,128]{2,1,0:T(4,128)S(1)}, f32[4,4,128]{2,1,0:T(4,128)}, u32[]{:S(2)}) %copy-start.5) | copy-done | bytes 8216
  2.1 0.1 shard_map.77.own_ref
  2.1 3.1 %collective-permute-start.1 = (f32[4,4,4,128]{3,2,1,0:T(4,128)S(1)}, f32[4,4,4,128]{3,2,1,0:T(4,128)S(1)}, u32[]{:S(2)}, u32[]{:S(2)}) collective-permute-start(f32[4,4,4,128]{3,2,1,0:T(4,128)S(1)} %shard_map.77.own_ref), channel_id=1, source_target_pairs={{0,1},{1,0},{2,3},{3,2},{4,8},{5,9},{6,10},{7,11},{8,4},{9,5},{10,... | collective-permute-start | bytes 98312 | tf_op jit(solution)/shard_map/ppermute | solution.py:38
  5.2 1.9 %collective-permute-done.1.odd_ref = f32[4,4,4,128]{3,2,1,0:T(4,128)S(1)} collective-permute-done((f32[4,4,4,128]{3,2,1,0:T(4,128)S(1)}, f32[4,4,4,128]{3,2,1,0:T(4,128)S(1)}, u32[]{:S(2)}, u32[]{:S(2)}) %collective-permute-start.1) | collective-permute-done | bytes 32800 | tf_op jit(solution)/shard_map/ppermute | solution.py:38
  7.1 0.1 shard_map.78
  7.2 2.1 %collective-permute-start.2 = (f32[96,128]{1,0:T(8,128)S(1)}, f32[96,128]{1,0:T(8,128)S(1)}, u32[]{:S(2)}, u32[]{:S(2)}) collective-permute-start(f32[96,128]{1,0:T(8,128)S(1)} %get-tuple-element.25), channel_id=1, source_target_pairs={{0,1},{1,0},{2,3},{3,2},{4,5},{5,4},{6,7},{7,6},{8,9},{9,8},{10,11... | collective-permute-start | bytes 147464 | tf_op jit(solution)/shard_map/ppermute | solution.py:38
  9.3 2.1 %collective-permute-done.2.even_ref = f32[96,128]{1,0:T(8,128)S(1)} collective-permute-done((f32[96,128]{1,0:T(8,128)S(1)}, f32[96,128]{1,0:T(8,128)S(1)}, u32[]{:S(2)}, u32[]{:S(2)}) %collective-permute-start.2) | collective-permute-done | bytes 49184 | tf_op jit(solution)/shard_map/ppermute | solution.py:38
  11.4 0.6 shard_map.79
  11.9 14.8 %all_to_all.15 = f32[32,8,128]{2,1,0:T(8,128)S(1)} all-to-all(f32[32,8,128]{2,1,0:T(8,128)S(1)} %broadcast_in_dim.4), channel_id=1, replica_groups=mesh['gx'=8,'gy'=4] {'gx','gy'}, dimensions={0} | all-to-all | bytes 262144 | tf_op jit(solution)/shard_map/all_to_all | solution.py:699
  26.7 0.7 %copy-done.4 = s32[1,1,8,128]{3,2,1,0:T(8,128)S(1)} copy-done((s32[1,1,8,128]{3,2,1,0:T(8,128)S(1)}, s32[1,1,8,128]{3,2,1,0:T(8,128)}, u32[]{:S(2)}) %copy-start.4) | copy-done | bytes 4120
  27.5 2.9 %shard_map.80 = (f32[4,4,4,128]{3,2,1,0:T(4,128)S(1)}, f32[6,6,4,128]{3,2,1,0:T(4,128)S(1)}, f32[80,128]{1,0:T(8,128)S(1)}, f32[80,128]{1,0:T(8,128)S(1)}, f32[1,128]{1,0:T(1,128)S(1)}) custom-call(f32[256,128]{1,0:T(8,128)S(1)} %bitcast.10, f32[8,8,4,128]{3,2,1,0:T(4,128)S(1)} %get-tuple-element.28.r_ref, ...), custom_call_target="tpu_custom_call" | custom-call | tf_op jit(solution)/shard_map/pallas_call | solution.py:654
  30.4 0.1 collective-permute-start.4
  30.4 0.3 collective-permute-start.5
  30.7 0.9 %collective-permute-done.4.even_ref = f32[80,128]{1,0:T(8,128)S(1)} collective-permute-done((f32[80,128]{1,0:T(8,128)S(1)}, f32[80,128]{1,0:T(8,128)S(1)}, u32[]{:S(2)}, u32[]{:S(2)}) %collective-permute-start.4) | collective-permute-done | bytes 40992 | tf_op jit(solution)/shard_map/ppermute | solution.py:38
  31.6 2.9 %collective-permute-done.5.odd_ref = f32[80,128]{1,0:T(8,128)S(1)} collective-permute-done((f32[80,128]{1,0:T(8,128)S(1)}, f32[80,128]{1,0:T(8,128)S(1)}, u32[]{:S(2)}, u32[]{:S(2)}) %collective-permute-start.5) | collective-permute-done | bytes 40992 | tf_op jit(solution)/shard_map/ppermute | solution.py:38
  34.5 0.1 shard_map.81
  34.6 0.3 collective-permute-start.6
  34.9 3.8 %collective-permute-done.6.even_ref = f32[88,128]{1,0:T(8,128)S(1)} collective-permute-done((f32[88,128]{1,0:T(8,128)S(1)}, f32[88,128]{1,0:T(8,128)S(1)}, u32[]{:S(2)}, u32[]{:S(2)}) %collective-permute-start.6) | collective-permute-done | bytes 45088 | tf_op jit(solution)/shard_map/ppermute | solution.py:38
  38.7 0.5 shard_map.82
  39.2 11.3 %all_to_all.16 = f32[32,8,128]{2,1,0:T(8,128)S(1)} all-to-all(f32[32,8,128]{2,1,0:T(8,128)S(1)} %broadcast_in_dim.5), channel_id=1, replica_groups=mesh['gx'=8,'gy'=4] {'gx','gy'}, dimensions={0} | all-to-all | bytes 262144 | tf_op jit(solution)/shard_map/all_to_all | solution.py:699
  50.5 3.2 %shard_map.83 = (f32[4,4,4,128]{3,2,1,0:T(4,128)S(1)}, f32[4,4,4,128]{3,2,1,0:T(4,128)S(1)}, f32[32,13,1,128]{3,2,1,0:T(1,128)S(1)}) custom-call(f32[256,128]{1,0:T(8,128)S(1)} %bitcast.11, f32[256,128]{1,0:T(8,128)S(1)} %bitcast.12, f32[8,8,4,128]{3,2,1,0:T(4,128)S(1)} %get-tuple-element.28.r_ref, f32[8,8,4,128]{3,2,1,0:T(4,128)S(1)} %get-tuple-element.41.w_ref, ...), custom_call_target="tpu_custom_call" | custom-call | tf_op jit(solution)/shard_map/pallas_call | solution.py:654
  53.7 11.3 %all_to_all.17.slots_ref = f32[32,13,1,128]{3,2,1,0:T(1,128)S(1)} all-to-all(f32[32,13,1,128]{3,2,1,0:T(1,128)S(1)} %get-tuple-element.42), channel_id=1, replica_groups=mesh['gx'=8,'gy'=4] {'gx','gy'}, dimensions={0} | all-to-all | bytes 425984 | tf_op jit(solution)/shard_map/all_to_all | solution.py:718
  64.9 0.9 %shard_map.84 = (f32[3,4,4,128]{3,2,1,0:T(4,128)}, f32[3,4,4,128]{3,2,1,0:T(4,128)}) custom-call(f32[32,13,1,128]{3,2,1,0:T(1,128)S(1)} %all_to_all.17.slots_ref, f32[256,128]{1,0:T(8,128)S(1)} %bitcast.13, f32[4,4,4,128]{3,2,1,0:T(4,128)S(1)} %get-tuple-element.43.z1_ref, f32[4,4,4,128]{3,2,1,0:T(4,128)S(1)} %get-tuple-element.44.z2_ref, ...), custom_call_target="tpu_custom_call" | custom-call | tf_op jit(solution)/shard_map/pallas_call | solution.py:654
  (17 shorter events, 0.1 us)
Async XLA Ops:
  0.6 0.7 %copy-start.1 = (f32[3,4,4,128]{3,2,1,0:T(4,128)S(1)}, f32[3,4,4,128]{3,2,1,0:T(4,128)}, u32[]{:S(2)}) copy-start(f32[3,4,4,128]{3,2,1,0:T(4,128)} %right_in.1) | copy-start | bytes 73732
  1.4 0.7 %copy-start.5 = (f32[4,4,128]{2,1,0:T(4,128)S(1)}, f32[4,4,128]{2,1,0:T(4,128)}, u32[]{:S(2)}) copy-start(f32[4,4,128]{2,1,0:T(4,128)} %mass_in.1) | copy-start | bytes 24580
  2.1 5.0 %collective-permute-start.1 = (f32[4,4,4,128]{3,2,1,0:T(4,128)S(1)}, f32[4,4,4,128]{3,2,1,0:T(4,128)S(1)}, u32[]{:S(2)}, u32[]{:S(2)}) collective-permute-start(f32[4,4,4,128]{3,2,1,0:T(4,128)S(1)} %shard_map.77.own_ref), channel_id=1, source_target_pairs={{0,1},{1,0},{2,3},{3,2},{4,8},{5,9},{6,10},{7,11},{8,4},{9,5},{10,... | collective-permute-start | bytes 98312 | tf_op jit(solution)/shard_map/ppermute | solution.py:38
  5.2 1.9 %collective-permute-start = (f32[4,4,4,128]{3,2,1,0:T(4,128)S(1)}, f32[4,4,4,128]{3,2,1,0:T(4,128)S(1)}, u32[]{:S(2)}, u32[]{:S(2)}) collective-permute-start(f32[4,4,4,128]{3,2,1,0:T(4,128)S(1)} %shard_map.77.own_ref), channel_id=1, source_target_pairs={{0,4},{1,5},{2,6},{3,7},{4,0},{5,1},{6,2},{7,3},{8,12},{9,13},{10,... | collective-permute-start | bytes 98312 | tf_op jit(solution)/shard_map/ppermute | solution.py:38
  7.2 19.6 %copy-start = (f32[1,1,8,3,27,128]{5,2,4,3,1,0:T(8,128)S(1)}, f32[1,1,8,3,27,128]{5,2,4,3,1,0:T(8,128)}, u32[]{:S(2)}) copy-start(f32[1,1,8,3,27,128]{5,2,4,3,1,0:T(8,128)} %param.8) | copy-start | bytes 995332
  7.2 4.2 %collective-permute-start.2 = (f32[96,128]{1,0:T(8,128)S(1)}, f32[96,128]{1,0:T(8,128)S(1)}, u32[]{:S(2)}, u32[]{:S(2)}) collective-permute-start(f32[96,128]{1,0:T(8,128)S(1)} %get-tuple-element.25), channel_id=1, source_target_pairs={{0,1},{1,0},{2,3},{3,2},{4,5},{5,4},{6,7},{7,6},{8,9},{9,8},{10,11... | collective-permute-start | bytes 147464 | tf_op jit(solution)/shard_map/ppermute | solution.py:38
  9.3 2.1 %collective-permute-start.3 = (f32[96,128]{1,0:T(8,128)S(1)}, f32[96,128]{1,0:T(8,128)S(1)}, u32[]{:S(2)}, u32[]{:S(2)}) collective-permute-start(f32[96,128]{1,0:T(8,128)S(1)} %get-tuple-element.26), channel_id=1, source_target_pairs={{0,4},{1,2},{2,1},{3,7},{4,0},{5,6},{6,5},{7,3},{8,12},{9,10},{10,... | collective-permute-start | bytes 147464 | tf_op jit(solution)/shard_map/ppermute | solution.py:38
  26.7 0.7 %copy-start.4 = (s32[1,1,8,128]{3,2,1,0:T(8,128)S(1)}, s32[1,1,8,128]{3,2,1,0:T(8,128)}, u32[]{:S(2)}) copy-start(s32[1,1,8,128]{3,2,1,0:T(8,128)} %param.10) | copy-start | bytes 12292
  26.7 0.7 %copy-start.3 = (f32[1,1,8,128]{3,2,1,0:T(8,128)S(1)}, f32[1,1,8,128]{3,2,1,0:T(8,128)}, u32[]{:S(2)}) copy-start(f32[1,1,8,128]{3,2,1,0:T(8,128)} %param.9) | copy-start | bytes 12292
  26.7 0.7 %copy-start.2 = (s32[1,1,8,128]{3,2,1,0:T(8,128)S(1)}, s32[1,1,8,128]{3,2,1,0:T(8,128)}, u32[]{:S(2)}) copy-start(s32[1,1,8,128]{3,2,1,0:T(8,128)} %param.11) | copy-start | bytes 12292
  30.4 1.3 %collective-permute-start.4 = (f32[80,128]{1,0:T(8,128)S(1)}, f32[80,128]{1,0:T(8,128)S(1)}, u32[]{:S(2)}, u32[]{:S(2)}) collective-permute-start(f32[80,128]{1,0:T(8,128)S(1)} %get-tuple-element.34), channel_id=1, source_target_pairs={{0,4},{1,5},{2,6},{3,7},{4,0},{5,1},{6,2},{7,3},{8,12},{9,13},{10,... | collective-permute-start | bytes 122888 | tf_op jit(solution)/shard_map/ppermute | solution.py:38
  30.4 4.1 %collective-permute-start.5 = (f32[80,128]{1,0:T(8,128)S(1)}, f32[80,128]{1,0:T(8,128)S(1)}, u32[]{:S(2)}, u32[]{:S(2)}) collective-permute-start(f32[80,128]{1,0:T(8,128)S(1)} %get-tuple-element.35), channel_id=1, source_target_pairs={{0,1},{1,0},{2,3},{3,2},{4,8},{5,9},{6,10},{7,11},{8,4},{9,5},{10,... | collective-permute-start | bytes 122888 | tf_op jit(solution)/shard_map/ppermute | solution.py:38
  34.6 4.1 %collective-permute-start.6 = (f32[88,128]{1,0:T(8,128)S(1)}, f32[88,128]{1,0:T(8,128)S(1)}, u32[]{:S(2)}, u32[]{:S(2)}) collective-permute-start(f32[88,128]{1,0:T(8,128)S(1)} %get-tuple-element.37), channel_id=1, source_target_pairs={{0,1},{1,0},{2,3},{3,2},{4,5},{5,4},{6,7},{7,6},{8,9},{9,8},{10,11... | collective-permute-start | bytes 135176 | tf_op jit(solution)/shard_map/ppermute | solution.py:38
  34.9 3.8 %collective-permute-start.7 = (f32[88,128]{1,0:T(8,128)S(1)}, f32[88,128]{1,0:T(8,128)S(1)}, u32[]{:S(2)}, u32[]{:S(2)}) collective-permute-start(f32[88,128]{1,0:T(8,128)S(1)} %get-tuple-element.38), channel_id=1, source_target_pairs={{0,4},{1,2},{2,1},{3,7},{4,0},{5,6},{6,5},{7,3},{8,12},{9,10},{10,... | collective-permute-start | bytes 135176 | tf_op jit(solution)/shard_map/ppermute | solution.py:38

commit v5 on v4

--- a/solution.py
+++ b/solution.py
@@ -38,12 +38,10 @@
     return lax.ppermute(first, AXES, even), lax.ppermute(second, AXES, odd)
 
 
-SIDE = (
-    [(x, -1) for x in range(-2, 6)] + [(x, -2) for x in range(-1, 5)] + [(x, -3) for x in range(4)]
-)
-SIDE_MASS = [(x, y) for y in (-1, -2) for x in range(-4, 8)] + [(x, y) for y in (-3, -4) for x in range(-2, 6)]
-SIDE_IMAGE = [(x, 0) for x in range(-3, 7)] + SIDE
-SIDE_X = [(x, y) for x in range(-3, 1) for y in range(-1, 5)]
+SIDE = [(x, -1) for x in range(-2, 6)] + [(x, -2) for x in range(-1, 5)]
+SIDE_IMAGE = [(x, 0) for x in range(-2, 6)] + SIDE
+SIDE_X = [(x, y) for x in (-2, -1) for y in range(BRICK)]
+SIDE_X_IMAGE = [(x, y) for x in (-2, -1, 0) for y in range(-1, 5)]
 
 
 def mirror(x, y):
@@ -128,75 +126,104 @@
     return at
 
 
-def restriction(r, mass0, weight0, mass1, weight1, place, shifts):
-    e0 = memo(lambda x, y: weight0(x, y) * r(x, y))
-    g0 = grid_apply(e0, mass0, 1.0, shifts, 1)
-    rem0 = memo(lambda x, y: r(x, y) - g0(x, y))
-
-    def r1_at(x, y):
-        total = rem0(2 * x, 2 * y) + rem0(2 * x + 1, 2 * y) + rem0(2 * x, 2 * y + 1) + rem0(2 * x + 1, 2 * y + 1)
-        return place.keep(shifts.pair_sum(total), x, y, 2)
-
-    r1 = memo(r1_at)
-    e1 = memo(lambda x, y: weight1(x, y) * r1(x, y))
-    g1 = grid_apply(e1, mass1, 2.0, shifts, 2)
-    total = 0.0
-    for x in range(2):
-        for y in range(2):
-            total = total + (r1(x, y) - g1(x, y))
-    return r1, shifts.quad_sum(total)
-
-
-def pack_slot(r1, r2_row, dots_row, shifts):
-    top = r1(0, 0) * shifts.even + r1(0, 1) * shifts.odd
-    low = r1(1, 0) * shifts.even + r1(1, 1) * shifts.odd
-    return jnp.concatenate([top[0:3], r2_row, low[0:3], dots_row], axis=0)
-
-
-def pack_quads(column):
-    lane = lax.broadcasted_iota(jnp.int32, (4, LANES), 1)
-    row = lax.broadcasted_iota(jnp.int32, (4, LANES), 0)
-    return jnp.sum(column * as_f32(lane % 4 == row), axis=0, keepdims=True)
-
-
-def unpack_quads(row):
-    lane = lax.broadcasted_iota(jnp.int32, (4, LANES), 1)
-    index = lax.broadcasted_iota(jnp.int32, (4, LANES), 0)
-    x = jnp.broadcast_to(row, (4, LANES)) * as_f32(lane % 4 == index)
-    return spread_quads(x, lane)
-
-
-def spread_quads(x, lane):
-    even = as_f32(lane % 2 == 0)
-    odd = 1.0 - even
-    x = x + turn(x, -1) * even + turn(x, 1) * odd
-    half = as_f32(lane % 4 < 2)
-    return x + turn(x, -2) * half + turn(x, 2) * (1.0 - half)
-
-
-def coarse_solve(r2, m2, count_x, count_y):
-    rows = count_x * count_y
-    lane = lax.broadcasted_iota(jnp.int32, (rows, LANES), 1)
-    row = lax.broadcasted_iota(jnp.int32, (rows, LANES), 0)
-    column = row % count_y
-    z_low, z_high = as_f32(lane >= 4), as_f32(lane < LANES - 4)
-    x_low, x_high = as_f32(row >= count_y), as_f32(row < rows - count_y)
-    y_low, y_high = as_f32(column > 0), as_f32(column < count_y - 1)
-    up = lambda v, k: pltpu.roll(v, k % rows, 0)
-    weight = DAMPING / (m2 + 24.0)
-    e = weight * r2
-    for _ in range(SWEEPS - 1):
-        beside = turn(e, 4) * z_low + turn(e, -4) * z_high
-        beside = beside + up(e, count_y) * x_low + up(e, -count_y) * x_high
-        beside = beside + up(e, 1) * y_low + up(e, -1) * y_high
-        e = e + weight * (r2 - (m2 * e + 4.0 * (6.0 * e - beside)))
-    return e
-
-
-def prolongation(r, r1, e2, mass0, weight0, mass1, weight1, place, shifts):
-    e1 = memo(lambda x, y: weight1(x, y) * r1(x, y) + e2(x // 2, y // 2))
-    g1 = grid_apply(e1, mass1, 2.0, shifts, 2)
-    f1 = memo(lambda x, y: place.keep(e1(x, y) + weight1(x, y) * (r1(x, y) - g1(x, y)), x, y, 2))
+def contribution(w, mass0, weight0, columns, cells, shifts):
+    inside = set(columns)
+    e0 = memo(lambda x, y: weight0(x, y) * w(x, y) if (x, y) in inside else None)
+
+    def rest(x, y):
+        beside = [v for v in (e0(x + 1, y), e0(x - 1, y), e0(x, y + 1), e0(x, y - 1)) if v is not None]
+        total = sum(beside) if beside else None
+        c = e0(x, y)
+        if c is None:
+            return total
+        near = shifts.beside(c, 1) if total is None else total + shifts.beside(c, 1)
+        return w(x, y) - (mass0(x, y) * c + (6.0 * c - near))
+
+    out = {}
+    for x, y in cells:
+        parts = [rest(2 * x + i, 2 * y + j) for i in range(2) for j in range(2)]
+        out[x, y] = shifts.pair_sum(sum(v for v in parts if v is not None))
+    return out
+
+
+class Levels:
+    def __init__(self, count_x, count_y, shifts):
+        rows = count_x * count_y
+        lane = lax.broadcasted_iota(jnp.int32, (rows, LANES), 1)
+        row = lax.broadcasted_iota(jnp.int32, (rows, LANES), 0)
+        column = row % count_y
+        self.rows, self.count_y, self.shifts = rows, count_y, shifts
+        self.x_low, self.x_high = as_f32(row >= count_y), as_f32(row < rows - count_y)
+        self.y_low, self.y_high = as_f32(column > 0), as_f32(column < count_y - 1)
+        self.even = as_f32(lane % 2 == 0)
+        self.odd = 1.0 - self.even
+        self.from_low = self.y_low * self.even
+        self.from_high = self.y_high * self.odd
+
+    def below_x(self, v):
+        return pltpu.roll(v, self.count_y, 0) * self.x_low
+
+    def above_x(self, v):
+        return pltpu.roll(v, self.rows - self.count_y, 0) * self.x_high
+
+    def row(self, v, k):
+        return pltpu.roll(v, k % self.rows, 0)
+
+    def gather_y(self, first, second):
+        return (first + self.row(second, 1) * self.y_low) * self.even + (
+            second + self.row(first, -1) * self.y_high
+        ) * self.odd
+
+    def apply_1(self, v, mass):
+        out = []
+        for x in range(2):
+            c, other = v[x], v[1 - x]
+            swapped = turn(c, -1) * self.even + turn(c, 1) * self.odd
+            near = other + (self.below_x(other) if x == 0 else self.above_x(other))
+            near = near + swapped + self.row(swapped, 1) * self.from_low + self.row(swapped, -1) * self.from_high
+            near = near + self.shifts.beside(c, 2)
+            out.append(mass[x] * c + 2.0 * (6.0 * c - near))
+        return out
+
+    def solve_2(self, r2, mass, weight):
+        e = weight * r2
+        for _ in range(SWEEPS - 1):
+            near = self.shifts.beside(e, 4) + self.below_x(e) + self.above_x(e)
+            near = near + self.row(e, 1) * self.y_low + self.row(e, -1) * self.y_high
+            e = e + weight * (r2 - (mass * e + 4.0 * (6.0 * e - near)))
+        return e
+
+    def sum_2(self, v):
+        return self.shifts.quad_sum(self.shifts.pair_sum(v[0] + v[1]))
+
+    def solve(self, r1, mass1):
+        weight1 = [DAMPING / (m + 12.0) for m in mass1]
+        mass2 = self.sum_2(mass1)
+        weight2 = DAMPING / (mass2 + 24.0)
+        out = []
+        for r in r1:
+            e = [weight1[x] * r[x] for x in range(2)]
+            g = self.apply_1(e, mass1)
+            e2 = self.solve_2(self.sum_2([r[x] - g[x] for x in range(2)]), mass2, weight2)
+            e = [e[x] + e2 for x in range(2)]
+            g = self.apply_1(e, mass1)
+            out.append([e[x] + weight1[x] * (r[x] - g[x]) for x in range(2)])
+        return out
+
+
+def pack_y(cells, x, shifts):
+    return (
+        cells[x, 0] * shifts.even + cells[x, -1] * shifts.odd,
+        cells[x, 1] * shifts.odd + cells[x, 2] * shifts.even,
+    )
+
+
+def put_rows(slot_ref, row, column):
+    for m in range(3):
+        slot_ref[row + m] = column[m : m + 1]
+
+
+def fine_level(r, f1, mass0, weight0, place, shifts):
     e0 = memo(lambda x, y: weight0(x, y) * r(x, y) + f1(x // 2, y // 2))
     g0 = grid_apply(e0, mass0, 1.0, shifts, 1)
     return memo(lambda x, y: place.keep(e0(x, y) + weight0(x, y) * (r(x, y) - g0(x, y)), x, y, BRICK))
@@ -344,13 +371,52 @@
         ref[ref.shape[0] - 8 :, :] = jnp.zeros((8, LANES), F32)
 
 
-def pack_kernel(counts, right_in, mass_in, own_ref, right_ref, mass_ref, semaphores):
+def weight_of(mass):
+    return DAMPING / (mass + 6.0)
+
+
+def spread_mass(column):
+    return jnp.broadcast_to(column[3:4], (4, LANES))
+
+
+def live_rows():
+    return as_f32(lax.broadcasted_iota(jnp.int32, (4, LANES), 0) < 3)
+
+
+FIRST_ROWS = 20
+SECOND_ROWS = 13
+
+
+def pack_kernel(counts, right_in, mass_in, own_ref, even_ref, odd_ref, slot_ref, right_ref, mass_ref, semaphores):
     fetch((right_in, mass_in), (right_ref, mass_ref), semaphores)()
+    place, shifts = Place(*counts), Shifts()
+    own = {}
     for x in range(BRICK):
         for y in range(BRICK):
-            for m in range(3):
-                own_ref[x, y, m : m + 1, :] = right_ref[m, x, y : y + 1, :]
-            own_ref[x, y, 3:4, :] = mass_ref[x, y : y + 1, :]
+            rows = [right_ref[m, x, y : y + 1, :] for m in range(3)] + [mass_ref[x, y : y + 1, :]]
+            own[x, y] = jnp.concatenate(rows, axis=0)
+            own_ref[x, y] = own[x, y]
+    odd_x = 1.0 - place.even_x
+    for k, (x, y) in enumerate(SIDE_X):
+        up, down = own[x + 4, y], own[-1 - x, y]
+        even_ref[k] = up * place.even_x + down * odd_x
+        odd_ref[k] = down * place.even_x + up * odd_x
+    live = live_rows()
+    mass0 = memo(lambda x, y: spread_mass(own[x, y]))
+    weight0 = memo(lambda x, y: weight_of(mass0(x, y)))
+    r = memo(lambda x, y: own[x, y] * live)
+    cells = [(x, y) for x in (0, 1) for y in range(-1, 3)] + [(x, y) for x in (-1, 2) for y in (0, 1)]
+    part = contribution(r, mass0, weight0, INNER, cells, shifts)
+    for x in (0, 1):
+        for k, column in enumerate(pack_y(part, x, shifts)):
+            put_rows(slot_ref, 6 * x + 3 * k, column)
+    for k, x in enumerate((-1, 2)):
+        put_rows(slot_ref, 12 + 3 * k, part[x, 0] * shifts.even + part[x, 1] * shifts.odd)
+    for x in (0, 1):
+        mass1 = [
+            shifts.pair_sum(sum(own[2 * x + i, 2 * y + j][3:4] for i in range(2) for j in range(2))) for y in (0, 1)
+        ]
+        slot_ref[18 + x] = mass1[0] * shifts.even + mass1[1] * shifts.odd
 
 
 def widen_kernel(counts, own_ref, even_ref, odd_ref, wide_ref, to_even_ref, to_odd_ref):
@@ -363,111 +429,73 @@
         if 0 <= x < BRICK:
             return own_ref[x, y]
         odd, even = left if x < 0 else right
-        return odd_ref[x % BRICK, y] * odd + even_ref[x % BRICK, y] * even
+        k = SIDE_X.index((x, y) if x < 0 else mirror_x(x, y))
+        return odd_ref[k] * odd + even_ref[k] * even
 
     value = memo(value)
-    for x in range(-4, 8):
+    for x in range(-2, 6):
         for y in range(BRICK):
-            wide_ref[x + 4, y] = value(x, y)
-    clear_tail(to_even_ref, to_odd_ref)
+            wide_ref[x + 2, y] = value(x, y)
+    odd_y = 1.0 - place.even_y
     for k, (x, y) in enumerate(SIDE):
-        put_sides(to_even_ref, to_odd_ref, 3 * k, 3, value(x, y + 4), value(x, -1 - y), place.even_y)
-    first = 3 * len(SIDE)
-    for k, (x, y) in enumerate(SIDE_MASS):
-        put_sides(to_even_ref, to_odd_ref, first + k, 1, value(x, y + 4)[3:4], value(x, -1 - y)[3:4], place.even_y)
-
-
-def start_kernel(counts, wide_ref, even_ref, odd_ref, r_ref, mass0_ref, weight0_ref, mass1_ref, weight1_ref, slot_ref):
-    place, shifts = Place(*counts), Shifts()
-    below, above = side_parts(even_ref, odd_ref, place.even_y, place.in_y[-1], place.in_y[1])
-    live = as_f32(lax.broadcasted_iota(jnp.int32, (4, LANES), 0) < 3)
-    zero = jnp.zeros((4, LANES), F32)
-
-    def r_at(x, y):
-        if 0 <= y < BRICK:
-            return wide_ref[x + 4, y] * live
-        part = below if y < 0 else above
-        key = (x, y) if y < 0 else mirror(x, y)
-        return part(3 * SIDE.index(key), 4) * live if key in SIDE else zero
-
-    def mass0_at(x, y):
-        if 0 <= y < BRICK:
-            return jnp.broadcast_to(wide_ref[x + 4, y, 3:4, :], (4, LANES))
-        part = below if y < 0 else above
-        key = (x, y) if y < 0 else mirror(x, y)
-        if key not in SIDE_MASS:
-            return zero
-        return jnp.broadcast_to(part(3 * len(SIDE) + SIDE_MASS.index(key), 1), (4, LANES))
-
-    r, mass0 = memo(r_at), memo(mass0_at)
-    weight0 = memo(lambda x, y: DAMPING / (mass0(x, y) + 6.0))
-
-    def mass1_at(x, y):
-        total = mass0(2 * x, 2 * y) + mass0(2 * x + 1, 2 * y) + mass0(2 * x, 2 * y + 1) + mass0(2 * x + 1, 2 * y + 1)
-        return shifts.pair_sum(total)
-
-    mass1 = memo(mass1_at)
-    weight1 = memo(lambda x, y: DAMPING / (mass1(x, y) + 12.0))
-    r1, r2 = restriction(r, mass0, weight0, mass1, weight1, place, shifts)
-    m2 = shifts.quad_sum(mass1(0, 0) + mass1(0, 1) + mass1(1, 0) + mass1(1, 1))
-    r2_row = pack_quads(jnp.concatenate([r2[0:3], m2[3:4]], axis=0))
-    slot_ref[...] = pack_slot(r1, r2_row, jnp.zeros((1, LANES), F32), shifts)
-    for x in range(-3, 7):
-        for y in range(-3, 7):
-            mass0_ref[x + 3, y + 3] = mass0(x, y)
-            weight0_ref[x + 3, y + 3] = weight0(x, y)
-            if -2 <= x < 6 and -2 <= y < 6:
-                r_ref[x + 2, y + 2] = r(x, y)
-    for x in range(-2, 4):
-        for y in range(-2, 4):
-            mass1_ref[x + 2, y + 2] = mass1(x, y)
-            weight1_ref[x + 2, y + 2] = weight1(x, y)
+        up, down = value(x, y + 4), value(x, -1 - y)
+        to_even_ref[k] = up * place.even_y + down * odd_y
+        to_odd_ref[k] = down * place.even_y + up * odd_y
+
+
+def start_kernel(counts, wide_ref, even_ref, odd_ref, r_ref, mass0_ref, weight0_ref):
+    place = Place(*counts)
+    live = live_rows()
+    odd_y = 1.0 - place.even_y
+    below = (place.in_y[-1] * place.even_y, place.in_y[-1] * odd_y)
+    above = (place.in_y[1] * odd_y, place.in_y[1] * place.even_y)
+    for x in range(-2, 6):
+        for y in range(-2, 6):
+            if 0 <= y < BRICK:
+                value = wide_ref[x + 2, y]
+            else:
+                key = (x, y) if y < 0 else mirror(x, y)
+                odd, even = below if y < 0 else above
+                if key in SIDE:
+                    k = SIDE.index(key)
+                    value = odd_ref[k] * odd + even_ref[k] * even
+                else:
+                    value = jnp.zeros((4, LANES), F32)
+            r_ref[x + 2, y + 2] = value * live
+            mass = spread_mass(value)
+            mass0_ref[x + 2, y + 2] = mass
+            weight0_ref[x + 2, y + 2] = weight_of(mass)
 
 
 def reader(ref, offset):
     return memo(lambda x, y: ref[x + offset, y + offset])
 
 
-def cycle_and_apply(place, shifts, r, gathered, mass_rows, fields, fetched, particles, scratch):
-    count_x, count_y = place.count_x, place.count_y
-    mass0, weight0, mass1, weight1 = fields
+def cycle_and_apply(place, shifts, levels, r, r1, mass1, fields, fetched, particles, scratch):
+    mass0, weight0 = fields
     coarse, *work = scratch
-    bricks = count_x * count_y
-    r2 = gathered(3, bricks, 8)
-    lane = lax.broadcasted_iota(jnp.int32, (bricks, LANES), 1)
-    m2 = spread_quads(mass_rows * as_f32(lane % 4 == 3), lane)
-    margin = coarse.shape[0] - bricks
+    margin = 8 * (place.count_y + 1)
     coarse[...] = jnp.zeros_like(coarse)
-    coarse[margin // 2 : margin // 2 + bricks, :] = coarse_solve(r2, m2, count_x, count_y)
-
-    def e2_at(x, y):
-        row = (place.gx + x) * count_y + place.gy + y + margin // 2
-        return place.keep(unpack_quads(coarse[pl.ds(row, 1), :]), x, y, 1)
-
-    e2 = memo(e2_at)
+    for m, pair in enumerate(levels.solve(r1, mass1)):
+        for x in range(2):
+            coarse[pl.ds(margin + 4 * x + m, levels.rows, stride=8), :] = pair[x]
 
     def neighbour(x, y):
-        other_x = jnp.clip(place.gx + x, 0, count_x - 1)
-        other_y = jnp.clip(place.gy + y, 0, count_y - 1)
-        row = pl.multiple_of((other_x * count_y + other_y) * 8, 8)
-        slot = gathered(row, 8, 1)
-        first, second = slot * shifts.even, slot * shifts.odd
+        brick = (place.gx + x) * place.count_y + place.gy + y
+        rows = coarse[pl.ds(pl.multiple_of(margin + brick * 8, 8), 8), :]
+        first, second = rows * shifts.even, rows * shifts.odd
         return first + turn(first, 1), second + turn(second, -1)
 
     neighbour = memo(neighbour)
 
-    def r1_at(x, y):
+    def f1_at(x, y):
         both = neighbour(x // 2, y // 2)[y % 2]
         return place.keep(both[4 * (x % 2) : 4 * (x % 2) + 4], x, y, 2)
 
-    r1 = memo(r1_at)
-    live = as_f32(lax.broadcasted_iota(jnp.int32, (4, LANES), 0) < 3)
-    full = prolongation(r, r1, e2, mass0, weight0, mass1, weight1, place, shifts)
-    z = memo(lambda x, y: full(x, y) * live)
+    z = fine_level(r, memo(f1_at), mass0, weight0, place, shifts)
     image = stiffness_apply(z, fetched, *particles, *work, shifts)
-    for x in range(BRICK):
-        for y in range(BRICK):
-            image[x, y] = image[x, y] + mass0(x, y) * z(x, y)
+    for x, y in INNER:
+        image[x, y] = image[x, y] + mass0(x, y) * z(x, y)
     return z, image
 
 
@@ -490,99 +518,107 @@
 RIMMED = [(x, y) for x in range(-1, BRICK + 1) for y in range(-1, BRICK + 1)]
 
 
-def first_kernel(counts, level_ref, r_ref, mass0_ref, weight0_ref, mass1_ref, weight1_ref,
-                 base_in, stiff_in, valid_in, grad_in, z_ref, image_ref, even_ref, odd_ref, dots_ref,
+def first_kernel(counts, level_ref, r_ref, mass0_ref, weight0_ref,
+                 base_in, stiff_in, valid_in, grad_in, z_ref, image_ref, even_ref, odd_ref, dots_ref, r1_ref, mass1_ref,
                  base_ref, stiff_ref, valid_ref, grad_ref, semaphores, *scratch):
     particles = (base_ref, stiff_ref, valid_ref, grad_ref)
     fetched = fetch((base_in, stiff_in, valid_in, grad_in), particles, semaphores)
     place, shifts = Place(*counts), Shifts()
+    levels = Levels(*counts, shifts)
+    rows = lambda q: level_ref[pl.ds(q, levels.rows, stride=FIRST_ROWS), :]
+    r1 = []
+    for m in range(3):
+        pair = [levels.gather_y(rows(6 * x + m), rows(6 * x + 3 + m)) for x in range(2)]
+        pair[1] = pair[1] + levels.above_x(rows(12 + m))
+        pair[0] = pair[0] + levels.below_x(rows(15 + m))
+        r1.append(pair)
+    mass1 = [rows(18), rows(19)]
+    for x in range(2):
+        mass1_ref[x] = mass1[x]
+        for m in range(3):
+            r1_ref[m, x] = r1[m][x]
     r = reader(r_ref, 2)
-    gathered = lambda start, size, stride: level_ref[pl.ds(start, size, stride=stride) if stride > 1 else pl.ds(start, size), :]
-    fields = (reader(mass0_ref, 3), reader(weight0_ref, 3), reader(mass1_ref, 2), reader(weight1_ref, 2))
-    mass_rows = gathered(3, counts[0] * counts[1], 8)
-    z, image = cycle_and_apply(place, shifts, r, gathered, mass_rows, fields, fetched, particles, scratch)
+    fields = (reader(mass0_ref, 2), reader(weight0_ref, 2))
+    z, image = cycle_and_apply(place, shifts, levels, r, r1, mass1, fields, fetched, particles, scratch)
     for x, y in INNER:
         z_ref[x, y] = z(x, y)
     for x, y in RIMMED:
         image_ref[x + 1, y + 1] = image[x, y]
     clear_tail(even_ref, odd_ref)
-    for k, (x, y) in enumerate(SIDE_X):
+    for k, (x, y) in enumerate(SIDE_X_IMAGE):
         put_sides(even_ref, odd_ref, 3 * k, 3, image[x + 4, y], image[-1 - x, y], place.even_x)
     rz = total_of((r(x, y), z(x, y)) for x, y in INNER)
     zaz = total_of((image[x, y], z(x, y)) for x, y in RIMMED)
     dots_ref[...] = dots_row(rz, zaz)
 
 
-def along_x_kernel(counts, image_ref, even_ref, odd_ref, wide_ref, to_even_ref, to_odd_ref):
-    place = Place(*counts)
+def along_x_kernel(counts, image_ref, even_ref, odd_ref, mass0_ref, weight0_ref, dots_ref,
+                   wide_ref, to_even_ref, to_odd_ref, slot_ref):
+    place, shifts = Place(*counts), Shifts()
     left, right = side_parts(even_ref, odd_ref, place.even_x, place.in_x[-1], place.in_x[1])
 
     def value(x, y):
         total = None
         if -1 <= x <= 4:
-            total = place.keep(image_ref[x + 1, y + 1], x, 0, BRICK)
+            total = place.keep(image_ref[x + 1, y + 1], x, y, BRICK)
         for part, key in ((left, (x, y)), (right, mirror_x(x, y))):
-            if key in SIDE_X:
-                more = part(3 * SIDE_X.index(key), 4)
+            if key in SIDE_X_IMAGE:
+                more = place.keep(part(3 * SIDE_X_IMAGE.index(key), 4), 0, y, BRICK)
                 total = more if total is None else total + more
         return total
 
     value = memo(value)
-    for x in range(-3, 7):
-        for y in range(-1, BRICK + 1):
-            wide_ref[x + 3, y + 1] = value(x, y)
     clear_tail(to_even_ref, to_odd_ref)
     for k, (x, y) in enumerate(SIDE_IMAGE):
         put_sides(to_even_ref, to_odd_ref, 3 * k, 3, value(x, y + 4), value(x, -1 - y), place.even_y)
-
-
-def middle_kernel(counts, wide_ref, even_ref, odd_ref, mass0_ref, weight0_ref, mass1_ref, weight1_ref, dots_ref,
-                  w_ref, slot_ref):
-    place, shifts = Place(*counts), Shifts()
+    for x in range(-2, 6):
+        for y in range(-1, BRICK + 1):
+            wide_ref[x + 2, y + 1] = value(x, y)
+    cells = [(x, y) for x in (0, 1) for y in range(-1, 3)]
+    part = contribution(value, reader(mass0_ref, 2), reader(weight0_ref, 2), RIMMED, cells, shifts)
+    for x in (0, 1):
+        for k, column in enumerate(pack_y(part, x, shifts)):
+            put_rows(slot_ref, 6 * x + 3 * k, column)
+    slot_ref[12] = dots_ref[...]
+
+
+def middle_kernel(counts, wide_ref, even_ref, odd_ref, w_ref):
+    place = Place(*counts)
     below, above = side_parts(even_ref, odd_ref, place.even_y, place.in_y[-1], place.in_y[1])
-    live = as_f32(lax.broadcasted_iota(jnp.int32, (4, LANES), 0) < 3)
-
-    def value(x, y):
-        total = None
-        if -1 <= y <= 4:
-            total = place.keep(wide_ref[x + 3, y + 1], 0, y, BRICK)
-        for part, key in ((below, (x, y)), (above, mirror(x, y))):
-            if key in SIDE_IMAGE:
-                more = part(3 * SIDE_IMAGE.index(key), 4)
-                total = more if total is None else total + more
-        return jnp.zeros((4, LANES), F32) if total is None else total * live
-
-    w = memo(value)
-    r1, r2 = restriction(w, reader(mass0_ref, 3), reader(weight0_ref, 3), reader(mass1_ref, 2), reader(weight1_ref, 2),
-                         place, shifts)
-    slot_ref[...] = pack_slot(r1, pack_quads(r2), dots_ref[...], shifts)
+    live = live_rows()
     for x in range(-2, 6):
         for y in range(-2, 6):
-            w_ref[x + 2, y + 2] = w(x, y)
+            total = jnp.zeros((4, LANES), F32)
+            if -1 <= y <= 4:
+                total = total + wide_ref[x + 2, y + 1]
+            for part, key in ((below, (x, y)), (above, mirror(x, y))):
+                if key in SIDE_IMAGE:
+                    total = total + part(3 * SIDE_IMAGE.index(key), 4)
+            w_ref[x + 2, y + 2] = total * live
 
 
 def sums_of(ref, count, first, stride):
     return jnp.sum(ref[pl.ds(first, count, stride=stride), :], axis=0, keepdims=True)
 
 
-def second_kernel(counts, level_ref, change_ref, r_ref, w_ref, mass0_ref, weight0_ref, mass1_ref, weight1_ref,
+def second_kernel(counts, change_ref, r1_ref, mass1_ref, r_ref, w_ref, mass0_ref, weight0_ref,
                   base_in, stiff_in, valid_in, grad_in, z_ref, image_ref, slots_ref,
                   base_ref, stiff_ref, valid_ref, grad_ref, semaphores, *scratch):
     particles = (base_ref, stiff_ref, valid_ref, grad_ref)
     fetched = fetch((base_in, stiff_in, valid_in, grad_in), particles, semaphores)
     place, shifts = Place(*counts), Shifts()
     bricks = counts[0] * counts[1]
-    sums = sums_of(change_ref, bricks, 7, 8)
+    levels = Levels(*counts, shifts)
+    sums = sums_of(change_ref, bricks, 12, SECOND_ROWS)
     step = sums[:, 0:1] / sums[:, 1:2]
     r = memo(lambda x, y: r_ref[x + 2, y + 2] - step * w_ref[x + 2, y + 2])
-
-    def gathered(start, size, stride):
-        rows = pl.ds(start, size, stride=stride) if stride > 1 else pl.ds(start, size)
-        return level_ref[rows, :] - step * change_ref[rows, :]
-
-    mass_rows = level_ref[pl.ds(3, bricks, stride=8), :]
-    fields = (reader(mass0_ref, 3), reader(weight0_ref, 3), reader(mass1_ref, 2), reader(weight1_ref, 2))
-    z, image = cycle_and_apply(place, shifts, r, gathered, mass_rows, fields, fetched, particles, scratch)
+    rows = lambda q: change_ref[pl.ds(q, bricks, stride=SECOND_ROWS), :]
+    r1 = [
+        [r1_ref[m, x] - step * levels.gather_y(rows(6 * x + m), rows(6 * x + 3 + m)) for x in range(2)] for m in range(3)
+    ]
+    fields = (reader(mass0_ref, 2), reader(weight0_ref, 2))
+    mass1 = [mass1_ref[0], mass1_ref[1]]
+    z, image = cycle_and_apply(place, shifts, levels, r, r1, mass1, fields, fetched, particles, scratch)
     for x, y in INNER:
         z_ref[x, y] = z(x, y)
         image_ref[x, y] = image[x, y]
@@ -619,7 +655,7 @@
 def last_kernel(counts, slots_ref, change_ref, z1_ref, z2_ref, r_ref, w_ref, image_ref, solution_ref, residual_ref):
     place = Place(*counts)
     bricks = counts[0] * counts[1]
-    sums1 = sums_of(change_ref, bricks, 7, 8)
+    sums1 = sums_of(change_ref, bricks, 12, SECOND_ROWS)
     sums2 = jnp.sum(slots_ref[:, 12], axis=0)
     rz1, zaz1 = sums1[:, 0:1], sums1[:, 1:2]
     rz2, zaz2, zw = sums2[:, 0:1], sums2[:, 1:2], sums2[:, 2:3]
@@ -670,50 +706,49 @@
     scratch = (
         *(pltpu.VMEM(p.shape, p.dtype) for p in particles),
         pltpu.SemaphoreType.DMA((4,)),
-        pltpu.VMEM((bricks + 2 * (8 + counts[1]), LANES), F32),
+        pltpu.VMEM((8 * (bricks + 2 * (counts[1] + 1)), LANES), F32),
         pltpu.VMEM((depth, width), jnp.bfloat16),
         pltpu.VMEM((tiles, depth), jnp.bfloat16),
         pltpu.VMEM((tiles, width), jnp.bfloat16),
         pltpu.VMEM((tiles, width), F32),
         pltpu.VMEM((tiles, depth), F32),
     )
-    rows = lambda columns, more=0: (-(-(3 * len(columns) + more + 1) // 8) * 8, LANES)
+    rows = lambda columns: (-(-(3 * len(columns) + 1) // 8) * 8, LANES)
+    block = lambda *dims: (*dims, 4, LANES)
+
+    def share(slot):
+        sent = jnp.broadcast_to(slot[None], (bricks, *slot.shape))
+        return lax.all_to_all(sent, AXES, 0, 0).reshape(bricks * slot.shape[0], LANES)
 
     fields = (right_side, node_mass)
-    (own,) = call(
-        pack_kernel, counts, [(4, 4, 4, LANES)], *fields, far=2,
+    own, to_even, to_odd, slot = call(
+        pack_kernel, counts, [block(4, 4), block(8), block(8), (FIRST_ROWS, 1, LANES)], *fields, far=2,
         scratch=(*(pltpu.VMEM(p.shape, p.dtype) for p in fields), pltpu.SemaphoreType.DMA((2,))),
     )
-    even, odd = exchange(own, own, "gx", counts)
-    side = rows(SIDE, len(SIDE_MASS))
-    wide, to_even, to_odd = call(widen_kernel, counts, [(12, 4, 4, LANES), side, side], own, even, odd)
+    level = share(slot)
+    even, odd = exchange(to_even, to_odd, "gx", counts)
+    side = block(len(SIDE))
+    wide, to_even, to_odd = call(widen_kernel, counts, [block(8, 4), side, side], own, even, odd)
     even, odd = exchange(to_even, to_odd, "gy", counts)
-    r, *fields, slot = call(
-        start_kernel, counts,
-        [(8, 8, 4, LANES), (10, 10, 4, LANES), (10, 10, 4, LANES), (6, 6, 4, LANES), (6, 6, 4, LANES), (8, LANES)],
-        wide, even, odd,
-    )
-
-    def share(slot):
-        sent = jnp.broadcast_to(slot[None], (bricks, 8, LANES))
-        return lax.all_to_all(sent, AXES, 0, 0).reshape(bricks * 8, LANES)
-
-    level = share(slot)
-    z1, image, to_even, to_odd, dots = call(
+    r, *fields = call(start_kernel, counts, [block(8, 8)] * 3, wide, even, odd)
+
+    side = rows(SIDE_X_IMAGE)
+    z1, image, to_even, to_odd, dots, r1, mass1 = call(
         first_kernel, counts,
-        [(4, 4, 4, LANES), (6, 6, 4, LANES), rows(SIDE_X), rows(SIDE_X), (1, LANES)],
+        [block(4, 4), block(6, 6), side, side, (1, LANES), (3, 2, bricks, LANES), (2, bricks, LANES)],
         level, r, *fields, *particles, scratch=scratch, far=4,
     )
     even, odd = exchange(to_even, to_odd, "gx", counts)
-    wide, to_even, to_odd = call(
-        along_x_kernel, counts, [(10, 6, 4, LANES), rows(SIDE_IMAGE), rows(SIDE_IMAGE)], image, even, odd
-    )
+    side = rows(SIDE_IMAGE)
+    wide, to_even, to_odd, slot = call(
+        along_x_kernel, counts, [block(8, 6), side, side, (SECOND_ROWS, 1, LANES)], image, even, odd, *fields, dots
+    )
+    change = share(slot)
     even, odd = exchange(to_even, to_odd, "gy", counts)
-    w, slot = call(middle_kernel, counts, [(8, 8, 4, LANES), (8, LANES)], wide, even, odd, *fields, dots)
-    change = share(slot)
+    (w,) = call(middle_kernel, counts, [block(8, 8)], wide, even, odd)
     z2, image, slots = call(
-        second_kernel, counts, [(4, 4, 4, LANES), (4, 4, 4, LANES), (bricks, 13, 1, LANES)],
-        level, change, r, w, *fields, *particles, scratch=scratch, far=4,
+        second_kernel, counts, [block(4, 4), block(4, 4), (bricks, 13, 1, LANES)],
+        change, r1, mass1, r, w, *fields, *particles, scratch=scratch, far=4,
     )
     slots = lax.all_to_all(slots, AXES, 0, 0)
     return tuple(

time: 66.2 us -> 61.1 us (0.923)
  blocking collectives: 37.3 us -> 11.8 us
  starting transfers between devices: 5.84 us -> 19.9 us
  waiting for transfers between devices: 11.5 us -> 16.1 us
  local copies, waits for them, and re-layouts: 2.17 us -> 3.84 us
    all_to_all x2 -> x0, blocking collectives: 26.1 us -> none  [share(): return lax.all_to_all(sent, AXES, 0, 0).reshape(bricks * 8, LANES)]
    all_to_all x0 -> x2, starting transfers between devices: none -> 10.9 us  [share(): lax.all_to_all(sent, AXES, 0, 0).reshape(bricks * slot.shape[0], LANES)]
    all_to_all x0 -> x2, waiting for transfers between devices: none -> 3.76 us  [share(): lax.all_to_all(sent, AXES, 0, 0).reshape(bricks * slot.shape[0], LANES)]
    ppermute x8, starting transfers between devices: 5.84 us -> 9.02 us  [exchange(): return (lax.ppermute(first, AXES, even), lax.ppermute(second, AXES, odd))]
    broadcast_in_dim x2, local copies, waits for them, and re-layouts: 0.02 us -> 1.69 us  [share(): sent = jnp.broadcast_to(slot[None], (bricks, *slot.shape))]
    ppermute x8, waiting for transfers between devices: 11.5 us -> 12.4 us  [exchange(): return (lax.ppermute(first, AXES, even), lax.ppermute(second, AXES, odd))]
    unnamed x12 -> x14, local copies, waits for them, and re-layouts: 2.14 us -> 2.15 us
  transfers between devices with their start and end apart: 8 -> 10, of which waited for: 5 -> 6; matrix products, arithmetic and copies ran while one was open for 0% -> 0% of each run, Pallas kernels for 0% -> 0%
where the time goes in v5:
time: 61.1 us; the launch traced here: 60.7 us
  starting transfers between devices  19.9 us (33%)
  waiting for transfers between devices  16.1 us (26%)
  blocking collectives  11.8 us (19%)
  Pallas kernels  8.35 us (14%)
  local copies, waits for them, and re-layouts  3.84 us (6%)
  between operations  0.72 us (1%)
    ppermute x8, waiting for transfers between devices, exchange(): return (lax.ppermute(first, AXES, even), lax.ppermute(second, AXES, odd))  12.4 us
    all_to_all x1, blocking collectives, per_device(): slots = lax.all_to_all(slots, AXES, 0, 0)  11.8 us
    all_to_all x2, starting transfers between devices, share(): lax.all_to_all(sent, AXES, 0, 0).reshape(bricks * slot.shape[0], LANES)  10.9 us
    ppermute x8, starting transfers between devices, exchange(): return (lax.ppermute(first, AXES, even), lax.ppermute(second, AXES, odd))  9.02 us
    pallas_call x8, Pallas kernels, call(): pl.pallas_call(functools.partial(kernel, counts), out_shape=[jax.ShapeDty...  8.35 us
    all_to_all x2, waiting for transfers between devices, share(): lax.all_to_all(sent, AXES, 0, 0).reshape(bricks * slot.shape[0], LANES)  3.76 us
    unnamed x14, local copies, waits for them, and re-layouts  2.15 us
    broadcast_in_dim x2, local copies, waits for them, and re-layouts, share(): sent = jnp.broadcast_to(slot[None], (bricks, *slot.shape))  1.69 us
  transfers between devices with their start and end apart: 10, of which 6 were waited for; matrix products, arithmetic and copies ran while one was open for 0% of the time, Pallas kernels for 0%

profile of v5, /device:TPU:0, one launch (start us, length us, event | category | flops | bytes accessed | tf_op | source)
XLA Modules:
  0.0 60.7 jit_solution(13562296444765677859)
XLA Ops:
  0.6 0.7 %copy-done.1 = f32[3,4,4,128]{3,2,1,0:T(4,128)S(1)} copy-done((f32[3,4,4,128]{3,2,1,0:T(4,128)S(1)}, f32[3,4,4,128]{3,2,1,0:T(4,128)}, u32[]{:S(2)}) %copy-start.1) | copy-done | bytes 24600
  1.4 0.7 %copy-done.5 = f32[4,4,128]{2,1,0:T(4,128)S(1)} copy-done((f32[4,4,128]{2,1,0:T(4,128)S(1)}, f32[4,4,128]{2,1,0:T(4,128)}, u32[]{:S(2)}) %copy-start.5) | copy-done | bytes 8216
  2.1 0.3 shard_map.77
  2.4 0.9 %broadcast_in_dim.17 = f32[32,20,1,128]{3,2,1,0:T(1,128)} broadcast(f32[20,128]{1,0:T(8,128)S(1)} %bitcast.25), dimensions={1,3} | broadcast | bytes 337920 | tf_op jit(solution)/shard_map/broadcast_in_dim | solution.py:720
  3.3 7.3 %all-to-all-start = ((f32[32,20,1,128]{3,2,1,0:T(1,128)}), f32[32,20,1,128]{3,2,1,0:T(1,128)S(1)}, u32[]{:S(2)}, u32[]{:S(2)}) async-start(f32[32,20,1,128]{3,2,1,0:T(1,128)} %broadcast_in_dim.17), calls=%async_computation | async-start | bytes 655360 | tf_op jit(solution)/shard_map/all_to_all | solution.py:721
  10.6 0.3 collective-permute-start
  10.9 1.7 %collective-permute-start.1 = (f32[8,4,128]{2,1,0:T(4,128)S(1)}, f32[8,4,128]{2,1,0:T(4,128)S(1)}, u32[]{:S(2)}, u32[]{:S(2)}) collective-permute-start(f32[8,4,128]{2,1,0:T(4,128)S(1)} %get-tuple-element.29), channel_id=1, source_target_pairs={{0,1},{1,0},{2,3},{3,2},{4,8},{5,9},{6,10},{7,11},{8,4},{9,5},{10,... | collective-permute-start | bytes 49160 | tf_op jit(solution)/shard_map/ppermute | solution.py:38
  12.6 4.2 %collective-permute-done.1.odd_ref = f32[8,4,128]{2,1,0:T(4,128)S(1)} collective-permute-done((f32[8,4,128]{2,1,0:T(4,128)S(1)}, f32[8,4,128]{2,1,0:T(4,128)S(1)}, u32[]{:S(2)}, u32[]{:S(2)}) %collective-permute-start.1) | collective-permute-done | bytes 16416 | tf_op jit(solution)/shard_map/ppermute | solution.py:38
  16.8 2.5 %collective-permute-start.2 = (f32[14,4,128]{2,1,0:T(4,128)S(1)}, f32[14,4,128]{2,1,0:T(4,128)S(1)}, u32[]{:S(2)}, u32[]{:S(2)}) collective-permute-start(f32[14,4,128]{2,1,0:T(4,128)S(1)} %get-tuple-element.31), channel_id=1, source_target_pairs={{0,1},{1,0},{2,3},{3,2},{4,5},{5,4},{6,7},{7,6},{8,9},{9,8},{10,11... | collective-permute-start | bytes 86024 | tf_op jit(solution)/shard_map/ppermute | solution.py:38
  19.3 2.0 %collective-permute-done.2.even_ref = f32[14,4,128]{2,1,0:T(4,128)S(1)} collective-permute-done((f32[14,4,128]{2,1,0:T(4,128)S(1)}, f32[14,4,128]{2,1,0:T(4,128)S(1)}, u32[]{:S(2)}, u32[]{:S(2)}) %collective-permute-start.2) | collective-permute-done | bytes 28704 | tf_op jit(solution)/shard_map/ppermute | solution.py:38
  21.6 0.7 %copy-done.4 = s32[1,1,8,128]{3,2,1,0:T(8,128)S(1)} copy-done((s32[1,1,8,128]{3,2,1,0:T(8,128)S(1)}, s32[1,1,8,128]{3,2,1,0:T(8,128)}, u32[]{:S(2)}) %copy-start.4) | copy-done | bytes 4120
  22.3 3.2 %shard_map.80 = (f32[4,4,4,128]{3,2,1,0:T(4,128)S(1)}, f32[6,6,4,128]{3,2,1,0:T(4,128)S(1)}, f32[56,128]{1,0:T(8,128)S(1)}, f32[56,128]{1,0:T(8,128)S(1)}, f32[1...) custom-call(f32[640,128]{1,0:T(8,128)S(1)} %bitcast.18, ...), custom_call_target="tpu_custom_call" | custom-call | tf_op jit(solution)/shard_map/pallas_call | solution.py:690
  25.5 0.9 %collective-permute-start.4 = (f32[56,128]{1,0:T(8,128)S(1)}, f32[56,128]{1,0:T(8,128)S(1)}, u32[]{:S(2)}, u32[]{:S(2)}) collective-permute-start(f32[56,128]{1,0:T(8,128)S(1)} %get-tuple-element.37), channel_id=1, source_target_pairs={{0,4},{1,5},{2,6},{3,7},{4,0},{5,1},{6,2},{7,3},{8,12},{9,13},{10,... | collective-permute-start | bytes 86024 | tf_op jit(solution)/shard_map/ppermute | solution.py:38
  26.4 1.8 %collective-permute-start.5 = (f32[56,128]{1,0:T(8,128)S(1)}, f32[56,128]{1,0:T(8,128)S(1)}, u32[]{:S(2)}, u32[]{:S(2)}) collective-permute-start(f32[56,128]{1,0:T(8,128)S(1)} %get-tuple-element.38), channel_id=1, source_target_pairs={{0,1},{1,0},{2,3},{3,2},{4,8},{5,9},{6,10},{7,11},{8,4},{9,5},{10,... | collective-permute-start | bytes 86024 | tf_op jit(solution)/shard_map/ppermute | solution.py:38
  28.1 2.1 %collective-permute-done.5.odd_ref = f32[56,128]{1,0:T(8,128)S(1)} collective-permute-done((f32[56,128]{1,0:T(8,128)S(1)}, f32[56,128]{1,0:T(8,128)S(1)}, u32[]{:S(2)}, u32[]{:S(2)}) %collective-permute-start.5) | collective-permute-done | bytes 28704 | tf_op jit(solution)/shard_map/ppermute | solution.py:38
  30.2 0.3 shard_map.81
  30.5 0.8 %broadcast_in_dim.19 = f32[32,13,1,128]{3,2,1,0:T(1,128)} broadcast(f32[13,128]{1,0:T(8,128)S(1)} %bitcast.26), dimensions={1,3} | broadcast | bytes 219648 | tf_op jit(solution)/shard_map/broadcast_in_dim | solution.py:720
  31.3 3.6 %all-to-all-start.1 = ((f32[32,13,1,128]{3,2,1,0:T(1,128)}), f32[32,13,1,128]{3,2,1,0:T(1,128)S(1)}, u32[]{:S(2)}, u32[]{:S(2)}) async-start(f32[32,13,1,128]{3,2,1,0:T(1,128)} %broadcast_in_dim.19), calls=%async_computation.1 | async-start | bytes 425984 | tf_op jit(solution)/shard_map/all_to_all | solution.py:721
  34.9 1.8 %collective-permute-start.6 = (f32[72,128]{1,0:T(8,128)S(1)}, f32[72,128]{1,0:T(8,128)S(1)}, u32[]{:S(2)}, u32[]{:S(2)}) collective-permute-start(f32[72,128]{1,0:T(8,128)S(1)} %get-tuple-element.44), channel_id=1, source_target_pairs={{0,1},{1,0},{2,3},{3,2},{4,5},{5,4},{6,7},{7,6},{8,9},{9,8},{10,11... | collective-permute-start | bytes 110600 | tf_op jit(solution)/shard_map/ppermute | solution.py:38
  36.8 4.1 %collective-permute-done.6.even_ref = f32[72,128]{1,0:T(8,128)S(1)} collective-permute-done((f32[72,128]{1,0:T(8,128)S(1)}, f32[72,128]{1,0:T(8,128)S(1)}, u32[]{:S(2)}, u32[]{:S(2)}) %collective-permute-start.6) | collective-permute-done | bytes 36896 | tf_op jit(solution)/shard_map/ppermute | solution.py:38
  40.9 3.6 %all-to-all-done.1 = f32[32,13,1,128]{3,2,1,0:T(1,128)S(1)} async-done(((f32[32,13,1,128]{3,2,1,0:T(1,128)}), f32[32,13,1,128]{3,2,1,0:T(1,128)S(1)}, u32[]{:S(2)}, u32[]{:S(2)}) %all-to-all-start.1) | async-done | bytes 213024 | tf_op jit(solution)/shard_map/all_to_all | solution.py:721
  44.5 3.5 %shard_map.83 = (f32[4,4,4,128]{3,2,1,0:T(4,128)S(1)}, f32[4,4,4,128]{3,2,1,0:T(4,128)S(1)}, f32[32,13,1,128]{3,2,1,0:T(1,128)S(1)}) custom-call(f32[416,128]{1,0:T(8,128)S(1)} %bitcast.14, f32[3,2,32,128]{3,2,1,0:T(8,128)S(1)} %get-tuple-element.41.r1_ref, f32[2,32,128]{2,1,0:T(8,128)S(1)} %get-tuple-element.42.mass1_ref, ...), custom_call_target="tpu_custom_call" | custom-call | tf_op jit(solution)/shard_map/pallas_call | solution.py:690
  48.0 11.8 %all_to_all.15.slots_ref = f32[32,13,1,128]{3,2,1,0:T(1,128)S(1)} all-to-all(f32[32,13,1,128]{3,2,1,0:T(1,128)S(1)} %get-tuple-element.46), channel_id=1, replica_groups=mesh['gx'=8,'gy'=4] {'gx','gy'}, dimensions={0} | all-to-all | bytes 425984 | tf_op jit(solution)/shard_map/all_to_all | solution.py:753
  59.8 0.9 %shard_map.84 = (f32[3,4,4,128]{3,2,1,0:T(4,128)}, f32[3,4,4,128]{3,2,1,0:T(4,128)}) custom-call(f32[32,13,1,128]{3,2,1,0:T(1,128)S(1)} %all_to_all.15.slots_ref, f32[416,128]{1,0:T(8,128)S(1)} %bitcast.15, f32[4,4,4,128]{3,2,1,0:T(4,128)S(1)} %get-tuple-element.47.z1_ref, f32[4,4,4,128]{3,2,1,0:T(4,128)S(1)} %get-tuple-element.48.z2_ref, ...), custom_call_target="tpu_custom_call" | custom-call | tf_op jit(solution)/shard_map/pallas_call | solution.py:690
  (21 shorter events, 0.4 us)
Async XLA Ops:
  0.6 0.7 %copy-start.1 = (f32[3,4,4,128]{3,2,1,0:T(4,128)S(1)}, f32[3,4,4,128]{3,2,1,0:T(4,128)}, u32[]{:S(2)}) copy-start(f32[3,4,4,128]{3,2,1,0:T(4,128)} %right_in.1) | copy-start | bytes 73732
  1.4 0.7 %copy-start.5 = (f32[4,4,128]{2,1,0:T(4,128)S(1)}, f32[4,4,128]{2,1,0:T(4,128)}, u32[]{:S(2)}) copy-start(f32[4,4,128]{2,1,0:T(4,128)} %mass_in.1) | copy-start | bytes 24580
  3.3 18.3 %copy-start = (f32[1,1,8,3,27,128]{5,2,4,3,1,0:T(8,128)S(1)}, f32[1,1,8,3,27,128]{5,2,4,3,1,0:T(8,128)}, u32[]{:S(2)}) copy-start(f32[1,1,8,3,27,128]{5,2,4,3,1,0:T(8,128)} %param.8) | copy-start | bytes 995332
  3.3 18.3 %all-to-all-start = ((f32[32,20,1,128]{3,2,1,0:T(1,128)}), f32[32,20,1,128]{3,2,1,0:T(1,128)S(1)}, u32[]{:S(2)}, u32[]{:S(2)}) async-start(f32[32,20,1,128]{3,2,1,0:T(1,128)} %broadcast_in_dim.17), calls=%async_computation | async-start | bytes 655360 | tf_op jit(solution)/shard_map/all_to_all | solution.py:721
  10.6 2.0 %collective-permute-start = (f32[8,4,128]{2,1,0:T(4,128)S(1)}, f32[8,4,128]{2,1,0:T(4,128)S(1)}, u32[]{:S(2)}, u32[]{:S(2)}) collective-permute-start(f32[8,4,128]{2,1,0:T(4,128)S(1)} %get-tuple-element.28), channel_id=1, source_target_pairs={{0,4},{1,5},{2,6},{3,7},{4,0},{5,1},{6,2},{7,3},{8,12},{9,13},{10,... | collective-permute-start | bytes 49160 | tf_op jit(solution)/shard_map/ppermute | solution.py:38
  10.9 5.9 %collective-permute-start.1 = (f32[8,4,128]{2,1,0:T(4,128)S(1)}, f32[8,4,128]{2,1,0:T(4,128)S(1)}, u32[]{:S(2)}, u32[]{:S(2)}) collective-permute-start(f32[8,4,128]{2,1,0:T(4,128)S(1)} %get-tuple-element.29), channel_id=1, source_target_pairs={{0,1},{1,0},{2,3},{3,2},{4,8},{5,9},{6,10},{7,11},{8,4},{9,5},{10,... | collective-permute-start | bytes 49160 | tf_op jit(solution)/shard_map/ppermute | solution.py:38
  16.8 4.5 %collective-permute-start.2 = (f32[14,4,128]{2,1,0:T(4,128)S(1)}, f32[14,4,128]{2,1,0:T(4,128)S(1)}, u32[]{:S(2)}, u32[]{:S(2)}) collective-permute-start(f32[14,4,128]{2,1,0:T(4,128)S(1)} %get-tuple-element.31), channel_id=1, source_target_pairs={{0,1},{1,0},{2,3},{3,2},{4,5},{5,4},{6,7},{7,6},{8,9},{9,8},{10,11... | collective-permute-start | bytes 86024 | tf_op jit(solution)/shard_map/ppermute | solution.py:38
  19.3 2.0 %collective-permute-start.3 = (f32[14,4,128]{2,1,0:T(4,128)S(1)}, f32[14,4,128]{2,1,0:T(4,128)S(1)}, u32[]{:S(2)}, u32[]{:S(2)}) collective-permute-start(f32[14,4,128]{2,1,0:T(4,128)S(1)} %get-tuple-element.32), channel_id=1, source_target_pairs={{0,4},{1,2},{2,1},{3,7},{4,0},{5,6},{6,5},{7,3},{8,12},{9,10},{10,... | collective-permute-start | bytes 86024 | tf_op jit(solution)/shard_map/ppermute | solution.py:38
  21.6 0.7 %copy-start.4 = (s32[1,1,8,128]{3,2,1,0:T(8,128)S(1)}, s32[1,1,8,128]{3,2,1,0:T(8,128)}, u32[]{:S(2)}) copy-start(s32[1,1,8,128]{3,2,1,0:T(8,128)} %param.10) | copy-start | bytes 12292
  21.6 0.7 %copy-start.3 = (f32[1,1,8,128]{3,2,1,0:T(8,128)S(1)}, f32[1,1,8,128]{3,2,1,0:T(8,128)}, u32[]{:S(2)}) copy-start(f32[1,1,8,128]{3,2,1,0:T(8,128)} %param.9) | copy-start | bytes 12292
  21.6 0.7 %copy-start.2 = (s32[1,1,8,128]{3,2,1,0:T(8,128)S(1)}, s32[1,1,8,128]{3,2,1,0:T(8,128)}, u32[]{:S(2)}) copy-start(s32[1,1,8,128]{3,2,1,0:T(8,128)} %param.11) | copy-start | bytes 12292
  25.5 2.7 %collective-permute-start.4 = (f32[56,128]{1,0:T(8,128)S(1)}, f32[56,128]{1,0:T(8,128)S(1)}, u32[]{:S(2)}, u32[]{:S(2)}) collective-permute-start(f32[56,128]{1,0:T(8,128)S(1)} %get-tuple-element.37), channel_id=1, source_target_pairs={{0,4},{1,5},{2,6},{3,7},{4,0},{5,1},{6,2},{7,3},{8,12},{9,13},{10,... | collective-permute-start | bytes 86024 | tf_op jit(solution)/shard_map/ppermute | solution.py:38
  26.4 3.9 %collective-permute-start.5 = (f32[56,128]{1,0:T(8,128)S(1)}, f32[56,128]{1,0:T(8,128)S(1)}, u32[]{:S(2)}, u32[]{:S(2)}) collective-permute-start(f32[56,128]{1,0:T(8,128)S(1)} %get-tuple-element.38), channel_id=1, source_target_pairs={{0,1},{1,0},{2,3},{3,2},{4,8},{5,9},{6,10},{7,11},{8,4},{9,5},{10,... | collective-permute-start | bytes 86024 | tf_op jit(solution)/shard_map/ppermute | solution.py:38
  31.3 13.2 %all-to-all-start.1 = ((f32[32,13,1,128]{3,2,1,0:T(1,128)}), f32[32,13,1,128]{3,2,1,0:T(1,128)S(1)}, u32[]{:S(2)}, u32[]{:S(2)}) async-start(f32[32,13,1,128]{3,2,1,0:T(1,128)} %broadcast_in_dim.19), calls=%async_computation.1 | async-start | bytes 425984 | tf_op jit(solution)/shard_map/all_to_all | solution.py:721
  34.9 6.0 %collective-permute-start.6 = (f32[72,128]{1,0:T(8,128)S(1)}, f32[72,128]{1,0:T(8,128)S(1)}, u32[]{:S(2)}, u32[]{:S(2)}) collective-permute-start(f32[72,128]{1,0:T(8,128)S(1)} %get-tuple-element.44), channel_id=1, source_target_pairs={{0,1},{1,0},{2,3},{3,2},{4,5},{5,4},{6,7},{7,6},{8,9},{9,8},{10,11... | collective-permute-start | bytes 110600 | tf_op jit(solution)/shard_map/ppermute | solution.py:38
  36.8 4.1 %collective-permute-start.7 = (f32[72,128]{1,0:T(8,128)S(1)}, f32[72,128]{1,0:T(8,128)S(1)}, u32[]{:S(2)}, u32[]{:S(2)}) collective-permute-start(f32[72,128]{1,0:T(8,128)S(1)} %get-tuple-element.45), channel_id=1, source_target_pairs={{0,4},{1,2},{2,1},{3,7},{4,0},{5,6},{6,5},{7,3},{8,12},{9,10},{10,... | collective-permute-start | bytes 110600 | tf_op jit(solution)/shard_map/ppermute | solution.py:38

commit v6 on v5

--- a/solution.py
+++ b/solution.py
@@ -229,7 +229,7 @@
     return memo(lambda x, y: place.keep(e0(x, y) + weight0(x, y) * (r(x, y) - g0(x, y)), x, y, BRICK))
 
 
-def stiffness_apply(z, fetched, base_ref, stiff_ref, valid_ref, grad_ref, hot, nodes, forces, picked, spread_sums, shifts):
+def stiffness_apply(z, hot, x_ref, effective_ref, grad_ref, nodes, forces, picked, spread_sums, shifts):
     blocks = grad_ref.shape[2]
     turns = [(b, c) for b in range(3) for c in range(3)]
     span = BRICK + 2
@@ -252,17 +252,7 @@
                 row = (u * span + x) * 8
                 nodes[row : row + 16, j * LANES : (j + 1) * LANES] = pair
 
-    fetched()
-    base = base_ref[...]
-    plane = base // (LANES + 2)
-    depth = base - plane * (LANES + 2)
-    node_x = plane // span
-    node_y = plane - node_x * span
-    sub = lax.broadcasted_iota(jnp.int32, (LANES, LANES), 0)
-    for s in range(blocks):
-        for j in range(BRICK):
-            wanted = jnp.where(node_y[s : s + 1] == j, depth[s : s + 1], -1)
-            hot[j * LANES : (j + 1) * LANES, s * LANES : (s + 1) * LANES] = as_f32(sub == wanted).astype(jnp.bfloat16)
+    node_x = x_ref[...]
     picked[...] = jnp.dot(nodes[...], hot[...], preferred_element_type=F32)
 
     first = POISSON / ((1.0 + POISSON) * (1.0 - 2.0 * POISSON))
@@ -288,7 +278,7 @@
                     h[l] = term if h[l] is None else h[l] + term
         h = [x[0:4] + x[4:8] for x in h]
         h = [[h[l][m : m + 1] for l in range(3)] for m in range(3)]
-        effective = stiff_ref[s : s + 1] * valid_ref[s : s + 1].astype(F32)
+        effective = effective_ref[s : s + 1]
         shear = effective * shear_of
         bulk = effective * first * (h[0][0] + h[1][1] + h[2][2])
         stress = []
@@ -334,16 +324,20 @@
     return out
 
 
-def fetch(sources, targets, semaphores):
-    copies = [pltpu.make_async_copy(a, b, semaphores.at[k]) for k, (a, b) in enumerate(zip(sources, targets))]
-    for copy in copies:
-        copy.start()
-
-    def wait():
-        for copy in copies:
-            copy.wait()
-
-    return wait
+def particle_kernel(counts, base_ref, stiff_ref, valid_ref, hot_ref, x_ref, effective_ref):
+    span = BRICK + 2
+    base = base_ref[...]
+    plane = base // (LANES + 2)
+    depth = base - plane * (LANES + 2)
+    node_x = plane // span
+    node_y = plane - node_x * span
+    x_ref[...] = node_x
+    effective_ref[...] = stiff_ref[...] * valid_ref[...].astype(F32)
+    sub = lax.broadcasted_iota(jnp.int32, (LANES, LANES), 0)
+    for s in range(base_ref.shape[0]):
+        for j in range(BRICK):
+            wanted = jnp.where(node_y[s : s + 1] == j, depth[s : s + 1], -1)
+            hot_ref[j * LANES : (j + 1) * LANES, s * LANES : (s + 1) * LANES] = as_f32(sub == wanted).astype(jnp.bfloat16)
 
 
 def side_parts(even_ref, odd_ref, is_even, inside_low, inside_high):
@@ -387,14 +381,12 @@
 SECOND_ROWS = 13
 
 
-def pack_kernel(counts, right_in, mass_in, own_ref, even_ref, odd_ref, slot_ref, right_ref, mass_ref, semaphores):
-    fetch((right_in, mass_in), (right_ref, mass_ref), semaphores)()
+def pack_kernel(counts, fields_ref, own_ref, even_ref, odd_ref, slot_ref):
     place, shifts = Place(*counts), Shifts()
     own = {}
     for x in range(BRICK):
         for y in range(BRICK):
-            rows = [right_ref[m, x, y : y + 1, :] for m in range(3)] + [mass_ref[x, y : y + 1, :]]
-            own[x, y] = jnp.concatenate(rows, axis=0)
+            own[x, y] = jnp.concatenate([fields_ref[m, x, y : y + 1, :] for m in range(4)], axis=0)
             own_ref[x, y] = own[x, y]
     odd_x = 1.0 - place.even_x
     for k, (x, y) in enumerate(SIDE_X):
@@ -471,7 +463,7 @@
     return memo(lambda x, y: ref[x + offset, y + offset])
 
 
-def cycle_and_apply(place, shifts, levels, r, r1, mass1, fields, fetched, particles, scratch):
+def cycle_and_apply(place, shifts, levels, r, r1, mass1, fields, particles, scratch):
     mass0, weight0 = fields
     coarse, *work = scratch
     margin = 8 * (place.count_y + 1)
@@ -493,7 +485,7 @@
         return place.keep(both[4 * (x % 2) : 4 * (x % 2) + 4], x, y, 2)
 
     z = fine_level(r, memo(f1_at), mass0, weight0, place, shifts)
-    image = stiffness_apply(z, fetched, *particles, *work, shifts)
+    image = stiffness_apply(z, *particles, *work, shifts)
     for x, y in INNER:
         image[x, y] = image[x, y] + mass0(x, y) * z(x, y)
     return z, image
@@ -519,10 +511,9 @@
 
 
 def first_kernel(counts, level_ref, r_ref, mass0_ref, weight0_ref,
-                 base_in, stiff_in, valid_in, grad_in, z_ref, image_ref, even_ref, odd_ref, dots_ref, r1_ref, mass1_ref,
-                 base_ref, stiff_ref, valid_ref, grad_ref, semaphores, *scratch):
-    particles = (base_ref, stiff_ref, valid_ref, grad_ref)
-    fetched = fetch((base_in, stiff_in, valid_in, grad_in), particles, semaphores)
+                 hot_ref, x_ref, effective_ref, grad_ref, z_ref, image_ref, even_ref, odd_ref, dots_ref, r1_ref, mass1_ref,
+                 *scratch):
+    particles = (hot_ref, x_ref, effective_ref, grad_ref)
     place, shifts = Place(*counts), Shifts()
     levels = Levels(*counts, shifts)
     rows = lambda q: level_ref[pl.ds(q, levels.rows, stride=FIRST_ROWS), :]
@@ -539,7 +530,7 @@
             r1_ref[m, x] = r1[m][x]
     r = reader(r_ref, 2)
     fields = (reader(mass0_ref, 2), reader(weight0_ref, 2))
-    z, image = cycle_and_apply(place, shifts, levels, r, r1, mass1, fields, fetched, particles, scratch)
+    z, image = cycle_and_apply(place, shifts, levels, r, r1, mass1, fields, particles, scratch)
     for x, y in INNER:
         z_ref[x, y] = z(x, y)
     for x, y in RIMMED:
@@ -602,10 +593,9 @@
 
 
 def second_kernel(counts, change_ref, r1_ref, mass1_ref, r_ref, w_ref, mass0_ref, weight0_ref,
-                  base_in, stiff_in, valid_in, grad_in, z_ref, image_ref, slots_ref,
-                  base_ref, stiff_ref, valid_ref, grad_ref, semaphores, *scratch):
-    particles = (base_ref, stiff_ref, valid_ref, grad_ref)
-    fetched = fetch((base_in, stiff_in, valid_in, grad_in), particles, semaphores)
+                  hot_ref, x_ref, effective_ref, grad_ref, z_ref, image_ref, x_even_ref, x_odd_ref, y_even_ref, y_odd_ref,
+                  slots_ref, *scratch):
+    particles = (hot_ref, x_ref, effective_ref, grad_ref)
     place, shifts = Place(*counts), Shifts()
     bricks = counts[0] * counts[1]
     levels = Levels(*counts, shifts)
@@ -618,7 +608,7 @@
     ]
     fields = (reader(mass0_ref, 2), reader(weight0_ref, 2))
     mass1 = [mass1_ref[0], mass1_ref[1]]
-    z, image = cycle_and_apply(place, shifts, levels, r, r1, mass1, fields, fetched, particles, scratch)
+    z, image = cycle_and_apply(place, shifts, levels, r, r1, mass1, fields, particles, scratch)
     for x, y in INNER:
         z_ref[x, y] = z(x, y)
         image_ref[x, y] = image[x, y]
@@ -626,55 +616,57 @@
     zaz = total_of((image[x, y], z(x, y)) for x, y in RIMMED)
     zw = total_of((w_ref[x + 2, y + 2], z(x, y)) for x, y in INNER)
     row = dots_row(rz, zaz, zw)
-    none = jnp.zeros((12, 1, LANES), F32)
+    none = jnp.zeros((3, 1, LANES), F32)
 
     def fill(k, carry):
-        slots_ref[k, 0:12] = none
-        slots_ref[k, 12] = row
+        slots_ref[k, 0:3] = none
+        slots_ref[k, 3] = row
         return carry
 
     lax.fori_loop(0, bricks, fill, 0)
-    for dx in (-1, 0, 1):
-        for dy in (-1, 0, 1):
-            if dx == 0 and dy == 0:
-                continue
-            xs = [-1] if dx < 0 else [BRICK] if dx > 0 else range(BRICK)
-            ys = [-1] if dy < 0 else [BRICK] if dy > 0 else range(BRICK)
-            columns = [image[x, y] for x in xs for y in ys]
+    for dx in (-1, 1):
+        for dy in (-1, 1):
             there_x = (place.gx + dx >= 0) & (place.gx + dx < counts[0])
             there_y = (place.gy + dy >= 0) & (place.gy + dy < counts[1])
+            column = image[BRICK if dx > 0 else -1, BRICK if dy > 0 else -1]
 
             @pl.when(there_x & there_y)
-            def _(columns=columns, dx=dx, dy=dy):
+            def _(column=column, dx=dx, dy=dy):
                 other = (place.gx + dx) * counts[1] + place.gy + dy
-                for k, column in enumerate(columns):
-                    for m in range(3):
-                        slots_ref[other, 3 * k + m] = column[m : m + 1]
-
-
-def last_kernel(counts, slots_ref, change_ref, z1_ref, z2_ref, r_ref, w_ref, image_ref, solution_ref, residual_ref):
+                for m in range(3):
+                    slots_ref[other, m] = column[m : m + 1]
+
+    clear_tail(x_even_ref, x_odd_ref, y_even_ref, y_odd_ref)
+    for k in range(BRICK):
+        put_sides(x_even_ref, x_odd_ref, 3 * k, 3, image[BRICK, k], image[-1, k], place.even_x)
+        put_sides(y_even_ref, y_odd_ref, 3 * k, 3, image[k, BRICK], image[k, -1], place.even_y)
+
+
+def last_kernel(counts, slots_ref, x_even_ref, x_odd_ref, y_even_ref, y_odd_ref, change_ref, z1_ref, z2_ref, r_ref, w_ref, image_ref, solution_ref, residual_ref):
     place = Place(*counts)
     bricks = counts[0] * counts[1]
     sums1 = sums_of(change_ref, bricks, 12, SECOND_ROWS)
-    sums2 = jnp.sum(slots_ref[:, 12], axis=0)
+    sums2 = jnp.sum(slots_ref[:, 3], axis=0)
     rz1, zaz1 = sums1[:, 0:1], sums1[:, 1:2]
     rz2, zaz2, zw = sums2[:, 0:1], sums2[:, 1:2], sums2[:, 2:3]
     step1 = rz1 / zaz1
     ratio = rz2 / rz1
     step2 = rz2 / (zaz2 + 2.0 * ratio * zw + ratio * ratio * zaz1)
     image = {(x, y): image_ref[x, y] for x, y in INNER}
-    for dx in (-1, 0, 1):
-        for dy in (-1, 0, 1):
-            if dx == 0 and dy == 0:
-                continue
-            xs = [0] if dx < 0 else [BRICK - 1] if dx > 0 else range(BRICK)
-            ys = [0] if dy < 0 else [BRICK - 1] if dy > 0 else range(BRICK)
+    left, right = side_parts(x_even_ref, x_odd_ref, place.even_x, place.in_x[-1], place.in_x[1])
+    below, above = side_parts(y_even_ref, y_odd_ref, place.even_y, place.in_y[-1], place.in_y[1])
+    end = BRICK - 1
+    for k in range(BRICK):
+        for at, part in (((0, k), left), ((end, k), right), ((k, 0), below), ((k, end), above)):
+            image[at] = image[at] + part(3 * k, 4)
+    for dx in (-1, 1):
+        for dy in (-1, 1):
             other_x = jnp.clip(place.gx + dx, 0, counts[0] - 1)
             other_y = jnp.clip(place.gy + dy, 0, counts[1] - 1)
             other = other_x * counts[1] + other_y
-            for k, (x, y) in enumerate((x, y) for x in xs for y in ys):
-                rows = [slots_ref[other, 3 * k + m] for m in range(3)] + [jnp.zeros((1, LANES), F32)]
-                image[x, y] = image[x, y] + place.keep(jnp.concatenate(rows, axis=0), dx, dy, 1)
+            column = jnp.concatenate([slots_ref[other, m] for m in range(3)] + [jnp.zeros((1, LANES), F32)], axis=0)
+            at = (end if dx > 0 else 0, end if dy > 0 else 0)
+            image[at] = image[at] + place.keep(column, dx, dy, 1)
     for x, y in INNER:
         w = w_ref[x + 2, y + 2]
         z1 = z1_ref[x, y]
@@ -685,12 +677,11 @@
             residual_ref[m, x, y : y + 1, :] = residual[m : m + 1]
 
 
-def call(kernel, counts, shapes, *args, scratch=(), far=0):
-    near = len(args) - far
+def call(kernel, counts, shapes, *args, scratch=()):
+    shapes = [s if isinstance(s[0], tuple) else (s, F32) for s in shapes]
     return pl.pallas_call(
         functools.partial(kernel, counts),
-        out_shape=[jax.ShapeDtypeStruct(s, F32) for s in shapes],
-        in_specs=[pl.BlockSpec(memory_space=pltpu.VMEM)] * near + [pl.BlockSpec(memory_space=pltpu.HBM)] * far,
+        out_shape=[jax.ShapeDtypeStruct(*s) for s in shapes],
         scratch_shapes=scratch,
         compiler_params=pltpu.CompilerParams(vmem_limit_bytes=VMEM_BYTES),
     )(*args)
@@ -699,15 +690,11 @@
 def per_device(counts, right_side, node_mass, gradients, stiffness, valid, node_base):
     bricks = counts[0] * counts[1]
     blocks = gradients.shape[2]
-    particles = (node_base[0, 0], stiffness[0, 0], valid[0, 0], gradients[0, 0].transpose(1, 2, 0, 3))
     tiles = 9 * (BRICK + 2) * 8
     depth = BRICK * LANES
     width = blocks * LANES
     scratch = (
-        *(pltpu.VMEM(p.shape, p.dtype) for p in particles),
-        pltpu.SemaphoreType.DMA((4,)),
         pltpu.VMEM((8 * (bricks + 2 * (counts[1] + 1)), LANES), F32),
-        pltpu.VMEM((depth, width), jnp.bfloat16),
         pltpu.VMEM((tiles, depth), jnp.bfloat16),
         pltpu.VMEM((tiles, width), jnp.bfloat16),
         pltpu.VMEM((tiles, width), F32),
@@ -720,23 +707,28 @@
         sent = jnp.broadcast_to(slot[None], (bricks, *slot.shape))
         return lax.all_to_all(sent, AXES, 0, 0).reshape(bricks * slot.shape[0], LANES)
 
-    fields = (right_side, node_mass)
+    fields = jnp.concatenate([right_side, node_mass[None]], axis=0)
     own, to_even, to_odd, slot = call(
-        pack_kernel, counts, [block(4, 4), block(8), block(8), (FIRST_ROWS, 1, LANES)], *fields, far=2,
-        scratch=(*(pltpu.VMEM(p.shape, p.dtype) for p in fields), pltpu.SemaphoreType.DMA((2,))),
+        pack_kernel, counts, [block(4, 4), block(8), block(8), (FIRST_ROWS, 1, LANES)], fields
     )
     level = share(slot)
     even, odd = exchange(to_even, to_odd, "gx", counts)
     side = block(len(SIDE))
     wide, to_even, to_odd = call(widen_kernel, counts, [block(8, 4), side, side], own, even, odd)
     even, odd = exchange(to_even, to_odd, "gy", counts)
+    row = (blocks, LANES)
+    prepared = call(
+        particle_kernel, counts, [((depth, width), jnp.bfloat16), (row, jnp.int32), row],
+        node_base[0, 0], stiffness[0, 0], valid[0, 0],
+    )
+    particles = (*prepared, gradients[0, 0].transpose(1, 2, 0, 3))
     r, *fields = call(start_kernel, counts, [block(8, 8)] * 3, wide, even, odd)
 
     side = rows(SIDE_X_IMAGE)
     z1, image, to_even, to_odd, dots, r1, mass1 = call(
         first_kernel, counts,
         [block(4, 4), block(6, 6), side, side, (1, LANES), (3, 2, bricks, LANES), (2, bricks, LANES)],
-        level, r, *fields, *particles, scratch=scratch, far=4,
+        level, r, *fields, *particles, scratch=scratch,
     )
     even, odd = exchange(to_even, to_odd, "gx", counts)
     side = rows(SIDE_IMAGE)
@@ -746,13 +738,15 @@
     change = share(slot)
     even, odd = exchange(to_even, to_odd, "gy", counts)
     (w,) = call(middle_kernel, counts, [block(8, 8)], wide, even, odd)
-    z2, image, slots = call(
-        second_kernel, counts, [block(4, 4), block(4, 4), (bricks, 13, 1, LANES)],
-        change, r1, mass1, r, w, *fields, *particles, scratch=scratch, far=4,
-    )
+    side = (2 * 8, LANES)
+    z2, image, x_even, x_odd, y_even, y_odd, slots = call(
+        second_kernel, counts, [block(4, 4), block(4, 4), side, side, side, side, (bricks, 4, 1, LANES)],
+        change, r1, mass1, r, w, *fields, *particles, scratch=scratch,
+    )
+    sides = (*exchange(x_even, x_odd, "gx", counts), *exchange(y_even, y_odd, "gy", counts))
     slots = lax.all_to_all(slots, AXES, 0, 0)
     return tuple(
-        call(last_kernel, counts, [right_side.shape, right_side.shape], slots, change, z1, z2, r, w, image)
+        call(last_kernel, counts, [right_side.shape, right_side.shape], slots, *sides, change, z1, z2, r, w, image)
     )
 
 

time: 61.1 us -> 58.1 us (0.951)
  blocking collectives: 11.8 us -> 0 us
  starting transfers between devices: 19.9 us -> 25.6 us
  waiting for transfers between devices: 16.1 us -> 20.2 us
  local copies, waits for them, and re-layouts: 3.84 us -> 1.75 us
  other arithmetic: 0 us -> 0.76 us
    all_to_all x1 -> x0, blocking collectives: 11.8 us -> none  [per_device(): slots = lax.all_to_all(slots, AXES, 0, 0)]
    ppermute x8 -> x12, starting transfers between devices: 9.02 us -> 12.2 us  [exchange(): return (lax.ppermute(first, AXES, even), lax.ppermute(second, AXES, odd))]
    all_to_all x0 -> x1, starting transfers between devices: none -> 2.57 us  [per_device(): slots = lax.all_to_all(slots, AXES, 0, 0)]
    unnamed x14 -> x10, local copies, waits for them, and re-layouts: 2.15 us -> 0.03 us
    ppermute x8 -> x12, waiting for transfers between devices: 12.4 us -> 14.4 us  [exchange(): return (lax.ppermute(first, AXES, even), lax.ppermute(second, AXES, odd))]
    all_to_all x0 -> x1, waiting for transfers between devices: none -> 2 us  [per_device(): slots = lax.all_to_all(slots, AXES, 0, 0)]
    concatenate x0 -> x1, other arithmetic: none -> 0.76 us  [per_device(): fields = jnp.concatenate([right_side, node_mass[None]], axis=0)]
    pallas_call x8 -> x9, Pallas kernels: 8.35 us -> 8.71 us  [call(): pl.pallas_call(functools.partial(kernel, counts), out_shape=[jax.ShapeDty...]
  transfers between devices with their start and end apart: 10 -> 15, of which waited for: 6 -> 9; matrix products, arithmetic and copies ran while one was open for 0% -> 0% of each run, Pallas kernels for 0% -> 1%
where the time goes in v6:
time: 58.1 us; the launch traced here: 57.7 us
  starting transfers between devices  25.6 us (44%)
  waiting for transfers between devices  20.2 us (35%)
  Pallas kernels  8.71 us (15%)
  local copies, waits for them, and re-layouts  1.75 us (3%)
  other arithmetic  0.76 us (1%)
  between operations  0.73 us (1%)
    ppermute x12, waiting for transfers between devices, exchange(): return (lax.ppermute(first, AXES, even), lax.ppermute(second, AXES, odd))  14.4 us
    ppermute x12, starting transfers between devices, exchange(): return (lax.ppermute(first, AXES, even), lax.ppermute(second, AXES, odd))  12.2 us
    all_to_all x2, starting transfers between devices, share(): lax.all_to_all(sent, AXES, 0, 0).reshape(bricks * slot.shape[0], LANES)  10.9 us
    pallas_call x9, Pallas kernels, call(): pl.pallas_call(functools.partial(kernel, counts), out_shape=[jax.ShapeDty...  8.71 us
    all_to_all x2, waiting for transfers between devices, share(): lax.all_to_all(sent, AXES, 0, 0).reshape(bricks * slot.shape[0], LANES)  3.73 us
    all_to_all x1, starting transfers between devices, per_device(): slots = lax.all_to_all(slots, AXES, 0, 0)  2.57 us
    all_to_all x1, waiting for transfers between devices, per_device(): slots = lax.all_to_all(slots, AXES, 0, 0)  2 us
    broadcast_in_dim x2, local copies, waits for them, and re-layouts, share(): sent = jnp.broadcast_to(slot[None], (bricks, *slot.shape))  1.72 us
  transfers between devices with their start and end apart: 15, of which 9 were waited for; matrix products, arithmetic and copies ran while one was open for 0% of the time, Pallas kernels for 1%

profile of v6, /device:TPU:0, one launch (start us, length us, event | category | flops | bytes accessed | tf_op | source)
XLA Modules:
  0.0 57.7 jit_solution(9753530012295879662)
XLA Ops:
  0.6 0.8 %pad_maximum_fusion.fields_ref = f32[4,4,4,128]{3,2,1,0:T(4,128)S(1)} fusion(f32[1,4,4,128]{3,2,1,0:T(4,128)} %bitcast.25, f32[3,4,4,128]{3,2,1,0:T(4,128)} %param.6), kind=kLoop, calls=%fused_computation | loop fusion | flops 8192 | bytes 65536 | tf_op jit(solution)/shard_map/concatenate | solution.py:710
  1.7 0.9 %broadcast_in_dim.21 = f32[32,20,1,128]{3,2,1,0:T(1,128)} broadcast(f32[20,128]{1,0:T(8,128)S(1)} %bitcast.23), dimensions={1,3} | broadcast | bytes 337920 | tf_op jit(solution)/shard_map/broadcast_in_dim | solution.py:707
  2.6 7.3 %all-to-all-start = ((f32[32,20,1,128]{3,2,1,0:T(1,128)}), f32[32,20,1,128]{3,2,1,0:T(1,128)S(1)}, u32[]{:S(2)}, u32[]{:S(2)}) async-start(f32[32,20,1,128]{3,2,1,0:T(1,128)} %broadcast_in_dim.21), calls=%async_computation | async-start | bytes 655360 | tf_op jit(solution)/shard_map/all_to_all | solution.py:708
  10.2 1.7 %collective-permute-start.1 = (f32[8,4,128]{2,1,0:T(4,128)S(1)}, f32[8,4,128]{2,1,0:T(4,128)S(1)}, u32[]{:S(2)}, u32[]{:S(2)}) collective-permute-start(f32[8,4,128]{2,1,0:T(4,128)S(1)} %get-tuple-element.36), channel_id=1, source_target_pairs={{0,1},{1,0},{2,3},{3,2},{4,8},{5,9},{6,10},{7,11},{8,4},{9,5},{10,... | collective-permute-start | bytes 49160 | tf_op jit(solution)/shard_map/ppermute | solution.py:38
  11.9 4.2 %collective-permute-done.1.odd_ref = f32[8,4,128]{2,1,0:T(4,128)S(1)} collective-permute-done((f32[8,4,128]{2,1,0:T(4,128)S(1)}, f32[8,4,128]{2,1,0:T(4,128)S(1)}, u32[]{:S(2)}, u32[]{:S(2)}) %collective-permute-start.1) | collective-permute-done | bytes 16416 | tf_op jit(solution)/shard_map/ppermute | solution.py:38
  16.1 2.5 %collective-permute-start.2 = (f32[14,4,128]{2,1,0:T(4,128)S(1)}, f32[14,4,128]{2,1,0:T(4,128)S(1)}, u32[]{:S(2)}, u32[]{:S(2)}) collective-permute-start(f32[14,4,128]{2,1,0:T(4,128)S(1)} %get-tuple-element.38), channel_id=1, source_target_pairs={{0,1},{1,0},{2,3},{3,2},{4,5},{5,4},{6,7},{7,6},{8,9},{9,8},{10,11... | collective-permute-start | bytes 86024 | tf_op jit(solution)/shard_map/ppermute | solution.py:38
  19.0 1.6 %collective-permute-done.2.even_ref = f32[14,4,128]{2,1,0:T(4,128)S(1)} collective-permute-done((f32[14,4,128]{2,1,0:T(4,128)S(1)}, f32[14,4,128]{2,1,0:T(4,128)S(1)}, u32[]{:S(2)}, u32[]{:S(2)}) %collective-permute-start.2) | collective-permute-done | bytes 28704 | tf_op jit(solution)/shard_map/ppermute | solution.py:38
  20.9 2.9 %shard_map.81 = (f32[4,4,4,128]{3,2,1,0:T(4,128)S(1)}, f32[6,6,4,128]{3,2,1,0:T(4,128)S(1)}, f32[56,128]{1,0:T(8,128)S(1)}, f32[56,128]{1,0:T(8,128)S(1)}, f32[1...) custom-call(f32[640,128]{1,0:T(8,128)S(1)} %bitcast.19, ...), custom_call_target="tpu_custom_call" | custom-call | tf_op jit(solution)/shard_map/pallas_call | solution.py:682
  23.8 0.8 %collective-permute-start.4 = (f32[56,128]{1,0:T(8,128)S(1)}, f32[56,128]{1,0:T(8,128)S(1)}, u32[]{:S(2)}, u32[]{:S(2)}) collective-permute-start(f32[56,128]{1,0:T(8,128)S(1)} %get-tuple-element.47), channel_id=1, source_target_pairs={{0,4},{1,5},{2,6},{3,7},{4,0},{5,1},{6,2},{7,3},{8,12},{9,13},{10,... | collective-permute-start | bytes 86024 | tf_op jit(solution)/shard_map/ppermute | solution.py:38
  24.6 1.7 %collective-permute-start.5 = (f32[56,128]{1,0:T(8,128)S(1)}, f32[56,128]{1,0:T(8,128)S(1)}, u32[]{:S(2)}, u32[]{:S(2)}) collective-permute-start(f32[56,128]{1,0:T(8,128)S(1)} %get-tuple-element.48), channel_id=1, source_target_pairs={{0,1},{1,0},{2,3},{3,2},{4,8},{5,9},{6,10},{7,11},{8,4},{9,5},{10,... | collective-permute-start | bytes 86024 | tf_op jit(solution)/shard_map/ppermute | solution.py:38
  26.4 2.1 %collective-permute-done.5.odd_ref = f32[56,128]{1,0:T(8,128)S(1)} collective-permute-done((f32[56,128]{1,0:T(8,128)S(1)}, f32[56,128]{1,0:T(8,128)S(1)}, u32[]{:S(2)}, u32[]{:S(2)}) %collective-permute-start.5) | collective-permute-done | bytes 28704 | tf_op jit(solution)/shard_map/ppermute | solution.py:38
  28.8 0.8 %broadcast_in_dim.23 = f32[32,13,1,128]{3,2,1,0:T(1,128)} broadcast(f32[13,128]{1,0:T(8,128)S(1)} %bitcast.24), dimensions={1,3} | broadcast | bytes 219648 | tf_op jit(solution)/shard_map/broadcast_in_dim | solution.py:707
  29.6 3.6 %all-to-all-start.1 = ((f32[32,13,1,128]{3,2,1,0:T(1,128)}), f32[32,13,1,128]{3,2,1,0:T(1,128)S(1)}, u32[]{:S(2)}, u32[]{:S(2)}) async-start(f32[32,13,1,128]{3,2,1,0:T(1,128)} %broadcast_in_dim.23), calls=%async_computation.1 | async-start | bytes 425984 | tf_op jit(solution)/shard_map/all_to_all | solution.py:708
  33.2 1.8 %collective-permute-start.6 = (f32[72,128]{1,0:T(8,128)S(1)}, f32[72,128]{1,0:T(8,128)S(1)}, u32[]{:S(2)}, u32[]{:S(2)}) collective-permute-start(f32[72,128]{1,0:T(8,128)S(1)} %get-tuple-element.54), channel_id=1, source_target_pairs={{0,1},{1,0},{2,3},{3,2},{4,5},{5,4},{6,7},{7,6},{8,9},{9,8},{10,11... | collective-permute-start | bytes 110600 | tf_op jit(solution)/shard_map/ppermute | solution.py:38
  35.0 4.1 %collective-permute-done.6.even_ref = f32[72,128]{1,0:T(8,128)S(1)} collective-permute-done((f32[72,128]{1,0:T(8,128)S(1)}, f32[72,128]{1,0:T(8,128)S(1)}, u32[]{:S(2)}, u32[]{:S(2)}) %collective-permute-start.6) | collective-permute-done | bytes 36896 | tf_op jit(solution)/shard_map/ppermute | solution.py:38
  39.2 3.6 %all-to-all-done.1 = f32[32,13,1,128]{3,2,1,0:T(1,128)S(1)} async-done(((f32[32,13,1,128]{3,2,1,0:T(1,128)}), f32[32,13,1,128]{3,2,1,0:T(1,128)S(1)}, u32[]{:S(2)}, u32[]{:S(2)}) %all-to-all-start.1) | async-done | bytes 213024 | tf_op jit(solution)/shard_map/all_to_all | solution.py:708
  42.8 3.9 %shard_map.84 = (f32[4,4,4,128]{3,2,1,0:T(4,128)S(1)}, f32[4,4,4,128]{3,2,1,0:T(4,128)S(1)}, f32[16,128]{1,0:T(8,128)S(1)}, f32[16,128]{1,0:T(8,128)S(1)}, f32[1...) custom-call(f32[416,128]{1,0:T(8,128)S(1)} %bitcast.15, ...), custom_call_target="tpu_custom_call" | custom-call | tf_op jit(solution)/shard_map/pallas_call | solution.py:682
  46.6 2.6 %all-to-all-start.2 = ((f32[32,4,1,128]{3,2,1,0:T(1,128)}), f32[32,4,1,128]{3,2,1,0:T(1,128)S(1)}, u32[]{:S(2)}, u32[]{:S(2)}) async-start(f32[32,4,1,128]{3,2,1,0:T(1,128)} %get-tuple-element.56), calls=%async_computation.2 | async-start | bytes 131072 | tf_op jit(solution)/shard_map/all_to_all | solution.py:747
  49.4 1.7 %collective-permute-start.9 = (f32[16,128]{1,0:T(8,128)S(1)}, f32[16,128]{1,0:T(8,128)S(1)}, u32[]{:S(2)}, u32[]{:S(2)}) collective-permute-start(f32[16,128]{1,0:T(8,128)S(1)} %get-tuple-element.58), channel_id=1, source_target_pairs={{0,1},{1,0},{2,3},{3,2},{4,8},{5,9},{6,10},{7,11},{8,4},{9,5},{10,... | collective-permute-start | bytes 24584 | tf_op jit(solution)/shard_map/ppermute | solution.py:38
  51.4 1.0 %collective-permute-start.11 = (f32[16,128]{1,0:T(8,128)S(1)}, f32[16,128]{1,0:T(8,128)S(1)}, u32[]{:S(2)}, u32[]{:S(2)}) collective-permute-start(f32[16,128]{1,0:T(8,128)S(1)} %get-tuple-element.60), channel_id=1, source_target_pairs={{0,4},{1,2},{2,1},{3,7},{4,0},{5,6},{6,5},{7,3},{8,12},{9,10},{10,... | collective-permute-start | bytes 24584 | tf_op jit(solution)/shard_map/ppermute | solution.py:38
  52.4 0.6 %collective-permute-done.9.x_odd_ref = f32[16,128]{1,0:T(8,128)S(1)} collective-permute-done((f32[16,128]{1,0:T(8,128)S(1)}, f32[16,128]{1,0:T(8,128)S(1)}, u32[]{:S(2)}, u32[]{:S(2)}) %collective-permute-start.9) | collective-permute-done | bytes 8224 | tf_op jit(solution)/shard_map/ppermute | solution.py:38
  53.1 1.7 %collective-permute-done.10.y_even_ref = f32[16,128]{1,0:T(8,128)S(1)} collective-permute-done((f32[16,128]{1,0:T(8,128)S(1)}, f32[16,128]{1,0:T(8,128)S(1)}, u32[]{:S(2)}, u32[]{:S(2)}) %collective-permute-start.10) | collective-permute-done | bytes 8224 | tf_op jit(solution)/shard_map/ppermute | solution.py:38
  54.8 2.0 %all-to-all-done.2.slots_ref = f32[32,4,1,128]{3,2,1,0:T(1,128)S(1)} async-done(((f32[32,4,1,128]{3,2,1,0:T(1,128)}), f32[32,4,1,128]{3,2,1,0:T(1,128)S(1)}, u32[]{:S(2)}, u32[]{:S(2)}) %all-to-all-start.2) | async-done | bytes 65568 | tf_op jit(solution)/shard_map/all_to_all | solution.py:747
  56.8 0.9 %shard_map.85 = (f32[3,4,4,128]{3,2,1,0:T(4,128)}, f32[3,4,4,128]{3,2,1,0:T(4,128)}) custom-call(f32[32,4,1,128]{3,2,1,0:T(1,128)S(1)} %all-to-all-done.2.slots_ref, f32[16,128]{1,0:T(8,128)S(1)} %collective-permute-done.8.x_even_ref, f32[16,128]{1,0:T(8,128)S(1)} %collective-permute-done.9.x_odd_ref, f32[16,128]{1,0:T(8,128)S(1)} %collective-permute-done.10.y_even_ref, ...), custom_call_target="tpu_custom_call" | custom-call | tf_op jit(solution)/shard_map/pallas_call | solution.py:682
  (28 shorter events, 2.0 us)
Async XLA Ops:
  2.6 18.3 %copy-start = (f32[1,1,8,3,27,128]{5,2,4,3,1,0:T(8,128)S(1)}, f32[1,1,8,3,27,128]{5,2,4,3,1,0:T(8,128)}, u32[]{:S(2)}) copy-start(f32[1,1,8,3,27,128]{5,2,4,3,1,0:T(8,128)} %param.8) | copy-start | bytes 995332
  2.6 18.3 %all-to-all-start = ((f32[32,20,1,128]{3,2,1,0:T(1,128)}), f32[32,20,1,128]{3,2,1,0:T(1,128)S(1)}, u32[]{:S(2)}, u32[]{:S(2)}) async-start(f32[32,20,1,128]{3,2,1,0:T(1,128)} %broadcast_in_dim.21), calls=%async_computation | async-start | bytes 655360 | tf_op jit(solution)/shard_map/all_to_all | solution.py:708
  9.9 2.0 %collective-permute-start = (f32[8,4,128]{2,1,0:T(4,128)S(1)}, f32[8,4,128]{2,1,0:T(4,128)S(1)}, u32[]{:S(2)}, u32[]{:S(2)}) collective-permute-start(f32[8,4,128]{2,1,0:T(4,128)S(1)} %get-tuple-element.35), channel_id=1, source_target_pairs={{0,4},{1,5},{2,6},{3,7},{4,0},{5,1},{6,2},{7,3},{8,12},{9,13},{10,... | collective-permute-start | bytes 49160 | tf_op jit(solution)/shard_map/ppermute | solution.py:38
  10.2 5.9 %collective-permute-start.1 = (f32[8,4,128]{2,1,0:T(4,128)S(1)}, f32[8,4,128]{2,1,0:T(4,128)S(1)}, u32[]{:S(2)}, u32[]{:S(2)}) collective-permute-start(f32[8,4,128]{2,1,0:T(4,128)S(1)} %get-tuple-element.36), channel_id=1, source_target_pairs={{0,1},{1,0},{2,3},{3,2},{4,8},{5,9},{6,10},{7,11},{8,4},{9,5},{10,... | collective-permute-start | bytes 49160 | tf_op jit(solution)/shard_map/ppermute | solution.py:38
  16.1 2.6 %copy-start.3 = (s32[1,1,8,128]{3,2,1,0:T(8,128)S(1)}, s32[1,1,8,128]{3,2,1,0:T(8,128)}, u32[]{:S(2)}) copy-start(s32[1,1,8,128]{3,2,1,0:T(8,128)} %param.10) | copy-start | bytes 12292
  16.1 2.6 %copy-start.2 = (f32[1,1,8,128]{3,2,1,0:T(8,128)S(1)}, f32[1,1,8,128]{3,2,1,0:T(8,128)}, u32[]{:S(2)}) copy-start(f32[1,1,8,128]{3,2,1,0:T(8,128)} %param.9) | copy-start | bytes 12292
  16.1 2.6 %copy-start.1 = (s32[1,1,8,128]{3,2,1,0:T(8,128)S(1)}, s32[1,1,8,128]{3,2,1,0:T(8,128)}, u32[]{:S(2)}) copy-start(s32[1,1,8,128]{3,2,1,0:T(8,128)} %param.11) | copy-start | bytes 12292
  16.1 4.5 %collective-permute-start.2 = (f32[14,4,128]{2,1,0:T(4,128)S(1)}, f32[14,4,128]{2,1,0:T(4,128)S(1)}, u32[]{:S(2)}, u32[]{:S(2)}) collective-permute-start(f32[14,4,128]{2,1,0:T(4,128)S(1)} %get-tuple-element.38), channel_id=1, source_target_pairs={{0,1},{1,0},{2,3},{3,2},{4,5},{5,4},{6,7},{7,6},{8,9},{9,8},{10,11... | collective-permute-start | bytes 86024 | tf_op jit(solution)/shard_map/ppermute | solution.py:38
  18.7 2.0 %collective-permute-start.3 = (f32[14,4,128]{2,1,0:T(4,128)S(1)}, f32[14,4,128]{2,1,0:T(4,128)S(1)}, u32[]{:S(2)}, u32[]{:S(2)}) collective-permute-start(f32[14,4,128]{2,1,0:T(4,128)S(1)} %get-tuple-element.39), channel_id=1, source_target_pairs={{0,4},{1,2},{2,1},{3,7},{4,0},{5,6},{6,5},{7,3},{8,12},{9,10},{10,... | collective-permute-start | bytes 86024 | tf_op jit(solution)/shard_map/ppermute | solution.py:38
  23.8 2.6 %collective-permute-start.4 = (f32[56,128]{1,0:T(8,128)S(1)}, f32[56,128]{1,0:T(8,128)S(1)}, u32[]{:S(2)}, u32[]{:S(2)}) collective-permute-start(f32[56,128]{1,0:T(8,128)S(1)} %get-tuple-element.47), channel_id=1, source_target_pairs={{0,4},{1,5},{2,6},{3,7},{4,0},{5,1},{6,2},{7,3},{8,12},{9,13},{10,... | collective-permute-start | bytes 86024 | tf_op jit(solution)/shard_map/ppermute | solution.py:38
  24.6 3.9 %collective-permute-start.5 = (f32[56,128]{1,0:T(8,128)S(1)}, f32[56,128]{1,0:T(8,128)S(1)}, u32[]{:S(2)}, u32[]{:S(2)}) collective-permute-start(f32[56,128]{1,0:T(8,128)S(1)} %get-tuple-element.48), channel_id=1, source_target_pairs={{0,1},{1,0},{2,3},{3,2},{4,8},{5,9},{6,10},{7,11},{8,4},{9,5},{10,... | collective-permute-start | bytes 86024 | tf_op jit(solution)/shard_map/ppermute | solution.py:38
  29.6 13.2 %all-to-all-start.1 = ((f32[32,13,1,128]{3,2,1,0:T(1,128)}), f32[32,13,1,128]{3,2,1,0:T(1,128)S(1)}, u32[]{:S(2)}, u32[]{:S(2)}) async-start(f32[32,13,1,128]{3,2,1,0:T(1,128)} %broadcast_in_dim.23), calls=%async_computation.1 | async-start | bytes 425984 | tf_op jit(solution)/shard_map/all_to_all | solution.py:708
  33.2 6.0 %collective-permute-start.6 = (f32[72,128]{1,0:T(8,128)S(1)}, f32[72,128]{1,0:T(8,128)S(1)}, u32[]{:S(2)}, u32[]{:S(2)}) collective-permute-start(f32[72,128]{1,0:T(8,128)S(1)} %get-tuple-element.54), channel_id=1, source_target_pairs={{0,1},{1,0},{2,3},{3,2},{4,5},{5,4},{6,7},{7,6},{8,9},{9,8},{10,11... | collective-permute-start | bytes 110600 | tf_op jit(solution)/shard_map/ppermute | solution.py:38
  35.0 4.1 %collective-permute-start.7 = (f32[72,128]{1,0:T(8,128)S(1)}, f32[72,128]{1,0:T(8,128)S(1)}, u32[]{:S(2)}, u32[]{:S(2)}) collective-permute-start(f32[72,128]{1,0:T(8,128)S(1)} %get-tuple-element.55), channel_id=1, source_target_pairs={{0,4},{1,2},{2,1},{3,7},{4,0},{5,6},{6,5},{7,3},{8,12},{9,10},{10,... | collective-permute-start | bytes 110600 | tf_op jit(solution)/shard_map/ppermute | solution.py:38
  46.6 10.2 %all-to-all-start.2 = ((f32[32,4,1,128]{3,2,1,0:T(1,128)}), f32[32,4,1,128]{3,2,1,0:T(1,128)S(1)}, u32[]{:S(2)}, u32[]{:S(2)}) async-start(f32[32,4,1,128]{3,2,1,0:T(1,128)} %get-tuple-element.56), calls=%async_computation.2 | async-start | bytes 131072 | tf_op jit(solution)/shard_map/all_to_all | solution.py:747
  49.2 3.2 %collective-permute-start.8 = (f32[16,128]{1,0:T(8,128)S(1)}, f32[16,128]{1,0:T(8,128)S(1)}, u32[]{:S(2)}, u32[]{:S(2)}) collective-permute-start(f32[16,128]{1,0:T(8,128)S(1)} %get-tuple-element.57), channel_id=1, source_target_pairs={{0,4},{1,5},{2,6},{3,7},{4,0},{5,1},{6,2},{7,3},{8,12},{9,13},{10,... | collective-permute-start | bytes 24584 | tf_op jit(solution)/shard_map/ppermute | solution.py:38
  49.4 3.7 %collective-permute-start.9 = (f32[16,128]{1,0:T(8,128)S(1)}, f32[16,128]{1,0:T(8,128)S(1)}, u32[]{:S(2)}, u32[]{:S(2)}) collective-permute-start(f32[16,128]{1,0:T(8,128)S(1)} %get-tuple-element.58), channel_id=1, source_target_pairs={{0,1},{1,0},{2,3},{3,2},{4,8},{5,9},{6,10},{7,11},{8,4},{9,5},{10,... | collective-permute-start | bytes 24584 | tf_op jit(solution)/shard_map/ppermute | solution.py:38
  51.1 3.7 %collective-permute-start.10 = (f32[16,128]{1,0:T(8,128)S(1)}, f32[16,128]{1,0:T(8,128)S(1)}, u32[]{:S(2)}, u32[]{:S(2)}) collective-permute-start(f32[16,128]{1,0:T(8,128)S(1)} %get-tuple-element.59), channel_id=1, source_target_pairs={{0,1},{1,0},{2,3},{3,2},{4,5},{5,4},{6,7},{7,6},{8,9},{9,8},{10,11... | collective-permute-start | bytes 24584 | tf_op jit(solution)/shard_map/ppermute | solution.py:38
  51.4 3.4 %collective-permute-start.11 = (f32[16,128]{1,0:T(8,128)S(1)}, f32[16,128]{1,0:T(8,128)S(1)}, u32[]{:S(2)}, u32[]{:S(2)}) collective-permute-start(f32[16,128]{1,0:T(8,128)S(1)} %get-tuple-element.60), channel_id=1, source_target_pairs={{0,4},{1,2},{2,1},{3,7},{4,0},{5,6},{6,5},{7,3},{8,12},{9,10},{10,... | collective-permute-start | bytes 24584 | tf_op jit(solution)/shard_map/ppermute | solution.py:38

commit v7 on v6

--- a/solution.py
+++ b/solution.py
@@ -9,6 +9,7 @@
 
 POISSON = 0.3
 DAMPING = 0.7
+KEPT = 1.0 - DAMPING
 SWEEPS = 4
 LANES = 128
 BRICK = 4
@@ -39,9 +40,9 @@
 
 
 SIDE = [(x, -1) for x in range(-2, 6)] + [(x, -2) for x in range(-1, 5)]
-SIDE_IMAGE = [(x, 0) for x in range(-2, 6)] + SIDE
 SIDE_X = [(x, y) for x in (-2, -1) for y in range(BRICK)]
-SIDE_X_IMAGE = [(x, y) for x in (-2, -1, 0) for y in range(-1, 5)]
+SIDE_Y_IMAGE = [(x, y) for y in (-2, -1, 0) for x in range(-1, 5)]
+SIDE_X_IMAGE = [(0, y) for y in range(-2, 6)] + [(y, x) for x, y in SIDE]
 
 
 def mirror(x, y):
@@ -92,7 +93,6 @@
         self.high = {d: as_f32(lane < LANES - d) for d in (1, 2, 4)}
         self.even = as_f32(lane % 2 == 0)
         self.odd = 1.0 - self.even
-        self.half = as_f32(lane % 4 < 2)
 
     def beside(self, x, d):
         return turn(x, d) * self.low[d] + turn(x, -d) * self.high[d]
@@ -100,10 +100,6 @@
     def pair_sum(self, x):
         t = (x + turn(x, -1)) * self.even
         return t + turn(t, 1)
-
-    def quad_sum(self, x):
-        t = (x + turn(x, -2)) * self.half
-        return t + turn(t, 2)
 
 
 def memo(fn):
@@ -117,16 +113,11 @@
     return wrapped
 
 
-def grid_apply(e, mass, coupling, shifts, step):
-    def at(x, y):
-        c = e(x, y)
-        beside = e(x + 1, y) + e(x - 1, y) + e(x, y + 1) + e(x, y - 1) + shifts.beside(c, step)
-        return mass(x, y) * c + coupling * (6.0 * c - beside)
-
-    return at
-
-
-def contribution(w, mass0, weight0, columns, cells, shifts):
+def beside_all(e, x, y, shifts, step):
+    return e(x + 1, y) + e(x - 1, y) + e(x, y + 1) + e(x, y - 1) + shifts.beside(e(x, y), step)
+
+
+def contribution(w, weight0, columns, cells, shifts):
     inside = set(columns)
     e0 = memo(lambda x, y: weight0(x, y) * w(x, y) if (x, y) in inside else None)
 
@@ -137,7 +128,7 @@
         if c is None:
             return total
         near = shifts.beside(c, 1) if total is None else total + shifts.beside(c, 1)
-        return w(x, y) - (mass0(x, y) * c + (6.0 * c - near))
+        return KEPT * w(x, y) + near
 
     out = {}
     for x, y in cells:
@@ -148,67 +139,57 @@
 
 class Levels:
     def __init__(self, count_x, count_y, shifts):
-        rows = count_x * count_y
-        lane = lax.broadcasted_iota(jnp.int32, (rows, LANES), 1)
-        row = lax.broadcasted_iota(jnp.int32, (rows, LANES), 0)
-        column = row % count_y
-        self.rows, self.count_y, self.shifts = rows, count_y, shifts
-        self.x_low, self.x_high = as_f32(row >= count_y), as_f32(row < rows - count_y)
-        self.y_low, self.y_high = as_f32(column > 0), as_f32(column < count_y - 1)
+        self.count_x, self.count_y, self.shifts = count_x, count_y, shifts
+        row = lax.broadcasted_iota(jnp.int32, (1, count_x, LANES), 1)
+        lane = lax.broadcasted_iota(jnp.int32, (1, 1, LANES), 2)
+        self.x_low, self.x_high = as_f32(row > 0), as_f32(row < count_x - 1)
         self.even = as_f32(lane % 2 == 0)
         self.odd = 1.0 - self.even
-        self.from_low = self.y_low * self.even
-        self.from_high = self.y_high * self.odd
+        self.first = as_f32(lane % 4 == 0)
+        self.low, self.high = as_f32(lane >= 4), as_f32(lane < LANES - 4)
+        self.z_low, self.z_high = self.low * as_f32(lane % 4 >= 2), self.high * as_f32(lane % 4 < 2)
+        self.edge = jnp.zeros((1, count_x, LANES), F32)
+
+    def load(self, ref, first, stride):
+        pick = lambda y: ref[pl.ds(first + stride * y, self.count_x, stride=stride * self.count_y), :]
+        return jnp.stack([pick(y) for y in range(self.count_y)])
 
     def below_x(self, v):
-        return pltpu.roll(v, self.count_y, 0) * self.x_low
+        return pltpu.roll(v, 1, 1) * self.x_low
 
     def above_x(self, v):
-        return pltpu.roll(v, self.rows - self.count_y, 0) * self.x_high
-
-    def row(self, v, k):
-        return pltpu.roll(v, k % self.rows, 0)
+        return pltpu.roll(v, self.count_x - 1, 1) * self.x_high
+
+    def below_y(self, v):
+        return jnp.concatenate([self.edge, v[:-1]], axis=0)
+
+    def above_y(self, v):
+        return jnp.concatenate([v[1:], self.edge], axis=0)
+
+    def beside(self, v, d):
+        return turn(v, d) * self.low + turn(v, -d) * self.high
 
     def gather_y(self, first, second):
-        return (first + self.row(second, 1) * self.y_low) * self.even + (
-            second + self.row(first, -1) * self.y_high
-        ) * self.odd
-
-    def apply_1(self, v, mass):
-        out = []
-        for x in range(2):
-            c, other = v[x], v[1 - x]
-            swapped = turn(c, -1) * self.even + turn(c, 1) * self.odd
-            near = other + (self.below_x(other) if x == 0 else self.above_x(other))
-            near = near + swapped + self.row(swapped, 1) * self.from_low + self.row(swapped, -1) * self.from_high
-            near = near + self.shifts.beside(c, 2)
-            out.append(mass[x] * c + 2.0 * (6.0 * c - near))
-        return out
-
-    def solve_2(self, r2, mass, weight):
-        e = weight * r2
+        return (first + self.below_y(second)) * self.even + (second + self.above_y(first)) * self.odd
+
+    def quad_sum(self, v):
+        v = (v + turn(v, -1) + turn(v, -2) + turn(v, -3)) * self.first
+        return v + turn(v, 1) + turn(v, 2) + turn(v, 3)
+
+    def restrict(self, r, e):
+        t = e[0] + e[1]
+        near = 3.0 * t + self.below_x(e[1]) + self.above_x(e[0]) + self.below_y(t) * self.odd
+        near = near + self.above_y(t) * self.even + turn(t, 4) * self.z_low + turn(t, -4) * self.z_high
+        return self.quad_sum(KEPT * (r[0] + r[1]) + 2.0 * near)
+
+    def solve_2(self, r2, weight):
+        start = weight * r2
+        weight = 4.0 * weight
+        e = start
         for _ in range(SWEEPS - 1):
-            near = self.shifts.beside(e, 4) + self.below_x(e) + self.above_x(e)
-            near = near + self.row(e, 1) * self.y_low + self.row(e, -1) * self.y_high
-            e = e + weight * (r2 - (mass * e + 4.0 * (6.0 * e - near)))
+            near = self.below_x(e) + self.above_x(e) + self.below_y(e) + self.above_y(e) + self.beside(e, 4)
+            e = (KEPT * e + start) + weight * near
         return e
-
-    def sum_2(self, v):
-        return self.shifts.quad_sum(self.shifts.pair_sum(v[0] + v[1]))
-
-    def solve(self, r1, mass1):
-        weight1 = [DAMPING / (m + 12.0) for m in mass1]
-        mass2 = self.sum_2(mass1)
-        weight2 = DAMPING / (mass2 + 24.0)
-        out = []
-        for r in r1:
-            e = [weight1[x] * r[x] for x in range(2)]
-            g = self.apply_1(e, mass1)
-            e2 = self.solve_2(self.sum_2([r[x] - g[x] for x in range(2)]), mass2, weight2)
-            e = [e[x] + e2 for x in range(2)]
-            g = self.apply_1(e, mass1)
-            out.append([e[x] + weight1[x] * (r[x] - g[x]) for x in range(2)])
-        return out
 
 
 def pack_y(cells, x, shifts):
@@ -223,10 +204,15 @@
         slot_ref[row + m] = column[m : m + 1]
 
 
-def fine_level(r, f1, mass0, weight0, place, shifts):
-    e0 = memo(lambda x, y: weight0(x, y) * r(x, y) + f1(x // 2, y // 2))
-    g0 = grid_apply(e0, mass0, 1.0, shifts, 1)
-    return memo(lambda x, y: place.keep(e0(x, y) + weight0(x, y) * (r(x, y) - g0(x, y)), x, y, BRICK))
+def fine_level(r, f1, weight0, place, shifts):
+    first = memo(lambda x, y: weight0(x, y) * r(x, y))
+    e0 = memo(lambda x, y: first(x, y) + f1(x // 2, y // 2))
+
+    def at(x, y):
+        value = KEPT * e0(x, y) + first(x, y) + weight0(x, y) * beside_all(e0, x, y, shifts, 1)
+        return place.keep(value, x, y, BRICK)
+
+    return memo(at)
 
 
 def stiffness_apply(z, hot, x_ref, effective_ref, grad_ref, nodes, forces, picked, spread_sums, shifts):
@@ -398,7 +384,7 @@
     weight0 = memo(lambda x, y: weight_of(mass0(x, y)))
     r = memo(lambda x, y: own[x, y] * live)
     cells = [(x, y) for x in (0, 1) for y in range(-1, 3)] + [(x, y) for x in (-1, 2) for y in (0, 1)]
-    part = contribution(r, mass0, weight0, INNER, cells, shifts)
+    part = contribution(r, weight0, INNER, cells, shifts)
     for x in (0, 1):
         for k, column in enumerate(pack_y(part, x, shifts)):
             put_rows(slot_ref, 6 * x + 3 * k, column)
@@ -465,26 +451,52 @@
 
 def cycle_and_apply(place, shifts, levels, r, r1, mass1, fields, particles, scratch):
     mass0, weight0 = fields
-    coarse, *work = scratch
-    margin = 8 * (place.count_y + 1)
+    middle, coarse, *work = scratch
+    width = place.count_x
+    margin = 8 * (width + 1)
+
+    def put(ref, row, value):
+        for y in range(place.count_y):
+            ref[pl.ds(margin + 8 * width * y + row, width, stride=8), :] = value[y]
+
+    def get(ref, x, y):
+        brick = (place.gy + y) * width + place.gx + x
+        return ref[pl.ds(pl.multiple_of(margin + brick * 8, 8), 8), :]
+
+    weight1 = [DAMPING / (m + 12.0) for m in mass1]
+    weight2 = DAMPING / (levels.quad_sum(mass1[0] + mass1[1]) + 24.0)
+    middle[...] = jnp.zeros_like(middle)
     coarse[...] = jnp.zeros_like(coarse)
-    for m, pair in enumerate(levels.solve(r1, mass1)):
+    for x in range(2):
+        put(middle, 4 * x + 3, weight1[x])
+    for m in range(3):
+        e = [weight1[x] * r1[m][x] for x in range(2)]
         for x in range(2):
-            coarse[pl.ds(margin + 4 * x + m, levels.rows, stride=8), :] = pair[x]
-
-    def neighbour(x, y):
-        brick = (place.gx + x) * place.count_y + place.gy + y
-        rows = coarse[pl.ds(pl.multiple_of(margin + brick * 8, 8), 8), :]
+            put(middle, 4 * x + m, e[x])
+        put(coarse, m, levels.solve_2(levels.restrict(r1[m], e), weight2))
+
+    def brick_at(x, y):
+        rows = get(middle, x, y)
         first, second = rows * shifts.even, rows * shifts.odd
         return first + turn(first, 1), second + turn(second, -1)
 
-    neighbour = memo(neighbour)
+    brick_at = memo(brick_at)
+
+    def first_at(x, y):
+        both = brick_at(x // 2, y // 2)[y % 2]
+        return place.keep(both[4 * (x % 2) : 4 * (x % 2) + 4], x, y, 2)
+
+    first = memo(first_at)
+    e2 = memo(lambda x, y: place.keep(get(coarse, x, y)[0:4], x, y, 1))
+    e1 = memo(lambda x, y: first(x, y) + e2(x // 2, y // 2))
+    live = live_rows()
 
     def f1_at(x, y):
-        both = neighbour(x // 2, y // 2)[y % 2]
-        return place.keep(both[4 * (x % 2) : 4 * (x % 2) + 4], x, y, 2)
-
-    z = fine_level(r, memo(f1_at), mass0, weight0, place, shifts)
+        weight = 2.0 * spread_mass(first(x, y))
+        value = KEPT * e1(x, y) + first(x, y) + weight * beside_all(e1, x, y, shifts, 2)
+        return place.keep(value * live, x, y, 2)
+
+    z = fine_level(r, memo(f1_at), weight0, place, shifts)
     image = stiffness_apply(z, *particles, *work, shifts)
     for x, y in INNER:
         image[x, y] = image[x, y] + mass0(x, y) * z(x, y)
@@ -516,7 +528,7 @@
     particles = (hot_ref, x_ref, effective_ref, grad_ref)
     place, shifts = Place(*counts), Shifts()
     levels = Levels(*counts, shifts)
-    rows = lambda q: level_ref[pl.ds(q, levels.rows, stride=FIRST_ROWS), :]
+    rows = lambda q: levels.load(level_ref, q, FIRST_ROWS)
     r1 = []
     for m in range(3):
         pair = [levels.gather_y(rows(6 * x + m), rows(6 * x + 3 + m)) for x in range(2)]
@@ -536,55 +548,54 @@
     for x, y in RIMMED:
         image_ref[x + 1, y + 1] = image[x, y]
     clear_tail(even_ref, odd_ref)
-    for k, (x, y) in enumerate(SIDE_X_IMAGE):
-        put_sides(even_ref, odd_ref, 3 * k, 3, image[x + 4, y], image[-1 - x, y], place.even_x)
+    for k, (x, y) in enumerate(SIDE_Y_IMAGE):
+        put_sides(even_ref, odd_ref, 3 * k, 3, image[x, y + 4], image[x, -1 - y], place.even_y)
     rz = total_of((r(x, y), z(x, y)) for x, y in INNER)
     zaz = total_of((image[x, y], z(x, y)) for x, y in RIMMED)
     dots_ref[...] = dots_row(rz, zaz)
 
 
-def along_x_kernel(counts, image_ref, even_ref, odd_ref, mass0_ref, weight0_ref, dots_ref,
-                   wide_ref, to_even_ref, to_odd_ref, slot_ref):
+def along_y_kernel(counts, image_ref, even_ref, odd_ref, weight0_ref, dots_ref,
+                   long_ref, to_even_ref, to_odd_ref, slot_ref):
     place, shifts = Place(*counts), Shifts()
-    left, right = side_parts(even_ref, odd_ref, place.even_x, place.in_x[-1], place.in_x[1])
+    below, above = side_parts(even_ref, odd_ref, place.even_y, place.in_y[-1], place.in_y[1])
 
     def value(x, y):
         total = None
-        if -1 <= x <= 4:
+        if -1 <= y <= 4:
             total = place.keep(image_ref[x + 1, y + 1], x, y, BRICK)
-        for part, key in ((left, (x, y)), (right, mirror_x(x, y))):
-            if key in SIDE_X_IMAGE:
-                more = place.keep(part(3 * SIDE_X_IMAGE.index(key), 4), 0, y, BRICK)
+        for part, key in ((below, (x, y)), (above, mirror(x, y))):
+            if key in SIDE_Y_IMAGE:
+                more = place.keep(part(3 * SIDE_Y_IMAGE.index(key), 4), x, 0, BRICK)
                 total = more if total is None else total + more
         return total
 
     value = memo(value)
+    cells = [(x, y) for x in range(-1, 3) for y in (0, 1)]
+    part = contribution(value, reader(weight0_ref, 2), RIMMED, cells, shifts)
+    for x in range(-1, 3):
+        put_rows(slot_ref, 3 * (x + 1), part[x, 0] * shifts.even + part[x, 1] * shifts.odd)
+    slot_ref[12] = dots_ref[...]
     clear_tail(to_even_ref, to_odd_ref)
-    for k, (x, y) in enumerate(SIDE_IMAGE):
-        put_sides(to_even_ref, to_odd_ref, 3 * k, 3, value(x, y + 4), value(x, -1 - y), place.even_y)
-    for x in range(-2, 6):
-        for y in range(-1, BRICK + 1):
-            wide_ref[x + 2, y + 1] = value(x, y)
-    cells = [(x, y) for x in (0, 1) for y in range(-1, 3)]
-    part = contribution(value, reader(mass0_ref, 2), reader(weight0_ref, 2), RIMMED, cells, shifts)
-    for x in (0, 1):
-        for k, column in enumerate(pack_y(part, x, shifts)):
-            put_rows(slot_ref, 6 * x + 3 * k, column)
-    slot_ref[12] = dots_ref[...]
-
-
-def middle_kernel(counts, wide_ref, even_ref, odd_ref, w_ref):
+    for k, (x, y) in enumerate(SIDE_X_IMAGE):
+        put_sides(to_even_ref, to_odd_ref, 3 * k, 3, value(x + 4, y), value(-1 - x, y), place.even_x)
+    for x in range(-1, BRICK + 1):
+        for y in range(-2, 6):
+            long_ref[x + 1, y + 2] = value(x, y)
+
+
+def middle_kernel(counts, long_ref, even_ref, odd_ref, w_ref):
     place = Place(*counts)
-    below, above = side_parts(even_ref, odd_ref, place.even_y, place.in_y[-1], place.in_y[1])
+    left, right = side_parts(even_ref, odd_ref, place.even_x, place.in_x[-1], place.in_x[1])
     live = live_rows()
     for x in range(-2, 6):
         for y in range(-2, 6):
             total = jnp.zeros((4, LANES), F32)
-            if -1 <= y <= 4:
-                total = total + wide_ref[x + 2, y + 1]
-            for part, key in ((below, (x, y)), (above, mirror(x, y))):
-                if key in SIDE_IMAGE:
-                    total = total + part(3 * SIDE_IMAGE.index(key), 4)
+            if -1 <= x <= 4:
+                total = total + long_ref[x + 1, y + 2]
+            for part, key in ((left, (x, y)), (right, mirror_x(x, y))):
+                if key in SIDE_X_IMAGE:
+                    total = total + part(3 * SIDE_X_IMAGE.index(key), 4)
             w_ref[x + 2, y + 2] = total * live
 
 
@@ -602,10 +613,12 @@
     sums = sums_of(change_ref, bricks, 12, SECOND_ROWS)
     step = sums[:, 0:1] / sums[:, 1:2]
     r = memo(lambda x, y: r_ref[x + 2, y + 2] - step * w_ref[x + 2, y + 2])
-    rows = lambda q: change_ref[pl.ds(q, bricks, stride=SECOND_ROWS), :]
-    r1 = [
-        [r1_ref[m, x] - step * levels.gather_y(rows(6 * x + m), rows(6 * x + 3 + m)) for x in range(2)] for m in range(3)
-    ]
+    rows = lambda q: levels.load(change_ref, q, SECOND_ROWS)
+    r1 = []
+    for m in range(3):
+        low = rows(3 + m) + levels.below_x(rows(9 + m))
+        high = rows(6 + m) + levels.above_x(rows(m))
+        r1.append([r1_ref[m, 0] - step * low, r1_ref[m, 1] - step * high])
     fields = (reader(mass0_ref, 2), reader(weight0_ref, 2))
     mass1 = [mass1_ref[0], mass1_ref[1]]
     z, image = cycle_and_apply(place, shifts, levels, r, r1, mass1, fields, particles, scratch)
@@ -690,11 +703,12 @@
 def per_device(counts, right_side, node_mass, gradients, stiffness, valid, node_base):
     bricks = counts[0] * counts[1]
     blocks = gradients.shape[2]
+    grid = (counts[1], counts[0], LANES)
     tiles = 9 * (BRICK + 2) * 8
     depth = BRICK * LANES
     width = blocks * LANES
     scratch = (
-        pltpu.VMEM((8 * (bricks + 2 * (counts[1] + 1)), LANES), F32),
+        *[pltpu.VMEM((8 * (bricks + 2 * (counts[0] + 1)), LANES), F32)] * 2,
         pltpu.VMEM((tiles, depth), jnp.bfloat16),
         pltpu.VMEM((tiles, width), jnp.bfloat16),
         pltpu.VMEM((tiles, width), F32),
@@ -724,20 +738,20 @@
     particles = (*prepared, gradients[0, 0].transpose(1, 2, 0, 3))
     r, *fields = call(start_kernel, counts, [block(8, 8)] * 3, wide, even, odd)
 
-    side = rows(SIDE_X_IMAGE)
+    side = rows(SIDE_Y_IMAGE)
     z1, image, to_even, to_odd, dots, r1, mass1 = call(
         first_kernel, counts,
-        [block(4, 4), block(6, 6), side, side, (1, LANES), (3, 2, bricks, LANES), (2, bricks, LANES)],
+        [block(4, 4), block(6, 6), side, side, (1, LANES), (3, 2, *grid), (2, *grid)],
         level, r, *fields, *particles, scratch=scratch,
     )
+    even, odd = exchange(to_even, to_odd, "gy", counts)
+    side = rows(SIDE_X_IMAGE)
+    long, to_even, to_odd, slot = call(
+        along_y_kernel, counts, [block(6, 8), side, side, (SECOND_ROWS, 1, LANES)], image, even, odd, fields[1], dots
+    )
+    change = share(slot)
     even, odd = exchange(to_even, to_odd, "gx", counts)
-    side = rows(SIDE_IMAGE)
-    wide, to_even, to_odd, slot = call(
-        along_x_kernel, counts, [block(8, 6), side, side, (SECOND_ROWS, 1, LANES)], image, even, odd, *fields, dots
-    )
-    change = share(slot)
-    even, odd = exchange(to_even, to_odd, "gy", counts)
-    (w,) = call(middle_kernel, counts, [block(8, 8)], wide, even, odd)
+    (w,) = call(middle_kernel, counts, [block(8, 8)], long, even, odd)
     side = (2 * 8, LANES)
     z2, image, x_even, x_odd, y_even, y_odd, slots = call(
         second_kernel, counts, [block(4, 4), block(4, 4), side, side, side, side, (bricks, 4, 1, LANES)],

time: 58.1 us -> 57.8 us (level)
  starting transfers between devices: 25.6 us -> 26.2 us
    ppermute x12, waiting for transfers between devices: 14.4 us -> 13.2 us  [exchange(): return (lax.ppermute(first, AXES, even), lax.ppermute(second, AXES, odd))]
    all_to_all x2, waiting for transfers between devices: 3.73 us -> 4.58 us  [share(): lax.all_to_all(sent, AXES, 0, 0).reshape(bricks * slot.shape[0], LANES)]
where the time goes in v7:
time: 57.8 us; the launch traced here: 57.5 us
  starting transfers between devices  26.2 us (45%)
  waiting for transfers between devices  19.7 us (34%)
  Pallas kernels  8.26 us (14%)
  local copies, waits for them, and re-layouts  1.75 us (3%)
  other arithmetic  0.76 us (1%)
  between operations  0.73 us (1%)
    ppermute x12, waiting for transfers between devices, exchange(): return (lax.ppermute(first, AXES, even), lax.ppermute(second, AXES, odd))  13.2 us
    ppermute x12, starting transfers between devices, exchange(): return (lax.ppermute(first, AXES, even), lax.ppermute(second, AXES, odd))  12.2 us
    all_to_all x2, starting transfers between devices, share(): lax.all_to_all(sent, AXES, 0, 0).reshape(bricks * slot.shape[0], LANES)  11.4 us
    pallas_call x9, Pallas kernels, call(): pl.pallas_call(functools.partial(kernel, counts), out_shape=[jax.ShapeDty...  8.26 us
    all_to_all x2, waiting for transfers between devices, share(): lax.all_to_all(sent, AXES, 0, 0).reshape(bricks * slot.shape[0], LANES)  4.58 us
    all_to_all x1, starting transfers between devices, per_device(): slots = lax.all_to_all(slots, AXES, 0, 0)  2.57 us
    all_to_all x1, waiting for transfers between devices, per_device(): slots = lax.all_to_all(slots, AXES, 0, 0)  2 us
    broadcast_in_dim x2, local copies, waits for them, and re-layouts, share(): sent = jnp.broadcast_to(slot[None], (bricks, *slot.shape))  1.72 us
  transfers between devices with their start and end apart: 15, of which 9 were waited for; matrix products, arithmetic and copies ran while one was open for 0% of the time, Pallas kernels for 1%

profile of v7, /device:TPU:0, one launch (start us, length us, event | category | flops | bytes accessed | tf_op | source)
XLA Modules:
  0.0 57.5 jit_solution(2526809710934830877)
XLA Ops:
  0.6 0.8 %pad_maximum_fusion.fields_ref = f32[4,4,4,128]{3,2,1,0:T(4,128)S(1)} fusion(f32[1,4,4,128]{3,2,1,0:T(4,128)} %bitcast.25, f32[3,4,4,128]{3,2,1,0:T(4,128)} %param.6), kind=kLoop, calls=%fused_computation | loop fusion | flops 8192 | bytes 65536 | tf_op jit(solution)/shard_map/concatenate | solution.py:724
  1.7 0.9 %broadcast_in_dim.21 = f32[32,20,1,128]{3,2,1,0:T(1,128)} broadcast(f32[20,128]{1,0:T(8,128)S(1)} %bitcast.23), dimensions={1,3} | broadcast | bytes 337920 | tf_op jit(solution)/shard_map/broadcast_in_dim | solution.py:721
  2.6 7.3 %all-to-all-start = ((f32[32,20,1,128]{3,2,1,0:T(1,128)}), f32[32,20,1,128]{3,2,1,0:T(1,128)S(1)}, u32[]{:S(2)}, u32[]{:S(2)}) async-start(f32[32,20,1,128]{3,2,1,0:T(1,128)} %broadcast_in_dim.21), calls=%async_computation | async-start | bytes 655360 | tf_op jit(solution)/shard_map/all_to_all | solution.py:722
  10.2 1.7 %collective-permute-start.1 = (f32[8,4,128]{2,1,0:T(4,128)S(1)}, f32[8,4,128]{2,1,0:T(4,128)S(1)}, u32[]{:S(2)}, u32[]{:S(2)}) collective-permute-start(f32[8,4,128]{2,1,0:T(4,128)S(1)} %get-tuple-element.36), channel_id=1, source_target_pairs={{0,1},{1,0},{2,3},{3,2},{4,8},{5,9},{6,10},{7,11},{8,4},{9,5},{10,... | collective-permute-start | bytes 49160 | tf_op jit(solution)/shard_map/ppermute | solution.py:39
  11.9 4.2 %collective-permute-done.1.odd_ref = f32[8,4,128]{2,1,0:T(4,128)S(1)} collective-permute-done((f32[8,4,128]{2,1,0:T(4,128)S(1)}, f32[8,4,128]{2,1,0:T(4,128)S(1)}, u32[]{:S(2)}, u32[]{:S(2)}) %collective-permute-start.1) | collective-permute-done | bytes 16416 | tf_op jit(solution)/shard_map/ppermute | solution.py:39
  16.1 2.5 %collective-permute-start.2 = (f32[14,4,128]{2,1,0:T(4,128)S(1)}, f32[14,4,128]{2,1,0:T(4,128)S(1)}, u32[]{:S(2)}, u32[]{:S(2)}) collective-permute-start(f32[14,4,128]{2,1,0:T(4,128)S(1)} %get-tuple-element.38), channel_id=1, source_target_pairs={{0,1},{1,0},{2,3},{3,2},{4,5},{5,4},{6,7},{7,6},{8,9},{9,8},{10,11... | collective-permute-start | bytes 86024 | tf_op jit(solution)/shard_map/ppermute | solution.py:39
  19.0 1.6 %collective-permute-done.2.even_ref = f32[14,4,128]{2,1,0:T(4,128)S(1)} collective-permute-done((f32[14,4,128]{2,1,0:T(4,128)S(1)}, f32[14,4,128]{2,1,0:T(4,128)S(1)}, u32[]{:S(2)}, u32[]{:S(2)}) %collective-permute-start.2) | collective-permute-done | bytes 28704 | tf_op jit(solution)/shard_map/ppermute | solution.py:39
  20.9 2.8 %shard_map.81 = (f32[4,4,4,128]{3,2,1,0:T(4,128)S(1)}, f32[6,6,4,128]{3,2,1,0:T(4,128)S(1)}, f32[56,128]{1,0:T(8,128)S(1)}, f32[56,128]{1,0:T(8,128)S(1)}, f32[1...) custom-call(f32[640,128]{1,0:T(8,128)S(1)} %bitcast.19, ...), custom_call_target="tpu_custom_call" | custom-call | tf_op jit(solution)/shard_map/pallas_call | solution.py:695
  23.6 2.5 %collective-permute-start.4 = (f32[56,128]{1,0:T(8,128)S(1)}, f32[56,128]{1,0:T(8,128)S(1)}, u32[]{:S(2)}, u32[]{:S(2)}) collective-permute-start(f32[56,128]{1,0:T(8,128)S(1)} %get-tuple-element.47), channel_id=1, source_target_pairs={{0,1},{1,0},{2,3},{3,2},{4,5},{5,4},{6,7},{7,6},{8,9},{9,8},{10,11... | collective-permute-start | bytes 86024 | tf_op jit(solution)/shard_map/ppermute | solution.py:39
  26.1 1.8 %collective-permute-done.4.even_ref = f32[56,128]{1,0:T(8,128)S(1)} collective-permute-done((f32[56,128]{1,0:T(8,128)S(1)}, f32[56,128]{1,0:T(8,128)S(1)}, u32[]{:S(2)}, u32[]{:S(2)}) %collective-permute-start.4) | collective-permute-done | bytes 28704 | tf_op jit(solution)/shard_map/ppermute | solution.py:39
  28.3 0.8 %broadcast_in_dim.23 = f32[32,13,1,128]{3,2,1,0:T(1,128)} broadcast(f32[13,128]{1,0:T(8,128)S(1)} %bitcast.24), dimensions={1,3} | broadcast | bytes 219648 | tf_op jit(solution)/shard_map/broadcast_in_dim | solution.py:721
  29.1 4.1 %all-to-all-start.1 = ((f32[32,13,1,128]{3,2,1,0:T(1,128)}), f32[32,13,1,128]{3,2,1,0:T(1,128)S(1)}, u32[]{:S(2)}, u32[]{:S(2)}) async-start(f32[32,13,1,128]{3,2,1,0:T(1,128)} %broadcast_in_dim.23), calls=%async_computation.1 | async-start | bytes 425984 | tf_op jit(solution)/shard_map/all_to_all | solution.py:722
  33.2 0.3 collective-permute-start.6
  33.5 1.7 %collective-permute-start.7 = (f32[72,128]{1,0:T(8,128)S(1)}, f32[72,128]{1,0:T(8,128)S(1)}, u32[]{:S(2)}, u32[]{:S(2)}) collective-permute-start(f32[72,128]{1,0:T(8,128)S(1)} %get-tuple-element.55), channel_id=1, source_target_pairs={{0,1},{1,0},{2,3},{3,2},{4,8},{5,9},{6,10},{7,11},{8,4},{9,5},{10,... | collective-permute-start | bytes 110600 | tf_op jit(solution)/shard_map/ppermute | solution.py:39
  35.2 3.1 %collective-permute-done.7.odd_ref = f32[72,128]{1,0:T(8,128)S(1)} collective-permute-done((f32[72,128]{1,0:T(8,128)S(1)}, f32[72,128]{1,0:T(8,128)S(1)}, u32[]{:S(2)}, u32[]{:S(2)}) %collective-permute-start.7) | collective-permute-done | bytes 36896 | tf_op jit(solution)/shard_map/ppermute | solution.py:39
  38.4 4.4 %all-to-all-done.1 = f32[32,13,1,128]{3,2,1,0:T(1,128)S(1)} async-done(((f32[32,13,1,128]{3,2,1,0:T(1,128)}), f32[32,13,1,128]{3,2,1,0:T(1,128)S(1)}, u32[]{:S(2)}, u32[]{:S(2)}) %all-to-all-start.1) | async-done | bytes 213024 | tf_op jit(solution)/shard_map/all_to_all | solution.py:722
  42.8 3.6 %shard_map.84 = (f32[4,4,4,128]{3,2,1,0:T(4,128)S(1)}, f32[4,4,4,128]{3,2,1,0:T(4,128)S(1)}, f32[16,128]{1,0:T(8,128)S(1)}, f32[16,128]{1,0:T(8,128)S(1)}, f32[1...) custom-call(f32[416,128]{1,0:T(8,128)S(1)} %bitcast.15, ...), custom_call_target="tpu_custom_call" | custom-call | tf_op jit(solution)/shard_map/pallas_call | solution.py:695
  46.4 2.6 %all-to-all-start.2 = ((f32[32,4,1,128]{3,2,1,0:T(1,128)}), f32[32,4,1,128]{3,2,1,0:T(1,128)S(1)}, u32[]{:S(2)}, u32[]{:S(2)}) async-start(f32[32,4,1,128]{3,2,1,0:T(1,128)} %get-tuple-element.56), calls=%async_computation.2 | async-start | bytes 131072 | tf_op jit(solution)/shard_map/all_to_all | solution.py:761
  49.1 1.7 %collective-permute-start.9 = (f32[16,128]{1,0:T(8,128)S(1)}, f32[16,128]{1,0:T(8,128)S(1)}, u32[]{:S(2)}, u32[]{:S(2)}) collective-permute-start(f32[16,128]{1,0:T(8,128)S(1)} %get-tuple-element.58), channel_id=1, source_target_pairs={{0,1},{1,0},{2,3},{3,2},{4,8},{5,9},{6,10},{7,11},{8,4},{9,5},{10,... | collective-permute-start | bytes 24584 | tf_op jit(solution)/shard_map/ppermute | solution.py:39
  51.2 1.0 %collective-permute-start.11 = (f32[16,128]{1,0:T(8,128)S(1)}, f32[16,128]{1,0:T(8,128)S(1)}, u32[]{:S(2)}, u32[]{:S(2)}) collective-permute-start(f32[16,128]{1,0:T(8,128)S(1)} %get-tuple-element.60), channel_id=1, source_target_pairs={{0,4},{1,2},{2,1},{3,7},{4,0},{5,6},{6,5},{7,3},{8,12},{9,10},{10,... | collective-permute-start | bytes 24584 | tf_op jit(solution)/shard_map/ppermute | solution.py:39
  52.2 0.6 %collective-permute-done.9.x_odd_ref = f32[16,128]{1,0:T(8,128)S(1)} collective-permute-done((f32[16,128]{1,0:T(8,128)S(1)}, f32[16,128]{1,0:T(8,128)S(1)}, u32[]{:S(2)}, u32[]{:S(2)}) %collective-permute-start.9) | collective-permute-done | bytes 8224 | tf_op jit(solution)/shard_map/ppermute | solution.py:39
  52.8 1.7 %collective-permute-done.10.y_even_ref = f32[16,128]{1,0:T(8,128)S(1)} collective-permute-done((f32[16,128]{1,0:T(8,128)S(1)}, f32[16,128]{1,0:T(8,128)S(1)}, u32[]{:S(2)}, u32[]{:S(2)}) %collective-permute-start.10) | collective-permute-done | bytes 8224 | tf_op jit(solution)/shard_map/ppermute | solution.py:39
  54.5 2.0 %all-to-all-done.2.slots_ref = f32[32,4,1,128]{3,2,1,0:T(1,128)S(1)} async-done(((f32[32,4,1,128]{3,2,1,0:T(1,128)}), f32[32,4,1,128]{3,2,1,0:T(1,128)S(1)}, u32[]{:S(2)}, u32[]{:S(2)}) %all-to-all-start.2) | async-done | bytes 65568 | tf_op jit(solution)/shard_map/all_to_all | solution.py:761
  56.5 0.9 %shard_map.85 = (f32[3,4,4,128]{3,2,1,0:T(4,128)}, f32[3,4,4,128]{3,2,1,0:T(4,128)}) custom-call(f32[32,4,1,128]{3,2,1,0:T(1,128)S(1)} %all-to-all-done.2.slots_ref, f32[16,128]{1,0:T(8,128)S(1)} %collective-permute-done.8.x_even_ref, f32[16,128]{1,0:T(8,128)S(1)} %collective-permute-done.9.x_odd_ref, f32[16,128]{1,0:T(8,128)S(1)} %collective-permute-done.10.y_even_ref, ...), custom_call_target="tpu_custom_call" | custom-call | tf_op jit(solution)/shard_map/pallas_call | solution.py:695
  (28 shorter events, 2.0 us)
Async XLA Ops:
  2.6 18.3 %copy-start = (f32[1,1,8,3,27,128]{5,2,4,3,1,0:T(8,128)S(1)}, f32[1,1,8,3,27,128]{5,2,4,3,1,0:T(8,128)}, u32[]{:S(2)}) copy-start(f32[1,1,8,3,27,128]{5,2,4,3,1,0:T(8,128)} %param.8) | copy-start | bytes 995332
  2.6 18.3 %all-to-all-start = ((f32[32,20,1,128]{3,2,1,0:T(1,128)}), f32[32,20,1,128]{3,2,1,0:T(1,128)S(1)}, u32[]{:S(2)}, u32[]{:S(2)}) async-start(f32[32,20,1,128]{3,2,1,0:T(1,128)} %broadcast_in_dim.21), calls=%async_computation | async-start | bytes 655360 | tf_op jit(solution)/shard_map/all_to_all | solution.py:722
  9.9 2.0 %collective-permute-start = (f32[8,4,128]{2,1,0:T(4,128)S(1)}, f32[8,4,128]{2,1,0:T(4,128)S(1)}, u32[]{:S(2)}, u32[]{:S(2)}) collective-permute-start(f32[8,4,128]{2,1,0:T(4,128)S(1)} %get-tuple-element.35), channel_id=1, source_target_pairs={{0,4},{1,5},{2,6},{3,7},{4,0},{5,1},{6,2},{7,3},{8,12},{9,13},{10,... | collective-permute-start | bytes 49160 | tf_op jit(solution)/shard_map/ppermute | solution.py:39
  10.2 5.9 %collective-permute-start.1 = (f32[8,4,128]{2,1,0:T(4,128)S(1)}, f32[8,4,128]{2,1,0:T(4,128)S(1)}, u32[]{:S(2)}, u32[]{:S(2)}) collective-permute-start(f32[8,4,128]{2,1,0:T(4,128)S(1)} %get-tuple-element.36), channel_id=1, source_target_pairs={{0,1},{1,0},{2,3},{3,2},{4,8},{5,9},{6,10},{7,11},{8,4},{9,5},{10,... | collective-permute-start | bytes 49160 | tf_op jit(solution)/shard_map/ppermute | solution.py:39
  16.1 2.6 %copy-start.3 = (s32[1,1,8,128]{3,2,1,0:T(8,128)S(1)}, s32[1,1,8,128]{3,2,1,0:T(8,128)}, u32[]{:S(2)}) copy-start(s32[1,1,8,128]{3,2,1,0:T(8,128)} %param.10) | copy-start | bytes 12292
  16.1 2.6 %copy-start.2 = (f32[1,1,8,128]{3,2,1,0:T(8,128)S(1)}, f32[1,1,8,128]{3,2,1,0:T(8,128)}, u32[]{:S(2)}) copy-start(f32[1,1,8,128]{3,2,1,0:T(8,128)} %param.9) | copy-start | bytes 12292
  16.1 2.6 %copy-start.1 = (s32[1,1,8,128]{3,2,1,0:T(8,128)S(1)}, s32[1,1,8,128]{3,2,1,0:T(8,128)}, u32[]{:S(2)}) copy-start(s32[1,1,8,128]{3,2,1,0:T(8,128)} %param.11) | copy-start | bytes 12292
  16.1 4.5 %collective-permute-start.2 = (f32[14,4,128]{2,1,0:T(4,128)S(1)}, f32[14,4,128]{2,1,0:T(4,128)S(1)}, u32[]{:S(2)}, u32[]{:S(2)}) collective-permute-start(f32[14,4,128]{2,1,0:T(4,128)S(1)} %get-tuple-element.38), channel_id=1, source_target_pairs={{0,1},{1,0},{2,3},{3,2},{4,5},{5,4},{6,7},{7,6},{8,9},{9,8},{10,11... | collective-permute-start | bytes 86024 | tf_op jit(solution)/shard_map/ppermute | solution.py:39
  18.7 2.0 %collective-permute-start.3 = (f32[14,4,128]{2,1,0:T(4,128)S(1)}, f32[14,4,128]{2,1,0:T(4,128)S(1)}, u32[]{:S(2)}, u32[]{:S(2)}) collective-permute-start(f32[14,4,128]{2,1,0:T(4,128)S(1)} %get-tuple-element.39), channel_id=1, source_target_pairs={{0,4},{1,2},{2,1},{3,7},{4,0},{5,6},{6,5},{7,3},{8,12},{9,10},{10,... | collective-permute-start | bytes 86024 | tf_op jit(solution)/shard_map/ppermute | solution.py:39
  23.6 4.4 %collective-permute-start.4 = (f32[56,128]{1,0:T(8,128)S(1)}, f32[56,128]{1,0:T(8,128)S(1)}, u32[]{:S(2)}, u32[]{:S(2)}) collective-permute-start(f32[56,128]{1,0:T(8,128)S(1)} %get-tuple-element.47), channel_id=1, source_target_pairs={{0,1},{1,0},{2,3},{3,2},{4,5},{5,4},{6,7},{7,6},{8,9},{9,8},{10,11... | collective-permute-start | bytes 86024 | tf_op jit(solution)/shard_map/ppermute | solution.py:39
  26.1 1.9 %collective-permute-start.5 = (f32[56,128]{1,0:T(8,128)S(1)}, f32[56,128]{1,0:T(8,128)S(1)}, u32[]{:S(2)}, u32[]{:S(2)}) collective-permute-start(f32[56,128]{1,0:T(8,128)S(1)} %get-tuple-element.48), channel_id=1, source_target_pairs={{0,4},{1,2},{2,1},{3,7},{4,0},{5,6},{6,5},{7,3},{8,12},{9,10},{10,... | collective-permute-start | bytes 86024 | tf_op jit(solution)/shard_map/ppermute | solution.py:39
  29.1 13.7 %all-to-all-start.1 = ((f32[32,13,1,128]{3,2,1,0:T(1,128)}), f32[32,13,1,128]{3,2,1,0:T(1,128)S(1)}, u32[]{:S(2)}, u32[]{:S(2)}) async-start(f32[32,13,1,128]{3,2,1,0:T(1,128)} %broadcast_in_dim.23), calls=%async_computation.1 | async-start | bytes 425984 | tf_op jit(solution)/shard_map/all_to_all | solution.py:722
  33.2 2.0 %collective-permute-start.6 = (f32[72,128]{1,0:T(8,128)S(1)}, f32[72,128]{1,0:T(8,128)S(1)}, u32[]{:S(2)}, u32[]{:S(2)}) collective-permute-start(f32[72,128]{1,0:T(8,128)S(1)} %get-tuple-element.54), channel_id=1, source_target_pairs={{0,4},{1,5},{2,6},{3,7},{4,0},{5,1},{6,2},{7,3},{8,12},{9,13},{10,... | collective-permute-start | bytes 110600 | tf_op jit(solution)/shard_map/ppermute | solution.py:39
  33.5 4.8 %collective-permute-start.7 = (f32[72,128]{1,0:T(8,128)S(1)}, f32[72,128]{1,0:T(8,128)S(1)}, u32[]{:S(2)}, u32[]{:S(2)}) collective-permute-start(f32[72,128]{1,0:T(8,128)S(1)} %get-tuple-element.55), channel_id=1, source_target_pairs={{0,1},{1,0},{2,3},{3,2},{4,8},{5,9},{6,10},{7,11},{8,4},{9,5},{10,... | collective-permute-start | bytes 110600 | tf_op jit(solution)/shard_map/ppermute | solution.py:39
  46.4 10.2 %all-to-all-start.2 = ((f32[32,4,1,128]{3,2,1,0:T(1,128)}), f32[32,4,1,128]{3,2,1,0:T(1,128)S(1)}, u32[]{:S(2)}, u32[]{:S(2)}) async-start(f32[32,4,1,128]{3,2,1,0:T(1,128)} %get-tuple-element.56), calls=%async_computation.2 | async-start | bytes 131072 | tf_op jit(solution)/shard_map/all_to_all | solution.py:761
  49.0 3.2 %collective-permute-start.8 = (f32[16,128]{1,0:T(8,128)S(1)}, f32[16,128]{1,0:T(8,128)S(1)}, u32[]{:S(2)}, u32[]{:S(2)}) collective-permute-start(f32[16,128]{1,0:T(8,128)S(1)} %get-tuple-element.57), channel_id=1, source_target_pairs={{0,4},{1,5},{2,6},{3,7},{4,0},{5,1},{6,2},{7,3},{8,12},{9,13},{10,... | collective-permute-start | bytes 24584 | tf_op jit(solution)/shard_map/ppermute | solution.py:39
  49.1 3.7 %collective-permute-start.9 = (f32[16,128]{1,0:T(8,128)S(1)}, f32[16,128]{1,0:T(8,128)S(1)}, u32[]{:S(2)}, u32[]{:S(2)}) collective-permute-start(f32[16,128]{1,0:T(8,128)S(1)} %get-tuple-element.58), channel_id=1, source_target_pairs={{0,1},{1,0},{2,3},{3,2},{4,8},{5,9},{6,10},{7,11},{8,4},{9,5},{10,... | collective-permute-start | bytes 24584 | tf_op jit(solution)/shard_map/ppermute | solution.py:39
  50.9 3.7 %collective-permute-start.10 = (f32[16,128]{1,0:T(8,128)S(1)}, f32[16,128]{1,0:T(8,128)S(1)}, u32[]{:S(2)}, u32[]{:S(2)}) collective-permute-start(f32[16,128]{1,0:T(8,128)S(1)} %get-tuple-element.59), channel_id=1, source_target_pairs={{0,1},{1,0},{2,3},{3,2},{4,5},{5,4},{6,7},{7,6},{8,9},{9,8},{10,11... | collective-permute-start | bytes 24584 | tf_op jit(solution)/shard_map/ppermute | solution.py:39
  51.2 3.4 %collective-permute-start.11 = (f32[16,128]{1,0:T(8,128)S(1)}, f32[16,128]{1,0:T(8,128)S(1)}, u32[]{:S(2)}, u32[]{:S(2)}) collective-permute-start(f32[16,128]{1,0:T(8,128)S(1)} %get-tuple-element.60), channel_id=1, source_target_pairs={{0,4},{1,2},{2,1},{3,7},{4,0},{5,6},{6,5},{7,3},{8,12},{9,10},{10,... | collective-permute-start | bytes 24584 | tf_op jit(solution)/shard_map/ppermute | solution.py:39

commit v8 on v7

--- a/solution.py
+++ b/solution.py
@@ -215,7 +215,7 @@
     return memo(at)
 
 
-def stiffness_apply(z, hot, x_ref, effective_ref, grad_ref, nodes, forces, picked, spread_sums, shifts):
+def stiffness_apply(z, hot, x_ref, effective_ref, grad_ref, nodes, forces_a, forces_b, picked_a, picked_b, spread_sums, shifts):
     blocks = grad_ref.shape[2]
     turns = [(b, c) for b in range(3) for c in range(3)]
     span = BRICK + 2
@@ -239,7 +239,10 @@
                 nodes[row : row + 16, j * LANES : (j + 1) * LANES] = pair
 
     node_x = x_ref[...]
-    picked[...] = jnp.dot(nodes[...], hot[...], preferred_element_type=F32)
+    half = blocks // 2
+    lanes_a, lanes_b = slice(0, half * LANES), slice(half * LANES, blocks * LANES)
+    picked_a[...] = jnp.dot(nodes[...], hot[:, lanes_a], preferred_element_type=F32)
+    picked_b[...] = jnp.dot(nodes[...], hot[:, lanes_b], preferred_element_type=F32)
 
     first = POISSON / ((1.0 + POISSON) * (1.0 - 2.0 * POISSON))
     shear_of = 0.5 / (1.0 + POISSON)
@@ -249,7 +252,8 @@
     zero = jnp.zeros((8, LANES), F32)
     wide = lambda row: jnp.broadcast_to(row, (8, LANES))
     for s in range(blocks):
-        lanes = slice(s * LANES, (s + 1) * LANES)
+        lanes = slice(s % half * LANES, (s % half + 1) * LANES)
+        picked, forces = (picked_a, forces_a) if s < half else (picked_b, forces_b)
         grad = lambda l, a, b, c: wide(grad_ref[l, 9 * a + 3 * b + c, s : s + 1, :])
         at_x = [wide(node_x[s : s + 1]) == i for i in range(BRICK)]
         h = [None] * 3
@@ -293,8 +297,12 @@
                 row = (u * span + x) * 8
                 pair = jnp.concatenate([tiles[x], tiles[x + 1]], axis=0).astype(jnp.bfloat16)
                 forces[row : row + 16, lanes] = pair
-    spread_sums[...] = lax.dot_general(
-        forces[...], hot[...], (((1,), (1,)), ((), ())), preferred_element_type=F32
+        if s == half - 1:
+            spread_sums[...] = lax.dot_general(
+                forces_a[...], hot[:, lanes_a], (((1,), (1,)), ((), ())), preferred_element_type=F32
+            )
+    spread_sums[...] += lax.dot_general(
+        forces_b[...], hot[:, lanes_b], (((1,), (1,)), ((), ())), preferred_element_type=F32
     )
     out = {}
     for x in range(span):
@@ -449,9 +457,7 @@
     return memo(lambda x, y: ref[x + offset, y + offset])
 
 
-def cycle_and_apply(place, shifts, levels, r, r1, mass1, fields, particles, scratch):
-    mass0, weight0 = fields
-    middle, coarse, *work = scratch
+def cycle(place, shifts, levels, r, r1, mass1, weight0, middle, coarse):
     width = place.count_x
     margin = 8 * (width + 1)
 
@@ -496,11 +502,14 @@
         value = KEPT * e1(x, y) + first(x, y) + weight * beside_all(e1, x, y, shifts, 2)
         return place.keep(value * live, x, y, 2)
 
-    z = fine_level(r, memo(f1_at), weight0, place, shifts)
+    return fine_level(r, memo(f1_at), weight0, place, shifts)
+
+
+def apply(z, mass0, particles, work, shifts):
     image = stiffness_apply(z, *particles, *work, shifts)
     for x, y in INNER:
         image[x, y] = image[x, y] + mass0(x, y) * z(x, y)
-    return z, image
+    return image
 
 
 def total_of(pairs):
@@ -523,7 +532,7 @@
 
 
 def first_kernel(counts, level_ref, r_ref, mass0_ref, weight0_ref,
-                 hot_ref, x_ref, effective_ref, grad_ref, z_ref, image_ref, even_ref, odd_ref, dots_ref, r1_ref, mass1_ref,
+                 hot_ref, x_ref, effective_ref, grad_ref, z_ref, image_ref, even_ref, odd_ref, dots_ref, mass1_ref,
                  *scratch):
     particles = (hot_ref, x_ref, effective_ref, grad_ref)
     place, shifts = Place(*counts), Shifts()
@@ -538,13 +547,12 @@
     mass1 = [rows(18), rows(19)]
     for x in range(2):
         mass1_ref[x] = mass1[x]
-        for m in range(3):
-            r1_ref[m, x] = r1[m][x]
     r = reader(r_ref, 2)
-    fields = (reader(mass0_ref, 2), reader(weight0_ref, 2))
-    z, image = cycle_and_apply(place, shifts, levels, r, r1, mass1, fields, particles, scratch)
-    for x, y in INNER:
-        z_ref[x, y] = z(x, y)
+    middle, coarse, *work = scratch
+    z = cycle(place, shifts, levels, r, r1, mass1, reader(weight0_ref, 2), middle, coarse)
+    image = apply(z, reader(mass0_ref, 2), particles, work, shifts)
+    for x, y in RIMMED:
+        z_ref[x + 1, y + 1] = z(x, y)
     for x, y in RIMMED:
         image_ref[x + 1, y + 1] = image[x, y]
     clear_tail(even_ref, odd_ref)
@@ -603,7 +611,7 @@
     return jnp.sum(ref[pl.ds(first, count, stride=stride), :], axis=0, keepdims=True)
 
 
-def second_kernel(counts, change_ref, r1_ref, mass1_ref, r_ref, w_ref, mass0_ref, weight0_ref,
+def second_kernel(counts, change_ref, z1_ref, mass1_ref, r_ref, w_ref, mass0_ref, weight0_ref,
                   hot_ref, x_ref, effective_ref, grad_ref, z_ref, image_ref, x_even_ref, x_odd_ref, y_even_ref, y_odd_ref,
                   slots_ref, *scratch):
     particles = (hot_ref, x_ref, effective_ref, grad_ref)
@@ -612,16 +620,16 @@
     levels = Levels(*counts, shifts)
     sums = sums_of(change_ref, bricks, 12, SECOND_ROWS)
     step = sums[:, 0:1] / sums[:, 1:2]
-    r = memo(lambda x, y: r_ref[x + 2, y + 2] - step * w_ref[x + 2, y + 2])
     rows = lambda q: levels.load(change_ref, q, SECOND_ROWS)
     r1 = []
     for m in range(3):
-        low = rows(3 + m) + levels.below_x(rows(9 + m))
-        high = rows(6 + m) + levels.above_x(rows(m))
-        r1.append([r1_ref[m, 0] - step * low, r1_ref[m, 1] - step * high])
-    fields = (reader(mass0_ref, 2), reader(weight0_ref, 2))
-    mass1 = [mass1_ref[0], mass1_ref[1]]
-    z, image = cycle_and_apply(place, shifts, levels, r, r1, mass1, fields, particles, scratch)
+        r1.append([rows(3 + m) + levels.below_x(rows(9 + m)), rows(6 + m) + levels.above_x(rows(m))])
+    w = reader(w_ref, 2)
+    middle, coarse, *work = scratch
+    of_w = cycle(place, shifts, levels, w, r1, [mass1_ref[0], mass1_ref[1]], reader(weight0_ref, 2), middle, coarse)
+    z = memo(lambda x, y: z1_ref[x + 1, y + 1] - step * of_w(x, y))
+    image = apply(z, reader(mass0_ref, 2), particles, work, shifts)
+    r = memo(lambda x, y: r_ref[x + 2, y + 2] - step * w(x, y))
     for x, y in INNER:
         z_ref[x, y] = z(x, y)
         image_ref[x, y] = image[x, y]
@@ -682,7 +690,7 @@
             image[at] = image[at] + place.keep(column, dx, dy, 1)
     for x, y in INNER:
         w = w_ref[x + 2, y + 2]
-        z1 = z1_ref[x, y]
+        z1 = z1_ref[x + 1, y + 1]
         solution = step1 * z1 + step2 * (z2_ref[x, y] + ratio * z1)
         residual = r_ref[x + 2, y + 2] - step1 * w - step2 * (image[x, y] + ratio * w)
         for m in range(3):
@@ -710,8 +718,8 @@
     scratch = (
         *[pltpu.VMEM((8 * (bricks + 2 * (counts[0] + 1)), LANES), F32)] * 2,
         pltpu.VMEM((tiles, depth), jnp.bfloat16),
-        pltpu.VMEM((tiles, width), jnp.bfloat16),
-        pltpu.VMEM((tiles, width), F32),
+        *[pltpu.VMEM((tiles, width // 2), jnp.bfloat16)] * 2,
+        *[pltpu.VMEM((tiles, width // 2), F32)] * 2,
         pltpu.VMEM((tiles, depth), F32),
     )
     rows = lambda columns: (-(-(3 * len(columns) + 1) // 8) * 8, LANES)
@@ -739,9 +747,9 @@
     r, *fields = call(start_kernel, counts, [block(8, 8)] * 3, wide, even, odd)
 
     side = rows(SIDE_Y_IMAGE)
-    z1, image, to_even, to_odd, dots, r1, mass1 = call(
+    z1, image, to_even, to_odd, dots, mass1 = call(
         first_kernel, counts,
-        [block(4, 4), block(6, 6), side, side, (1, LANES), (3, 2, *grid), (2, *grid)],
+        [block(6, 6), block(6, 6), side, side, (1, LANES), (2, *grid)],
         level, r, *fields, *particles, scratch=scratch,
     )
     even, odd = exchange(to_even, to_odd, "gy", counts)
@@ -755,7 +763,7 @@
     side = (2 * 8, LANES)
     z2, image, x_even, x_odd, y_even, y_odd, slots = call(
         second_kernel, counts, [block(4, 4), block(4, 4), side, side, side, side, (bricks, 4, 1, LANES)],
-        change, r1, mass1, r, w, *fields, *particles, scratch=scratch,
+        change, z1, mass1, r, w, *fields, *particles, scratch=scratch,
     )
     sides = (*exchange(x_even, x_odd, "gx", counts), *exchange(y_even, y_odd, "gy", counts))
     slots = lax.all_to_all(slots, AXES, 0, 0)

time: 57.8 us -> 57.7 us (level)
  no operation moved by 1% of the time
where the time goes in v8:
time: 57.7 us; the launch traced here: 57.3 us
  starting transfers between devices  26.2 us (45%)
  waiting for transfers between devices  19.7 us (34%)
  Pallas kernels  8.09 us (14%)
  local copies, waits for them, and re-layouts  1.75 us (3%)
  other arithmetic  0.76 us (1%)
  between operations  0.73 us (1%)
    ppermute x12, waiting for transfers between devices, exchange(): return (lax.ppermute(first, AXES, even), lax.ppermute(second, AXES, odd))  13.2 us
    ppermute x12, starting transfers between devices, exchange(): return (lax.ppermute(first, AXES, even), lax.ppermute(second, AXES, odd))  12.3 us
    all_to_all x2, starting transfers between devices, share(): lax.all_to_all(sent, AXES, 0, 0).reshape(bricks * slot.shape[0], LANES)  11.4 us
    pallas_call x9, Pallas kernels, call(): pl.pallas_call(functools.partial(kernel, counts), out_shape=[jax.ShapeDty...  8.09 us
    all_to_all x2, waiting for transfers between devices, share(): lax.all_to_all(sent, AXES, 0, 0).reshape(bricks * slot.shape[0], LANES)  4.58 us
    all_to_all x1, starting transfers between devices, per_device(): slots = lax.all_to_all(slots, AXES, 0, 0)  2.57 us
    all_to_all x1, waiting for transfers between devices, per_device(): slots = lax.all_to_all(slots, AXES, 0, 0)  2 us
    broadcast_in_dim x2, local copies, waits for them, and re-layouts, share(): sent = jnp.broadcast_to(slot[None], (bricks, *slot.shape))  1.72 us
  transfers between devices with their start and end apart: 15, of which 9 were waited for; matrix products, arithmetic and copies ran while one was open for 0% of the time, Pallas kernels for 1%

profile of v8, /device:TPU:0, one launch (start us, length us, event | category | flops | bytes accessed | tf_op | source)
XLA Modules:
  0.0 57.3 jit_solution(2330589306687615479)
XLA Ops:
  0.6 0.8 %pad_maximum_fusion.fields_ref = f32[4,4,4,128]{3,2,1,0:T(4,128)S(1)} fusion(f32[1,4,4,128]{3,2,1,0:T(4,128)} %bitcast.25, f32[3,4,4,128]{3,2,1,0:T(4,128)} %param.6), kind=kLoop, calls=%fused_computation | loop fusion | flops 8192 | bytes 65536 | tf_op jit(solution)/shard_map/concatenate | solution.py:732
  1.7 0.9 %broadcast_in_dim.21 = f32[32,20,1,128]{3,2,1,0:T(1,128)} broadcast(f32[20,128]{1,0:T(8,128)S(1)} %bitcast.23), dimensions={1,3} | broadcast | bytes 337920 | tf_op jit(solution)/shard_map/broadcast_in_dim | solution.py:729
  2.6 7.3 %all-to-all-start = ((f32[32,20,1,128]{3,2,1,0:T(1,128)}), f32[32,20,1,128]{3,2,1,0:T(1,128)S(1)}, u32[]{:S(2)}, u32[]{:S(2)}) async-start(f32[32,20,1,128]{3,2,1,0:T(1,128)} %broadcast_in_dim.21), calls=%async_computation | async-start | bytes 655360 | tf_op jit(solution)/shard_map/all_to_all | solution.py:730
  10.2 1.7 %collective-permute-start.1 = (f32[8,4,128]{2,1,0:T(4,128)S(1)}, f32[8,4,128]{2,1,0:T(4,128)S(1)}, u32[]{:S(2)}, u32[]{:S(2)}) collective-permute-start(f32[8,4,128]{2,1,0:T(4,128)S(1)} %get-tuple-element.35), channel_id=1, source_target_pairs={{0,1},{1,0},{2,3},{3,2},{4,8},{5,9},{6,10},{7,11},{8,4},{9,5},{10,... | collective-permute-start | bytes 49160 | tf_op jit(solution)/shard_map/ppermute | solution.py:39
  11.9 4.2 %collective-permute-done.1.odd_ref = f32[8,4,128]{2,1,0:T(4,128)S(1)} collective-permute-done((f32[8,4,128]{2,1,0:T(4,128)S(1)}, f32[8,4,128]{2,1,0:T(4,128)S(1)}, u32[]{:S(2)}, u32[]{:S(2)}) %collective-permute-start.1) | collective-permute-done | bytes 16416 | tf_op jit(solution)/shard_map/ppermute | solution.py:39
  16.1 2.5 %collective-permute-start.2 = (f32[14,4,128]{2,1,0:T(4,128)S(1)}, f32[14,4,128]{2,1,0:T(4,128)S(1)}, u32[]{:S(2)}, u32[]{:S(2)}) collective-permute-start(f32[14,4,128]{2,1,0:T(4,128)S(1)} %get-tuple-element.37), channel_id=1, source_target_pairs={{0,1},{1,0},{2,3},{3,2},{4,5},{5,4},{6,7},{7,6},{8,9},{9,8},{10,11... | collective-permute-start | bytes 86024 | tf_op jit(solution)/shard_map/ppermute | solution.py:39
  19.0 1.6 %collective-permute-done.2.even_ref = f32[14,4,128]{2,1,0:T(4,128)S(1)} collective-permute-done((f32[14,4,128]{2,1,0:T(4,128)S(1)}, f32[14,4,128]{2,1,0:T(4,128)S(1)}, u32[]{:S(2)}, u32[]{:S(2)}) %collective-permute-start.2) | collective-permute-done | bytes 28704 | tf_op jit(solution)/shard_map/ppermute | solution.py:39
  20.9 2.7 %shard_map.81 = (f32[6,6,4,128]{3,2,1,0:T(4,128)S(1)}, f32[6,6,4,128]{3,2,1,0:T(4,128)S(1)}, f32[56,128]{1,0:T(8,128)S(1)}, f32[56,128]{1,0:T(8,128)S(1)}, f32[1...) custom-call(f32[640,128]{1,0:T(8,128)S(1)} %bitcast.19, f32[8,8,4,128]{3,2,1,0:T(4,128)S(1)} %get-tuple-element.39.r_ref, ...), custom_call_target="tpu_custom_call" | custom-call | tf_op jit(solution)/shard_map/pallas_call | solution.py:703
  23.6 2.5 %collective-permute-start.4 = (f32[56,128]{1,0:T(8,128)S(1)}, f32[56,128]{1,0:T(8,128)S(1)}, u32[]{:S(2)}, u32[]{:S(2)}) collective-permute-start(f32[56,128]{1,0:T(8,128)S(1)} %get-tuple-element.46), channel_id=1, source_target_pairs={{0,1},{1,0},{2,3},{3,2},{4,5},{5,4},{6,7},{7,6},{8,9},{9,8},{10,11... | collective-permute-start | bytes 86024 | tf_op jit(solution)/shard_map/ppermute | solution.py:39
  26.1 1.8 %collective-permute-done.4.even_ref = f32[56,128]{1,0:T(8,128)S(1)} collective-permute-done((f32[56,128]{1,0:T(8,128)S(1)}, f32[56,128]{1,0:T(8,128)S(1)}, u32[]{:S(2)}, u32[]{:S(2)}) %collective-permute-start.4) | collective-permute-done | bytes 28704 | tf_op jit(solution)/shard_map/ppermute | solution.py:39
  28.2 0.8 %broadcast_in_dim.23 = f32[32,13,1,128]{3,2,1,0:T(1,128)} broadcast(f32[13,128]{1,0:T(8,128)S(1)} %bitcast.24), dimensions={1,3} | broadcast | bytes 219648 | tf_op jit(solution)/shard_map/broadcast_in_dim | solution.py:729
  29.0 4.1 %all-to-all-start.1 = ((f32[32,13,1,128]{3,2,1,0:T(1,128)}), f32[32,13,1,128]{3,2,1,0:T(1,128)S(1)}, u32[]{:S(2)}, u32[]{:S(2)}) async-start(f32[32,13,1,128]{3,2,1,0:T(1,128)} %broadcast_in_dim.23), calls=%async_computation.1 | async-start | bytes 425984 | tf_op jit(solution)/shard_map/all_to_all | solution.py:730
  33.1 0.3 collective-permute-start.6
  33.5 1.7 %collective-permute-start.7 = (f32[72,128]{1,0:T(8,128)S(1)}, f32[72,128]{1,0:T(8,128)S(1)}, u32[]{:S(2)}, u32[]{:S(2)}) collective-permute-start(f32[72,128]{1,0:T(8,128)S(1)} %get-tuple-element.54), channel_id=1, source_target_pairs={{0,1},{1,0},{2,3},{3,2},{4,8},{5,9},{6,10},{7,11},{8,4},{9,5},{10,... | collective-permute-start | bytes 110600 | tf_op jit(solution)/shard_map/ppermute | solution.py:39
  35.1 3.1 %collective-permute-done.7.odd_ref = f32[72,128]{1,0:T(8,128)S(1)} collective-permute-done((f32[72,128]{1,0:T(8,128)S(1)}, f32[72,128]{1,0:T(8,128)S(1)}, u32[]{:S(2)}, u32[]{:S(2)}) %collective-permute-start.7) | collective-permute-done | bytes 36896 | tf_op jit(solution)/shard_map/ppermute | solution.py:39
  38.3 4.4 %all-to-all-done.1 = f32[32,13,1,128]{3,2,1,0:T(1,128)S(1)} async-done(((f32[32,13,1,128]{3,2,1,0:T(1,128)}), f32[32,13,1,128]{3,2,1,0:T(1,128)S(1)}, u32[]{:S(2)}, u32[]{:S(2)}) %all-to-all-start.1) | async-done | bytes 213024 | tf_op jit(solution)/shard_map/all_to_all | solution.py:730
  42.8 3.5 %shard_map.84 = (f32[4,4,4,128]{3,2,1,0:T(4,128)S(1)}, f32[4,4,4,128]{3,2,1,0:T(4,128)S(1)}, f32[16,128]{1,0:T(8,128)S(1)}, f32[16,128]{1,0:T(8,128)S(1)}, f32[1...) custom-call(f32[416,128]{1,0:T(8,128)S(1)} %bitcast.15, ...), custom_call_target="tpu_custom_call" | custom-call | tf_op jit(solution)/shard_map/pallas_call | solution.py:703
  46.2 2.6 %all-to-all-start.2 = ((f32[32,4,1,128]{3,2,1,0:T(1,128)}), f32[32,4,1,128]{3,2,1,0:T(1,128)S(1)}, u32[]{:S(2)}, u32[]{:S(2)}) async-start(f32[32,4,1,128]{3,2,1,0:T(1,128)} %get-tuple-element.55), calls=%async_computation.2 | async-start | bytes 131072 | tf_op jit(solution)/shard_map/all_to_all | solution.py:769
  49.0 1.7 %collective-permute-start.9 = (f32[16,128]{1,0:T(8,128)S(1)}, f32[16,128]{1,0:T(8,128)S(1)}, u32[]{:S(2)}, u32[]{:S(2)}) collective-permute-start(f32[16,128]{1,0:T(8,128)S(1)} %get-tuple-element.57), channel_id=1, source_target_pairs={{0,1},{1,0},{2,3},{3,2},{4,8},{5,9},{6,10},{7,11},{8,4},{9,5},{10,... | collective-permute-start | bytes 24584 | tf_op jit(solution)/shard_map/ppermute | solution.py:39
  51.0 1.0 %collective-permute-start.11 = (f32[16,128]{1,0:T(8,128)S(1)}, f32[16,128]{1,0:T(8,128)S(1)}, u32[]{:S(2)}, u32[]{:S(2)}) collective-permute-start(f32[16,128]{1,0:T(8,128)S(1)} %get-tuple-element.59), channel_id=1, source_target_pairs={{0,4},{1,2},{2,1},{3,7},{4,0},{5,6},{6,5},{7,3},{8,12},{9,10},{10,... | collective-permute-start | bytes 24584 | tf_op jit(solution)/shard_map/ppermute | solution.py:39
  52.0 0.6 %collective-permute-done.9.x_odd_ref = f32[16,128]{1,0:T(8,128)S(1)} collective-permute-done((f32[16,128]{1,0:T(8,128)S(1)}, f32[16,128]{1,0:T(8,128)S(1)}, u32[]{:S(2)}, u32[]{:S(2)}) %collective-permute-start.9) | collective-permute-done | bytes 8224 | tf_op jit(solution)/shard_map/ppermute | solution.py:39
  52.6 1.7 %collective-permute-done.10.y_even_ref = f32[16,128]{1,0:T(8,128)S(1)} collective-permute-done((f32[16,128]{1,0:T(8,128)S(1)}, f32[16,128]{1,0:T(8,128)S(1)}, u32[]{:S(2)}, u32[]{:S(2)}) %collective-permute-start.10) | collective-permute-done | bytes 8224 | tf_op jit(solution)/shard_map/ppermute | solution.py:39
  54.4 2.0 %all-to-all-done.2.slots_ref = f32[32,4,1,128]{3,2,1,0:T(1,128)S(1)} async-done(((f32[32,4,1,128]{3,2,1,0:T(1,128)}), f32[32,4,1,128]{3,2,1,0:T(1,128)S(1)}, u32[]{:S(2)}, u32[]{:S(2)}) %all-to-all-start.2) | async-done | bytes 65568 | tf_op jit(solution)/shard_map/all_to_all | solution.py:769
  56.4 0.9 %shard_map.85 = (f32[3,4,4,128]{3,2,1,0:T(4,128)}, f32[3,4,4,128]{3,2,1,0:T(4,128)}) custom-call(f32[32,4,1,128]{3,2,1,0:T(1,128)S(1)} %all-to-all-done.2.slots_ref, f32[16,128]{1,0:T(8,128)S(1)} %collective-permute-done.8.x_even_ref, f32[16,128]{1,0:T(8,128)S(1)} %collective-permute-done.9.x_odd_ref, f32[16,128]{1,0:T(8,128)S(1)} %collective-permute-done.10.y_even_ref, ...), custom_call_target="tpu_custom_call" | custom-call | tf_op jit(solution)/shard_map/pallas_call | solution.py:703
  (28 shorter events, 2.0 us)
Async XLA Ops:
  2.6 18.3 %copy-start = (f32[1,1,8,3,27,128]{5,2,4,3,1,0:T(8,128)S(1)}, f32[1,1,8,3,27,128]{5,2,4,3,1,0:T(8,128)}, u32[]{:S(2)}) copy-start(f32[1,1,8,3,27,128]{5,2,4,3,1,0:T(8,128)} %param.8) | copy-start | bytes 995332
  2.6 18.3 %all-to-all-start = ((f32[32,20,1,128]{3,2,1,0:T(1,128)}), f32[32,20,1,128]{3,2,1,0:T(1,128)S(1)}, u32[]{:S(2)}, u32[]{:S(2)}) async-start(f32[32,20,1,128]{3,2,1,0:T(1,128)} %broadcast_in_dim.21), calls=%async_computation | async-start | bytes 655360 | tf_op jit(solution)/shard_map/all_to_all | solution.py:730
  9.9 2.0 %collective-permute-start = (f32[8,4,128]{2,1,0:T(4,128)S(1)}, f32[8,4,128]{2,1,0:T(4,128)S(1)}, u32[]{:S(2)}, u32[]{:S(2)}) collective-permute-start(f32[8,4,128]{2,1,0:T(4,128)S(1)} %get-tuple-element.34), channel_id=1, source_target_pairs={{0,4},{1,5},{2,6},{3,7},{4,0},{5,1},{6,2},{7,3},{8,12},{9,13},{10,... | collective-permute-start | bytes 49160 | tf_op jit(solution)/shard_map/ppermute | solution.py:39
  10.2 5.9 %collective-permute-start.1 = (f32[8,4,128]{2,1,0:T(4,128)S(1)}, f32[8,4,128]{2,1,0:T(4,128)S(1)}, u32[]{:S(2)}, u32[]{:S(2)}) collective-permute-start(f32[8,4,128]{2,1,0:T(4,128)S(1)} %get-tuple-element.35), channel_id=1, source_target_pairs={{0,1},{1,0},{2,3},{3,2},{4,8},{5,9},{6,10},{7,11},{8,4},{9,5},{10,... | collective-permute-start | bytes 49160 | tf_op jit(solution)/shard_map/ppermute | solution.py:39
  16.1 2.6 %copy-start.3 = (s32[1,1,8,128]{3,2,1,0:T(8,128)S(1)}, s32[1,1,8,128]{3,2,1,0:T(8,128)}, u32[]{:S(2)}) copy-start(s32[1,1,8,128]{3,2,1,0:T(8,128)} %param.10) | copy-start | bytes 12292
  16.1 2.6 %copy-start.2 = (f32[1,1,8,128]{3,2,1,0:T(8,128)S(1)}, f32[1,1,8,128]{3,2,1,0:T(8,128)}, u32[]{:S(2)}) copy-start(f32[1,1,8,128]{3,2,1,0:T(8,128)} %param.9) | copy-start | bytes 12292
  16.1 2.6 %copy-start.1 = (s32[1,1,8,128]{3,2,1,0:T(8,128)S(1)}, s32[1,1,8,128]{3,2,1,0:T(8,128)}, u32[]{:S(2)}) copy-start(s32[1,1,8,128]{3,2,1,0:T(8,128)} %param.11) | copy-start | bytes 12292
  16.1 4.5 %collective-permute-start.2 = (f32[14,4,128]{2,1,0:T(4,128)S(1)}, f32[14,4,128]{2,1,0:T(4,128)S(1)}, u32[]{:S(2)}, u32[]{:S(2)}) collective-permute-start(f32[14,4,128]{2,1,0:T(4,128)S(1)} %get-tuple-element.37), channel_id=1, source_target_pairs={{0,1},{1,0},{2,3},{3,2},{4,5},{5,4},{6,7},{7,6},{8,9},{9,8},{10,11... | collective-permute-start | bytes 86024 | tf_op jit(solution)/shard_map/ppermute | solution.py:39
  18.7 2.0 %collective-permute-start.3 = (f32[14,4,128]{2,1,0:T(4,128)S(1)}, f32[14,4,128]{2,1,0:T(4,128)S(1)}, u32[]{:S(2)}, u32[]{:S(2)}) collective-permute-start(f32[14,4,128]{2,1,0:T(4,128)S(1)} %get-tuple-element.38), channel_id=1, source_target_pairs={{0,4},{1,2},{2,1},{3,7},{4,0},{5,6},{6,5},{7,3},{8,12},{9,10},{10,... | collective-permute-start | bytes 86024 | tf_op jit(solution)/shard_map/ppermute | solution.py:39
  23.6 4.4 %collective-permute-start.4 = (f32[56,128]{1,0:T(8,128)S(1)}, f32[56,128]{1,0:T(8,128)S(1)}, u32[]{:S(2)}, u32[]{:S(2)}) collective-permute-start(f32[56,128]{1,0:T(8,128)S(1)} %get-tuple-element.46), channel_id=1, source_target_pairs={{0,1},{1,0},{2,3},{3,2},{4,5},{5,4},{6,7},{7,6},{8,9},{9,8},{10,11... | collective-permute-start | bytes 86024 | tf_op jit(solution)/shard_map/ppermute | solution.py:39
  26.1 1.9 %collective-permute-start.5 = (f32[56,128]{1,0:T(8,128)S(1)}, f32[56,128]{1,0:T(8,128)S(1)}, u32[]{:S(2)}, u32[]{:S(2)}) collective-permute-start(f32[56,128]{1,0:T(8,128)S(1)} %get-tuple-element.47), channel_id=1, source_target_pairs={{0,4},{1,2},{2,1},{3,7},{4,0},{5,6},{6,5},{7,3},{8,12},{9,10},{10,... | collective-permute-start | bytes 86024 | tf_op jit(solution)/shard_map/ppermute | solution.py:39
  29.0 13.7 %all-to-all-start.1 = ((f32[32,13,1,128]{3,2,1,0:T(1,128)}), f32[32,13,1,128]{3,2,1,0:T(1,128)S(1)}, u32[]{:S(2)}, u32[]{:S(2)}) async-start(f32[32,13,1,128]{3,2,1,0:T(1,128)} %broadcast_in_dim.23), calls=%async_computation.1 | async-start | bytes 425984 | tf_op jit(solution)/shard_map/all_to_all | solution.py:730
  33.1 2.0 %collective-permute-start.6 = (f32[72,128]{1,0:T(8,128)S(1)}, f32[72,128]{1,0:T(8,128)S(1)}, u32[]{:S(2)}, u32[]{:S(2)}) collective-permute-start(f32[72,128]{1,0:T(8,128)S(1)} %get-tuple-element.53), channel_id=1, source_target_pairs={{0,4},{1,5},{2,6},{3,7},{4,0},{5,1},{6,2},{7,3},{8,12},{9,13},{10,... | collective-permute-start | bytes 110600 | tf_op jit(solution)/shard_map/ppermute | solution.py:39
  33.5 4.8 %collective-permute-start.7 = (f32[72,128]{1,0:T(8,128)S(1)}, f32[72,128]{1,0:T(8,128)S(1)}, u32[]{:S(2)}, u32[]{:S(2)}) collective-permute-start(f32[72,128]{1,0:T(8,128)S(1)} %get-tuple-element.54), channel_id=1, source_target_pairs={{0,1},{1,0},{2,3},{3,2},{4,8},{5,9},{6,10},{7,11},{8,4},{9,5},{10,... | collective-permute-start | bytes 110600 | tf_op jit(solution)/shard_map/ppermute | solution.py:39
  46.2 10.2 %all-to-all-start.2 = ((f32[32,4,1,128]{3,2,1,0:T(1,128)}), f32[32,4,1,128]{3,2,1,0:T(1,128)S(1)}, u32[]{:S(2)}, u32[]{:S(2)}) async-start(f32[32,4,1,128]{3,2,1,0:T(1,128)} %get-tuple-element.55), calls=%async_computation.2 | async-start | bytes 131072 | tf_op jit(solution)/shard_map/all_to_all | solution.py:769
  48.8 3.2 %collective-permute-start.8 = (f32[16,128]{1,0:T(8,128)S(1)}, f32[16,128]{1,0:T(8,128)S(1)}, u32[]{:S(2)}, u32[]{:S(2)}) collective-permute-start(f32[16,128]{1,0:T(8,128)S(1)} %get-tuple-element.56), channel_id=1, source_target_pairs={{0,4},{1,5},{2,6},{3,7},{4,0},{5,1},{6,2},{7,3},{8,12},{9,13},{10,... | collective-permute-start | bytes 24584 | tf_op jit(solution)/shard_map/ppermute | solution.py:39
  49.0 3.7 %collective-permute-start.9 = (f32[16,128]{1,0:T(8,128)S(1)}, f32[16,128]{1,0:T(8,128)S(1)}, u32[]{:S(2)}, u32[]{:S(2)}) collective-permute-start(f32[16,128]{1,0:T(8,128)S(1)} %get-tuple-element.57), channel_id=1, source_target_pairs={{0,1},{1,0},{2,3},{3,2},{4,8},{5,9},{6,10},{7,11},{8,4},{9,5},{10,... | collective-permute-start | bytes 24584 | tf_op jit(solution)/shard_map/ppermute | solution.py:39
  50.7 3.7 %collective-permute-start.10 = (f32[16,128]{1,0:T(8,128)S(1)}, f32[16,128]{1,0:T(8,128)S(1)}, u32[]{:S(2)}, u32[]{:S(2)}) collective-permute-start(f32[16,128]{1,0:T(8,128)S(1)} %get-tuple-element.58), channel_id=1, source_target_pairs={{0,1},{1,0},{2,3},{3,2},{4,5},{5,4},{6,7},{7,6},{8,9},{9,8},{10,11... | collective-permute-start | bytes 24584 | tf_op jit(solution)/shard_map/ppermute | solution.py:39
  51.0 3.4 %collective-permute-start.11 = (f32[16,128]{1,0:T(8,128)S(1)}, f32[16,128]{1,0:T(8,128)S(1)}, u32[]{:S(2)}, u32[]{:S(2)}) collective-permute-start(f32[16,128]{1,0:T(8,128)S(1)} %get-tuple-element.59), channel_id=1, source_target_pairs={{0,4},{1,2},{2,1},{3,7},{4,0},{5,6},{6,5},{7,3},{8,12},{9,10},{10,... | collective-permute-start | bytes 24584 | tf_op jit(solution)/shard_map/ppermute | solution.py:39

commit v9 on v8

--- a/solution.py
+++ b/solution.py
@@ -393,16 +393,20 @@
     r = memo(lambda x, y: own[x, y] * live)
     cells = [(x, y) for x in (0, 1) for y in range(-1, 3)] + [(x, y) for x in (-1, 2) for y in (0, 1)]
     part = contribution(r, weight0, INNER, cells, shifts)
+    rows = []
     for x in (0, 1):
-        for k, column in enumerate(pack_y(part, x, shifts)):
-            put_rows(slot_ref, 6 * x + 3 * k, column)
-    for k, x in enumerate((-1, 2)):
-        put_rows(slot_ref, 12 + 3 * k, part[x, 0] * shifts.even + part[x, 1] * shifts.odd)
+        for column in pack_y(part, x, shifts):
+            rows += [column[m : m + 1] for m in range(3)]
+    for x in (-1, 2):
+        column = part[x, 0] * shifts.even + part[x, 1] * shifts.odd
+        rows += [column[m : m + 1] for m in range(3)]
     for x in (0, 1):
         mass1 = [
             shifts.pair_sum(sum(own[2 * x + i, 2 * y + j][3:4] for i in range(2) for j in range(2))) for y in (0, 1)
         ]
-        slot_ref[18 + x] = mass1[0] * shifts.even + mass1[1] * shifts.odd
+        rows.append(mass1[0] * shifts.even + mass1[1] * shifts.odd)
+    for k in range(FIRST_ROWS // 4):
+        slot_ref[k] = jnp.concatenate(rows[4 * k : 4 * k + 4], axis=0)
 
 
 def widen_kernel(counts, own_ref, even_ref, odd_ref, wide_ref, to_even_ref, to_odd_ref):
@@ -637,11 +641,10 @@
     zaz = total_of((image[x, y], z(x, y)) for x, y in RIMMED)
     zw = total_of((w_ref[x + 2, y + 2], z(x, y)) for x, y in INNER)
     row = dots_row(rz, zaz, zw)
-    none = jnp.zeros((3, 1, LANES), F32)
+    plain = jnp.concatenate([jnp.zeros((3, LANES), F32), row], axis=0)
 
     def fill(k, carry):
-        slots_ref[k, 0:3] = none
-        slots_ref[k, 3] = row
+        slots_ref[k, 0] = plain
         return carry
 
     lax.fori_loop(0, bricks, fill, 0)
@@ -654,8 +657,7 @@
             @pl.when(there_x & there_y)
             def _(column=column, dx=dx, dy=dy):
                 other = (place.gx + dx) * counts[1] + place.gy + dy
-                for m in range(3):
-                    slots_ref[other, m] = column[m : m + 1]
+                slots_ref[other, 0] = jnp.concatenate([column[0:3], row], axis=0)
 
     clear_tail(x_even_ref, x_odd_ref, y_even_ref, y_odd_ref)
     for k in range(BRICK):
@@ -667,7 +669,7 @@
     place = Place(*counts)
     bricks = counts[0] * counts[1]
     sums1 = sums_of(change_ref, bricks, 12, SECOND_ROWS)
-    sums2 = jnp.sum(slots_ref[:, 3], axis=0)
+    sums2 = jnp.sum(slots_ref[:, 0], axis=0)[3:4]
     rz1, zaz1 = sums1[:, 0:1], sums1[:, 1:2]
     rz2, zaz2, zw = sums2[:, 0:1], sums2[:, 1:2], sums2[:, 2:3]
     step1 = rz1 / zaz1
@@ -685,7 +687,7 @@
             other_x = jnp.clip(place.gx + dx, 0, counts[0] - 1)
             other_y = jnp.clip(place.gy + dy, 0, counts[1] - 1)
             other = other_x * counts[1] + other_y
-            column = jnp.concatenate([slots_ref[other, m] for m in range(3)] + [jnp.zeros((1, LANES), F32)], axis=0)
+            column = slots_ref[other, 0]
             at = (end if dx > 0 else 0, end if dy > 0 else 0)
             image[at] = image[at] + place.keep(column, dx, dy, 1)
     for x, y in INNER:
@@ -727,11 +729,11 @@
 
     def share(slot):
         sent = jnp.broadcast_to(slot[None], (bricks, *slot.shape))
-        return lax.all_to_all(sent, AXES, 0, 0).reshape(bricks * slot.shape[0], LANES)
+        return lax.all_to_all(sent, AXES, 0, 0).reshape(-1, LANES)
 
     fields = jnp.concatenate([right_side, node_mass[None]], axis=0)
     own, to_even, to_odd, slot = call(
-        pack_kernel, counts, [block(4, 4), block(8), block(8), (FIRST_ROWS, 1, LANES)], fields
+        pack_kernel, counts, [block(4, 4), block(8), block(8), block(FIRST_ROWS // 4)], fields
     )
     level = share(slot)
     even, odd = exchange(to_even, to_odd, "gx", counts)
@@ -762,7 +764,7 @@
     (w,) = call(middle_kernel, counts, [block(8, 8)], long, even, odd)
     side = (2 * 8, LANES)
     z2, image, x_even, x_odd, y_even, y_odd, slots = call(
-        second_kernel, counts, [block(4, 4), block(4, 4), side, side, side, side, (bricks, 4, 1, LANES)],
+        second_kernel, counts, [block(4, 4), block(4, 4), side, side, side, side, (bricks, 1, 4, LANES)],
         change, z1, mass1, r, w, *fields, *particles, scratch=scratch,
     )
     sides = (*exchange(x_even, x_odd, "gx", counts), *exchange(y_even, y_odd, "gy", counts))

time: 57.7 us -> 57.5 us (level)
  no operation moved by 1% of the time
where the time goes in v9:
time: 57.5 us; the launch traced here: 57.1 us
  starting transfers between devices  26.2 us (46%)
  waiting for transfers between devices  19.7 us (34%)
  Pallas kernels  8.05 us (14%)
  local copies, waits for them, and re-layouts  1.61 us (3%)
  other arithmetic  0.76 us (1%)
  between operations  0.73 us (1%)
    ppermute x12, waiting for transfers between devices, exchange(): return (lax.ppermute(first, AXES, even), lax.ppermute(second, AXES, odd))  13.2 us
    ppermute x12, starting transfers between devices, exchange(): return (lax.ppermute(first, AXES, even), lax.ppermute(second, AXES, odd))  12.2 us
    all_to_all x2, starting transfers between devices, share(): return lax.all_to_all(sent, AXES, 0, 0).reshape(-1, LANES)  11.4 us
    pallas_call x9, Pallas kernels, call(): pl.pallas_call(functools.partial(kernel, counts), out_shape=[jax.ShapeDty...  8.05 us
    all_to_all x2, waiting for transfers between devices, share(): return lax.all_to_all(sent, AXES, 0, 0).reshape(-1, LANES)  4.58 us
    all_to_all x1, starting transfers between devices, per_device(): slots = lax.all_to_all(slots, AXES, 0, 0)  2.57 us
    all_to_all x1, waiting for transfers between devices, per_device(): slots = lax.all_to_all(slots, AXES, 0, 0)  2 us
    broadcast_in_dim x2, local copies, waits for them, and re-layouts, share(): sent = jnp.broadcast_to(slot[None], (bricks, *slot.shape))  1.58 us
  transfers between devices with their start and end apart: 15, of which 9 were waited for; matrix products, arithmetic and copies ran while one was open for 0% of the time, Pallas kernels for 1%

profile of v9, /device:TPU:0, one launch (start us, length us, event | category | flops | bytes accessed | tf_op | source)
XLA Modules:
  0.0 57.1 jit_solution(11500186518356443707)
XLA Ops:
  0.6 0.8 %pad_maximum_fusion.fields_ref = f32[4,4,4,128]{3,2,1,0:T(4,128)S(1)} fusion(f32[1,4,4,128]{3,2,1,0:T(4,128)} %bitcast.21, f32[3,4,4,128]{3,2,1,0:T(4,128)} %param.6), kind=kLoop, calls=%fused_computation | loop fusion | flops 8192 | bytes 65536 | tf_op jit(solution)/shard_map/concatenate | solution.py:734
  1.7 0.8 %broadcast_in_dim.18 = f32[32,5,4,128]{3,2,1,0:T(4,128)} broadcast(f32[5,4,128]{2,1,0:T(4,128)S(1)} %get-tuple-element.32), dimensions={1,2,3} | broadcast | bytes 337920 | tf_op jit(solution)/shard_map/broadcast_in_dim | solution.py:731
  2.4 7.3 %all-to-all-start = ((f32[32,5,4,128]{3,2,1,0:T(4,128)}), f32[32,5,4,128]{3,2,1,0:T(4,128)S(1)}, u32[]{:S(2)}, u32[]{:S(2)}) async-start(f32[32,5,4,128]{3,2,1,0:T(4,128)} %broadcast_in_dim.18), calls=%async_computation | async-start | bytes 655360 | tf_op jit(solution)/shard_map/all_to_all | solution.py:732
  9.7 0.3 collective-permute-start
  10.1 1.7 %collective-permute-start.1 = (f32[8,4,128]{2,1,0:T(4,128)S(1)}, f32[8,4,128]{2,1,0:T(4,128)S(1)}, u32[]{:S(2)}, u32[]{:S(2)}) collective-permute-start(f32[8,4,128]{2,1,0:T(4,128)S(1)} %get-tuple-element.35), channel_id=1, source_target_pairs={{0,1},{1,0},{2,3},{3,2},{4,8},{5,9},{6,10},{7,11},{8,4},{9,5},{10,... | collective-permute-start | bytes 49160 | tf_op jit(solution)/shard_map/ppermute | solution.py:39
  11.7 4.2 %collective-permute-done.1.odd_ref = f32[8,4,128]{2,1,0:T(4,128)S(1)} collective-permute-done((f32[8,4,128]{2,1,0:T(4,128)S(1)}, f32[8,4,128]{2,1,0:T(4,128)S(1)}, u32[]{:S(2)}, u32[]{:S(2)}) %collective-permute-start.1) | collective-permute-done | bytes 16416 | tf_op jit(solution)/shard_map/ppermute | solution.py:39
  16.0 2.5 %collective-permute-start.2 = (f32[14,4,128]{2,1,0:T(4,128)S(1)}, f32[14,4,128]{2,1,0:T(4,128)S(1)}, u32[]{:S(2)}, u32[]{:S(2)}) collective-permute-start(f32[14,4,128]{2,1,0:T(4,128)S(1)} %get-tuple-element.37), channel_id=1, source_target_pairs={{0,1},{1,0},{2,3},{3,2},{4,5},{5,4},{6,7},{7,6},{8,9},{9,8},{10,11... | collective-permute-start | bytes 86024 | tf_op jit(solution)/shard_map/ppermute | solution.py:39
  18.9 1.6 %collective-permute-done.2.even_ref = f32[14,4,128]{2,1,0:T(4,128)S(1)} collective-permute-done((f32[14,4,128]{2,1,0:T(4,128)S(1)}, f32[14,4,128]{2,1,0:T(4,128)S(1)}, u32[]{:S(2)}, u32[]{:S(2)}) %collective-permute-start.2) | collective-permute-done | bytes 28704 | tf_op jit(solution)/shard_map/ppermute | solution.py:39
  20.7 2.7 %shard_map.81 = (f32[6,6,4,128]{3,2,1,0:T(4,128)S(1)}, f32[6,6,4,128]{3,2,1,0:T(4,128)S(1)}, f32[56,128]{1,0:T(8,128)S(1)}, f32[56,128]{1,0:T(8,128)S(1)}, f32[1...) custom-call(f32[640,128]{1,0:T(8,128)S(1)} %bitcast.16, f32[8,8,4,128]{3,2,1,0:T(4,128)S(1)} %get-tuple-element.39.r_ref, ...), custom_call_target="tpu_custom_call" | custom-call | tf_op jit(solution)/shard_map/pallas_call | solution.py:705
  23.4 2.5 %collective-permute-start.4 = (f32[56,128]{1,0:T(8,128)S(1)}, f32[56,128]{1,0:T(8,128)S(1)}, u32[]{:S(2)}, u32[]{:S(2)}) collective-permute-start(f32[56,128]{1,0:T(8,128)S(1)} %get-tuple-element.46), channel_id=1, source_target_pairs={{0,1},{1,0},{2,3},{3,2},{4,5},{5,4},{6,7},{7,6},{8,9},{9,8},{10,11... | collective-permute-start | bytes 86024 | tf_op jit(solution)/shard_map/ppermute | solution.py:39
  25.9 1.8 %collective-permute-done.4.even_ref = f32[56,128]{1,0:T(8,128)S(1)} collective-permute-done((f32[56,128]{1,0:T(8,128)S(1)}, f32[56,128]{1,0:T(8,128)S(1)}, u32[]{:S(2)}, u32[]{:S(2)}) %collective-permute-start.4) | collective-permute-done | bytes 28704 | tf_op jit(solution)/shard_map/ppermute | solution.py:39
  28.1 0.8 %broadcast_in_dim.20 = f32[32,13,1,128]{3,2,1,0:T(1,128)} broadcast(f32[13,128]{1,0:T(8,128)S(1)} %bitcast.20), dimensions={1,3} | broadcast | bytes 219648 | tf_op jit(solution)/shard_map/broadcast_in_dim | solution.py:731
  28.9 4.1 %all-to-all-start.1 = ((f32[32,13,1,128]{3,2,1,0:T(1,128)}), f32[32,13,1,128]{3,2,1,0:T(1,128)S(1)}, u32[]{:S(2)}, u32[]{:S(2)}) async-start(f32[32,13,1,128]{3,2,1,0:T(1,128)} %broadcast_in_dim.20), calls=%async_computation.1 | async-start | bytes 425984 | tf_op jit(solution)/shard_map/all_to_all | solution.py:732
  33.3 1.7 %collective-permute-start.7 = (f32[72,128]{1,0:T(8,128)S(1)}, f32[72,128]{1,0:T(8,128)S(1)}, u32[]{:S(2)}, u32[]{:S(2)}) collective-permute-start(f32[72,128]{1,0:T(8,128)S(1)} %get-tuple-element.54), channel_id=1, source_target_pairs={{0,1},{1,0},{2,3},{3,2},{4,8},{5,9},{6,10},{7,11},{8,4},{9,5},{10,... | collective-permute-start | bytes 110600 | tf_op jit(solution)/shard_map/ppermute | solution.py:39
  35.0 3.1 %collective-permute-done.7.odd_ref = f32[72,128]{1,0:T(8,128)S(1)} collective-permute-done((f32[72,128]{1,0:T(8,128)S(1)}, f32[72,128]{1,0:T(8,128)S(1)}, u32[]{:S(2)}, u32[]{:S(2)}) %collective-permute-start.7) | collective-permute-done | bytes 36896 | tf_op jit(solution)/shard_map/ppermute | solution.py:39
  38.2 4.4 %all-to-all-done.1 = f32[32,13,1,128]{3,2,1,0:T(1,128)S(1)} async-done(((f32[32,13,1,128]{3,2,1,0:T(1,128)}), f32[32,13,1,128]{3,2,1,0:T(1,128)S(1)}, u32[]{:S(2)}, u32[]{:S(2)}) %all-to-all-start.1) | async-done | bytes 213024 | tf_op jit(solution)/shard_map/all_to_all | solution.py:732
  42.6 3.4 %shard_map.84 = (f32[4,4,4,128]{3,2,1,0:T(4,128)S(1)}, f32[4,4,4,128]{3,2,1,0:T(4,128)S(1)}, f32[16,128]{1,0:T(8,128)S(1)}, f32[16,128]{1,0:T(8,128)S(1)}, f32[1...) custom-call(f32[416,128]{1,0:T(8,128)S(1)} %bitcast.12, ...), custom_call_target="tpu_custom_call" | custom-call | tf_op jit(solution)/shard_map/pallas_call | solution.py:705
  46.0 2.6 %all-to-all-start.2 = ((f32[32,1,4,128]{3,2,1,0:T(4,128)}), f32[32,1,4,128]{3,2,1,0:T(4,128)S(1)}, u32[]{:S(2)}, u32[]{:S(2)}) async-start(f32[32,1,4,128]{3,2,1,0:T(4,128)} %get-tuple-element.55), calls=%async_computation.2 | async-start | bytes 131072 | tf_op jit(solution)/shard_map/all_to_all | solution.py:771
  48.8 1.7 %collective-permute-start.9 = (f32[16,128]{1,0:T(8,128)S(1)}, f32[16,128]{1,0:T(8,128)S(1)}, u32[]{:S(2)}, u32[]{:S(2)}) collective-permute-start(f32[16,128]{1,0:T(8,128)S(1)} %get-tuple-element.57), channel_id=1, source_target_pairs={{0,1},{1,0},{2,3},{3,2},{4,8},{5,9},{6,10},{7,11},{8,4},{9,5},{10,... | collective-permute-start | bytes 24584 | tf_op jit(solution)/shard_map/ppermute | solution.py:39
  50.8 1.0 %collective-permute-start.11 = (f32[16,128]{1,0:T(8,128)S(1)}, f32[16,128]{1,0:T(8,128)S(1)}, u32[]{:S(2)}, u32[]{:S(2)}) collective-permute-start(f32[16,128]{1,0:T(8,128)S(1)} %get-tuple-element.59), channel_id=1, source_target_pairs={{0,4},{1,2},{2,1},{3,7},{4,0},{5,6},{6,5},{7,3},{8,12},{9,10},{10,... | collective-permute-start | bytes 24584 | tf_op jit(solution)/shard_map/ppermute | solution.py:39
  51.8 0.6 %collective-permute-done.9.x_odd_ref = f32[16,128]{1,0:T(8,128)S(1)} collective-permute-done((f32[16,128]{1,0:T(8,128)S(1)}, f32[16,128]{1,0:T(8,128)S(1)}, u32[]{:S(2)}, u32[]{:S(2)}) %collective-permute-start.9) | collective-permute-done | bytes 8224 | tf_op jit(solution)/shard_map/ppermute | solution.py:39
  52.4 1.7 %collective-permute-done.10.y_even_ref = f32[16,128]{1,0:T(8,128)S(1)} collective-permute-done((f32[16,128]{1,0:T(8,128)S(1)}, f32[16,128]{1,0:T(8,128)S(1)}, u32[]{:S(2)}, u32[]{:S(2)}) %collective-permute-start.10) | collective-permute-done | bytes 8224 | tf_op jit(solution)/shard_map/ppermute | solution.py:39
  54.2 2.0 %all-to-all-done.2.slots_ref = f32[32,1,4,128]{3,2,1,0:T(4,128)S(1)} async-done(((f32[32,1,4,128]{3,2,1,0:T(4,128)}), f32[32,1,4,128]{3,2,1,0:T(4,128)S(1)}, u32[]{:S(2)}, u32[]{:S(2)}) %all-to-all-start.2) | async-done | bytes 65568 | tf_op jit(solution)/shard_map/all_to_all | solution.py:771
  56.2 0.9 %shard_map.85 = (f32[3,4,4,128]{3,2,1,0:T(4,128)}, f32[3,4,4,128]{3,2,1,0:T(4,128)}) custom-call(f32[32,1,4,128]{3,2,1,0:T(4,128)S(1)} %all-to-all-done.2.slots_ref, f32[16,128]{1,0:T(8,128)S(1)} %collective-permute-done.8.x_even_ref, f32[16,128]{1,0:T(8,128)S(1)} %collective-permute-done.9.x_odd_ref, f32[16,128]{1,0:T(8,128)S(1)} %collective-permute-done.10.y_even_ref, ...), custom_call_target="tpu_custom_call" | custom-call | tf_op jit(solution)/shard_map/pallas_call | solution.py:705
  (27 shorter events, 2.0 us)
Async XLA Ops:
  2.4 18.3 %copy-start = (f32[1,1,8,3,27,128]{5,2,4,3,1,0:T(8,128)S(1)}, f32[1,1,8,3,27,128]{5,2,4,3,1,0:T(8,128)}, u32[]{:S(2)}) copy-start(f32[1,1,8,3,27,128]{5,2,4,3,1,0:T(8,128)} %param.8) | copy-start | bytes 995332
  2.4 18.3 %all-to-all-start = ((f32[32,5,4,128]{3,2,1,0:T(4,128)}), f32[32,5,4,128]{3,2,1,0:T(4,128)S(1)}, u32[]{:S(2)}, u32[]{:S(2)}) async-start(f32[32,5,4,128]{3,2,1,0:T(4,128)} %broadcast_in_dim.18), calls=%async_computation | async-start | bytes 655360 | tf_op jit(solution)/shard_map/all_to_all | solution.py:732
  9.7 2.0 %collective-permute-start = (f32[8,4,128]{2,1,0:T(4,128)S(1)}, f32[8,4,128]{2,1,0:T(4,128)S(1)}, u32[]{:S(2)}, u32[]{:S(2)}) collective-permute-start(f32[8,4,128]{2,1,0:T(4,128)S(1)} %get-tuple-element.34), channel_id=1, source_target_pairs={{0,4},{1,5},{2,6},{3,7},{4,0},{5,1},{6,2},{7,3},{8,12},{9,13},{10,... | collective-permute-start | bytes 49160 | tf_op jit(solution)/shard_map/ppermute | solution.py:39
  10.1 5.9 %collective-permute-start.1 = (f32[8,4,128]{2,1,0:T(4,128)S(1)}, f32[8,4,128]{2,1,0:T(4,128)S(1)}, u32[]{:S(2)}, u32[]{:S(2)}) collective-permute-start(f32[8,4,128]{2,1,0:T(4,128)S(1)} %get-tuple-element.35), channel_id=1, source_target_pairs={{0,1},{1,0},{2,3},{3,2},{4,8},{5,9},{6,10},{7,11},{8,4},{9,5},{10,... | collective-permute-start | bytes 49160 | tf_op jit(solution)/shard_map/ppermute | solution.py:39
  15.9 2.6 %copy-start.3 = (s32[1,1,8,128]{3,2,1,0:T(8,128)S(1)}, s32[1,1,8,128]{3,2,1,0:T(8,128)}, u32[]{:S(2)}) copy-start(s32[1,1,8,128]{3,2,1,0:T(8,128)} %param.10) | copy-start | bytes 12292
  16.0 2.6 %copy-start.2 = (f32[1,1,8,128]{3,2,1,0:T(8,128)S(1)}, f32[1,1,8,128]{3,2,1,0:T(8,128)}, u32[]{:S(2)}) copy-start(f32[1,1,8,128]{3,2,1,0:T(8,128)} %param.9) | copy-start | bytes 12292
  16.0 2.6 %copy-start.1 = (s32[1,1,8,128]{3,2,1,0:T(8,128)S(1)}, s32[1,1,8,128]{3,2,1,0:T(8,128)}, u32[]{:S(2)}) copy-start(s32[1,1,8,128]{3,2,1,0:T(8,128)} %param.11) | copy-start | bytes 12292
  16.0 4.5 %collective-permute-start.2 = (f32[14,4,128]{2,1,0:T(4,128)S(1)}, f32[14,4,128]{2,1,0:T(4,128)S(1)}, u32[]{:S(2)}, u32[]{:S(2)}) collective-permute-start(f32[14,4,128]{2,1,0:T(4,128)S(1)} %get-tuple-element.37), channel_id=1, source_target_pairs={{0,1},{1,0},{2,3},{3,2},{4,5},{5,4},{6,7},{7,6},{8,9},{9,8},{10,11... | collective-permute-start | bytes 86024 | tf_op jit(solution)/shard_map/ppermute | solution.py:39
  18.5 2.0 %collective-permute-start.3 = (f32[14,4,128]{2,1,0:T(4,128)S(1)}, f32[14,4,128]{2,1,0:T(4,128)S(1)}, u32[]{:S(2)}, u32[]{:S(2)}) collective-permute-start(f32[14,4,128]{2,1,0:T(4,128)S(1)} %get-tuple-element.38), channel_id=1, source_target_pairs={{0,4},{1,2},{2,1},{3,7},{4,0},{5,6},{6,5},{7,3},{8,12},{9,10},{10,... | collective-permute-start | bytes 86024 | tf_op jit(solution)/shard_map/ppermute | solution.py:39
  23.4 4.4 %collective-permute-start.4 = (f32[56,128]{1,0:T(8,128)S(1)}, f32[56,128]{1,0:T(8,128)S(1)}, u32[]{:S(2)}, u32[]{:S(2)}) collective-permute-start(f32[56,128]{1,0:T(8,128)S(1)} %get-tuple-element.46), channel_id=1, source_target_pairs={{0,1},{1,0},{2,3},{3,2},{4,5},{5,4},{6,7},{7,6},{8,9},{9,8},{10,11... | collective-permute-start | bytes 86024 | tf_op jit(solution)/shard_map/ppermute | solution.py:39
  25.9 1.9 %collective-permute-start.5 = (f32[56,128]{1,0:T(8,128)S(1)}, f32[56,128]{1,0:T(8,128)S(1)}, u32[]{:S(2)}, u32[]{:S(2)}) collective-permute-start(f32[56,128]{1,0:T(8,128)S(1)} %get-tuple-element.47), channel_id=1, source_target_pairs={{0,4},{1,2},{2,1},{3,7},{4,0},{5,6},{6,5},{7,3},{8,12},{9,10},{10,... | collective-permute-start | bytes 86024 | tf_op jit(solution)/shard_map/ppermute | solution.py:39
  28.9 13.7 %all-to-all-start.1 = ((f32[32,13,1,128]{3,2,1,0:T(1,128)}), f32[32,13,1,128]{3,2,1,0:T(1,128)S(1)}, u32[]{:S(2)}, u32[]{:S(2)}) async-start(f32[32,13,1,128]{3,2,1,0:T(1,128)} %broadcast_in_dim.20), calls=%async_computation.1 | async-start | bytes 425984 | tf_op jit(solution)/shard_map/all_to_all | solution.py:732
  33.0 2.0 %collective-permute-start.6 = (f32[72,128]{1,0:T(8,128)S(1)}, f32[72,128]{1,0:T(8,128)S(1)}, u32[]{:S(2)}, u32[]{:S(2)}) collective-permute-start(f32[72,128]{1,0:T(8,128)S(1)} %get-tuple-element.53), channel_id=1, source_target_pairs={{0,4},{1,5},{2,6},{3,7},{4,0},{5,1},{6,2},{7,3},{8,12},{9,13},{10,... | collective-permute-start | bytes 110600 | tf_op jit(solution)/shard_map/ppermute | solution.py:39
  33.3 4.8 %collective-permute-start.7 = (f32[72,128]{1,0:T(8,128)S(1)}, f32[72,128]{1,0:T(8,128)S(1)}, u32[]{:S(2)}, u32[]{:S(2)}) collective-permute-start(f32[72,128]{1,0:T(8,128)S(1)} %get-tuple-element.54), channel_id=1, source_target_pairs={{0,1},{1,0},{2,3},{3,2},{4,8},{5,9},{6,10},{7,11},{8,4},{9,5},{10,... | collective-permute-start | bytes 110600 | tf_op jit(solution)/shard_map/ppermute | solution.py:39
  46.0 10.2 %all-to-all-start.2 = ((f32[32,1,4,128]{3,2,1,0:T(4,128)}), f32[32,1,4,128]{3,2,1,0:T(4,128)S(1)}, u32[]{:S(2)}, u32[]{:S(2)}) async-start(f32[32,1,4,128]{3,2,1,0:T(4,128)} %get-tuple-element.55), calls=%async_computation.2 | async-start | bytes 131072 | tf_op jit(solution)/shard_map/all_to_all | solution.py:771
  48.6 3.2 %collective-permute-start.8 = (f32[16,128]{1,0:T(8,128)S(1)}, f32[16,128]{1,0:T(8,128)S(1)}, u32[]{:S(2)}, u32[]{:S(2)}) collective-permute-start(f32[16,128]{1,0:T(8,128)S(1)} %get-tuple-element.56), channel_id=1, source_target_pairs={{0,4},{1,5},{2,6},{3,7},{4,0},{5,1},{6,2},{7,3},{8,12},{9,13},{10,... | collective-permute-start | bytes 24584 | tf_op jit(solution)/shard_map/ppermute | solution.py:39
  48.8 3.7 %collective-permute-start.9 = (f32[16,128]{1,0:T(8,128)S(1)}, f32[16,128]{1,0:T(8,128)S(1)}, u32[]{:S(2)}, u32[]{:S(2)}) collective-permute-start(f32[16,128]{1,0:T(8,128)S(1)} %get-tuple-element.57), channel_id=1, source_target_pairs={{0,1},{1,0},{2,3},{3,2},{4,8},{5,9},{6,10},{7,11},{8,4},{9,5},{10,... | collective-permute-start | bytes 24584 | tf_op jit(solution)/shard_map/ppermute | solution.py:39
  50.5 3.7 %collective-permute-start.10 = (f32[16,128]{1,0:T(8,128)S(1)}, f32[16,128]{1,0:T(8,128)S(1)}, u32[]{:S(2)}, u32[]{:S(2)}) collective-permute-start(f32[16,128]{1,0:T(8,128)S(1)} %get-tuple-element.58), channel_id=1, source_target_pairs={{0,1},{1,0},{2,3},{3,2},{4,5},{5,4},{6,7},{7,6},{8,9},{9,8},{10,11... | collective-permute-start | bytes 24584 | tf_op jit(solution)/shard_map/ppermute | solution.py:39
  50.8 3.4 %collective-permute-start.11 = (f32[16,128]{1,0:T(8,128)S(1)}, f32[16,128]{1,0:T(8,128)S(1)}, u32[]{:S(2)}, u32[]{:S(2)}) collective-permute-start(f32[16,128]{1,0:T(8,128)S(1)} %get-tuple-element.59), channel_id=1, source_target_pairs={{0,4},{1,2},{2,1},{3,7},{4,0},{5,6},{6,5},{7,3},{8,12},{9,10},{10,... | collective-permute-start | bytes 24584 | tf_op jit(solution)/shard_map/ppermute | solution.py:39

commit v10 on v9

--- a/solution.py
+++ b/solution.py
@@ -690,14 +690,16 @@
             column = slots_ref[other, 0]
             at = (end if dx > 0 else 0, end if dy > 0 else 0)
             image[at] = image[at] + place.keep(column, dx, dy, 1)
+    solution, residual = {}, {}
     for x, y in INNER:
         w = w_ref[x + 2, y + 2]
         z1 = z1_ref[x + 1, y + 1]
-        solution = step1 * z1 + step2 * (z2_ref[x, y] + ratio * z1)
-        residual = r_ref[x + 2, y + 2] - step1 * w - step2 * (image[x, y] + ratio * w)
-        for m in range(3):
-            solution_ref[m, x, y : y + 1, :] = solution[m : m + 1]
-            residual_ref[m, x, y : y + 1, :] = residual[m : m + 1]
+        solution[x, y] = step1 * z1 + step2 * (z2_ref[x, y] + ratio * z1)
+        residual[x, y] = r_ref[x + 2, y + 2] - step1 * w - step2 * (image[x, y] + ratio * w)
+    for x in range(BRICK):
+        for ref, field in ((solution_ref, solution), (residual_ref, residual)):
+            for m in range(3):
+                ref[m, x] = jnp.concatenate([field[x, y][m : m + 1] for y in range(BRICK)], axis=0)
 
 
 def call(kernel, counts, shapes, *args, scratch=()):

time: 57.5 us -> 57.5 us (level)
  no operation moved by 1% of the time
where the time goes in v10:
time: 57.5 us; the launch traced here: 57.1 us
  starting transfers between devices  26.2 us (46%)
  waiting for transfers between devices  19.7 us (34%)
  Pallas kernels  8.06 us (14%)
  local copies, waits for them, and re-layouts  1.61 us (3%)
  other arithmetic  0.76 us (1%)
  between operations  0.73 us (1%)
    ppermute x12, waiting for transfers between devices, exchange(): return (lax.ppermute(first, AXES, even), lax.ppermute(second, AXES, odd))  13.2 us
    ppermute x12, starting transfers between devices, exchange(): return (lax.ppermute(first, AXES, even), lax.ppermute(second, AXES, odd))  12.2 us
    all_to_all x2, starting transfers between devices, share(): return lax.all_to_all(sent, AXES, 0, 0).reshape(-1, LANES)  11.4 us
    pallas_call x9, Pallas kernels, call(): pl.pallas_call(functools.partial(kernel, counts), out_shape=[jax.ShapeDty...  8.06 us
    all_to_all x2, waiting for transfers between devices, share(): return lax.all_to_all(sent, AXES, 0, 0).reshape(-1, LANES)  4.58 us
    all_to_all x1, starting transfers between devices, per_device(): slots = lax.all_to_all(slots, AXES, 0, 0)  2.57 us
    all_to_all x1, waiting for transfers between devices, per_device(): slots = lax.all_to_all(slots, AXES, 0, 0)  2 us
    broadcast_in_dim x2, local copies, waits for them, and re-layouts, share(): sent = jnp.broadcast_to(slot[None], (bricks, *slot.shape))  1.58 us
  transfers between devices with their start and end apart: 15, of which 9 were waited for; matrix products, arithmetic and copies ran while one was open for 0% of the time, Pallas kernels for 1%

profile of v10, /device:TPU:0, one launch (start us, length us, event | category | flops | bytes accessed | tf_op | source)
XLA Modules:
  0.0 57.1 jit_solution(7078536733367881476)
XLA Ops:
  0.6 0.8 %pad_maximum_fusion.fields_ref = f32[4,4,4,128]{3,2,1,0:T(4,128)S(1)} fusion(f32[1,4,4,128]{3,2,1,0:T(4,128)} %bitcast.21, f32[3,4,4,128]{3,2,1,0:T(4,128)} %param.6), kind=kLoop, calls=%fused_computation | loop fusion | flops 8192 | bytes 65536 | tf_op jit(solution)/shard_map/concatenate | solution.py:736
  1.7 0.8 %broadcast_in_dim.18 = f32[32,5,4,128]{3,2,1,0:T(4,128)} broadcast(f32[5,4,128]{2,1,0:T(4,128)S(1)} %get-tuple-element.32), dimensions={1,2,3} | broadcast | bytes 337920 | tf_op jit(solution)/shard_map/broadcast_in_dim | solution.py:733
  2.4 7.3 %all-to-all-start = ((f32[32,5,4,128]{3,2,1,0:T(4,128)}), f32[32,5,4,128]{3,2,1,0:T(4,128)S(1)}, u32[]{:S(2)}, u32[]{:S(2)}) async-start(f32[32,5,4,128]{3,2,1,0:T(4,128)} %broadcast_in_dim.18), calls=%async_computation | async-start | bytes 655360 | tf_op jit(solution)/shard_map/all_to_all | solution.py:734
  9.7 0.3 collective-permute-start
  10.1 1.7 %collective-permute-start.1 = (f32[8,4,128]{2,1,0:T(4,128)S(1)}, f32[8,4,128]{2,1,0:T(4,128)S(1)}, u32[]{:S(2)}, u32[]{:S(2)}) collective-permute-start(f32[8,4,128]{2,1,0:T(4,128)S(1)} %get-tuple-element.35), channel_id=1, source_target_pairs={{0,1},{1,0},{2,3},{3,2},{4,8},{5,9},{6,10},{7,11},{8,4},{9,5},{10,... | collective-permute-start | bytes 49160 | tf_op jit(solution)/shard_map/ppermute | solution.py:39
  11.7 4.2 %collective-permute-done.1.odd_ref = f32[8,4,128]{2,1,0:T(4,128)S(1)} collective-permute-done((f32[8,4,128]{2,1,0:T(4,128)S(1)}, f32[8,4,128]{2,1,0:T(4,128)S(1)}, u32[]{:S(2)}, u32[]{:S(2)}) %collective-permute-start.1) | collective-permute-done | bytes 16416 | tf_op jit(solution)/shard_map/ppermute | solution.py:39
  16.0 2.5 %collective-permute-start.2 = (f32[14,4,128]{2,1,0:T(4,128)S(1)}, f32[14,4,128]{2,1,0:T(4,128)S(1)}, u32[]{:S(2)}, u32[]{:S(2)}) collective-permute-start(f32[14,4,128]{2,1,0:T(4,128)S(1)} %get-tuple-element.37), channel_id=1, source_target_pairs={{0,1},{1,0},{2,3},{3,2},{4,5},{5,4},{6,7},{7,6},{8,9},{9,8},{10,11... | collective-permute-start | bytes 86024 | tf_op jit(solution)/shard_map/ppermute | solution.py:39
  18.9 1.6 %collective-permute-done.2.even_ref = f32[14,4,128]{2,1,0:T(4,128)S(1)} collective-permute-done((f32[14,4,128]{2,1,0:T(4,128)S(1)}, f32[14,4,128]{2,1,0:T(4,128)S(1)}, u32[]{:S(2)}, u32[]{:S(2)}) %collective-permute-start.2) | collective-permute-done | bytes 28704 | tf_op jit(solution)/shard_map/ppermute | solution.py:39
  20.7 2.7 %shard_map.81 = (f32[6,6,4,128]{3,2,1,0:T(4,128)S(1)}, f32[6,6,4,128]{3,2,1,0:T(4,128)S(1)}, f32[56,128]{1,0:T(8,128)S(1)}, f32[56,128]{1,0:T(8,128)S(1)}, f32[1...) custom-call(f32[640,128]{1,0:T(8,128)S(1)} %bitcast.16, f32[8,8,4,128]{3,2,1,0:T(4,128)S(1)} %get-tuple-element.39.r_ref, ...), custom_call_target="tpu_custom_call" | custom-call | tf_op jit(solution)/shard_map/pallas_call | solution.py:707
  23.4 2.5 %collective-permute-start.4 = (f32[56,128]{1,0:T(8,128)S(1)}, f32[56,128]{1,0:T(8,128)S(1)}, u32[]{:S(2)}, u32[]{:S(2)}) collective-permute-start(f32[56,128]{1,0:T(8,128)S(1)} %get-tuple-element.46), channel_id=1, source_target_pairs={{0,1},{1,0},{2,3},{3,2},{4,5},{5,4},{6,7},{7,6},{8,9},{9,8},{10,11... | collective-permute-start | bytes 86024 | tf_op jit(solution)/shard_map/ppermute | solution.py:39
  25.9 1.8 %collective-permute-done.4.even_ref = f32[56,128]{1,0:T(8,128)S(1)} collective-permute-done((f32[56,128]{1,0:T(8,128)S(1)}, f32[56,128]{1,0:T(8,128)S(1)}, u32[]{:S(2)}, u32[]{:S(2)}) %collective-permute-start.4) | collective-permute-done | bytes 28704 | tf_op jit(solution)/shard_map/ppermute | solution.py:39
  28.1 0.8 %broadcast_in_dim.20 = f32[32,13,1,128]{3,2,1,0:T(1,128)} broadcast(f32[13,128]{1,0:T(8,128)S(1)} %bitcast.20), dimensions={1,3} | broadcast | bytes 219648 | tf_op jit(solution)/shard_map/broadcast_in_dim | solution.py:733
  28.9 4.1 %all-to-all-start.1 = ((f32[32,13,1,128]{3,2,1,0:T(1,128)}), f32[32,13,1,128]{3,2,1,0:T(1,128)S(1)}, u32[]{:S(2)}, u32[]{:S(2)}) async-start(f32[32,13,1,128]{3,2,1,0:T(1,128)} %broadcast_in_dim.20), calls=%async_computation.1 | async-start | bytes 425984 | tf_op jit(solution)/shard_map/all_to_all | solution.py:734
  33.3 1.7 %collective-permute-start.7 = (f32[72,128]{1,0:T(8,128)S(1)}, f32[72,128]{1,0:T(8,128)S(1)}, u32[]{:S(2)}, u32[]{:S(2)}) collective-permute-start(f32[72,128]{1,0:T(8,128)S(1)} %get-tuple-element.54), channel_id=1, source_target_pairs={{0,1},{1,0},{2,3},{3,2},{4,8},{5,9},{6,10},{7,11},{8,4},{9,5},{10,... | collective-permute-start | bytes 110600 | tf_op jit(solution)/shard_map/ppermute | solution.py:39
  35.0 3.1 %collective-permute-done.7.odd_ref = f32[72,128]{1,0:T(8,128)S(1)} collective-permute-done((f32[72,128]{1,0:T(8,128)S(1)}, f32[72,128]{1,0:T(8,128)S(1)}, u32[]{:S(2)}, u32[]{:S(2)}) %collective-permute-start.7) | collective-permute-done | bytes 36896 | tf_op jit(solution)/shard_map/ppermute | solution.py:39
  38.2 4.4 %all-to-all-done.1 = f32[32,13,1,128]{3,2,1,0:T(1,128)S(1)} async-done(((f32[32,13,1,128]{3,2,1,0:T(1,128)}), f32[32,13,1,128]{3,2,1,0:T(1,128)S(1)}, u32[]{:S(2)}, u32[]{:S(2)}) %all-to-all-start.1) | async-done | bytes 213024 | tf_op jit(solution)/shard_map/all_to_all | solution.py:734
  42.6 3.4 %shard_map.84 = (f32[4,4,4,128]{3,2,1,0:T(4,128)S(1)}, f32[4,4,4,128]{3,2,1,0:T(4,128)S(1)}, f32[16,128]{1,0:T(8,128)S(1)}, f32[16,128]{1,0:T(8,128)S(1)}, f32[1...) custom-call(f32[416,128]{1,0:T(8,128)S(1)} %bitcast.12, ...), custom_call_target="tpu_custom_call" | custom-call | tf_op jit(solution)/shard_map/pallas_call | solution.py:707
  46.0 2.6 %all-to-all-start.2 = ((f32[32,1,4,128]{3,2,1,0:T(4,128)}), f32[32,1,4,128]{3,2,1,0:T(4,128)S(1)}, u32[]{:S(2)}, u32[]{:S(2)}) async-start(f32[32,1,4,128]{3,2,1,0:T(4,128)} %get-tuple-element.55), calls=%async_computation.2 | async-start | bytes 131072 | tf_op jit(solution)/shard_map/all_to_all | solution.py:773
  48.8 1.7 %collective-permute-start.9 = (f32[16,128]{1,0:T(8,128)S(1)}, f32[16,128]{1,0:T(8,128)S(1)}, u32[]{:S(2)}, u32[]{:S(2)}) collective-permute-start(f32[16,128]{1,0:T(8,128)S(1)} %get-tuple-element.57), channel_id=1, source_target_pairs={{0,1},{1,0},{2,3},{3,2},{4,8},{5,9},{6,10},{7,11},{8,4},{9,5},{10,... | collective-permute-start | bytes 24584 | tf_op jit(solution)/shard_map/ppermute | solution.py:39
  50.8 1.0 %collective-permute-start.11 = (f32[16,128]{1,0:T(8,128)S(1)}, f32[16,128]{1,0:T(8,128)S(1)}, u32[]{:S(2)}, u32[]{:S(2)}) collective-permute-start(f32[16,128]{1,0:T(8,128)S(1)} %get-tuple-element.59), channel_id=1, source_target_pairs={{0,4},{1,2},{2,1},{3,7},{4,0},{5,6},{6,5},{7,3},{8,12},{9,10},{10,... | collective-permute-start | bytes 24584 | tf_op jit(solution)/shard_map/ppermute | solution.py:39
  51.8 0.6 %collective-permute-done.9.x_odd_ref = f32[16,128]{1,0:T(8,128)S(1)} collective-permute-done((f32[16,128]{1,0:T(8,128)S(1)}, f32[16,128]{1,0:T(8,128)S(1)}, u32[]{:S(2)}, u32[]{:S(2)}) %collective-permute-start.9) | collective-permute-done | bytes 8224 | tf_op jit(solution)/shard_map/ppermute | solution.py:39
  52.4 1.7 %collective-permute-done.10.y_even_ref = f32[16,128]{1,0:T(8,128)S(1)} collective-permute-done((f32[16,128]{1,0:T(8,128)S(1)}, f32[16,128]{1,0:T(8,128)S(1)}, u32[]{:S(2)}, u32[]{:S(2)}) %collective-permute-start.10) | collective-permute-done | bytes 8224 | tf_op jit(solution)/shard_map/ppermute | solution.py:39
  54.2 2.0 %all-to-all-done.2.slots_ref = f32[32,1,4,128]{3,2,1,0:T(4,128)S(1)} async-done(((f32[32,1,4,128]{3,2,1,0:T(4,128)}), f32[32,1,4,128]{3,2,1,0:T(4,128)S(1)}, u32[]{:S(2)}, u32[]{:S(2)}) %all-to-all-start.2) | async-done | bytes 65568 | tf_op jit(solution)/shard_map/all_to_all | solution.py:773
  56.2 0.9 %shard_map.85 = (f32[3,4,4,128]{3,2,1,0:T(4,128)}, f32[3,4,4,128]{3,2,1,0:T(4,128)}) custom-call(f32[32,1,4,128]{3,2,1,0:T(4,128)S(1)} %all-to-all-done.2.slots_ref, f32[16,128]{1,0:T(8,128)S(1)} %collective-permute-done.8.x_even_ref, f32[16,128]{1,0:T(8,128)S(1)} %collective-permute-done.9.x_odd_ref, f32[16,128]{1,0:T(8,128)S(1)} %collective-permute-done.10.y_even_ref, ...), custom_call_target="tpu_custom_call" | custom-call | tf_op jit(solution)/shard_map/pallas_call | solution.py:707
  (27 shorter events, 2.0 us)
Async XLA Ops:
  2.4 18.3 %copy-start = (f32[1,1,8,3,27,128]{5,2,4,3,1,0:T(8,128)S(1)}, f32[1,1,8,3,27,128]{5,2,4,3,1,0:T(8,128)}, u32[]{:S(2)}) copy-start(f32[1,1,8,3,27,128]{5,2,4,3,1,0:T(8,128)} %param.8) | copy-start | bytes 995332
  2.4 18.3 %all-to-all-start = ((f32[32,5,4,128]{3,2,1,0:T(4,128)}), f32[32,5,4,128]{3,2,1,0:T(4,128)S(1)}, u32[]{:S(2)}, u32[]{:S(2)}) async-start(f32[32,5,4,128]{3,2,1,0:T(4,128)} %broadcast_in_dim.18), calls=%async_computation | async-start | bytes 655360 | tf_op jit(solution)/shard_map/all_to_all | solution.py:734
  9.7 2.0 %collective-permute-start = (f32[8,4,128]{2,1,0:T(4,128)S(1)}, f32[8,4,128]{2,1,0:T(4,128)S(1)}, u32[]{:S(2)}, u32[]{:S(2)}) collective-permute-start(f32[8,4,128]{2,1,0:T(4,128)S(1)} %get-tuple-element.34), channel_id=1, source_target_pairs={{0,4},{1,5},{2,6},{3,7},{4,0},{5,1},{6,2},{7,3},{8,12},{9,13},{10,... | collective-permute-start | bytes 49160 | tf_op jit(solution)/shard_map/ppermute | solution.py:39
  10.1 5.9 %collective-permute-start.1 = (f32[8,4,128]{2,1,0:T(4,128)S(1)}, f32[8,4,128]{2,1,0:T(4,128)S(1)}, u32[]{:S(2)}, u32[]{:S(2)}) collective-permute-start(f32[8,4,128]{2,1,0:T(4,128)S(1)} %get-tuple-element.35), channel_id=1, source_target_pairs={{0,1},{1,0},{2,3},{3,2},{4,8},{5,9},{6,10},{7,11},{8,4},{9,5},{10,... | collective-permute-start | bytes 49160 | tf_op jit(solution)/shard_map/ppermute | solution.py:39
  15.9 2.6 %copy-start.3 = (s32[1,1,8,128]{3,2,1,0:T(8,128)S(1)}, s32[1,1,8,128]{3,2,1,0:T(8,128)}, u32[]{:S(2)}) copy-start(s32[1,1,8,128]{3,2,1,0:T(8,128)} %param.10) | copy-start | bytes 12292
  16.0 2.6 %copy-start.2 = (f32[1,1,8,128]{3,2,1,0:T(8,128)S(1)}, f32[1,1,8,128]{3,2,1,0:T(8,128)}, u32[]{:S(2)}) copy-start(f32[1,1,8,128]{3,2,1,0:T(8,128)} %param.9) | copy-start | bytes 12292
  16.0 2.6 %copy-start.1 = (s32[1,1,8,128]{3,2,1,0:T(8,128)S(1)}, s32[1,1,8,128]{3,2,1,0:T(8,128)}, u32[]{:S(2)}) copy-start(s32[1,1,8,128]{3,2,1,0:T(8,128)} %param.11) | copy-start | bytes 12292
  16.0 4.5 %collective-permute-start.2 = (f32[14,4,128]{2,1,0:T(4,128)S(1)}, f32[14,4,128]{2,1,0:T(4,128)S(1)}, u32[]{:S(2)}, u32[]{:S(2)}) collective-permute-start(f32[14,4,128]{2,1,0:T(4,128)S(1)} %get-tuple-element.37), channel_id=1, source_target_pairs={{0,1},{1,0},{2,3},{3,2},{4,5},{5,4},{6,7},{7,6},{8,9},{9,8},{10,11... | collective-permute-start | bytes 86024 | tf_op jit(solution)/shard_map/ppermute | solution.py:39
  18.5 2.0 %collective-permute-start.3 = (f32[14,4,128]{2,1,0:T(4,128)S(1)}, f32[14,4,128]{2,1,0:T(4,128)S(1)}, u32[]{:S(2)}, u32[]{:S(2)}) collective-permute-start(f32[14,4,128]{2,1,0:T(4,128)S(1)} %get-tuple-element.38), channel_id=1, source_target_pairs={{0,4},{1,2},{2,1},{3,7},{4,0},{5,6},{6,5},{7,3},{8,12},{9,10},{10,... | collective-permute-start | bytes 86024 | tf_op jit(solution)/shard_map/ppermute | solution.py:39
  23.4 4.4 %collective-permute-start.4 = (f32[56,128]{1,0:T(8,128)S(1)}, f32[56,128]{1,0:T(8,128)S(1)}, u32[]{:S(2)}, u32[]{:S(2)}) collective-permute-start(f32[56,128]{1,0:T(8,128)S(1)} %get-tuple-element.46), channel_id=1, source_target_pairs={{0,1},{1,0},{2,3},{3,2},{4,5},{5,4},{6,7},{7,6},{8,9},{9,8},{10,11... | collective-permute-start | bytes 86024 | tf_op jit(solution)/shard_map/ppermute | solution.py:39
  25.9 1.9 %collective-permute-start.5 = (f32[56,128]{1,0:T(8,128)S(1)}, f32[56,128]{1,0:T(8,128)S(1)}, u32[]{:S(2)}, u32[]{:S(2)}) collective-permute-start(f32[56,128]{1,0:T(8,128)S(1)} %get-tuple-element.47), channel_id=1, source_target_pairs={{0,4},{1,2},{2,1},{3,7},{4,0},{5,6},{6,5},{7,3},{8,12},{9,10},{10,... | collective-permute-start | bytes 86024 | tf_op jit(solution)/shard_map/ppermute | solution.py:39
  28.9 13.7 %all-to-all-start.1 = ((f32[32,13,1,128]{3,2,1,0:T(1,128)}), f32[32,13,1,128]{3,2,1,0:T(1,128)S(1)}, u32[]{:S(2)}, u32[]{:S(2)}) async-start(f32[32,13,1,128]{3,2,1,0:T(1,128)} %broadcast_in_dim.20), calls=%async_computation.1 | async-start | bytes 425984 | tf_op jit(solution)/shard_map/all_to_all | solution.py:734
  33.0 2.0 %collective-permute-start.6 = (f32[72,128]{1,0:T(8,128)S(1)}, f32[72,128]{1,0:T(8,128)S(1)}, u32[]{:S(2)}, u32[]{:S(2)}) collective-permute-start(f32[72,128]{1,0:T(8,128)S(1)} %get-tuple-element.53), channel_id=1, source_target_pairs={{0,4},{1,5},{2,6},{3,7},{4,0},{5,1},{6,2},{7,3},{8,12},{9,13},{10,... | collective-permute-start | bytes 110600 | tf_op jit(solution)/shard_map/ppermute | solution.py:39
  33.3 4.8 %collective-permute-start.7 = (f32[72,128]{1,0:T(8,128)S(1)}, f32[72,128]{1,0:T(8,128)S(1)}, u32[]{:S(2)}, u32[]{:S(2)}) collective-permute-start(f32[72,128]{1,0:T(8,128)S(1)} %get-tuple-element.54), channel_id=1, source_target_pairs={{0,1},{1,0},{2,3},{3,2},{4,8},{5,9},{6,10},{7,11},{8,4},{9,5},{10,... | collective-permute-start | bytes 110600 | tf_op jit(solution)/shard_map/ppermute | solution.py:39
  46.0 10.2 %all-to-all-start.2 = ((f32[32,1,4,128]{3,2,1,0:T(4,128)}), f32[32,1,4,128]{3,2,1,0:T(4,128)S(1)}, u32[]{:S(2)}, u32[]{:S(2)}) async-start(f32[32,1,4,128]{3,2,1,0:T(4,128)} %get-tuple-element.55), calls=%async_computation.2 | async-start | bytes 131072 | tf_op jit(solution)/shard_map/all_to_all | solution.py:773
  48.6 3.2 %collective-permute-start.8 = (f32[16,128]{1,0:T(8,128)S(1)}, f32[16,128]{1,0:T(8,128)S(1)}, u32[]{:S(2)}, u32[]{:S(2)}) collective-permute-start(f32[16,128]{1,0:T(8,128)S(1)} %get-tuple-element.56), channel_id=1, source_target_pairs={{0,4},{1,5},{2,6},{3,7},{4,0},{5,1},{6,2},{7,3},{8,12},{9,13},{10,... | collective-permute-start | bytes 24584 | tf_op jit(solution)/shard_map/ppermute | solution.py:39
  48.8 3.7 %collective-permute-start.9 = (f32[16,128]{1,0:T(8,128)S(1)}, f32[16,128]{1,0:T(8,128)S(1)}, u32[]{:S(2)}, u32[]{:S(2)}) collective-permute-start(f32[16,128]{1,0:T(8,128)S(1)} %get-tuple-element.57), channel_id=1, source_target_pairs={{0,1},{1,0},{2,3},{3,2},{4,8},{5,9},{6,10},{7,11},{8,4},{9,5},{10,... | collective-permute-start | bytes 24584 | tf_op jit(solution)/shard_map/ppermute | solution.py:39
  50.5 3.7 %collective-permute-start.10 = (f32[16,128]{1,0:T(8,128)S(1)}, f32[16,128]{1,0:T(8,128)S(1)}, u32[]{:S(2)}, u32[]{:S(2)}) collective-permute-start(f32[16,128]{1,0:T(8,128)S(1)} %get-tuple-element.58), channel_id=1, source_target_pairs={{0,1},{1,0},{2,3},{3,2},{4,5},{5,4},{6,7},{7,6},{8,9},{9,8},{10,11... | collective-permute-start | bytes 24584 | tf_op jit(solution)/shard_map/ppermute | solution.py:39
  50.8 3.4 %collective-permute-start.11 = (f32[16,128]{1,0:T(8,128)S(1)}, f32[16,128]{1,0:T(8,128)S(1)}, u32[]{:S(2)}, u32[]{:S(2)}) collective-permute-start(f32[16,128]{1,0:T(8,128)S(1)} %get-tuple-element.59), channel_id=1, source_target_pairs={{0,4},{1,2},{2,1},{3,7},{4,0},{5,6},{6,5},{7,3},{8,12},{9,10},{10,... | collective-permute-start | bytes 24584 | tf_op jit(solution)/shard_map/ppermute | solution.py:39
